TPU v7x, 32 devices: a whole 2x2x4 slice. The times are simulated.
32 devices in a mesh: groups: 2 (over y), row: 4 (over z), col: 4 (over x, core).
Axes of the slice: x: 2, y: 2, z: 4, core: 2. Of those that a mesh axis runs over, the one named last changes fastest.
Arguments:
- b_occ_i: bfloat16 [12, 2048, 6144], P('groups', 'row', 'col'), parts along dimension 0, may hold values from -0.625 to 0.625
- b_occ_j: bfloat16 [4, 2048, 6144], P('groups', 'row', 'col'), parts along dimension 0, may hold values from -0.625 to 0.625
- eps_occ_i: float32 [12], P('groups'), parts along dimension 0, may hold values from -1.5 to -0.4
- eps_occ_j: float32 [4], P('groups'), parts along dimension 0, may hold values from -1.5 to -0.4
- eps_vir: float32 [4096], P('groups'), parts along dimension 0, may hold values from 0.2 to 4
Outputs:
- gamma: float32 [12, 2048, 6144], P('groups', 'row', 'col'), parts along dimension 0
There are 2 independent parts, one for each index of `groups`. A program takes and returns all parts, laid end to end along the dimension named above; each array names one. Nothing has to cross between parts.
All inputs are finite; a program needn't handle non-finite values.
Results may differ from a plain program's by a relative error of at most 0.01.
Values may be sent and summed in bfloat16 or wider, within the bound.
No kernel may reach another device: no remote copies, remote signals or barrier semaphores. Data moves between devices by JAX's collectives and lax.ppermute only.
A program may use at most 320 MiB of HBM per device.

v0:
```python
import jax
import jax.numpy as jnp
from jax import lax
from jax.sharding import PartitionSpec as P


def combine_pair(amplitudes, mirror_amps):
    return (2.0 * amplitudes.astype(jnp.float32) - mirror_amps.astype(jnp.float32)).astype(
        jnp.bfloat16
    )


def mirror_full(amplitudes):
    swapped = lax.all_to_all(amplitudes, "row", split_axis=3, concat_axis=2, tiled=True)
    return combine_pair(amplitudes, jnp.swapaxes(swapped, 2, 3))


def per_device(b_occ_i, b_occ_j, eps_occ_i, eps_occ_j, eps_vir):
    rows = b_occ_i.shape[1]
    own_energy = lax.dynamic_slice_in_dim(eps_vir, lax.axis_index("row") * rows, rows, 0)
    gathered = lax.all_gather(b_occ_j, "row", axis=1, tiled=True)
    partial_value = jnp.einsum(
        "iap,jbp->jiab", b_occ_i, gathered, preferred_element_type=jnp.float32
    )
    totals = lax.psum(partial_value.astype(jnp.bfloat16), "col").astype(jnp.float32)
    denominator = (
        eps_occ_j[:, None, None, None]
        + eps_occ_i[None, :, None, None]
        - own_energy[None, None, :, None]
        - eps_vir[None, None, None, :]
    )
    combined = mirror_full((totals / denominator).astype(jnp.bfloat16))
    gamma = jnp.einsum("jiab,jbp->iap", combined, gathered, preferred_element_type=jnp.float32)
    return gamma


def solution(mesh):
    placed = (
        P("groups", "row", "col"),
        P("groups", "row", "col"),
        P("groups"),
        P("groups"),
        P("groups"),
    )
    return jax.shard_map(
        per_device, mesh=mesh, in_specs=placed, out_specs=P("groups", "row", "col"), check_vma=False
    )
```

profile of v0, /device:TPU:1, one launch (start us, length us, event | category | flops | bytes accessed | tf_op | source)
XLA Modules:
  0.0 1469.2 jit_solution(16822701788601795534)
XLA Ops:
  6.5 0.0 all-gather.2.cloned.1.call-start
  6.5 0.7 all-gather.2.cloned.1.call-update
  7.3 0.0 all-reduce.2.cloned.1.call-start
  7.3 222.2 %all-gather.2.cloned.1.call-done = bf16[2,2048,1536]{2,1,0:T(8,128)(2,1)} async-done(((bf16[2,512,1536]{2,1,0:T(8,128)(2,1)}), bf16[2,2048,1536]{2,1,0:T(8,128)(2,1)}) %all-gather.2.cloned.1.call-update) | async-done | bytes 12582928 | tf_op jit(solution)/shard_map/all_gather | solution.py:21
  229.5 46.5 %convert_bitcast_fusion = bf16[2,6,512,2048]{2,3,1,0:T(8,128)(2,1)} fusion(bf16[2,2048,1536]{2,1,0:T(8,128)(2,1)} %all-gather.2.cloned.1.call-done, bf16[6,512,1536]{2,1,0:T(8,128)(2,1)} %param.5), kind=kOutput, calls=%fused_computation.3 | convolution fusion | flops 38667288576 | bytes 47185920 | tf_op jit(solution)/shard_map/iap,jbp->jiab/dot_general | solution.py:22
  276.0 0.0 copy-start
  276.0 0.0 copy-start.1
  276.0 0.0 copy-start.2
  276.0 0.0 all-reduce.2.cloned.1.call-update
  276.0 0.7 copy-done
  276.6 0.1 dynamic_slice.3
  276.7 0.0 copy-done.1
  276.7 0.0 copy-done.2
  276.7 0.1 broadcast_add_fusion
  276.8 0.1 broadcast_subtract_fusion
  276.9 419.9 %all-reduce.2.cloned.1.call-done = bf16[2,6,512,2048]{2,3,1,0:T(8,128)(2,1)} async-done(((bf16[2,6,512,2048]{2,3,1,0:T(8,128)(2,1)}), bf16[2,6,512,2048]{2,3,1,0:T(8,128)(2,1)}) %all-reduce.2.cloned.1.call-update) | async-done | bytes 25165840 | tf_op jit(solution)/shard_map/psum | solution.py:25
  696.8 24.6 %divide_convert_fusion = bf16[2,6,512,2048]{2,3,1,0:T(8,128)(2,1)} fusion(bf16[2,6,512,2048]{2,3,1,0:T(8,128)(2,1)} %all-reduce.2.cloned.1.call-done, f32[2048]{0:T(1024)S(1)} %copy-done, f32[2,6,512]{2,1,0:T(8,128)S(1)} %broadcast_subtract_fusion), kind=kLoop, calls=%fused_computation.2 | loop fusion | flops 50331648 | bytes 50364416 | tf_op jit(solution)/shard_map/convert_element_type | solution.py:32
  721.3 44.9 %copy.11 = bf16[2,6,512,2048]{2,0,1,3:T(2,128)(2,1)S(1)} copy(bf16[2,6,512,2048]{2,3,1,0:T(8,128)(2,1)} %divide_convert_fusion) | data formatting | bytes 50331648 | tf_op jit(solution)/shard_map/convert_element_type | solution.py:32
  766.2 546.9 %all_to_all.4 = bf16[2,6,512,2048]{2,0,1,3:T(2,128)(2,1)} all-to-all(bf16[2,6,512,2048]{2,0,1,3:T(2,128)(2,1)S(1)} %copy.11), channel_id=1, replica_groups=mesh['groups'=2,'row'=4,'col'=4] {'row'}, dimensions={3} | all-to-all | bytes 50331648 | tf_op jit(solution)/shard_map/all_to_all | solution.py:14
  1313.1 67.8 %copy.12 = f32[2,6,512,4,512]{4,2,3,1,0:T(8,128)} copy(bf16[2,6,512,4,512]{2,0,1,4,3:T(2,128)(2,1)} %bitcast.27) | data formatting | bytes 75497472 | tf_op jit(solution)/shard_map/convert_element_type | solution.py:8
  1380.9 32.9 %fusion = bf16[2,6,512,2048]{2,3,1,0:T(8,128)(2,1)} fusion(f32[2,6,512,4,512]{4,2,3,1,0:T(8,128)} %copy.12, f32[2048]{0:T(1024)S(1)} %copy-done, f32[2,6,512]{2,1,0:T(8,128)S(1)} %broadcast_subtract_fusion, bf16[2,6,512,2048]{2,3,1,0:T(8,128)(2,1)} %all-reduce.2.cloned.1.call-done), kind=kLoop, calls=%fused_computation.1 | loop fusion | flops 100663296 | bytes 100696064 | tf_op jit(solution)/shard_map/convert_element_type | solution.py:8
  1413.8 48.6 %fusion.5 = f32[6,512,1536]{2,1,0:T(8,128)} fusion(bf16[2,6,512,2048]{2,3,1,0:T(8,128)(2,1)} %fusion, bf16[2,2048,1536]{2,1,0:T(8,128)(2,1)} %all-gather.2.cloned.1.call-done), kind=kOutput, calls=%fused_computation.8 | convolution fusion | flops 38654705664 | bytes 56623104 | tf_op jit(solution)/shard_map/jiab,jbp->iap/dot_general | solution.py:33
Async XLA Ops:
  6.5 222.9 %all-gather.2.cloned.1.call-start = ((), (), s32[]{:S(2)}) async-start(), calls=%async_computation.1 | async-start | bytes 15728640 | tf_op jit(solution)/shard_map/all_gather | solution.py:21
  7.3 689.5 %all-reduce.2.cloned.1.call-start = ((), (), s32[]{:S(2)}) async-start(), calls=%async_computation.2 | async-start | bytes 50331648 | tf_op jit(solution)/shard_map/psum | solution.py:25
  276.0 0.7 copy-start
  276.0 0.8 copy-start.1
  276.0 0.8 copy-start.2
Sparse Core Ops, SparseCore 0:
  8.9 220.4 all-gather.1
  276.1 420.6 all-reduce.1
where the time goes:
time: 1470 us
  waiting for transfers between devices  643 us (44%)
  blocking collectives  547 us (37%)
  local copies, waits for them, and re-layouts  113 us (8%)
  matrix products  95.1 us (6%)
  other arithmetic  57.6 us (4%)
    all_to_all x1, blocking collectives, mirror_full(): lax.all_to_all(amplitudes, 'row', split_axis=3, concat_axis=2, tiled=True)  547 us
    psum x1, waiting for transfers between devices, per_device(): lax.psum(partial_value.astype(jnp.bfloat16), 'col').astype(jnp.float32)  420 us
    all_gather x1, waiting for transfers between devices, per_device(): gathered = lax.all_gather(b_occ_j, 'row', axis=1, tiled=True)  222 us
    convert_element_type x1, local copies, waits for them, and re-layouts, combine_pair(): mirror_amps.astype(jnp.float32)  67.8 us
    dot_general x1, matrix products, per_device(): jnp.einsum('jiab,jbp->iap', combined, gathered, preferred_element_type=jn...  48.6 us
    dot_general x1, matrix products, per_device(): jnp.einsum('iap,jbp->jiab', b_occ_i, gathered, preferred_element_type=jnp...  46.5 us
    convert_element_type x1, local copies, waits for them, and re-layouts, per_device(): combined = mirror_full((totals / denominator).astype(jnp.bfloat16))  44.9 us
    convert_element_type x1, other arithmetic, combine_pair(): (2.0 * amplitudes.astype(jnp.float32) - mirror_amps.astype(jnp.float32))....  32.9 us
  transfers between devices with their start and end apart: 2, of which 2 were waited for; matrix products, arithmetic and copies ran while one was open for 0% of the time, Pallas kernels for 0%

commit v1 on v0

v1 whole, which is shorter than its diff:
```python
import functools

import jax
import jax.numpy as jnp
from jax import lax
from jax.experimental import pallas as pl
from jax.experimental.pallas import tpu as pltpu
from jax.sharding import PartitionSpec as P

F32 = jnp.float32
BF16 = jnp.bfloat16
ANY = pl.BlockSpec(memory_space=pl.ANY)
PARAMS = pltpu.CompilerParams(vmem_limit_bytes=48 * 2**20)


def cost(flops, *arrays):
    size = sum(a.size * a.dtype.itemsize for a in arrays)
    return pl.CostEstimate(flops=flops, bytes_accessed=size, transcendentals=0)


def times_transposed(left, right):
    return lax.dot_general(left, right, (((1,), (1,)), ((), ())), preferred_element_type=F32)


def send_kernel(place, b_i, block, out):
    out[0, 0] = times_transposed(b_i[0], block[0]).astype(BF16)


def pairs_for_core(place, b_i, block):
    n_j, cols, depth = block.shape
    half, rows = b_i.shape[0] // 2, b_i.shape[1]
    out = jax.ShapeDtypeStruct((n_j, half, rows, cols), BF16)
    return pl.pallas_call(
        send_kernel,
        out_shape=out,
        grid_spec=pltpu.PrefetchScalarGridSpec(
            num_scalar_prefetch=1,
            grid=(half, n_j),
            in_specs=[
                pl.BlockSpec((1, rows, depth), lambda i, j, s: ((1 - s[1]) * half + i, 0, 0)),
                pl.BlockSpec((1, cols, depth), lambda i, j, s: (j, 0, 0)),
            ],
            out_specs=pl.BlockSpec((1, 1, rows, cols), lambda i, j, s: (j, i, 0, 0)),
        ),
        compiler_params=PARAMS,
        cost_estimate=cost(2 * n_j * half * rows * cols * depth, b_i, block, out),
        name="pairs_for_core",
    )(place, b_i, block)


def chip_kernel(place, b_i, block, core, out):
    out[0] = (times_transposed(b_i[0], block[0]) + core[0, 0].astype(F32)).astype(BF16)


def pairs_for_chip(place, b_i, block, core):
    n_j, cols, depth = block.shape
    half, rows = b_i.shape[0] // 2, b_i.shape[1]
    out = jax.ShapeDtypeStruct((half, rows, cols), BF16)
    return pl.pallas_call(
        chip_kernel,
        out_shape=out,
        grid_spec=pltpu.PrefetchScalarGridSpec(
            num_scalar_prefetch=1,
            grid=(half,),
            in_specs=[
                pl.BlockSpec((1, rows, depth), lambda i, s: (s[1] * half + i, 0, 0)),
                pl.BlockSpec((1, cols, depth), lambda i, s: (1 - s[0], 0, 0)),
                pl.BlockSpec((1, 1, rows, cols), lambda i, s: (1 - s[0], i, 0, 0)),
            ],
            out_specs=pl.BlockSpec((1, rows, cols), lambda i, s: (i, 0, 0)),
        ),
        compiler_params=PARAMS,
        cost_estimate=cost(2 * half * rows * cols * depth, out, out, out),
        name="pairs_for_chip",
    )(place, b_i, block, core)


def own_kernel(place, occ, b_i, block, core, chip, vir_a, vir_b, out):
    total = times_transposed(b_i[0], block[0]) + core[0, 0].astype(F32) + chip[0].astype(F32)
    denominator = (occ[pl.program_id(0)] - vir_a[...]) - vir_b[...]
    out[0] = (total / denominator).astype(BF16)


def own_amplitudes(place, occ, b_i, block, core, chip, vir_a, vir_b):
    n_j, cols, depth = block.shape
    half, rows = b_i.shape[0] // 2, b_i.shape[1]
    out = jax.ShapeDtypeStruct((half, rows, cols), BF16)
    return pl.pallas_call(
        own_kernel,
        out_shape=out,
        grid_spec=pltpu.PrefetchScalarGridSpec(
            num_scalar_prefetch=2,
            grid=(half,),
            in_specs=[
                pl.BlockSpec((1, rows, depth), lambda i, s, o: (s[1] * half + i, 0, 0)),
                pl.BlockSpec((1, cols, depth), lambda i, s, o: (s[0], 0, 0)),
                pl.BlockSpec((1, 1, rows, cols), lambda i, s, o: (s[0], i, 0, 0)),
                pl.BlockSpec((1, rows, cols), lambda i, s, o: (i, 0, 0)),
                pl.BlockSpec((rows, 1), lambda i, s, o: (0, 0)),
                pl.BlockSpec((1, cols), lambda i, s, o: (0, 0)),
            ],
            out_specs=pl.BlockSpec((1, rows, cols), lambda i, s, o: (i, 0, 0)),
        ),
        compiler_params=PARAMS,
        cost_estimate=cost(2 * half * rows * cols * depth, out, out, out),
        name="own_amplitudes",
    )(place, occ, b_i, block, core, chip, vir_a, vir_b)


def combine_kernel(held, mirror, out):
    out[0] = (2.0 * held[0].astype(F32) - mirror[0].astype(F32).T).astype(BF16)


def combine_pairs(held, mirror):
    spec = pl.BlockSpec((1,) + held.shape[1:], lambda i: (i, 0, 0))
    return pl.pallas_call(
        combine_kernel,
        out_shape=jax.ShapeDtypeStruct(held.shape, BF16),
        grid=(held.shape[0],),
        in_specs=[spec, spec],
        out_specs=spec,
        compiler_params=PARAMS,
        cost_estimate=cost(0, held, mirror, held),
        name="combine_pairs",
    )(held, mirror)


def gamma_kernel(has_sum, place, same_j, other_j, block, *rest):
    x = place[0]
    total = jnp.dot(same_j[0], block[x], preferred_element_type=F32)
    total += jnp.dot(other_j[0], block[1 - x], preferred_element_type=F32)
    if has_sum:
        total += rest[0][0]
    rest[-1][0] = total


def add_gamma(place, mine, same_j, other_j, block, shape, before, fresh):
    n_j, cols, depth = block.shape
    half, rows = same_j.shape[0], same_j.shape[1]
    tile = depth // 2 if depth % 256 == 0 else depth

    def target(p, i, s):
        return (s[1] if mine else 1 - s[1]) * half + i, 0, p

    pair = pl.BlockSpec((1, rows, cols), lambda p, i, s: (i, 0, 0))
    out_spec = pl.BlockSpec((1, rows, tile), target)
    in_specs = [pair, pair, pl.BlockSpec((n_j, cols, tile), lambda p, i, s: (0, 0, p))]
    args = [place, same_j, other_j, block]
    aliases = {}
    if before is not None:
        in_specs.append(ANY if fresh else out_spec)
        args.append(before)
        aliases = {len(args) - 1: 0}
    out = jax.ShapeDtypeStruct(shape, F32)
    moved = jax.ShapeDtypeStruct((half, rows, depth), F32)
    return pl.pallas_call(
        functools.partial(gamma_kernel, not fresh),
        out_shape=out,
        grid_spec=pltpu.PrefetchScalarGridSpec(
            num_scalar_prefetch=1,
            grid=(depth // tile, half),
            in_specs=in_specs,
            out_specs=out_spec,
        ),
        input_output_aliases=aliases,
        compiler_params=PARAMS,
        cost_estimate=cost(2 * n_j * half * rows * cols * depth, moved, moved, block, same_j, other_j),
        name="add_gamma",
    )(*args)


def chain_device(b_occ_i, b_occ_j, eps_occ_i, eps_occ_j, eps_vir):
    n_i, rows, depth = b_occ_i.shape
    half = n_i // 2
    z, col = lax.axis_index("row"), lax.axis_index("col")
    x, core = col // 2, col % 2
    place = jnp.stack([x, core]).astype(jnp.int32)
    occ = lax.dynamic_slice_in_dim(eps_occ_i, core * half, half, 0) + eps_occ_j[x]

    def energies(block):
        return lax.dynamic_slice_in_dim(eps_vir, block * rows, rows, 0)

    vir_a = energies(z)[:, None]
    to_core = [(q, q ^ 1) for q in range(4)]
    to_chip = [(q, q ^ 2) for q in range(4)]

    def along(values, steps):
        return lax.ppermute(values, "row", steps)

    ends, middle = [(1, 0), (2, 3)], [(1, 2), (2, 1)]
    near = along(b_occ_j, [(k, k ^ 1) for k in range(4)])
    across = along(b_occ_j, middle)
    far_end = along(across, ends)
    far_mid = along(near, middle)
    far = jnp.where((z == 1) | (z == 2), far_mid, far_end)
    last = along(far_mid, ends)

    rounds = [
        (b_occ_j, 0, None),
        (near, 1, [(0, 1), (1, 0), (2, 3), (3, 2)]),
        (across, 3, middle),
        (far, 2, [(0, 2), (2, 0), (1, 3), (3, 1)]),
        (last, 3, [(0, 3), (3, 0)]),
    ]
    gamma = None
    for block, shift, swap in rounds:
        vir_b = energies(z ^ shift)[None, :]
        from_core = lax.ppermute(pairs_for_core(place, b_occ_i, block), "col", to_core)
        from_chip = lax.ppermute(pairs_for_chip(place, b_occ_i, block, from_core), "col", to_chip)
        held = own_amplitudes(place, occ, b_occ_i, block, from_core, from_chip, vir_a, vir_b)
        mirror = held if swap is None else along(held, swap)
        combined = combine_pairs(held, mirror)
        other_j = lax.ppermute(combined, "col", to_chip)
        core_same = lax.ppermute(combined, "col", to_core)
        core_other = lax.ppermute(other_j, "col", to_core)
        first = gamma is None
        gamma = add_gamma(place, True, combined, other_j, block, b_occ_i.shape, gamma, first)
        gamma = add_gamma(place, False, core_same, core_other, block, b_occ_i.shape, gamma, first)
    return gamma


def general_device(b_occ_i, b_occ_j, eps_occ_i, eps_occ_j, eps_vir):
    rows = b_occ_i.shape[1]
    own_energy = lax.dynamic_slice_in_dim(eps_vir, lax.axis_index("row") * rows, rows, 0)
    gathered = lax.all_gather(b_occ_j, "row", axis=1, tiled=True)
    partial_value = jnp.einsum("iap,jbp->jiab", b_occ_i, gathered, preferred_element_type=F32)
    totals = lax.psum(partial_value.astype(BF16), "col").astype(F32)
    denominator = (
        eps_occ_j[:, None, None, None]
        + eps_occ_i[None, :, None, None]
        - own_energy[None, None, :, None]
        - eps_vir[None, None, None, :]
    )
    held = (totals / denominator).astype(BF16)
    mirror = jnp.swapaxes(lax.all_to_all(held, "row", split_axis=3, concat_axis=2, tiled=True), 2, 3)
    combined = (2.0 * held.astype(F32) - mirror.astype(F32)).astype(BF16)
    return jnp.einsum("jiab,jbp->iap", combined, gathered, preferred_element_type=F32)


def solution(mesh):
    placed = (
        P("groups", "row", "col"),
        P("groups", "row", "col"),
        P("groups"),
        P("groups"),
        P("groups"),
    )
    chain = mesh.shape["row"] == 4 and mesh.shape["col"] == 4
    return jax.shard_map(
        chain_device if chain else general_device,
        mesh=mesh,
        in_specs=placed,
        out_specs=P("groups", "row", "col"),
        check_vma=False,
    )
```

time: 1470 us -> 652 us (0.44)
  blocking collectives: 547 us -> 0 us
  waiting for transfers between devices: 643 us -> 335 us
  Pallas kernels: 0 us -> 259 us
  local copies, waits for them, and re-layouts: 113 us -> 8.84 us
  matrix products: 95.1 us -> 0 us
  other arithmetic: 57.6 us -> 4.63 us
  starting transfers between devices: 0.04 us -> 42.4 us
    all_to_all x1 -> x0, blocking collectives: 547 us -> none  [mirror_full(): lax.all_to_all(amplitudes, 'row', split_axis=3, concat_axis=2, tiled=True)]
    psum x1 -> x0, waiting for transfers between devices: 420 us -> none  [per_device(): lax.psum(partial_value.astype(jnp.bfloat16), 'col').astype(jnp.float32)]
    ppermute x0 -> x34, waiting for transfers between devices: none -> 335 us  [the longest x9 207 us: along(): return lax.ppermute(values, 'row', steps)]
    pallas_call x0 -> x30, Pallas kernels: none -> 259 us  [the longest x10 124 us: add_gamma(): pl.pallas_call(functools.partial(gamma_kernel, not fresh), out_shape=out,...]
    all_gather x1 -> x0, waiting for transfers between devices: 222 us -> none  [per_device(): gathered = lax.all_gather(b_occ_j, 'row', axis=1, tiled=True)]
    convert_element_type x2 -> x0, local copies, waits for them, and re-layouts: 113 us -> none  [the longest x1 67.8 us: combine_pair(): mirror_amps.astype(jnp.float32)]
    dot_general x2 -> x0, matrix products: 95.1 us -> none  [the longest x1 48.6 us: per_device(): jnp.einsum('jiab,jbp->iap', combined, gathered, preferred_element_type=jn...]
    convert_element_type x2 -> x0, other arithmetic: 57.4 us -> none  [the longest x1 32.9 us: combine_pair(): (2.0 * amplitudes.astype(jnp.float32) - mirror_amps.astype(jnp.float32))....]
  transfers between devices with their start and end apart: 2 -> 34, of which waited for: 2 -> 11; matrix products, arithmetic and copies ran while one was open for 0% -> 1% of each run, Pallas kernels for 0% -> 38%
where the time goes in v1:
time: 652 us; the launch traced here: 650 us
  waiting for transfers between devices  335 us (51%)
  Pallas kernels  259 us (40%)
  starting transfers between devices  42.4 us (7%)
  local copies, waits for them, and re-layouts  8.84 us (1%)
    ppermute x9, waiting for transfers between devices, along(): return lax.ppermute(values, 'row', steps)  207 us
    pallas_call x10, Pallas kernels, add_gamma(): pl.pallas_call(functools.partial(gamma_kernel, not fresh), out_shape=out,...  124 us
    ppermute x5, waiting for transfers between devices, chain_device(): lax.ppermute(pairs_for_chip(place, b_occ_i, block, from_core), 'col', to_...  99.1 us
    pallas_call x5, Pallas kernels, pairs_for_core(): pl.pallas_call(send_kernel, out_shape=out, grid_spec=pltpu.PrefetchScalar...  57.9 us
    pallas_call x5, Pallas kernels, pairs_for_chip(): pl.pallas_call(chip_kernel, out_shape=out, grid_spec=pltpu.PrefetchScalar...  34.2 us
    pallas_call x5, Pallas kernels, own_amplitudes(): pl.pallas_call(own_kernel, out_shape=out, grid_spec=pltpu.PrefetchScalarG...  33.6 us
    ppermute x5, waiting for transfers between devices, chain_device(): other_j = lax.ppermute(combined, 'col', to_chip)  28.1 us
    ppermute x9, starting transfers between devices, along(): return lax.ppermute(values, 'row', steps)  18.3 us
  transfers between devices with their start and end apart: 34, of which 11 were waited for; matrix products, arithmetic and copies ran while one was open for 1% of the time, Pallas kernels for 38%

profile of v1, /device:TPU:1, one launch (start us, length us, event | category | flops | bytes accessed | tf_op | source)
XLA Modules:
  0.0 650.2 jit_solution(16540600042515163695)
XLA Ops:
  4.4 65.8 %collective-permute-done.block = bf16[2,512,1536]{2,1,0:T(8,128)(2,1)S(1)} collective-permute-done((bf16[2,512,1536]{2,1,0:T(8,128)(2,1)}, bf16[2,512,1536]{2,1,0:T(8,128)(2,1)S(1)}, u32[]{:S(2)}, u32[]{:S(2)}) %collective-permute-start) | collective-permute-done | bytes 3145760 | tf_op jit(solution)/shard_map/ppermute | solution.py:188
  75.6 11.8 %pairs_for_core.9 = bf16[2,3,512,512]{3,2,1,0:T(8,128)(2,1)} custom-call(s32[2]{0:T(128)S(1)} %pad_add_fusion.place, bf16[6,512,1536]{2,1,0:T(8,128)(2,1)} %b_i.29, bf16[2,512,1536]{2,1,0:T(8,128)(2,1)} %block.9), custom_call_target="tpu_custom_call" | custom-call | flops 4831838208 | bytes 15728640 | tf_op jit(solution)/shard_map/pairs_for_core/pallas_call | solution.py:33
  99.0 11.9 %pairs_for_core.7 = bf16[2,3,512,512]{3,2,1,0:T(8,128)(2,1)} custom-call(s32[2]{0:T(128)S(1)} %pad_add_fusion.place, bf16[6,512,1536]{2,1,0:T(8,128)(2,1)} %b_i.29, bf16[2,512,1536]{2,1,0:T(8,128)(2,1)} %collective-permute-done.9.block), custom_call_target="tpu_custom_call" | custom-call | flops 4831838208 | bytes 15728640 | tf_op jit(solution)/shard_map/pairs_for_core/pallas_call | solution.py:33
  111.4 32.1 %collective-permute-done.10 = bf16[2,512,1536]{2,1,0:T(8,128)(2,1)} collective-permute-done((bf16[2,512,1536]{2,1,0:T(8,128)(2,1)}, bf16[2,512,1536]{2,1,0:T(8,128)(2,1)}, u32[]{:S(2)}, u32[]{:S(2)}) %collective-permute-start.10) | collective-permute-done | bytes 3145760 | tf_op jit(solution)/shard_map/ppermute | solution.py:188
  147.3 11.8 %pairs_for_core.6 = bf16[2,3,512,512]{3,2,1,0:T(8,128)(2,1)} custom-call(s32[2]{0:T(128)S(1)} %pad_add_fusion.place, bf16[6,512,1536]{2,1,0:T(8,128)(2,1)} %b_i.29, bf16[2,512,1536]{2,1,0:T(8,128)(2,1)} %broadcast_select_fusion.block), custom_call_target="tpu_custom_call" | custom-call | flops 4831838208 | bytes 15728640 | tf_op jit(solution)/shard_map/pairs_for_core/pallas_call | solution.py:33
  162.1 48.6 %collective-permute-done.2.block = bf16[2,512,1536]{2,1,0:T(8,128)(2,1)S(1)} collective-permute-done((bf16[2,512,1536]{2,1,0:T(8,128)(2,1)}, bf16[2,512,1536]{2,1,0:T(8,128)(2,1)S(1)}, u32[]{:S(2)}, u32[]{:S(2)}) %collective-permute-start.2) | collective-permute-done | bytes 3145760 | tf_op jit(solution)/shard_map/ppermute | solution.py:188
  212.4 12.1 %pairs_for_core.5 = bf16[2,3,512,512]{3,2,1,0:T(8,128)(2,1)} custom-call(s32[2]{0:T(128)S(1)} %pad_add_fusion.place, bf16[6,512,1536]{2,1,0:T(8,128)(2,1)} %b_i.29, bf16[2,512,1536]{2,1,0:T(8,128)(2,1)} %copy-done.1), custom_call_target="tpu_custom_call" | custom-call | flops 4831838208 | bytes 15728640 | tf_op jit(solution)/shard_map/pairs_for_core/pallas_call | solution.py:33
  258.7 11.2 %collective-permute-done.24.chip = bf16[3,512,512]{2,1,0:T(8,128)(2,1)} collective-permute-done((bf16[3,512,512]{2,1,0:T(8,128)(2,1)}, bf16[3,512,512]{2,1,0:T(8,128)(2,1)}, u32[]{:S(2)}, u32[]{:S(2)}) %collective-permute-start.24) | collective-permute-done | bytes 1572896 | tf_op jit(solution)/shard_map/ppermute | solution.py:209
  284.9 18.8 %collective-permute-done.30.chip = bf16[3,512,512]{2,1,0:T(8,128)(2,1)} collective-permute-done((bf16[3,512,512]{2,1,0:T(8,128)(2,1)}, bf16[3,512,512]{2,1,0:T(8,128)(2,1)}, u32[]{:S(2)}, u32[]{:S(2)}) %collective-permute-start.30) | collective-permute-done | bytes 1572896 | tf_op jit(solution)/shard_map/ppermute | solution.py:209
  312.4 25.0 %collective-permute-done.18.chip = bf16[3,512,512]{2,1,0:T(8,128)(2,1)} collective-permute-done((bf16[3,512,512]{2,1,0:T(8,128)(2,1)}, bf16[3,512,512]{2,1,0:T(8,128)(2,1)}, u32[]{:S(2)}, u32[]{:S(2)}) %collective-permute-start.18) | collective-permute-done | bytes 1572896 | tf_op jit(solution)/shard_map/ppermute | solution.py:209
  345.5 25.5 %collective-permute-done.12.chip = bf16[3,512,512]{2,1,0:T(8,128)(2,1)S(1)} collective-permute-done((bf16[3,512,512]{2,1,0:T(8,128)(2,1)}, bf16[3,512,512]{2,1,0:T(8,128)(2,1)S(1)}, u32[]{:S(2)}, u32[]{:S(2)}) %collective-permute-start.12) | collective-permute-done | bytes 1572896 | tf_op jit(solution)/shard_map/ppermute | solution.py:209
  386.0 18.7 %collective-permute-done.4.chip = bf16[3,512,512]{2,1,0:T(8,128)(2,1)S(1)} collective-permute-done((bf16[3,512,512]{2,1,0:T(8,128)(2,1)}, bf16[3,512,512]{2,1,0:T(8,128)(2,1)S(1)}, u32[]{:S(2)}, u32[]{:S(2)}) %collective-permute-start.4) | collective-permute-done | bytes 1572896 | tf_op jit(solution)/shard_map/ppermute | solution.py:209
  414.7 23.8 %collective-permute-done.32.other_j = bf16[3,512,512]{2,1,0:T(8,128)(2,1)} collective-permute-done((bf16[3,512,512]{2,1,0:T(8,128)(2,1)S(1)}, bf16[3,512,512]{2,1,0:T(8,128)(2,1)}, u32[]{:S(2)}, u32[]{:S(2)}) %collective-permute-start.32) | collective-permute-done | bytes 1572896 | tf_op jit(solution)/shard_map/ppermute | solution.py:213
  449.0 61.1 %collective-permute-done.13.mirror = bf16[3,512,512]{2,1,0:T(8,128)(2,1)} collective-permute-done((bf16[3,512,512]{2,1,0:T(8,128)(2,1)S(1)}, bf16[3,512,512]{2,1,0:T(8,128)(2,1)}, u32[]{:S(2)}, u32[]{:S(2)}) %collective-permute-start.13) | collective-permute-done | bytes 1572896 | tf_op jit(solution)/shard_map/ppermute | solution.py:188
  517.0 10.9 %add_gamma.10.rest_0_ = f32[6,512,1536]{2,1,0:T(8,128)} custom-call(s32[2]{0:T(128)S(1)} %pad_add_fusion.place, bf16[3,512,512]{2,1,0:T(8,128)(2,1)S(1)} %copy-done.7, bf16[3,512,512]{2,1,0:T(8,128)(2,1)} %collective-permute-done.32.other_j, bf16[2,512,1536]{2,1,0:T(8,128)(2,1)} %block.9), custom_call_target="tpu_custom_call" | custom-call | flops 4831838208 | bytes 25165824 | tf_op jit(solution)/shard_map/add_gamma/pallas_call | solution.py:156
  529.8 10.9 %add_gamma.11.rest_0_ = f32[6,512,1536]{2,1,0:T(8,128)} custom-call(s32[2]{0:T(128)S(1)} %pad_add_fusion.place, bf16[3,512,512]{2,1,0:T(8,128)(2,1)S(1)} %copy-done.9, bf16[3,512,512]{2,1,0:T(8,128)(2,1)} %collective-permute-done.33.other_j, bf16[2,512,1536]{2,1,0:T(8,128)(2,1)} %block.9, ...), custom_call_target="tpu_custom_call", output_to_operand_aliasing={{}: (4, {})} | custom-call | flops 4831838208 | bytes 25165824 | tf_op jit(solution)/shard_map/add_gamma/pallas_call | solution.py:156
  540.7 12.9 %add_gamma.12.rest_0_ = f32[6,512,1536]{2,1,0:T(8,128)} custom-call(s32[2]{0:T(128)S(1)} %pad_add_fusion.place, bf16[3,512,512]{2,1,0:T(8,128)(2,1)S(1)} %combine_pairs.8.same_j, bf16[3,512,512]{2,1,0:T(8,128)(2,1)} %collective-permute-done.27.other_j, bf16[2,512,1536]{2,1,0:T(8,128)(2,1)} %copy-done.3, ...), custom_call_target="tpu_custom_call", output_to_operand_aliasing={{}: (4, {})} | custom-call | flops 4831838208 | bytes 25165824 | tf_op jit(solution)/shard_map/add_gamma/pallas_call | solution.py:156
  554.3 13.6 %add_gamma.13.rest_0_ = f32[6,512,1536]{2,1,0:T(8,128)} custom-call(s32[2]{0:T(128)S(1)} %pad_add_fusion.place, bf16[3,512,512]{2,1,0:T(8,128)(2,1)} %collective-permute-done.26.same_j, bf16[3,512,512]{2,1,0:T(8,128)(2,1)} %collective-permute-done.28.other_j, bf16[2,512,1536]{2,1,0:T(8,128)(2,1)} %copy-done.3, ...), custom_call_target="tpu_custom_call", output_to_operand_aliasing={{}: (4, {})} | custom-call | flops 4831838208 | bytes 25165824 | tf_op jit(solution)/shard_map/add_gamma/pallas_call | solution.py:156
  567.9 12.3 %add_gamma.14.rest_0_ = f32[6,512,1536]{2,1,0:T(8,128)} custom-call(s32[2]{0:T(128)S(1)} %pad_add_fusion.place, bf16[3,512,512]{2,1,0:T(8,128)(2,1)S(1)} %combine_pairs.7.same_j, bf16[3,512,512]{2,1,0:T(8,128)(2,1)S(1)} %collective-permute-done.21.other_j, bf16[2,512,1536]{2,1,0:T(8,128)(2,1)} %collective-permute-done.9.block, ...), custom_call_target="tpu_custom_call", output_to_operand_aliasing={{}: (4, {})} | custom-call | flops 4831838208 | bytes 25165824 | tf_op jit(solution)/shard_map/add_gamma/pallas_call | solution.py:156
  586.3 13.6 %add_gamma.15.rest_0_ = f32[6,512,1536]{2,1,0:T(8,128)} custom-call(s32[2]{0:T(128)S(1)} %pad_add_fusion.place, bf16[3,512,512]{2,1,0:T(8,128)(2,1)} %collective-permute-done.20.same_j, bf16[3,512,512]{2,1,0:T(8,128)(2,1)} %collective-permute-done.22.other_j, bf16[2,512,1536]{2,1,0:T(8,128)(2,1)} %collective-permute-done.9.block, ...), custom_call_target="tpu_custom_call", output_to_operand_aliasing={{}: (4, {})} | custom-call | flops 4831838208 | bytes 25165824 | tf_op jit(solution)/shard_map/add_gamma/pallas_call | solution.py:156
  599.8 12.9 %add_gamma.16.rest_0_ = f32[6,512,1536]{2,1,0:T(8,128)} custom-call(s32[2]{0:T(128)S(1)} %pad_add_fusion.place, bf16[3,512,512]{2,1,0:T(8,128)(2,1)S(1)} %combine_pairs.6.same_j, bf16[3,512,512]{2,1,0:T(8,128)(2,1)} %collective-permute-done.15.other_j, bf16[2,512,1536]{2,1,0:T(8,128)(2,1)} %broadcast_select_fusion.block, ...), custom_call_target="tpu_custom_call", output_to_operand_aliasing={{}: (4, {})} | custom-call | flops 4831838208 | bytes 25165824 | tf_op jit(solution)/shard_map/add_gamma/pallas_call | solution.py:156
  612.7 12.3 %add_gamma.17.rest_0_ = f32[6,512,1536]{2,1,0:T(8,128)} custom-call(s32[2]{0:T(128)S(1)} %pad_add_fusion.place, bf16[3,512,512]{2,1,0:T(8,128)(2,1)S(1)} %collective-permute-done.14.same_j, bf16[3,512,512]{2,1,0:T(8,128)(2,1)S(1)} %collective-permute-done.16.other_j, ...), custom_call_target="tpu_custom_call", output_to_operand_aliasing={{}: (4, {})} | custom-call | flops 4831838208 | bytes 25165824 | tf_op jit(solution)/shard_map/add_gamma/pallas_call | solution.py:156
  625.0 12.3 %add_gamma.18.rest_0_ = f32[6,512,1536]{2,1,0:T(8,128)} custom-call(s32[2]{0:T(128)S(1)} %pad_add_fusion.place, bf16[3,512,512]{2,1,0:T(8,128)(2,1)S(1)} %combine_pairs.5.same_j, bf16[3,512,512]{2,1,0:T(8,128)(2,1)S(1)} %collective-permute-done.7.other_j, bf16[2,512,1536]{2,1,0:T(8,128)(2,1)} %copy-done.1, ...), custom_call_target="tpu_custom_call", output_to_operand_aliasing={{}: (4, {})} | custom-call | flops 4831838208 | bytes 25165824 | tf_op jit(solution)/shard_map/add_gamma/pallas_call | solution.py:156
  637.3 12.9 %add_gamma.19 = f32[6,512,1536]{2,1,0:T(8,128)} custom-call(s32[2]{0:T(128)S(1)} %pad_add_fusion.place, bf16[3,512,512]{2,1,0:T(8,128)(2,1)S(1)} %collective-permute-done.6.same_j, bf16[3,512,512]{2,1,0:T(8,128)(2,1)} %collective-permute-done.8.other_j, bf16[2,512,1536]{2,1,0:T(8,128)(2,1)} %copy-done.1, ...), custom_call_target="tpu_custom_call", output_to_operand_aliasing={{}: (4, {})} | custom-call | flops 4831838208 | bytes 25165824 | tf_op jit(solution)/shard_map/add_gamma/pallas_call | solution.py:156
  (118 shorter events, 147.4 us)
Async XLA Ops:
  0.0 70.2 %collective-permute-start = (bf16[2,512,1536]{2,1,0:T(8,128)(2,1)}, bf16[2,512,1536]{2,1,0:T(8,128)(2,1)S(1)}, u32[]{:S(2)}, u32[]{:S(2)}) collective-permute-start(bf16[2,512,1536]{2,1,0:T(8,128)(2,1)} %block.9), channel_id=1, source_target_pairs={{0,4},{4,0},{8,12},{12,8},{1,5},{5,1},{9,13},{13,9},{2,6},{6,2},{1... | collective-permute-start | bytes 9437192 | tf_op jit(solution)/shard_map/ppermute | solution.py:188
  2.1 70.7 %collective-permute-start.9 = (bf16[2,512,1536]{2,1,0:T(8,128)(2,1)}, bf16[2,512,1536]{2,1,0:T(8,128)(2,1)}, u32[]{:S(2)}, u32[]{:S(2)}) collective-permute-start(bf16[2,512,1536]{2,1,0:T(8,128)(2,1)} %block.9), channel_id=1, source_target_pairs={{4,8},{8,4},{5,9},{9,5},{6,10},{10,6},{7,11},{11,7},{20,24},{24,20... | collective-permute-start | bytes 9437192 | tf_op jit(solution)/shard_map/ppermute | solution.py:188
  72.9 70.6 %collective-permute-start.10 = (bf16[2,512,1536]{2,1,0:T(8,128)(2,1)}, bf16[2,512,1536]{2,1,0:T(8,128)(2,1)}, u32[]{:S(2)}, u32[]{:S(2)}) collective-permute-start(bf16[2,512,1536]{2,1,0:T(8,128)(2,1)} %collective-permute-done.9.block), channel_id=1, source_target_pairs={{4,0},{8,12},{5,1},{9,13},{6,2},{10,14},{7,3},{11,15},{20,16},{24,... | collective-permute-start | bytes 9437192 | tf_op jit(solution)/shard_map/ppermute | solution.py:188
  74.2 136.5 %collective-permute-start.2 = (bf16[2,512,1536]{2,1,0:T(8,128)(2,1)}, bf16[2,512,1536]{2,1,0:T(8,128)(2,1)S(1)}, u32[]{:S(2)}, u32[]{:S(2)}) collective-permute-start(bf16[2,512,1536]{2,1,0:T(8,128)(2,1)} %collective-permute-done.1), channel_id=1, source_target_pairs={{4,0},{8,12},{5,1},{9,13},{6,2},{10,14},{7,3},{11,15},{20,16},{24,... | collective-permute-start | bytes 9437192 | tf_op jit(solution)/shard_map/ppermute | solution.py:188
  87.4 147.9 %collective-permute-start.29 = (bf16[2,3,512,512]{3,2,1,0:T(8,128)(2,1)}, bf16[2,3,512,512]{3,2,1,0:T(8,128)(2,1)}, u32[]{:S(2)}, u32[]{:S(2)}) collective-permute-start(bf16[2,3,512,512]{3,2,1,0:T(8,128)(2,1)} %pairs_for_core.9), channel_id=1, source_target_pairs={{0,1},{1,0},{2,3},{3,2},{4,5},{5,4},{6,7},{7,6},{8,9},{9,8},{10,11... | collective-permute-start | bytes 9437192 | tf_op jit(solution)/shard_map/ppermute | solution.py:208
  98.9 127.8 %collective-permute-start.23 = (bf16[2,3,512,512]{3,2,1,0:T(8,128)(2,1)S(1)}, bf16[2,3,512,512]{3,2,1,0:T(8,128)(2,1)}, u32[]{:S(2)}, u32[]{:S(2)}) collective-permute-start(bf16[2,3,512,512]{3,2,1,0:T(8,128)(2,1)S(1)} %pairs_for_core.8), channel_id=1, source_target_pairs={{0,1},{1,0},{2,3},{3,2},{4,5},{5,4},{6,7},{7,6},{8,9},{9,8},{10,11... | collective-permute-start | bytes 9437192 | tf_op jit(solution)/shard_map/ppermute | solution.py:208
  110.9 132.2 %collective-permute-start.17 = (bf16[2,3,512,512]{3,2,1,0:T(8,128)(2,1)}, bf16[2,3,512,512]{3,2,1,0:T(8,128)(2,1)}, u32[]{:S(2)}, u32[]{:S(2)}) collective-permute-start(bf16[2,3,512,512]{3,2,1,0:T(8,128)(2,1)} %pairs_for_core.7), channel_id=1, source_target_pairs={{0,1},{1,0},{2,3},{3,2},{4,5},{5,4},{6,7},{7,6},{8,9},{9,8},{10,11... | collective-permute-start | bytes 9437192 | tf_op jit(solution)/shard_map/ppermute | solution.py:208
  159.2 92.5 %collective-permute-start.11 = (bf16[2,3,512,512]{3,2,1,0:T(8,128)(2,1)}, bf16[2,3,512,512]{3,2,1,0:T(8,128)(2,1)}, u32[]{:S(2)}, u32[]{:S(2)}) collective-permute-start(bf16[2,3,512,512]{3,2,1,0:T(8,128)(2,1)} %pairs_for_core.6), channel_id=1, source_target_pairs={{0,1},{1,0},{2,3},{3,2},{4,5},{5,4},{6,7},{7,6},{8,9},{9,8},{10,11... | collective-permute-start | bytes 9437192 | tf_op jit(solution)/shard_map/ppermute | solution.py:208
  241.9 61.7 %collective-permute-start.30 = (bf16[3,512,512]{2,1,0:T(8,128)(2,1)}, bf16[3,512,512]{2,1,0:T(8,128)(2,1)}, u32[]{:S(2)}, u32[]{:S(2)}) collective-permute-start(bf16[3,512,512]{2,1,0:T(8,128)(2,1)} %pairs_for_chip.9), channel_id=1, source_target_pairs={{0,2},{1,3},{2,0},{3,1},{4,6},{5,7},{6,4},{7,5},{8,10},{9,11},{10,... | collective-permute-start | bytes 4718600 | tf_op jit(solution)/shard_map/ppermute | solution.py:209
  250.5 86.9 %collective-permute-start.18 = (bf16[3,512,512]{2,1,0:T(8,128)(2,1)}, bf16[3,512,512]{2,1,0:T(8,128)(2,1)}, u32[]{:S(2)}, u32[]{:S(2)}) collective-permute-start(bf16[3,512,512]{2,1,0:T(8,128)(2,1)} %pairs_for_chip.7), channel_id=1, source_target_pairs={{0,2},{1,3},{2,0},{3,1},{4,6},{5,7},{6,4},{7,5},{8,10},{9,11},{10,... | collective-permute-start | bytes 4718600 | tf_op jit(solution)/shard_map/ppermute | solution.py:209
  258.3 112.6 %collective-permute-start.12 = (bf16[3,512,512]{2,1,0:T(8,128)(2,1)}, bf16[3,512,512]{2,1,0:T(8,128)(2,1)S(1)}, u32[]{:S(2)}, u32[]{:S(2)}) collective-permute-start(bf16[3,512,512]{2,1,0:T(8,128)(2,1)} %pairs_for_chip.6), channel_id=1, source_target_pairs={{0,2},{1,3},{2,0},{3,1},{4,6},{5,7},{6,4},{7,5},{8,10},{9,11},{10,... | collective-permute-start | bytes 4718600 | tf_op jit(solution)/shard_map/ppermute | solution.py:209
  277.1 104.7 %collective-permute-start.25 = (bf16[3,512,512]{2,1,0:T(8,128)(2,1)S(1)}, bf16[3,512,512]{2,1,0:T(8,128)(2,1)}, u32[]{:S(2)}, u32[]{:S(2)}) collective-permute-start(bf16[3,512,512]{2,1,0:T(8,128)(2,1)S(1)} %own_amplitudes.8.held), channel_id=1, source_target_pairs={{0,4},{4,0},{8,12},{12,8},{1,5},{5,1},{9,13},{13,9},{2,6},{6,2},{1... | collective-permute-start | bytes 4718600 | tf_op jit(solution)/shard_map/ppermute | solution.py:188
  283.8 120.9 %collective-permute-start.4 = (bf16[3,512,512]{2,1,0:T(8,128)(2,1)}, bf16[3,512,512]{2,1,0:T(8,128)(2,1)S(1)}, u32[]{:S(2)}, u32[]{:S(2)}) collective-permute-start(bf16[3,512,512]{2,1,0:T(8,128)(2,1)} %pairs_for_chip.5), channel_id=1, source_target_pairs={{0,2},{1,3},{2,0},{3,1},{4,6},{5,7},{6,4},{7,5},{8,10},{9,11},{10,... | collective-permute-start | bytes 4718600 | tf_op jit(solution)/shard_map/ppermute | solution.py:209
  311.3 127.2 %collective-permute-start.32 = (bf16[3,512,512]{2,1,0:T(8,128)(2,1)S(1)}, bf16[3,512,512]{2,1,0:T(8,128)(2,1)}, u32[]{:S(2)}, u32[]{:S(2)}) collective-permute-start(bf16[3,512,512]{2,1,0:T(8,128)(2,1)S(1)} %combine_pairs.9.same_j), channel_id=1, source_target_pairs={{0,2},{1,3},{2,0},{3,1},{4,6},{5,7},{6,4},{7,5},{8,10},{9,11},{10,... | collective-permute-start | bytes 4718600 | tf_op jit(solution)/shard_map/ppermute | solution.py:213
  337.4 110.4 %collective-permute-start.31 = (bf16[3,512,512]{2,1,0:T(8,128)(2,1)S(1)}, bf16[3,512,512]{2,1,0:T(8,128)(2,1)S(1)}, u32[]{:S(2)}, u32[]{:S(2)}) collective-permute-start(bf16[3,512,512]{2,1,0:T(8,128)(2,1)S(1)} %combine_pairs.9.same_j), channel_id=1, source_target_pairs={{0,1},{1,0},{2,3},{3,2},{4,5},{5,4},{6,7},{7,6},{8,9},{9,8},{10,11... | collective-permute-start | bytes 4718600 | tf_op jit(solution)/shard_map/ppermute | solution.py:214
  372.1 71.5 %collective-permute-start.19 = (bf16[3,512,512]{2,1,0:T(8,128)(2,1)S(1)}, bf16[3,512,512]{2,1,0:T(8,128)(2,1)}, u32[]{:S(2)}, u32[]{:S(2)}) collective-permute-start(bf16[3,512,512]{2,1,0:T(8,128)(2,1)S(1)} %own_amplitudes.7.held), channel_id=1, source_target_pairs={{4,8},{8,4},{5,9},{9,5},{6,10},{10,6},{7,11},{11,7},{20,24},{24,20... | collective-permute-start | bytes 4718600 | tf_op jit(solution)/shard_map/ppermute | solution.py:188
  381.8 128.3 %collective-permute-start.13 = (bf16[3,512,512]{2,1,0:T(8,128)(2,1)S(1)}, bf16[3,512,512]{2,1,0:T(8,128)(2,1)}, u32[]{:S(2)}, u32[]{:S(2)}) collective-permute-start(bf16[3,512,512]{2,1,0:T(8,128)(2,1)S(1)} %own_amplitudes.6.held), channel_id=1, source_target_pairs={{0,8},{8,0},{4,12},{12,4},{1,9},{9,1},{5,13},{13,5},{2,10},{10,2},... | collective-permute-start | bytes 4718600 | tf_op jit(solution)/shard_map/ppermute | solution.py:188
  405.8 108.7 %collective-permute-start.27 = (bf16[3,512,512]{2,1,0:T(8,128)(2,1)S(1)}, bf16[3,512,512]{2,1,0:T(8,128)(2,1)}, u32[]{:S(2)}, u32[]{:S(2)}) collective-permute-start(bf16[3,512,512]{2,1,0:T(8,128)(2,1)S(1)} %combine_pairs.8.same_j), channel_id=1, source_target_pairs={{0,2},{1,3},{2,0},{3,1},{4,6},{5,7},{6,4},{7,5},{8,10},{9,11},{10,... | collective-permute-start | bytes 4718600 | tf_op jit(solution)/shard_map/ppermute | solution.py:213
  438.5 76.1 %collective-permute-start.5 = (bf16[3,512,512]{2,1,0:T(8,128)(2,1)S(1)}, bf16[3,512,512]{2,1,0:T(8,128)(2,1)S(1)}, u32[]{:S(2)}, u32[]{:S(2)}) collective-permute-start(bf16[3,512,512]{2,1,0:T(8,128)(2,1)S(1)} %own_amplitudes.5.held), channel_id=1, source_target_pairs={{0,12},{12,0},{1,13},{13,1},{2,14},{14,2},{3,15},{15,3},{16,28},{2... | collective-permute-start | bytes 4718600 | tf_op jit(solution)/shard_map/ppermute | solution.py:188
  443.6 85.0 %collective-permute-start.33 = (bf16[3,512,512]{2,1,0:T(8,128)(2,1)}, bf16[3,512,512]{2,1,0:T(8,128)(2,1)}, u32[]{:S(2)}, u32[]{:S(2)}) collective-permute-start(bf16[3,512,512]{2,1,0:T(8,128)(2,1)} %collective-permute-done.32.other_j), channel_id=1, source_target_pairs={{0,1},{1,0},{2,3},{3,2},{4,5},{5,4},{6,7},{7,6},{8,9},{9,8},{10,11... | collective-permute-start | bytes 4718600 | tf_op jit(solution)/shard_map/ppermute | solution.py:215
  447.7 81.7 %collective-permute-start.21 = (bf16[3,512,512]{2,1,0:T(8,128)(2,1)S(1)}, bf16[3,512,512]{2,1,0:T(8,128)(2,1)S(1)}, u32[]{:S(2)}, u32[]{:S(2)}) collective-permute-start(bf16[3,512,512]{2,1,0:T(8,128)(2,1)S(1)} %combine_pairs.7.same_j), channel_id=1, source_target_pairs={{0,2},{1,3},{2,0},{3,1},{4,6},{5,7},{6,4},{7,5},{8,10},{9,11},{10,... | collective-permute-start | bytes 4718600 | tf_op jit(solution)/shard_map/ppermute | solution.py:213
  553.5 59.2 %collective-permute-start.14 = (bf16[3,512,512]{2,1,0:T(8,128)(2,1)S(1)}, bf16[3,512,512]{2,1,0:T(8,128)(2,1)S(1)}, u32[]{:S(2)}, u32[]{:S(2)}) collective-permute-start(bf16[3,512,512]{2,1,0:T(8,128)(2,1)S(1)} %combine_pairs.6.same_j), channel_id=1, source_target_pairs={{0,1},{1,0},{2,3},{3,2},{4,5},{5,4},{6,7},{7,6},{8,9},{9,8},{10,11... | collective-permute-start | bytes 4718600 | tf_op jit(solution)/shard_map/ppermute | solution.py:214
  554.2 58.5 %collective-permute-start.16 = (bf16[3,512,512]{2,1,0:T(8,128)(2,1)}, bf16[3,512,512]{2,1,0:T(8,128)(2,1)S(1)}, u32[]{:S(2)}, u32[]{:S(2)}) collective-permute-start(bf16[3,512,512]{2,1,0:T(8,128)(2,1)} %collective-permute-done.15.other_j), channel_id=1, source_target_pairs={{0,1},{1,0},{2,3},{3,2},{4,5},{5,4},{6,7},{7,6},{8,9},{9,8},{10,11... | collective-permute-start | bytes 4718600 | tf_op jit(solution)/shard_map/ppermute | solution.py:215
  580.2 57.1 %collective-permute-start.6 = (bf16[3,512,512]{2,1,0:T(8,128)(2,1)S(1)}, bf16[3,512,512]{2,1,0:T(8,128)(2,1)S(1)}, u32[]{:S(2)}, u32[]{:S(2)}) collective-permute-start(bf16[3,512,512]{2,1,0:T(8,128)(2,1)S(1)} %combine_pairs.5.same_j), channel_id=1, source_target_pairs={{0,1},{1,0},{2,3},{3,2},{4,5},{5,4},{6,7},{7,6},{8,9},{9,8},{10,11... | collective-permute-start | bytes 4718600 | tf_op jit(solution)/shard_map/ppermute | solution.py:214
  (29 other events, 664.8 us)

commit v2 on v0

v2 whole, which is shorter than its diff:
```python
import functools

import jax
import jax.numpy as jnp
from jax import lax
from jax.experimental import pallas as pl
from jax.experimental.pallas import tpu as pltpu
from jax.sharding import PartitionSpec as P

F32 = jnp.float32
BF16 = jnp.bfloat16
ANY = pl.BlockSpec(memory_space=pl.ANY)
TOKEN = jax.ShapeDtypeStruct((8, 128), F32)
TILE = 256


def tile_of(size):
    return TILE if size % TILE == 0 else size


def call(kernel, name, token, place, grid, in_specs, args, out_specs, out, aliases=None):
    def body(*refs):
        n = len(place)
        kernel(*refs[:n], *refs[n + 1 : -1])

    shift = len(place) + 1
    return pl.pallas_call(
        body,
        out_shape=(*out, TOKEN),
        grid_spec=pltpu.PrefetchScalarGridSpec(
            num_scalar_prefetch=len(place),
            grid=grid,
            in_specs=[ANY] + in_specs,
            out_specs=(*out_specs, ANY),
        ),
        input_output_aliases={k + shift: v for k, v in (aliases or {}).items()},
        compiler_params=pltpu.CompilerParams(vmem_limit_bytes=60 * 2**20),
        cost_estimate=pl.CostEstimate(flops=0, bytes_accessed=1024, transcendentals=0),
        name=name,
    )(*place, token, *args)


def tie_kernel(place, held, out):
    del place, held, out


def tie(token, place, held):
    return call(tie_kernel, "tie", token, place, (1,), [ANY], [held], [ANY], [held_shape(held)], {0: 0})


def held_shape(a):
    return jax.ShapeDtypeStruct(a.shape, a.dtype)


def pairs_kernel(n_place, n_more, *refs):
    place, rest = refs[:n_place], refs[n_place:]
    b_i, block, rest = rest[0], rest[1], rest[2:]
    out = rest[-1]
    half, rows, depth = b_i.shape
    left = b_i[...].reshape(half * rows, depth)
    total = lax.dot_general(left, block[0], (((1,), (1,)), ((), ())), preferred_element_type=F32)
    for i in range(half):
        value = total[i * rows : (i + 1) * rows]
        if n_more > 0:
            value = value + rest[0][i].astype(F32)
        if n_more > 1:
            chip, vir_a, vir_b = rest[1:4]
            value = value + chip[i].astype(F32)
            value = value / ((place[1][i] - vir_a[...]) - vir_b[...])
        out[i] = value.astype(BF16)


def pairs(token, place, b_i, block, own_i, own_j, core=None, last=None):
    n_j, cols, depth = block.shape
    half, rows = b_i.shape[0] // 2, b_i.shape[1]
    tile = tile_of(cols)

    def j_of(s):
        return s[0] if own_j else 1 - s[0]

    every = pl.BlockSpec((half, rows, tile), lambda t, s, *_: (0, 0, t))
    in_specs = [
        pl.BlockSpec((half, rows, depth), lambda t, s, *_: (s[1] if own_i else 1 - s[1], 0, 0)),
        pl.BlockSpec((1, tile, depth), lambda t, s, *_: (j_of(s), t, 0)),
    ]
    args, n_more, name = [b_i, block], 0, "pairs_for_core"
    if core is not None:
        in_specs.append(every)
        args.append(core)
        n_more, name = 1, "pairs_for_chip"
    if last is not None:
        chip, occ, vir_a, vir_b = last
        place = place + (occ,)
        in_specs += [
            every,
            pl.BlockSpec((rows, 1), lambda t, s, *_: (0, 0)),
            pl.BlockSpec((1, tile), lambda t, s, *_: (0, t)),
        ]
        args += [chip, vir_a, vir_b]
        n_more, name = 2, "own_amplitudes"
    out = jax.ShapeDtypeStruct((half, rows, cols), BF16)
    kernel = functools.partial(pairs_kernel, len(place), n_more)
    return call(kernel, name, token, place, (cols // tile,), in_specs, args, [every], [out])


def combine_kernel(place, held, mirror, out):
    out[0] = (2.0 * held[0].astype(F32) - mirror[0].astype(F32).T).astype(BF16)


def combine_pairs(token, place, held, mirror):
    spec = pl.BlockSpec((1,) + held.shape[1:], lambda i, s: (i, 0, 0))
    return call(
        combine_kernel, "combine_pairs", token, place, held.shape[:1], [spec, spec], [held, mirror], [spec], [held_shape(held)]
    )


def gamma_kernel(n_blocks, has_sum, place, *refs):
    x = place[0]
    out = refs[-1]
    half, rows, tile = out.shape
    total = refs[-2][...].reshape(half * rows, tile) if has_sum else None
    for k in range(n_blocks):
        same_j, other_j, block = refs[3 * k : 3 * k + 3]
        for held, j in ((same_j, x), (other_j, 1 - x)):
            left = held[...].reshape(half * rows, held.shape[2])
            term = jnp.dot(left, block[j], preferred_element_type=F32)
            total = term if total is None else total + term
    out[...] = total.reshape(half, rows, tile)


def add_gamma(token, place, mine, terms, shape, before, fresh):
    half, rows, depth = shape[0] // 2, shape[1], shape[2]
    tile = tile_of(depth)
    out_spec = pl.BlockSpec((half, rows, tile), lambda p, s: (s[1] if mine else 1 - s[1], 0, p))
    in_specs, args = [], []
    for same_j, other_j, block in terms:
        held = [same_j, other_j]
        in_specs += [pl.BlockSpec(h.shape, lambda p, s: (0, 0, 0)) for h in held]
        in_specs.append(pl.BlockSpec(block.shape[:2] + (tile,), lambda p, s: (0, 0, p)))
        args += [*held, block]
    aliases = None
    if before is not None:
        aliases = {len(args): 0}
        in_specs.append(ANY if fresh else out_spec)
        args.append(before)
    kernel = functools.partial(gamma_kernel, len(terms), not fresh)
    return call(
        kernel, "add_gamma", token, place, (depth // tile,), in_specs, args, [out_spec], [jax.ShapeDtypeStruct(shape, F32)], aliases
    )


def chain_device(b_occ_i, b_occ_j, eps_occ_i, eps_occ_j, eps_vir):
    n_i, rows, depth = b_occ_i.shape
    half = n_i // 2
    z, col = lax.axis_index("row"), lax.axis_index("col")
    x, core = col // 2, col % 2
    place = (jnp.stack([x, core]).astype(jnp.int32),)
    occ = lax.dynamic_slice_in_dim(eps_occ_i, core * half, half, 0) + eps_occ_j[x]
    token = jnp.zeros(TOKEN.shape, F32)

    def energies(block):
        return lax.dynamic_slice_in_dim(eps_vir, block * rows, rows, 0)

    vir_a = energies(z)[:, None]

    def to_core(values):
        return lax.ppermute(values, "col", [(q, q ^ 1) for q in range(4)])

    def to_chip(values):
        return lax.ppermute(values, "col", [(q, q ^ 2) for q in range(4)])

    def along(values, steps):
        return lax.ppermute(values, "row", steps)

    ends, middle = [(1, 0), (2, 3)], [(1, 2), (2, 1)]
    pairs_1 = [(0, 1), (1, 0), (2, 3), (3, 2)]
    pairs_2 = [(0, 2), (2, 0), (1, 3), (3, 1)]
    pairs_3 = [(0, 3), (3, 0)]
    in_middle = (z == 1) | (z == 2)

    def send(block, own_j):
        nonlocal token
        out, token = pairs(token, place, b_occ_i, block, False, own_j)
        return to_core(out)

    def pass_on(block, core_sum):
        nonlocal token
        out, token = pairs(token, place, b_occ_i, block, True, False, core_sum)
        return to_chip(out)

    def own(block, core_sum, chip_sum, shift):
        nonlocal token
        vir_b = energies(z ^ shift)[None, :]
        out, token = pairs(token, place, b_occ_i, block, True, True, core_sum, (chip_sum, occ, vir_a, vir_b))
        return out

    def combine(held, mirror):
        nonlocal token
        out, token = combine_pairs(token, place, held, mirror)
        return out, to_chip(out), to_core(out)

    def forward(values):
        nonlocal token
        out, token = tie(token, place, values)
        return out

    def spread(other):
        other = forward(other)
        return other, to_core(other)

    gamma = None

    def add(mine, terms, fresh=False):
        nonlocal token, gamma
        gamma, token = add_gamma(token, place, mine, terms, b_occ_i.shape, gamma, fresh)

    near = along(b_occ_j, pairs_1)
    across = along(b_occ_j, middle)

    pass_0 = send(b_occ_j, False)
    keep_0 = send(b_occ_j, True)
    chip_0 = pass_on(b_occ_j, pass_0)
    held_0 = own(b_occ_j, keep_0, chip_0, 0)
    mine_0, other_0, same_0 = combine(held_0, held_0)

    near = forward(near)
    across = forward(across)
    far_mid = along(near, middle)
    far_end = along(across, ends)
    pass_1 = send(near, False)
    pass_12 = send(across, False)
    keep_1 = send(near, True)
    chip_1 = pass_on(near, pass_1)
    keep_12 = send(across, True)
    chip_12 = pass_on(across, pass_12)

    other_0, both_0 = spread(other_0)
    add(True, [(mine_0, other_0, b_occ_j)], True)
    add(False, [(same_0, both_0, b_occ_j)], True)

    held_1 = own(near, keep_1, chip_1, 1)
    mirror_1 = along(held_1, pairs_1)

    far_mid = forward(far_mid)
    last = along(far_mid, ends)
    far = jnp.where(in_middle, far_mid, far_end)
    pass_2 = send(far, False)
    keep_2 = send(far, True)
    chip_2 = pass_on(far, pass_2)

    held_12 = own(across, keep_12, chip_12, 3)
    mirror_12 = along(held_12, middle)

    mine_1, other_1, same_1 = combine(held_1, mirror_1)

    held_2 = own(far, keep_2, chip_2, 2)
    mirror_2 = along(held_2, pairs_2)

    mine_12, other_12, same_12 = combine(held_12, mirror_12)

    last = forward(last)
    pass_3 = send(last, False)
    keep_3 = send(last, True)
    chip_3 = pass_on(last, pass_3)

    other_1, both_1 = spread(other_1)
    other_12, both_12 = spread(other_12)
    add(True, [(mine_1, other_1, near), (mine_12, other_12, across)])
    add(False, [(same_1, both_1, near), (same_12, both_12, across)])

    mine_2, other_2, same_2 = combine(held_2, mirror_2)
    held_3 = own(last, keep_3, chip_3, 3)
    mirror_3 = along(held_3, pairs_3)

    other_2, both_2 = spread(other_2)
    add(True, [(mine_2, other_2, far)])
    add(False, [(same_2, both_2, far)])

    mine_3, other_3, same_3 = combine(held_3, mirror_3)
    other_3, both_3 = spread(other_3)
    add(True, [(mine_3, other_3, last)])
    add(False, [(same_3, both_3, last)])
    return gamma


def general_device(b_occ_i, b_occ_j, eps_occ_i, eps_occ_j, eps_vir):
    rows = b_occ_i.shape[1]
    own_energy = lax.dynamic_slice_in_dim(eps_vir, lax.axis_index("row") * rows, rows, 0)
    gathered = lax.all_gather(b_occ_j, "row", axis=1, tiled=True)
    partial_value = jnp.einsum("iap,jbp->jiab", b_occ_i, gathered, preferred_element_type=F32)
    totals = lax.psum(partial_value.astype(BF16), "col").astype(F32)
    denominator = (
        eps_occ_j[:, None, None, None]
        + eps_occ_i[None, :, None, None]
        - own_energy[None, None, :, None]
        - eps_vir[None, None, None, :]
    )
    held = (totals / denominator).astype(BF16)
    mirror = jnp.swapaxes(lax.all_to_all(held, "row", split_axis=3, concat_axis=2, tiled=True), 2, 3)
    combined = (2.0 * held.astype(F32) - mirror.astype(F32)).astype(BF16)
    return jnp.einsum("jiab,jbp->iap", combined, gathered, preferred_element_type=F32)


def solution(mesh):
    placed = (
        P("groups", "row", "col"),
        P("groups", "row", "col"),
        P("groups"),
        P("groups"),
        P("groups"),
    )
    chain = mesh.shape["row"] == 4 and mesh.shape["col"] == 4
    return jax.shard_map(
        chain_device if chain else general_device,
        mesh=mesh,
        in_specs=placed,
        out_specs=P("groups", "row", "col"),
        check_vma=False,
    )
```

time: 1470 us -> 631 us (0.43)
  blocking collectives: 547 us -> 0 us
  waiting for transfers between devices: 643 us -> 277 us
  Pallas kernels: 0 us -> 290 us
  local copies, waits for them, and re-layouts: 113 us -> 15.2 us
  matrix products: 95.1 us -> 0 us
  other arithmetic: 57.6 us -> 5.64 us
  starting transfers between devices: 0.04 us -> 40.4 us
    all_to_all x1 -> x0, blocking collectives: 547 us -> none  [mirror_full(): lax.all_to_all(amplitudes, 'row', split_axis=3, concat_axis=2, tiled=True)]
    psum x1 -> x0, waiting for transfers between devices: 420 us -> none  [per_device(): lax.psum(partial_value.astype(jnp.bfloat16), 'col').astype(jnp.float32)]
    pallas_call x0 -> x42, Pallas kernels: none -> 290 us  [call(): pl.pallas_call(body, out_shape=(*out, TOKEN), grid_spec=pltpu.PrefetchSca...]
    ppermute x0 -> x39, waiting for transfers between devices: none -> 277 us  [the longest x10 172 us: to_chip(): return lax.ppermute(values, 'col', [(q, q ^ 2) for q in range(4)])]
    all_gather x1 -> x0, waiting for transfers between devices: 222 us -> none  [per_device(): gathered = lax.all_gather(b_occ_j, 'row', axis=1, tiled=True)]
    convert_element_type x2 -> x0, local copies, waits for them, and re-layouts: 113 us -> none  [the longest x1 67.8 us: combine_pair(): mirror_amps.astype(jnp.float32)]
    dot_general x2 -> x0, matrix products: 95.1 us -> none  [the longest x1 48.6 us: per_device(): jnp.einsum('jiab,jbp->iap', combined, gathered, preferred_element_type=jn...]
    convert_element_type x2 -> x0, other arithmetic: 57.4 us -> none  [the longest x1 32.9 us: combine_pair(): (2.0 * amplitudes.astype(jnp.float32) - mirror_amps.astype(jnp.float32))....]
  transfers between devices with their start and end apart: 2 -> 39, of which waited for: 2 -> 12; matrix products, arithmetic and copies ran while one was open for 0% -> 1% of each run, Pallas kernels for 0% -> 39%
where the time goes in v2:
time: 631 us; the launch traced here: 629 us
  Pallas kernels  290 us (46%)
  waiting for transfers between devices  277 us (44%)
  starting transfers between devices  40.4 us (6%)
  local copies, waits for them, and re-layouts  15.2 us (2%)
    pallas_call x42, Pallas kernels, call(): pl.pallas_call(body, out_shape=(*out, TOKEN), grid_spec=pltpu.PrefetchSca...  290 us
    ppermute x10, waiting for transfers between devices, to_chip(): return lax.ppermute(values, 'col', [(q, q ^ 2) for q in range(4)])  172 us
    ppermute x9, waiting for transfers between devices, along(): return lax.ppermute(values, 'row', steps)  106 us
    ppermute x9, starting transfers between devices, along(): return lax.ppermute(values, 'row', steps)  18.3 us
    ppermute x20, starting transfers between devices, to_core(): return lax.ppermute(values, 'col', [(q, q ^ 1) for q in range(4)])  13.2 us
  transfers between devices with their start and end apart: 39, of which 12 were waited for; matrix products, arithmetic and copies ran while one was open for 1% of the time, Pallas kernels for 39%

profile of v2, /device:TPU:1, one launch (start us, length us, event | category | flops | bytes accessed | tf_op | source)
XLA Modules:
  0.0 629.4 jit_solution(209474027580141464)
XLA Ops:
  19.2 7.4 %pairs_for_chip.5 = (bf16[3,512,512]{2,1,0:T(8,128)(2,1)}, f32[8,128]{1,0:T(8,128)}) custom-call(s32[2]{0:T(128)} %pad_add_fusion.refs_0_, f32[8,128]{1,0:T(8,128)} %get-tuple-element.89.refs_1_, bf16[6,512,1536]{2,1,0:T(8,128)(2,1)} %refs_3_.15, bf16[2,512,1536]{2,1,0:T(8,128)(2,1)} %refs_4_.5, bf16[3,512,512]{2,1,0:T(8,128)(2,1)} %collective-permute-done.refs_4_), custom_call_target="tpu_custom_call" | custom-call | bytes 1024 | tf_op jit(solution)/shard_map/pairs_for_chip/pallas_call | solution.py:27
  31.2 31.5 %collective-permute-done.2.refs_6_ = bf16[3,512,512]{2,1,0:T(8,128)(2,1)} collective-permute-done((bf16[3,512,512]{2,1,0:T(8,128)(2,1)}, bf16[3,512,512]{2,1,0:T(8,128)(2,1)}, u32[]{:S(2)}, u32[]{:S(2)}) %collective-permute-start.2) | collective-permute-done | bytes 1572896 | tf_op jit(solution)/shard_map/ppermute | solution.py:170
  62.7 8.1 %own_amplitudes.5 = (bf16[3,512,512]{2,1,0:T(8,128)(2,1)}, f32[8,128]{1,0:T(8,128)}) custom-call(s32[2]{0:T(128)} %pad_add_fusion.refs_0_, f32[3]{0:T(128)} %dynamic-slice_add_fusion.refs_1_, f32[8,128]{1,0:T(8,128)} %get-tuple-element.91.refs_2_, bf16[6,512,1536]{2,1,0:T(8,128)(2,1)} %refs_3_.15, bf16[2,512,1536]{2,1,0:T(8,128)(2,1)} %refs_4_.5, ...), custom_call_target="tpu_custom_call" | custom-call | bytes 1024 | tf_op jit(solution)/shard_map/own_amplitudes/pallas_call | solution.py:27
  137.0 11.0 %add_gamma.8 = (f32[6,512,1536]{2,1,0:T(8,128)}, f32[8,128]{1,0:T(8,128)}) custom-call(s32[2]{0:T(128)} %pad_add_fusion.refs_0_, f32[8,128]{1,0:T(8,128)} %get-tuple-element.110.refs_1_, bf16[3,512,512]{2,1,0:T(8,128)(2,1)} %get-tuple-element.109.refs_2_, bf16[3,512,512]{2,1,0:T(8,128)(2,1)} %get-tuple-element.111.refs_3_, bf16[2,512,1536]{2,1,0:T(8,128)(2,1)} %refs_4_.5), custom_call_target="tpu_custom_call" | custom-call | bytes 1024 | tf_op jit(solution)/shard_map/add_gamma/pallas_call | solution.py:27
  148.0 11.0 %add_gamma.9 = (f32[6,512,1536]{2,1,0:T(8,128)}, f32[8,128]{1,0:T(8,128)}) custom-call(s32[2]{0:T(128)} %pad_add_fusion.refs_0_, f32[8,128]{1,0:T(8,128)} %get-tuple-element.112.refs_1_, bf16[3,512,512]{2,1,0:T(8,128)(2,1)} %collective-permute-done.8.refs_2_, bf16[3,512,512]{2,1,0:T(8,128)(2,1)} %collective-permute-done.9.refs_3_, ...), custom_call_target="tpu_custom_call", output_to_operand_aliasing={{0}: (5, {})} | custom-call | bytes 1024 | tf_op jit(solution)/shard_map/add_gamma/pallas_call | solution.py:27
  159.0 12.5 %collective-permute-done.11.refs_6_ = bf16[3,512,512]{2,1,0:T(8,128)(2,1)} collective-permute-done((bf16[3,512,512]{2,1,0:T(8,128)(2,1)}, bf16[3,512,512]{2,1,0:T(8,128)(2,1)}, u32[]{:S(2)}, u32[]{:S(2)}) %collective-permute-start.11) | collective-permute-done | bytes 1572896 | tf_op jit(solution)/shard_map/ppermute | solution.py:170
  171.5 8.1 %own_amplitudes.6 = (bf16[3,512,512]{2,1,0:T(8,128)(2,1)}, f32[8,128]{1,0:T(8,128)}) custom-call(s32[2]{0:T(128)} %pad_add_fusion.refs_0_, f32[3]{0:T(128)} %dynamic-slice_add_fusion.refs_1_, f32[8,128]{1,0:T(8,128)} %get-tuple-element.114.refs_2_, bf16[6,512,1536]{2,1,0:T(8,128)(2,1)} %refs_3_.15, bf16[2,512,1536]{2,1,0:T(8,128)(2,1)} %get-tuple-element.99.refs_3_.refs_4_, ...), custom_call_target="tpu_custom_call" | custom-call | bytes 1024 | tf_op jit(solution)/shard_map/own_amplitudes/pallas_call | solution.py:27
  214.2 14.8 %collective-permute-done.16.refs_6_ = bf16[3,512,512]{2,1,0:T(8,128)(2,1)} collective-permute-done((bf16[3,512,512]{2,1,0:T(8,128)(2,1)}, bf16[3,512,512]{2,1,0:T(8,128)(2,1)}, u32[]{:S(2)}, u32[]{:S(2)}) %collective-permute-start.16) | collective-permute-done | bytes 1572896 | tf_op jit(solution)/shard_map/ppermute | solution.py:170
  230.3 8.2 %own_amplitudes.7 = (bf16[3,512,512]{2,1,0:T(8,128)(2,1)}, f32[8,128]{1,0:T(8,128)}) custom-call(s32[2]{0:T(128)} %pad_add_fusion.refs_0_, f32[3]{0:T(128)} %dynamic-slice_add_fusion.refs_1_, f32[8,128]{1,0:T(8,128)} %get-tuple-element.123.refs_2_, bf16[6,512,1536]{2,1,0:T(8,128)(2,1)} %refs_3_.15, ...), custom_call_target="tpu_custom_call" | custom-call | bytes 1024 | tf_op jit(solution)/shard_map/own_amplitudes/pallas_call | solution.py:27
  240.3 61.1 %collective-permute-done.17.refs_3_ = bf16[3,512,512]{2,1,0:T(8,128)(2,1)} collective-permute-done((bf16[3,512,512]{2,1,0:T(8,128)(2,1)}, bf16[3,512,512]{2,1,0:T(8,128)(2,1)}, u32[]{:S(2)}, u32[]{:S(2)}) %collective-permute-start.17) | collective-permute-done | bytes 1572896 | tf_op jit(solution)/shard_map/ppermute | solution.py:173
  306.1 8.1 %own_amplitudes.8 = (bf16[3,512,512]{2,1,0:T(8,128)(2,1)}, f32[8,128]{1,0:T(8,128)}) custom-call(s32[2]{0:T(128)} %pad_add_fusion.refs_0_, f32[3]{0:T(128)} %dynamic-slice_add_fusion.refs_1_, f32[8,128]{1,0:T(8,128)} %get-tuple-element.128.refs_2_, bf16[6,512,1536]{2,1,0:T(8,128)(2,1)} %refs_3_.15, ...), custom_call_target="tpu_custom_call" | custom-call | bytes 1024 | tf_op jit(solution)/shard_map/own_amplitudes/pallas_call | solution.py:27
  345.6 19.7 %collective-permute-done.23.refs_2_ = bf16[3,512,512]{2,1,0:T(8,128)(2,1)S(1)} collective-permute-done((bf16[3,512,512]{2,1,0:T(8,128)(2,1)}, bf16[3,512,512]{2,1,0:T(8,128)(2,1)S(1)}, u32[]{:S(2)}, u32[]{:S(2)}) %collective-permute-start.23) | collective-permute-done | bytes 1572896 | tf_op jit(solution)/shard_map/ppermute | solution.py:170
  367.2 31.8 %collective-permute-done.24.refs_2_ = bf16[3,512,512]{2,1,0:T(8,128)(2,1)S(1)} collective-permute-done((bf16[3,512,512]{2,1,0:T(8,128)(2,1)}, bf16[3,512,512]{2,1,0:T(8,128)(2,1)S(1)}, u32[]{:S(2)}, u32[]{:S(2)}) %collective-permute-start.24) | collective-permute-done | bytes 1572896 | tf_op jit(solution)/shard_map/ppermute | solution.py:170
  402.3 17.7 %add_gamma.10 = (f32[6,512,1536]{2,1,0:T(8,128)}, f32[8,128]{1,0:T(8,128)}) custom-call(s32[2]{0:T(128)} %pad_add_fusion.refs_0_, f32[8,128]{1,0:T(8,128)} %get-tuple-element.143.refs_1_, bf16[3,512,512]{2,1,0:T(8,128)(2,1)} %get-tuple-element.140.refs_2_, bf16[3,512,512]{2,1,0:T(8,128)(2,1)} %get-tuple-element.144.refs_3_, ...), custom_call_target="tpu_custom_call", output_to_operand_aliasing={{0}: (8, {})} | custom-call | bytes 1024 | tf_op jit(solution)/shard_map/add_gamma/pallas_call | solution.py:27
  422.2 17.7 %add_gamma.11 = (f32[6,512,1536]{2,1,0:T(8,128)}, f32[8,128]{1,0:T(8,128)}) custom-call(s32[2]{0:T(128)} %pad_add_fusion.refs_0_, f32[8,128]{1,0:T(8,128)} %get-tuple-element.147.refs_1_, bf16[3,512,512]{2,1,0:T(8,128)(2,1)} %collective-permute-done.25.refs_2_, ...), custom_call_target="tpu_custom_call", output_to_operand_aliasing={{0}: (8, {})} | custom-call | bytes 1024 | tf_op jit(solution)/shard_map/add_gamma/pallas_call | solution.py:27
  440.0 33.1 %collective-permute-done.29.refs_3_ = bf16[3,512,512]{2,1,0:T(8,128)(2,1)} collective-permute-done((bf16[3,512,512]{2,1,0:T(8,128)(2,1)}, bf16[3,512,512]{2,1,0:T(8,128)(2,1)}, u32[]{:S(2)}, u32[]{:S(2)}) %collective-permute-start.29) | collective-permute-done | bytes 1572896 | tf_op jit(solution)/shard_map/ppermute | solution.py:173
  478.8 8.2 %own_amplitudes.9 = (bf16[3,512,512]{2,1,0:T(8,128)(2,1)}, f32[8,128]{1,0:T(8,128)}) custom-call(s32[2]{0:T(128)} %pad_add_fusion.refs_0_, f32[3]{0:T(128)} %dynamic-slice_add_fusion.refs_1_, f32[8,128]{1,0:T(8,128)} %get-tuple-element.151.refs_2_, bf16[6,512,1536]{2,1,0:T(8,128)(2,1)} %refs_3_.15, bf16[2,512,1536]{2,1,0:T(8,128)(2,1)} %get-tuple-element.135.refs_3_.refs_4_, ...), custom_call_target="tpu_custom_call" | custom-call | bytes 1024 | tf_op jit(solution)/shard_map/own_amplitudes/pallas_call | solution.py:27
  487.0 26.5 %collective-permute-done.32.refs_2_ = bf16[3,512,512]{2,1,0:T(8,128)(2,1)S(1)} collective-permute-done((bf16[3,512,512]{2,1,0:T(8,128)(2,1)}, bf16[3,512,512]{2,1,0:T(8,128)(2,1)S(1)}, u32[]{:S(2)}, u32[]{:S(2)}) %collective-permute-start.32) | collective-permute-done | bytes 1572896 | tf_op jit(solution)/shard_map/ppermute | solution.py:170
  520.3 13.7 %add_gamma.12 = (f32[6,512,1536]{2,1,0:T(8,128)}, f32[8,128]{1,0:T(8,128)}) custom-call(s32[2]{0:T(128)} %pad_add_fusion.refs_0_, f32[8,128]{1,0:T(8,128)} %get-tuple-element.156.refs_1_, bf16[3,512,512]{2,1,0:T(8,128)(2,1)} %get-tuple-element.155.refs_2_, bf16[3,512,512]{2,1,0:T(8,128)(2,1)} %get-tuple-element.157.refs_3_, ...), custom_call_target="tpu_custom_call", output_to_operand_aliasing={{0}: (5, {})} | custom-call | bytes 1024 | tf_op jit(solution)/shard_map/add_gamma/pallas_call | solution.py:27
  535.7 13.7 %add_gamma.13 = (f32[6,512,1536]{2,1,0:T(8,128)}, f32[8,128]{1,0:T(8,128)}) custom-call(s32[2]{0:T(128)} %pad_add_fusion.refs_0_, f32[8,128]{1,0:T(8,128)} %get-tuple-element.159.refs_1_, bf16[3,512,512]{2,1,0:T(8,128)(2,1)} %copy-done.9, bf16[3,512,512]{2,1,0:T(8,128)(2,1)} %copy-done.11, ...), custom_call_target="tpu_custom_call", output_to_operand_aliasing={{0}: (5, {})} | custom-call | bytes 1024 | tf_op jit(solution)/shard_map/add_gamma/pallas_call | solution.py:27
  549.4 7.4 %collective-permute-done.35.refs_3_ = bf16[3,512,512]{2,1,0:T(8,128)(2,1)} collective-permute-done((bf16[3,512,512]{2,1,0:T(8,128)(2,1)}, bf16[3,512,512]{2,1,0:T(8,128)(2,1)}, u32[]{:S(2)}, u32[]{:S(2)}) %collective-permute-start.35) | collective-permute-done | bytes 1572896 | tf_op jit(solution)/shard_map/ppermute | solution.py:173
  562.8 34.0 %collective-permute-done.36.refs_2_ = bf16[3,512,512]{2,1,0:T(8,128)(2,1)S(1)} collective-permute-done((bf16[3,512,512]{2,1,0:T(8,128)(2,1)}, bf16[3,512,512]{2,1,0:T(8,128)(2,1)S(1)}, u32[]{:S(2)}, u32[]{:S(2)}) %collective-permute-start.36) | collective-permute-done | bytes 1572896 | tf_op jit(solution)/shard_map/ppermute | solution.py:170
  600.4 13.7 %add_gamma.14 = (f32[6,512,1536]{2,1,0:T(8,128)}, f32[8,128]{1,0:T(8,128)}) custom-call(s32[2]{0:T(128)} %pad_add_fusion.refs_0_, f32[8,128]{1,0:T(8,128)} %get-tuple-element.165.refs_1_, bf16[3,512,512]{2,1,0:T(8,128)(2,1)} %get-tuple-element.164.refs_2_, bf16[3,512,512]{2,1,0:T(8,128)(2,1)} %get-tuple-element.166.refs_3_, ...), custom_call_target="tpu_custom_call", output_to_operand_aliasing={{0}: (5, {})} | custom-call | bytes 1024 | tf_op jit(solution)/shard_map/add_gamma/pallas_call | solution.py:27
  615.7 13.7 %add_gamma.15 = (f32[6,512,1536]{2,1,0:T(8,128)}, f32[8,128]{1,0:T(8,128)}) custom-call(s32[2]{0:T(128)} %pad_add_fusion.refs_0_, f32[8,128]{1,0:T(8,128)} %get-tuple-element.168.refs_1_, bf16[3,512,512]{2,1,0:T(8,128)(2,1)} %copy-done.10, bf16[3,512,512]{2,1,0:T(8,128)(2,1)} %copy-done.12, ...), custom_call_target="tpu_custom_call", output_to_operand_aliasing={{0}: (5, {})} | custom-call | bytes 1024 | tf_op jit(solution)/shard_map/add_gamma/pallas_call | solution.py:27
  (137 shorter events, 196.4 us)
Async XLA Ops:
  8.3 71.5 %collective-permute-start.3 = (bf16[2,512,1536]{2,1,0:T(8,128)(2,1)}, bf16[2,512,1536]{2,1,0:T(8,128)(2,1)}, u32[]{:S(2)}, u32[]{:S(2)}) collective-permute-start(bf16[2,512,1536]{2,1,0:T(8,128)(2,1)} %refs_4_.5), channel_id=1, source_target_pairs={{0,4},{4,0},{8,12},{12,8},{1,5},{5,1},{9,13},{13,9},{2,6},{6,2},{1... | collective-permute-start | bytes 9437192 | tf_op jit(solution)/shard_map/ppermute | solution.py:173
  11.0 69.5 %collective-permute-start.4 = (bf16[2,512,1536]{2,1,0:T(8,128)(2,1)}, bf16[2,512,1536]{2,1,0:T(8,128)(2,1)S(1)}, u32[]{:S(2)}, u32[]{:S(2)}) collective-permute-start(bf16[2,512,1536]{2,1,0:T(8,128)(2,1)} %refs_4_.5), channel_id=1, source_target_pairs={{4,8},{8,4},{5,9},{9,5},{6,10},{10,6},{7,11},{11,7},{20,24},{24,20... | collective-permute-start | bytes 9437192 | tf_op jit(solution)/shard_map/ppermute | solution.py:173
  26.7 36.1 %collective-permute-start.2 = (bf16[3,512,512]{2,1,0:T(8,128)(2,1)}, bf16[3,512,512]{2,1,0:T(8,128)(2,1)}, u32[]{:S(2)}, u32[]{:S(2)}) collective-permute-start(bf16[3,512,512]{2,1,0:T(8,128)(2,1)} %get-tuple-element.93), channel_id=1, source_target_pairs={{0,2},{1,3},{2,0},{3,1},{4,6},{5,7},{6,4},{7,5},{8,10},{9,11},{10,... | collective-permute-start | bytes 4718600 | tf_op jit(solution)/shard_map/ppermute | solution.py:170
  99.1 36.6 %collective-permute-start.8 = (bf16[3,512,512]{2,1,0:T(8,128)(2,1)}, bf16[3,512,512]{2,1,0:T(8,128)(2,1)}, u32[]{:S(2)}, u32[]{:S(2)}) collective-permute-start(bf16[3,512,512]{2,1,0:T(8,128)(2,1)} %get-tuple-element.109.refs_2_), channel_id=1, source_target_pairs={{0,1},{1,0},{2,3},{3,2},{4,5},{5,4},{6,7},{7,6},{8,9},{9,8},{10,11... | collective-permute-start | bytes 4718600 | tf_op jit(solution)/shard_map/ppermute | solution.py:167
  99.9 79.8 %collective-permute-start.12 = (bf16[2,512,1536]{2,1,0:T(8,128)(2,1)}, bf16[2,512,1536]{2,1,0:T(8,128)(2,1)}, u32[]{:S(2)}, u32[]{:S(2)}) collective-permute-start(bf16[2,512,1536]{2,1,0:T(8,128)(2,1)} %get-tuple-element.99.refs_3_.refs_4_), channel_id=1, source_target_pairs={{4,8},{8,4},{5,9},{9,5},{6,10},{10,6},{7,11},{11,7},{20,24},{24,20... | collective-permute-start | bytes 9437192 | tf_op jit(solution)/shard_map/ppermute | solution.py:173
  102.3 78.0 %collective-permute-start.13 = (bf16[2,512,1536]{2,1,0:T(8,128)(2,1)S(1)}, bf16[2,512,1536]{2,1,0:T(8,128)(2,1)}, u32[]{:S(2)}, u32[]{:S(2)}) collective-permute-start(bf16[2,512,1536]{2,1,0:T(8,128)(2,1)S(1)} %copy-done.1), channel_id=1, source_target_pairs={{4,0},{8,12},{5,1},{9,13},{6,2},{10,14},{7,3},{11,15},{20,16},{24,... | collective-permute-start | bytes 9437192 | tf_op jit(solution)/shard_map/ppermute | solution.py:173
  135.7 35.9 %collective-permute-start.11 = (bf16[3,512,512]{2,1,0:T(8,128)(2,1)}, bf16[3,512,512]{2,1,0:T(8,128)(2,1)}, u32[]{:S(2)}, u32[]{:S(2)}) collective-permute-start(bf16[3,512,512]{2,1,0:T(8,128)(2,1)} %get-tuple-element.116), channel_id=1, source_target_pairs={{0,2},{1,3},{2,0},{3,1},{4,6},{5,7},{6,4},{7,5},{8,10},{9,11},{10,... | collective-permute-start | bytes 4718600 | tf_op jit(solution)/shard_map/ppermute | solution.py:170
  192.6 36.3 %collective-permute-start.16 = (bf16[3,512,512]{2,1,0:T(8,128)(2,1)}, bf16[3,512,512]{2,1,0:T(8,128)(2,1)}, u32[]{:S(2)}, u32[]{:S(2)}) collective-permute-start(bf16[3,512,512]{2,1,0:T(8,128)(2,1)} %get-tuple-element.125), channel_id=1, source_target_pairs={{0,2},{1,3},{2,0},{3,1},{4,6},{5,7},{6,4},{7,5},{8,10},{9,11},{10,... | collective-permute-start | bytes 4718600 | tf_op jit(solution)/shard_map/ppermute | solution.py:170
  193.9 36.3 %collective-permute-start.15 = (bf16[3,512,512]{2,1,0:T(8,128)(2,1)}, bf16[3,512,512]{2,1,0:T(8,128)(2,1)}, u32[]{:S(2)}, u32[]{:S(2)}) collective-permute-start(bf16[3,512,512]{2,1,0:T(8,128)(2,1)} %get-tuple-element.124), channel_id=1, source_target_pairs={{0,1},{1,0},{2,3},{3,2},{4,5},{5,4},{6,7},{7,6},{8,9},{9,8},{10,11... | collective-permute-start | bytes 4718600 | tf_op jit(solution)/shard_map/ppermute | solution.py:167
  194.2 124.8 %collective-permute-start.21 = (bf16[2,512,1536]{2,1,0:T(8,128)(2,1)}, bf16[2,512,1536]{2,1,0:T(8,128)(2,1)S(1)}, u32[]{:S(2)}, u32[]{:S(2)}) collective-permute-start(bf16[2,512,1536]{2,1,0:T(8,128)(2,1)} %get-tuple-element.119), channel_id=1, source_target_pairs={{4,0},{8,12},{5,1},{9,13},{6,2},{10,14},{7,3},{11,15},{20,16},{24,... | collective-permute-start | bytes 9437192 | tf_op jit(solution)/shard_map/ppermute | solution.py:173
  202.6 98.8 %collective-permute-start.17 = (bf16[3,512,512]{2,1,0:T(8,128)(2,1)}, bf16[3,512,512]{2,1,0:T(8,128)(2,1)}, u32[]{:S(2)}, u32[]{:S(2)}) collective-permute-start(bf16[3,512,512]{2,1,0:T(8,128)(2,1)} %get-tuple-element.127.refs_2_), channel_id=1, source_target_pairs={{0,4},{4,0},{8,12},{12,8},{1,5},{5,1},{9,13},{13,9},{2,6},{6,2},{1... | collective-permute-start | bytes 4718600 | tf_op jit(solution)/shard_map/ppermute | solution.py:173
  206.3 99.8 %collective-permute-start.18 = (bf16[3,512,512]{2,1,0:T(8,128)(2,1)}, bf16[3,512,512]{2,1,0:T(8,128)(2,1)}, u32[]{:S(2)}, u32[]{:S(2)}) collective-permute-start(bf16[3,512,512]{2,1,0:T(8,128)(2,1)} %get-tuple-element.129), channel_id=1, source_target_pairs={{0,1},{1,0},{2,3},{3,2},{4,5},{5,4},{6,7},{7,6},{8,9},{9,8},{10,11... | collective-permute-start | bytes 4718600 | tf_op jit(solution)/shard_map/ppermute | solution.py:167
  228.9 77.2 %collective-permute-start.19 = (bf16[3,512,512]{2,1,0:T(8,128)(2,1)}, bf16[3,512,512]{2,1,0:T(8,128)(2,1)}, u32[]{:S(2)}, u32[]{:S(2)}) collective-permute-start(bf16[3,512,512]{2,1,0:T(8,128)(2,1)} %get-tuple-element.130), channel_id=1, source_target_pairs={{0,2},{1,3},{2,0},{3,1},{4,6},{5,7},{6,4},{7,5},{8,10},{9,11},{10,... | collective-permute-start | bytes 4718600 | tf_op jit(solution)/shard_map/ppermute | solution.py:170
  238.4 75.8 %collective-permute-start.20 = (bf16[3,512,512]{2,1,0:T(8,128)(2,1)}, bf16[3,512,512]{2,1,0:T(8,128)(2,1)}, u32[]{:S(2)}, u32[]{:S(2)}) collective-permute-start(bf16[3,512,512]{2,1,0:T(8,128)(2,1)} %get-tuple-element.132.refs_2_), channel_id=1, source_target_pairs={{4,8},{8,4},{5,9},{9,5},{6,10},{10,6},{7,11},{11,7},{20,24},{24,20... | collective-permute-start | bytes 4718600 | tf_op jit(solution)/shard_map/ppermute | solution.py:173
  329.1 36.2 %collective-permute-start.23 = (bf16[3,512,512]{2,1,0:T(8,128)(2,1)}, bf16[3,512,512]{2,1,0:T(8,128)(2,1)S(1)}, u32[]{:S(2)}, u32[]{:S(2)}) collective-permute-start(bf16[3,512,512]{2,1,0:T(8,128)(2,1)} %get-tuple-element.140.refs_2_), channel_id=1, source_target_pairs={{0,2},{1,3},{2,0},{3,1},{4,6},{5,7},{6,4},{7,5},{8,10},{9,11},{10,... | collective-permute-start | bytes 4718600 | tf_op jit(solution)/shard_map/ppermute | solution.py:170
  329.9 69.2 %collective-permute-start.24 = (bf16[3,512,512]{2,1,0:T(8,128)(2,1)}, bf16[3,512,512]{2,1,0:T(8,128)(2,1)S(1)}, u32[]{:S(2)}, u32[]{:S(2)}) collective-permute-start(bf16[3,512,512]{2,1,0:T(8,128)(2,1)} %get-tuple-element.142.refs_5_), channel_id=1, source_target_pairs={{0,2},{1,3},{2,0},{3,1},{4,6},{5,7},{6,4},{7,5},{8,10},{9,11},{10,... | collective-permute-start | bytes 4718600 | tf_op jit(solution)/shard_map/ppermute | solution.py:170
  330.6 89.4 %collective-permute-start.25 = (bf16[3,512,512]{2,1,0:T(8,128)(2,1)}, bf16[3,512,512]{2,1,0:T(8,128)(2,1)}, u32[]{:S(2)}, u32[]{:S(2)}) collective-permute-start(bf16[3,512,512]{2,1,0:T(8,128)(2,1)} %get-tuple-element.140.refs_2_), channel_id=1, source_target_pairs={{0,1},{1,0},{2,3},{3,2},{4,5},{5,4},{6,7},{7,6},{8,9},{9,8},{10,11... | collective-permute-start | bytes 4718600 | tf_op jit(solution)/shard_map/ppermute | solution.py:167
  331.2 89.6 %collective-permute-start.27 = (bf16[3,512,512]{2,1,0:T(8,128)(2,1)}, bf16[3,512,512]{2,1,0:T(8,128)(2,1)}, u32[]{:S(2)}, u32[]{:S(2)}) collective-permute-start(bf16[3,512,512]{2,1,0:T(8,128)(2,1)} %get-tuple-element.142.refs_5_), channel_id=1, source_target_pairs={{0,1},{1,0},{2,3},{3,2},{4,5},{5,4},{6,7},{7,6},{8,9},{9,8},{10,11... | collective-permute-start | bytes 4718600 | tf_op jit(solution)/shard_map/ppermute | solution.py:167
  401.8 71.2 %collective-permute-start.29 = (bf16[3,512,512]{2,1,0:T(8,128)(2,1)}, bf16[3,512,512]{2,1,0:T(8,128)(2,1)}, u32[]{:S(2)}, u32[]{:S(2)}) collective-permute-start(bf16[3,512,512]{2,1,0:T(8,128)(2,1)} %get-tuple-element.150.refs_2_), channel_id=1, source_target_pairs={{0,8},{8,0},{4,12},{12,4},{1,9},{9,1},{5,13},{13,5},{2,10},{10,2},... | collective-permute-start | bytes 4718600 | tf_op jit(solution)/shard_map/ppermute | solution.py:173
  420.0 58.8 %collective-permute-start.30 = (bf16[3,512,512]{2,1,0:T(8,128)(2,1)}, bf16[3,512,512]{2,1,0:T(8,128)(2,1)}, u32[]{:S(2)}, u32[]{:S(2)}) collective-permute-start(bf16[3,512,512]{2,1,0:T(8,128)(2,1)} %get-tuple-element.152), channel_id=1, source_target_pairs={{0,1},{1,0},{2,3},{3,2},{4,5},{5,4},{6,7},{7,6},{8,9},{9,8},{10,11... | collective-permute-start | bytes 4718600 | tf_op jit(solution)/shard_map/ppermute | solution.py:167
  420.7 58.1 %collective-permute-start.31 = (bf16[3,512,512]{2,1,0:T(8,128)(2,1)}, bf16[3,512,512]{2,1,0:T(8,128)(2,1)}, u32[]{:S(2)}, u32[]{:S(2)}) collective-permute-start(bf16[3,512,512]{2,1,0:T(8,128)(2,1)} %get-tuple-element.153), channel_id=1, source_target_pairs={{0,2},{1,3},{2,0},{3,1},{4,6},{5,7},{6,4},{7,5},{8,10},{9,11},{10,... | collective-permute-start | bytes 4718600 | tf_op jit(solution)/shard_map/ppermute | solution.py:170
  478.1 55.9 %collective-permute-start.33 = (bf16[3,512,512]{2,1,0:T(8,128)(2,1)}, bf16[3,512,512]{2,1,0:T(8,128)(2,1)S(1)}, u32[]{:S(2)}, u32[]{:S(2)}) collective-permute-start(bf16[3,512,512]{2,1,0:T(8,128)(2,1)} %get-tuple-element.155.refs_2_), channel_id=1, source_target_pairs={{0,1},{1,0},{2,3},{3,2},{4,5},{5,4},{6,7},{7,6},{8,9},{9,8},{10,11... | collective-permute-start | bytes 4718600 | tf_op jit(solution)/shard_map/ppermute | solution.py:167
  516.8 40.0 %collective-permute-start.35 = (bf16[3,512,512]{2,1,0:T(8,128)(2,1)}, bf16[3,512,512]{2,1,0:T(8,128)(2,1)}, u32[]{:S(2)}, u32[]{:S(2)}) collective-permute-start(bf16[3,512,512]{2,1,0:T(8,128)(2,1)} %get-tuple-element.162.refs_2_), channel_id=1, source_target_pairs={{0,12},{12,0},{1,13},{13,1},{2,14},{14,2},{3,15},{15,3},{16,28},{2... | collective-permute-start | bytes 4718600 | tf_op jit(solution)/shard_map/ppermute | solution.py:173
  561.7 52.3 %collective-permute-start.37 = (bf16[3,512,512]{2,1,0:T(8,128)(2,1)}, bf16[3,512,512]{2,1,0:T(8,128)(2,1)S(1)}, u32[]{:S(2)}, u32[]{:S(2)}) collective-permute-start(bf16[3,512,512]{2,1,0:T(8,128)(2,1)} %get-tuple-element.164.refs_2_), channel_id=1, source_target_pairs={{0,1},{1,0},{2,3},{3,2},{4,5},{5,4},{6,7},{7,6},{8,9},{9,8},{10,11... | collective-permute-start | bytes 4718600 | tf_op jit(solution)/shard_map/ppermute | solution.py:167
  (32 other events, 430.8 us)

commit v3 on v0

v3 whole, which is shorter than its diff:
```python
import functools

import jax
import jax.numpy as jnp
from jax import lax
from jax.experimental import pallas as pl
from jax.experimental.pallas import tpu as pltpu
from jax.sharding import PartitionSpec as P

F32 = jnp.float32
BF16 = jnp.bfloat16
ANY = pl.BlockSpec(memory_space=pl.ANY)
TOKEN = jax.ShapeDtypeStruct((8, 128), F32)
TILE = 256


def tile_of(size):
    return TILE if size % TILE == 0 else size


def call(kernel, name, token, place, grid, in_specs, args, out_specs, out, aliases=None):
    def body(*refs):
        n = len(place)
        kernel(*refs[:n], *refs[n + 1 : -1])

    shift = len(place) + 1
    return pl.pallas_call(
        body,
        out_shape=(*out, TOKEN),
        grid_spec=pltpu.PrefetchScalarGridSpec(
            num_scalar_prefetch=len(place),
            grid=grid,
            in_specs=[ANY] + in_specs,
            out_specs=(*out_specs, ANY),
        ),
        input_output_aliases={k + shift: v for k, v in (aliases or {}).items()},
        compiler_params=pltpu.CompilerParams(vmem_limit_bytes=40 * 2**20),
        cost_estimate=pl.CostEstimate(flops=0, bytes_accessed=1024, transcendentals=0),
        name=name,
    )(*place, token, *args)


def tie_kernel(place, *refs):
    del place, refs


def tie(token, place, *held):
    n = len(held)
    shapes = [held_shape(h) for h in held]
    return call(tie_kernel, "tie", token, place, (1,), [ANY] * n, held, [ANY] * n, shapes, {k: k for k in range(n)})


def held_shape(a):
    return jax.ShapeDtypeStruct(a.shape, a.dtype)


def takes_part(place, part):
    return place[3 if part == "middle" else 4] == 1


def only(place, part, out):
    def run(body):
        if part is None:
            body()
            return
        pl.when(takes_part(place, part))(body)

        @pl.when(jnp.logical_not(takes_part(place, part)))
        def _():
            out[...] = jnp.zeros_like(out)

    return run


def pairs_kernel(n_place, has_last, part, *refs):
    place, (b_i, b_i_core, block, block_core, *rest) = refs[:n_place], refs[n_place:]
    out = rest[-1]
    across = (((1,), (1,)), ((), ()))

    @only(place[0], part, out)
    def _():
        value = lax.dot_general(b_i[0], block[0], across, preferred_element_type=F32)
        value += lax.dot_general(b_i_core[0], block_core[0], across, preferred_element_type=F32)
        if has_last:
            chip, vir_a, vir_b = rest[:3]
            value = value + chip[0].astype(F32)
            value = value / ((place[1][pl.program_id(0)] - vir_a[...]) - vir_b[...])
        out[0] = value.astype(BF16)


def pairs(token, place, b_i, block, own_j, part, last=None):
    (mine, core_part), (block, block_core) = b_i, block
    n_j, cols, depth = block.shape
    half, rows = core_part.shape[:2]

    def j_of(s):
        return s[0] if own_j else 1 - s[0]

    one = pl.BlockSpec((1, rows, cols), lambda i, s, *_: (i, 0, 0))
    block_spec = pl.BlockSpec((1, cols, depth), lambda i, s, *_: (j_of(s), 0, 0))
    in_specs = [
        pl.BlockSpec((1, rows, depth), lambda i, s, *_: (s[1] * half + i, 0, 0)),
        pl.BlockSpec((1, rows, depth), lambda i, s, *_: (i, 0, 0)),
        block_spec,
        block_spec,
    ]
    args, name = [mine, core_part, block, block_core], "pairs_for_chip"
    if last is not None:
        chip, occ, vir_a, vir_b = last
        place = place + (occ,)
        in_specs += [
            one,
            pl.BlockSpec((rows, 1), lambda i, s, *_: (0, 0)),
            pl.BlockSpec((1, cols), lambda i, s, *_: (0, 0)),
        ]
        args += [chip, vir_a, vir_b]
        name = "own_amplitudes"
    out = jax.ShapeDtypeStruct((half, rows, cols), BF16)
    kernel = functools.partial(pairs_kernel, len(place), last is not None, part)
    return call(kernel, name, token, place, (half,), in_specs, args, [one], [out])


def combine_kernel(part, place, held, mirror, out):
    @only(place, part, out)
    def _():
        out[0] = (2.0 * held[0].astype(F32) - mirror[0].astype(F32).T).astype(BF16)


def combine_pairs(token, place, held, mirror, part):
    spec = pl.BlockSpec((1,) + held.shape[1:], lambda i, s: (i, 0, 0))
    kernel = functools.partial(combine_kernel, part)
    return call(kernel, "combine_pairs", token, place, held.shape[:1], [spec, spec], [held, mirror], [spec], [held_shape(held)])


def gamma_kernel(n_blocks, n_out, has_sum, place, *refs):
    x = place[0]
    outs = refs[len(refs) - n_out :]
    befores = refs[len(refs) - 2 * n_out : len(refs) - n_out]
    half, rows, tile = outs[0].shape
    step = 2 + n_out
    for k in range(n_out):
        total = befores[k][...].reshape(half * rows, tile) if has_sum else None
        for n in range(n_blocks):
            same_j, other_j = refs[step * n : step * n + 2]
            block = refs[step * n + 2 + k]
            for held, j in ((same_j, x), (other_j, 1 - x)):
                left = held[...].reshape(half * rows, held.shape[2])
                term = jnp.dot(left, block[j], preferred_element_type=F32)
                total = term if total is None else total + term
        outs[k][...] = total.reshape(half, rows, tile)


def gamma_operands(terms, tile):
    in_specs, args = [], []
    for *held, blocks in terms:
        in_specs += [pl.BlockSpec(h.shape, lambda p, s: (0, 0, 0), pipeline_mode=pl.Buffered(1)) for h in held]
        in_specs += [pl.BlockSpec(b.shape[:2] + (tile,), lambda p, s: (0, 0, p)) for b in blocks]
        args += [*held, *blocks]
    return in_specs, args


def chip_gamma(token, place, terms, before):
    half, rows = terms[0][0].shape[:2]
    depth = terms[0][2][0].shape[2]
    tile = tile_of(depth)
    in_specs, args = gamma_operands(terms, tile)
    spec = pl.BlockSpec((half, rows, tile), lambda p, s: (0, 0, p))
    aliases = None
    if before is not None:
        aliases = {len(args): 0, len(args) + 1: 1}
        in_specs += [spec, spec]
        args += before
    out = [jax.ShapeDtypeStruct((half, rows, depth), F32)] * 2
    kernel = functools.partial(gamma_kernel, len(terms), 2, before is not None)
    *out, token = call(kernel, "chip_gamma", token, place, (depth // tile,), in_specs, args, [spec, spec], out, aliases)
    return out, token


def last_gamma(token, place, mine, terms, before, shape, result):
    half, rows, depth = shape[0] // 2, shape[1], shape[2]
    tile = tile_of(depth)
    in_specs, args = gamma_operands(terms, tile)
    spec = pl.BlockSpec((half, rows, tile), lambda p, s: (0, 0, p))
    aliases, out_spec, out = None, spec, held_shape(before)
    if mine is None:
        aliases = {len(args): 0}
    else:
        out_spec = pl.BlockSpec((half, rows, tile), lambda p, s: (s[1] if mine else 1 - s[1], 0, p))
        out = jax.ShapeDtypeStruct(shape, F32)
    if result is not None:
        aliases = {len(args): 0}
        in_specs.append(ANY)
        args.append(result)
    in_specs.append(spec)
    args.append(before)
    kernel = functools.partial(gamma_kernel, len(terms), 1, True)
    return call(kernel, "last_gamma", token, place, (depth // tile,), in_specs, args, [out_spec], [out], aliases)


def chain_device(b_occ_i, b_occ_j, eps_occ_i, eps_occ_j, eps_vir):
    n_i, rows, depth = b_occ_i.shape
    half = n_i // 2
    z, col = lax.axis_index("row"), lax.axis_index("col")
    x, core = col // 2, col % 2
    in_middle = (z == 1) | (z == 2)
    place = (jnp.stack([x, core, z, in_middle, ~in_middle]).astype(jnp.int32),)
    occ = lax.dynamic_slice_in_dim(eps_occ_i, core * half, half, 0) + eps_occ_j[x]
    token = jnp.zeros(TOKEN.shape, F32)

    def energies(block):
        return lax.dynamic_slice_in_dim(eps_vir, block * rows, rows, 0)

    vir_a = energies(z)[:, None]

    def to_col(values, flip, part):
        rows_in = {None: range(4), "middle": (1, 2), "ends": (0, 3)}[part]
        steps = [(4 * r + q, 4 * r + (q ^ flip)) for r in rows_in for q in range(4)]
        return lax.ppermute(values, ("row", "col"), steps)

    def to_core(values, part=None):
        return to_col(values, 1, part)

    def to_chip(values, part=None):
        return to_col(values, 2, part)

    def along(values, steps):
        return lax.ppermute(values, "row", steps)

    ends, middle = [(1, 0), (2, 3)], [(1, 2), (2, 1)]
    pairs_1 = [(0, 1), (1, 0), (2, 3), (3, 2)]
    pairs_2 = [(0, 2), (2, 0), (1, 3), (3, 1)]
    pairs_3 = [(0, 3), (3, 0)]
    b_i = b_occ_i, to_core(lax.dynamic_slice_in_dim(b_occ_i, (1 - core) * half, half, 0))

    def pass_on(block, part=None):
        nonlocal token
        out, token = pairs(token, place, b_i, block, False, part)
        return to_chip(out, part)

    def own(block, chip_sum, shift, part=None):
        nonlocal token
        vir_b = energies(z ^ shift)[None, :]
        out, token = pairs(token, place, b_i, block, True, part, (chip_sum, occ, vir_a, vir_b))
        return out

    def combine(held, mirror, part=None):
        nonlocal token
        out, token = combine_pairs(token, place, held, mirror, part)
        return out, to_chip(out, part)

    def forward(*values):
        nonlocal token
        *out, token = tie(token, place, *values)
        return out

    gamma = None

    def add(*terms):
        nonlocal token, gamma
        gamma, token = chip_gamma(token, place, terms, gamma)

    def both(values, part=None):
        return values, to_core(values, part)

    near = along(b_occ_j, pairs_1)
    across = along(b_occ_j, middle)
    here = both(b_occ_j)

    chip_0 = pass_on(here)
    held_0 = own(here, chip_0, 0)
    mine_0, other_0 = combine(held_0, held_0)

    near, across = forward(near, across)
    far_mid = along(near, middle)
    far_end = along(across, ends)
    near = both(near)
    across = both(across, "middle")
    chip_1 = pass_on(near)
    chip_12 = pass_on(across, "middle")

    add((mine_0, other_0, here))

    held_1 = own(near, chip_1, 1)
    mirror_1 = along(held_1, pairs_1)

    (far_mid,) = forward(far_mid)
    last = along(far_mid, ends)
    far = both(jnp.where(in_middle, far_mid, far_end))
    chip_2 = pass_on(far)

    held_12 = own(across, chip_12, 3, "middle")
    mirror_12 = along(held_12, middle)

    mine_1, other_1 = combine(held_1, mirror_1)
    held_2 = own(far, chip_2, 2)
    mirror_2 = along(held_2, pairs_2)
    mine_12, other_12 = combine(held_12, mirror_12, "middle")

    add((mine_1, other_1, near))
    gamma, rest = gamma[0], to_core(gamma[1])
    shape = b_occ_i.shape

    (last,) = forward(last)
    last = both(last, "ends")
    chip_3 = pass_on(last, "ends")

    same_12 = to_core(mine_12, "middle")
    (other_12,) = forward(other_12)
    both_12 = to_core(other_12, "middle")

    mine_2, other_2 = combine(held_2, mirror_2)
    same_2 = to_core(mine_2)
    held_3 = own(last, chip_3, 3, "ends")
    mirror_3 = along(held_3, pairs_3)

    (other_2,) = forward(other_2)
    both_2 = to_core(other_2)
    terms = [(mine_12, other_12, across[:1]), (mine_2, other_2, far[:1])]
    gamma, token = last_gamma(token, place, None, terms, gamma, shape, None)

    mine_3, other_3 = combine(held_3, mirror_3, "ends")
    same_3 = to_core(mine_3, "ends")
    terms = [(same_12, both_12, across[:1]), (same_2, both_2, far[:1])]
    rest, token = last_gamma(token, place, None, terms, rest, shape, None)

    (other_3,) = forward(other_3)
    both_3 = to_core(other_3, "ends")
    result, token = last_gamma(token, place, True, [(mine_3, other_3, last[:1])], gamma, shape, None)
    result, token = last_gamma(token, place, False, [(same_3, both_3, last[:1])], rest, shape, result)
    return result


def general_device(b_occ_i, b_occ_j, eps_occ_i, eps_occ_j, eps_vir):
    rows = b_occ_i.shape[1]
    own_energy = lax.dynamic_slice_in_dim(eps_vir, lax.axis_index("row") * rows, rows, 0)
    gathered = lax.all_gather(b_occ_j, "row", axis=1, tiled=True)
    partial_value = jnp.einsum("iap,jbp->jiab", b_occ_i, gathered, preferred_element_type=F32)
    totals = lax.psum(partial_value.astype(BF16), "col").astype(F32)
    denominator = (
        eps_occ_j[:, None, None, None]
        + eps_occ_i[None, :, None, None]
        - own_energy[None, None, :, None]
        - eps_vir[None, None, None, :]
    )
    held = (totals / denominator).astype(BF16)
    mirror = jnp.swapaxes(lax.all_to_all(held, "row", split_axis=3, concat_axis=2, tiled=True), 2, 3)
    combined = (2.0 * held.astype(F32) - mirror.astype(F32)).astype(BF16)
    return jnp.einsum("jiab,jbp->iap", combined, gathered, preferred_element_type=F32)


def solution(mesh):
    placed = (
        P("groups", "row", "col"),
        P("groups", "row", "col"),
        P("groups"),
        P("groups"),
        P("groups"),
    )
    chain = mesh.shape["row"] == 4 and mesh.shape["col"] == 4
    return jax.shard_map(
        chain_device if chain else general_device,
        mesh=mesh,
        in_specs=placed,
        out_specs=P("groups", "row", "col"),
        check_vma=False,
    )
```

time: 1470 us -> 508 us (0.35)
  blocking collectives: 547 us -> 0 us
  waiting for transfers between devices: 643 us -> 210 us
  Pallas kernels: 0 us -> 193 us
  matrix products: 95.1 us -> 0 us
  local copies, waits for them, and re-layouts: 113 us -> 24.5 us
  starting transfers between devices: 0.04 us -> 75.7 us
  other arithmetic: 57.6 us -> 2.92 us
    all_to_all x1 -> x0, blocking collectives: 547 us -> none  [mirror_full(): lax.all_to_all(amplitudes, 'row', split_axis=3, concat_axis=2, tiled=True)]
    psum x1 -> x0, waiting for transfers between devices: 420 us -> none  [per_device(): lax.psum(partial_value.astype(jnp.bfloat16), 'col').astype(jnp.float32)]
    all_gather x1 -> x0, waiting for transfers between devices: 222 us -> none  [per_device(): gathered = lax.all_gather(b_occ_j, 'row', axis=1, tiled=True)]
    ppermute x0 -> x32, waiting for transfers between devices: none -> 210 us  [the longest x23 139 us: to_col(): return lax.ppermute(values, ('row', 'col'), steps)]
    pallas_call x0 -> x27, Pallas kernels: none -> 193 us  [call(): pl.pallas_call(body, out_shape=(*out, TOKEN), grid_spec=pltpu.PrefetchSca...]
    convert_element_type x2 -> x0, local copies, waits for them, and re-layouts: 113 us -> none  [the longest x1 67.8 us: combine_pair(): mirror_amps.astype(jnp.float32)]
    dot_general x2 -> x0, matrix products: 95.1 us -> none  [the longest x1 48.6 us: per_device(): jnp.einsum('jiab,jbp->iap', combined, gathered, preferred_element_type=jn...]
    ppermute x0 -> x32, starting transfers between devices: none -> 75.7 us  [the longest x9 45 us: along(): return lax.ppermute(values, 'row', steps)]
  transfers between devices with their start and end apart: 2 -> 32, of which waited for: 2 -> 11; matrix products, arithmetic and copies ran while one was open for 0% -> 0% of each run, Pallas kernels for 0% -> 36%
where the time goes in v3:
time: 508 us; the launch traced here: 507 us
  waiting for transfers between devices  210 us (41%)
  Pallas kernels  193 us (38%)
  starting transfers between devices  75.7 us (15%)
  local copies, waits for them, and re-layouts  24.5 us (5%)
    pallas_call x27, Pallas kernels, call(): pl.pallas_call(body, out_shape=(*out, TOKEN), grid_spec=pltpu.PrefetchSca...  193 us
    ppermute x23, waiting for transfers between devices, to_col(): return lax.ppermute(values, ('row', 'col'), steps)  139 us
    ppermute x9, waiting for transfers between devices, along(): return lax.ppermute(values, 'row', steps)  71 us
    ppermute x9, starting transfers between devices, along(): return lax.ppermute(values, 'row', steps)  45 us
    ppermute x23, starting transfers between devices, to_col(): return lax.ppermute(values, ('row', 'col'), steps)  30.7 us
    unnamed x54, local copies, waits for them, and re-layouts  18.7 us
  transfers between devices with their start and end apart: 32, of which 11 were waited for; matrix products, arithmetic and copies ran while one was open for 0% of the time, Pallas kernels for 36%

profile of v3, /device:TPU:1, one launch (start us, length us, event | category | flops | bytes accessed | tf_op | source)
XLA Modules:
  0.0 506.5 jit_solution(9567014823172475844)
XLA Ops:
  8.6 9.0 %collective-permute-done.1.refs_5_.refs_6_ = bf16[2,512,1536]{2,1,0:T(8,128)(2,1)} collective-permute-done((bf16[2,512,1536]{2,1,0:T(8,128)(2,1)}, bf16[2,512,1536]{2,1,0:T(8,128)(2,1)}, u32[]{:S(2)}, u32[]{:S(2)}) %collective-permute-start.1) | collective-permute-done | bytes 3145760 | tf_op jit(solution)/shard_map/ppermute | solution.py:218
  17.6 9.9 %pairs_for_chip.5 = (bf16[3,512,512]{2,1,0:T(8,128)(2,1)}, f32[8,128]{1,0:T(8,128)S(1)}) custom-call(s32[5]{0:T(128)S(1)} %stack.31.refs_0_, f32[8,128]{1,0:T(8,128)S(1)} %broadcast_in_dim.19.refs_1_, bf16[6,512,1536]{2,1,0:T(8,128)(2,1)} %refs_3_.9, bf16[3,512,1536]{2,1,0:T(8,128)(2,1)} %collective-permute-done.refs_3_.refs_4_, ...), custom_call_target="tpu_custom_call" | custom-call | bytes 1024 | tf_op jit(solution)/shard_map/pairs_for_chip/pallas_call | solution.py:27
  31.4 33.2 %collective-permute-done.2.refs_7_ = bf16[3,512,512]{2,1,0:T(8,128)(2,1)} collective-permute-done((bf16[3,512,512]{2,1,0:T(8,128)(2,1)}, bf16[3,512,512]{2,1,0:T(8,128)(2,1)}, u32[]{:S(2)}, u32[]{:S(2)}) %collective-permute-start.2) | collective-permute-done | bytes 1572896 | tf_op jit(solution)/shard_map/ppermute | solution.py:218
  64.6 9.7 %own_amplitudes.5 = (bf16[3,512,512]{2,1,0:T(8,128)(2,1)S(1)}, f32[8,128]{1,0:T(8,128)S(1)}) custom-call(s32[5]{0:T(128)S(1)} %stack.31.refs_0_, f32[3]{0:T(128)S(1)} %dynamic-slice_add_fusion.refs_1_, f32[8,128]{1,0:T(8,128)S(1)} %get-tuple-element.61.refs_2_, bf16[6,512,1536]{2,1,0:T(8,128)(2,1)} %refs_3_.9, ...), custom_call_target="tpu_custom_call" | custom-call | bytes 1024 | tf_op jit(solution)/shard_map/own_amplitudes/pallas_call | solution.py:27
  83.6 10.0 %pairs_for_chip.6 = (bf16[3,512,512]{2,1,0:T(8,128)(2,1)}, f32[8,128]{1,0:T(8,128)S(1)}) custom-call(s32[5]{0:T(128)S(1)} %stack.31.refs_0_, f32[8,128]{1,0:T(8,128)S(1)} %get-tuple-element.66.refs_1_, bf16[6,512,1536]{2,1,0:T(8,128)(2,1)} %refs_3_.9, bf16[3,512,1536]{2,1,0:T(8,128)(2,1)} %collective-permute-done.refs_3_.refs_4_, ...), custom_call_target="tpu_custom_call" | custom-call | bytes 1024 | tf_op jit(solution)/shard_map/pairs_for_chip/pallas_call | solution.py:27
  101.3 17.0 %collective-permute-done.7.refs_3_ = bf16[3,512,512]{2,1,0:T(8,128)(2,1)S(1)} collective-permute-done((bf16[3,512,512]{2,1,0:T(8,128)(2,1)S(1)}, bf16[3,512,512]{2,1,0:T(8,128)(2,1)S(1)}, u32[]{:S(2)}, u32[]{:S(2)}) %collective-permute-start.7) | collective-permute-done | bytes 1572896 | tf_op jit(solution)/shard_map/ppermute | solution.py:218
  120.9 15.0 %chip_gamma.2 = (f32[3,512,1536]{2,1,0:T(8,128)}, f32[3,512,1536]{2,1,0:T(8,128)}, f32[8,128]{1,0:T(8,128)S(1)}) custom-call(s32[5]{0:T(128)S(1)} %stack.31.refs_0_, f32[8,128]{1,0:T(8,128)S(1)} %get-tuple-element.70.refs_1_, bf16[3,512,512]{2,1,0:T(8,128)(2,1)S(1)} %copy-done.21, bf16[3,512,512]{2,1,0:T(8,128)(2,1)S(1)} %copy-done.23, ...), custom_call_target="tpu_custom_call" | custom-call | bytes 1024 | tf_op jit(solution)/shard_map/chip_gamma/pallas_call | solution.py:27
  135.9 16.2 %collective-permute-done.8.refs_7_ = bf16[3,512,512]{2,1,0:T(8,128)(2,1)S(1)} collective-permute-done((bf16[3,512,512]{2,1,0:T(8,128)(2,1)}, bf16[3,512,512]{2,1,0:T(8,128)(2,1)S(1)}, u32[]{:S(2)}, u32[]{:S(2)}) %collective-permute-start.8) | collective-permute-done | bytes 1572896 | tf_op jit(solution)/shard_map/ppermute | solution.py:218
  154.6 9.5 %own_amplitudes.6 = (bf16[3,512,512]{2,1,0:T(8,128)(2,1)}, f32[8,128]{1,0:T(8,128)S(1)}) custom-call(s32[5]{0:T(128)S(1)} %stack.31.refs_0_, f32[3]{0:T(128)S(1)} %dynamic-slice_add_fusion.refs_1_, f32[8,128]{1,0:T(8,128)S(1)} %get-tuple-element.72.refs_2_, bf16[6,512,1536]{2,1,0:T(8,128)(2,1)} %refs_3_.9, ...), custom_call_target="tpu_custom_call" | custom-call | bytes 1024 | tf_op jit(solution)/shard_map/own_amplitudes/pallas_call | solution.py:27
  168.5 10.4 %collective-permute-start.13 = (bf16[3,512,512]{2,1,0:T(8,128)(2,1)}, bf16[3,512,512]{2,1,0:T(8,128)(2,1)}, u32[]{:S(2)}, u32[]{:S(2)}) collective-permute-start(bf16[3,512,512]{2,1,0:T(8,128)(2,1)} %get-tuple-element.80.refs_2_), channel_id=1, source_target_pairs={{0,4},{4,0},{8,12},{12,8},{1,5},{5,1},{9,13},{13,9},{2,6},{6,2},{1... | collective-permute-start | bytes 4718600 | tf_op jit(solution)/shard_map/ppermute | solution.py:227
  180.4 9.5 %pairs_for_chip.8 = (bf16[3,512,512]{2,1,0:T(8,128)(2,1)}, f32[8,128]{1,0:T(8,128)S(1)}) custom-call(s32[5]{0:T(128)S(1)} %stack.31.refs_0_, f32[8,128]{1,0:T(8,128)S(1)} %get-tuple-element.75.refs_1_, bf16[6,512,1536]{2,1,0:T(8,128)(2,1)} %refs_3_.9, bf16[3,512,1536]{2,1,0:T(8,128)(2,1)} %collective-permute-done.refs_3_.refs_4_, ...), custom_call_target="tpu_custom_call" | custom-call | bytes 1024 | tf_op jit(solution)/shard_map/pairs_for_chip/pallas_call | solution.py:27
  200.0 13.7 %collective-permute-done.13.refs_3_ = bf16[3,512,512]{2,1,0:T(8,128)(2,1)} collective-permute-done((bf16[3,512,512]{2,1,0:T(8,128)(2,1)}, bf16[3,512,512]{2,1,0:T(8,128)(2,1)}, u32[]{:S(2)}, u32[]{:S(2)}) %collective-permute-start.13) | collective-permute-done | bytes 1572896 | tf_op jit(solution)/shard_map/ppermute | solution.py:227
  239.8 19.5 %collective-permute-done.16.refs_3_ = bf16[3,512,512]{2,1,0:T(8,128)(2,1)} collective-permute-done((bf16[3,512,512]{2,1,0:T(8,128)(2,1)}, bf16[3,512,512]{2,1,0:T(8,128)(2,1)}, u32[]{:S(2)}, u32[]{:S(2)}) %collective-permute-start.16) | collective-permute-done | bytes 1572896 | tf_op jit(solution)/shard_map/ppermute | solution.py:218
  259.2 20.9 %chip_gamma.3 = (f32[3,512,1536]{2,1,0:T(8,128)}, f32[3,512,1536]{2,1,0:T(8,128)}, f32[8,128]{1,0:T(8,128)S(1)}) custom-call(s32[5]{0:T(128)S(1)} %stack.31.refs_0_, f32[8,128]{1,0:T(8,128)S(1)} %get-tuple-element.85.refs_1_, bf16[3,512,512]{2,1,0:T(8,128)(2,1)} %get-tuple-element.86.refs_2_, ...), custom_call_target="tpu_custom_call", output_to_operand_aliasing={{0}: (6, {}), {1}: (7, {})} | custom-call | bytes 1024 | tf_op jit(solution)/shard_map/chip_gamma/pallas_call | solution.py:27
  286.1 21.3 %collective-permute-start.20 = (bf16[3,512,512]{2,1,0:T(8,128)(2,1)S(1)}, bf16[3,512,512]{2,1,0:T(8,128)(2,1)S(1)}, u32[]{:S(2)}, u32[]{:S(2)}) collective-permute-start(bf16[3,512,512]{2,1,0:T(8,128)(2,1)S(1)} %get-tuple-element.95.refs_2_), channel_id=1, source_target_pairs={{0,8},{8,0},{4,12},{12,4},{1,9},{9,1},{5,13},{13,5},{2,10},{10,2},... | collective-permute-start | bytes 4718600 | tf_op jit(solution)/shard_map/ppermute | solution.py:227
  307.4 8.6 %pairs_for_chip.9 = (bf16[3,512,512]{2,1,0:T(8,128)(2,1)S(1)}, f32[8,128]{1,0:T(8,128)S(1)}) custom-call(s32[5]{0:T(128)S(1)} %stack.31.refs_0_, f32[8,128]{1,0:T(8,128)S(1)} %get-tuple-element.90.refs_1_, bf16[6,512,1536]{2,1,0:T(8,128)(2,1)} %refs_3_.9, bf16[3,512,1536]{2,1,0:T(8,128)(2,1)} %collective-permute-done.refs_3_.refs_4_, ...), custom_call_target="tpu_custom_call" | custom-call | bytes 1024 | tf_op jit(solution)/shard_map/pairs_for_chip/pallas_call | solution.py:27
  318.7 57.0 %collective-permute-done.20.refs_3_ = bf16[3,512,512]{2,1,0:T(8,128)(2,1)S(1)} collective-permute-done((bf16[3,512,512]{2,1,0:T(8,128)(2,1)S(1)}, bf16[3,512,512]{2,1,0:T(8,128)(2,1)S(1)}, u32[]{:S(2)}, u32[]{:S(2)}) %collective-permute-start.20) | collective-permute-done | bytes 1572896 | tf_op jit(solution)/shard_map/ppermute | solution.py:227
  378.5 8.1 %own_amplitudes.9 = (bf16[3,512,512]{2,1,0:T(8,128)(2,1)S(1)}, f32[8,128]{1,0:T(8,128)S(1)}) custom-call(s32[5]{0:T(128)S(1)} %stack.31.refs_0_, f32[3]{0:T(128)S(1)} %dynamic-slice_add_fusion.refs_1_, f32[8,128]{1,0:T(8,128)S(1)} %get-tuple-element.96.refs_2_, bf16[6,512,1536]{2,1,0:T(8,128)(2,1)} %refs_3_.9, ...), custom_call_target="tpu_custom_call" | custom-call | bytes 1024 | tf_op jit(solution)/shard_map/own_amplitudes/pallas_call | solution.py:27
  394.1 19.5 %collective-permute-done.22.refs_2_ = bf16[3,512,512]{2,1,0:T(8,128)(2,1)S(1)} collective-permute-done((bf16[3,512,512]{2,1,0:T(8,128)(2,1)}, bf16[3,512,512]{2,1,0:T(8,128)(2,1)S(1)}, u32[]{:S(2)}, u32[]{:S(2)}) %collective-permute-start.22) | collective-permute-done | bytes 1572896 | tf_op jit(solution)/shard_map/ppermute | solution.py:218
  418.6 16.2 %last_gamma.4 = (f32[3,512,1536]{2,1,0:T(8,128)}, f32[8,128]{1,0:T(8,128)S(1)}) custom-call(s32[5]{0:T(128)S(1)} %stack.31.refs_0_, f32[8,128]{1,0:T(8,128)S(1)} %get-tuple-element.100.refs_1_, bf16[3,512,512]{2,1,0:T(8,128)(2,1)} %get-tuple-element.93.refs_2_, bf16[3,512,512]{2,1,0:T(8,128)(2,1)} %get-tuple-element.101.refs_3_, ...), custom_call_target="tpu_custom_call", output_to_operand_aliasing={{0}: (8, {})} | custom-call | bytes 1024 | tf_op jit(solution)/shard_map/last_gamma/pallas_call | solution.py:27
  446.2 16.2 %last_gamma.5 = (f32[3,512,1536]{2,1,0:T(8,128)}, f32[8,128]{1,0:T(8,128)S(1)}) custom-call(s32[5]{0:T(128)S(1)} %stack.31.refs_0_, f32[8,128]{1,0:T(8,128)S(1)} %get-tuple-element.106.refs_1_, bf16[3,512,512]{2,1,0:T(8,128)(2,1)} %collective-permute-done.24.refs_2_, ...), custom_call_target="tpu_custom_call", output_to_operand_aliasing={{0}: (8, {})} | custom-call | bytes 1024 | tf_op jit(solution)/shard_map/last_gamma/pallas_call | solution.py:27
  462.4 17.6 %collective-permute-done.29.refs_2_ = bf16[3,512,512]{2,1,0:T(8,128)(2,1)S(1)} collective-permute-done((bf16[3,512,512]{2,1,0:T(8,128)(2,1)}, bf16[3,512,512]{2,1,0:T(8,128)(2,1)S(1)}, u32[]{:S(2)}, u32[]{:S(2)}) %collective-permute-start.29) | collective-permute-done | bytes 1572896 | tf_op jit(solution)/shard_map/ppermute | solution.py:218
  483.2 11.9 %last_gamma.6 = (f32[6,512,1536]{2,1,0:T(8,128)}, f32[8,128]{1,0:T(8,128)S(1)}) custom-call(s32[5]{0:T(128)S(1)} %stack.31.refs_0_, f32[8,128]{1,0:T(8,128)S(1)} %get-tuple-element.110.refs_1_, bf16[3,512,512]{2,1,0:T(8,128)(2,1)} %get-tuple-element.109.refs_2_, bf16[3,512,512]{2,1,0:T(8,128)(2,1)S(1)} %get-tuple-element.111.refs_3_, ...), custom_call_target="tpu_custom_call" | custom-call | bytes 1024 | tf_op jit(solution)/shard_map/last_gamma/pallas_call | solution.py:27
  495.1 11.4 %last_gamma.7 = (f32[6,512,1536]{2,1,0:T(8,128)}, f32[8,128]{1,0:T(8,128)}) custom-call(s32[5]{0:T(128)S(1)} %stack.31.refs_0_, f32[8,128]{1,0:T(8,128)S(1)} %get-tuple-element.113.refs_1_, bf16[3,512,512]{2,1,0:T(8,128)(2,1)S(1)} %collective-permute-done.30.refs_2_, ...), custom_call_target="tpu_custom_call", output_to_operand_aliasing={{0}: (5, {})} | custom-call | bytes 1024 | tf_op jit(solution)/shard_map/last_gamma/pallas_call | solution.py:27
  (129 shorter events, 114.8 us)
Async XLA Ops:
  5.3 70.6 %collective-permute-start.3 = (bf16[2,512,1536]{2,1,0:T(8,128)(2,1)}, bf16[2,512,1536]{2,1,0:T(8,128)(2,1)}, u32[]{:S(2)}, u32[]{:S(2)}) collective-permute-start(bf16[2,512,1536]{2,1,0:T(8,128)(2,1)} %refs_4_.3), channel_id=1, source_target_pairs={{0,4},{4,0},{8,12},{12,8},{1,5},{5,1},{9,13},{13,9},{2,6},{6,2},{1... | collective-permute-start | bytes 9437192 | tf_op jit(solution)/shard_map/ppermute | solution.py:227
  7.6 68.3 %collective-permute-start.4 = (bf16[2,512,1536]{2,1,0:T(8,128)(2,1)}, bf16[2,512,1536]{2,1,0:T(8,128)(2,1)S(1)}, u32[]{:S(2)}, u32[]{:S(2)}) collective-permute-start(bf16[2,512,1536]{2,1,0:T(8,128)(2,1)} %refs_4_.3), channel_id=1, source_target_pairs={{4,8},{8,4},{5,9},{9,5},{6,10},{10,6},{7,11},{11,7},{20,24},{24,20... | collective-permute-start | bytes 9437192 | tf_op jit(solution)/shard_map/ppermute | solution.py:227
  27.5 37.1 %collective-permute-start.2 = (bf16[3,512,512]{2,1,0:T(8,128)(2,1)}, bf16[3,512,512]{2,1,0:T(8,128)(2,1)}, u32[]{:S(2)}, u32[]{:S(2)}) collective-permute-start(bf16[3,512,512]{2,1,0:T(8,128)(2,1)} %get-tuple-element.62), channel_id=1, source_target_pairs={{0,2},{1,3},{2,0},{3,1},{4,6},{5,7},{6,4},{7,5},{8,10},{9,11},{10,... | collective-permute-start | bytes 4718600 | tf_op jit(solution)/shard_map/ppermute | solution.py:218
  78.5 85.7 %collective-permute-start.9 = (bf16[2,512,1536]{2,1,0:T(8,128)(2,1)}, bf16[2,512,1536]{2,1,0:T(8,128)(2,1)}, u32[]{:S(2)}, u32[]{:S(2)}) collective-permute-start(bf16[2,512,1536]{2,1,0:T(8,128)(2,1)} %get-tuple-element.67.refs_4_.refs_5_), channel_id=1, source_target_pairs={{4,8},{8,4},{5,9},{9,5},{6,10},{10,6},{7,11},{11,7},{20,24},{24,20... | collective-permute-start | bytes 9437192 | tf_op jit(solution)/shard_map/ppermute | solution.py:227
  80.9 83.8 %collective-permute-start.10 = (bf16[2,512,1536]{2,1,0:T(8,128)(2,1)S(1)}, bf16[2,512,1536]{2,1,0:T(8,128)(2,1)}, u32[]{:S(2)}, u32[]{:S(2)}) collective-permute-start(bf16[2,512,1536]{2,1,0:T(8,128)(2,1)S(1)} %get-tuple-element.69.refs_4_.refs_5_), channel_id=1, source_target_pairs={{4,0},{8,12},{5,1},{9,13},{6,2},{10,14},{7,3},{11,15},{20,16},{24,... | collective-permute-start | bytes 9437192 | tf_op jit(solution)/shard_map/ppermute | solution.py:227
  82.2 36.2 %collective-permute-start.7 = (bf16[3,512,512]{2,1,0:T(8,128)(2,1)S(1)}, bf16[3,512,512]{2,1,0:T(8,128)(2,1)S(1)}, u32[]{:S(2)}, u32[]{:S(2)}) collective-permute-start(bf16[3,512,512]{2,1,0:T(8,128)(2,1)S(1)} %get-tuple-element.71.refs_2_), channel_id=1, source_target_pairs={{0,2},{1,3},{2,0},{3,1},{4,6},{5,7},{6,4},{7,5},{8,10},{9,11},{10,... | collective-permute-start | bytes 4718600 | tf_op jit(solution)/shard_map/ppermute | solution.py:218
  93.6 58.4 %collective-permute-start.8 = (bf16[3,512,512]{2,1,0:T(8,128)(2,1)}, bf16[3,512,512]{2,1,0:T(8,128)(2,1)S(1)}, u32[]{:S(2)}, u32[]{:S(2)}) collective-permute-start(bf16[3,512,512]{2,1,0:T(8,128)(2,1)} %get-tuple-element.73), channel_id=1, source_target_pairs={{0,2},{1,3},{2,0},{3,1},{4,6},{5,7},{6,4},{7,5},{8,10},{9,11},{10,... | collective-permute-start | bytes 4718600 | tf_op jit(solution)/shard_map/ppermute | solution.py:218
  168.5 45.2 %collective-permute-start.13 = (bf16[3,512,512]{2,1,0:T(8,128)(2,1)}, bf16[3,512,512]{2,1,0:T(8,128)(2,1)}, u32[]{:S(2)}, u32[]{:S(2)}) collective-permute-start(bf16[3,512,512]{2,1,0:T(8,128)(2,1)} %get-tuple-element.80.refs_2_), channel_id=1, source_target_pairs={{0,4},{4,0},{8,12},{12,8},{1,5},{5,1},{9,13},{13,9},{2,6},{6,2},{1... | collective-permute-start | bytes 4718600 | tf_op jit(solution)/shard_map/ppermute | solution.py:227
  178.9 102.8 %collective-permute-start.17 = (bf16[2,512,1536]{2,1,0:T(8,128)(2,1)}, bf16[2,512,1536]{2,1,0:T(8,128)(2,1)S(1)}, u32[]{:S(2)}, u32[]{:S(2)}) collective-permute-start(bf16[2,512,1536]{2,1,0:T(8,128)(2,1)} %get-tuple-element.76), channel_id=1, source_target_pairs={{4,0},{8,12},{5,1},{9,13},{6,2},{10,14},{7,3},{11,15},{20,16},{24,... | collective-permute-start | bytes 9437192 | tf_op jit(solution)/shard_map/ppermute | solution.py:227
  189.9 35.6 %collective-permute-start.14 = (bf16[3,512,512]{2,1,0:T(8,128)(2,1)}, bf16[3,512,512]{2,1,0:T(8,128)(2,1)S(1)}, u32[]{:S(2)}, u32[]{:S(2)}) collective-permute-start(bf16[3,512,512]{2,1,0:T(8,128)(2,1)} %get-tuple-element.82), channel_id=1, source_target_pairs={{0,2},{1,3},{2,0},{3,1},{4,6},{5,7},{6,4},{7,5},{8,10},{9,11},{10,... | collective-permute-start | bytes 4718600 | tf_op jit(solution)/shard_map/ppermute | solution.py:218
  199.2 34.3 %collective-permute-start.15 = (bf16[3,512,512]{2,1,0:T(8,128)(2,1)S(1)}, bf16[3,512,512]{2,1,0:T(8,128)(2,1)S(1)}, u32[]{:S(2)}, u32[]{:S(2)}) collective-permute-start(bf16[3,512,512]{2,1,0:T(8,128)(2,1)S(1)} %get-tuple-element.84.refs_2_), channel_id=1, source_target_pairs={{4,8},{8,4},{5,9},{9,5},{6,10},{10,6},{7,11},{11,7},{20,24},{24,20... | collective-permute-start | bytes 4718600 | tf_op jit(solution)/shard_map/ppermute | solution.py:227
  218.6 40.6 %collective-permute-start.16 = (bf16[3,512,512]{2,1,0:T(8,128)(2,1)}, bf16[3,512,512]{2,1,0:T(8,128)(2,1)}, u32[]{:S(2)}, u32[]{:S(2)}) collective-permute-start(bf16[3,512,512]{2,1,0:T(8,128)(2,1)} %get-tuple-element.86.refs_2_), channel_id=1, source_target_pairs={{0,2},{1,3},{2,0},{3,1},{4,6},{5,7},{6,4},{7,5},{8,10},{9,11},{10,... | collective-permute-start | bytes 4718600 | tf_op jit(solution)/shard_map/ppermute | solution.py:218
  280.2 166.0 %collective-permute-start.28 = (f32[3,512,1536]{2,1,0:T(8,128)}, f32[3,512,1536]{2,1,0:T(8,128)}, u32[]{:S(2)}, u32[]{:S(2)}) collective-permute-start(f32[3,512,1536]{2,1,0:T(8,128)} %get-tuple-element.107), channel_id=1, source_target_pairs={{0,1},{1,0},{2,3},{3,2},{4,5},{5,4},{6,7},{7,6},{8,9},{9,8},{10,11... | collective-permute-start | bytes 28311560 | tf_op jit(solution)/shard_map/ppermute | solution.py:218
  282.2 25.2 %collective-permute-start.18 = (bf16[2,512,1536]{2,1,0:T(8,128)(2,1)S(1)}, bf16[2,512,1536]{2,1,0:T(8,128)(2,1)S(1)}, u32[]{:S(2)}, u32[]{:S(2)}) collective-permute-start(bf16[2,512,1536]{2,1,0:T(8,128)(2,1)S(1)} %get-tuple-element.91.refs_4_.refs_5_), channel_id=1, source_target_pairs={{0,1},{1,0},{2,3},{3,2},{12,13},{13,12},{14,15},{15,14},{16,17},{1... | collective-permute-start | bytes 9437192 | tf_op jit(solution)/shard_map/ppermute | solution.py:218
  284.3 33.8 %collective-permute-start.19 = (bf16[3,512,512]{2,1,0:T(8,128)(2,1)}, bf16[3,512,512]{2,1,0:T(8,128)(2,1)}, u32[]{:S(2)}, u32[]{:S(2)}) collective-permute-start(bf16[3,512,512]{2,1,0:T(8,128)(2,1)} %get-tuple-element.93.refs_2_), channel_id=1, source_target_pairs={{4,6},{5,7},{6,4},{7,5},{8,10},{9,11},{10,8},{11,9},{20,22},{21,23... | collective-permute-start | bytes 4718600 | tf_op jit(solution)/shard_map/ppermute | solution.py:218
  286.1 89.5 %collective-permute-start.20 = (bf16[3,512,512]{2,1,0:T(8,128)(2,1)S(1)}, bf16[3,512,512]{2,1,0:T(8,128)(2,1)S(1)}, u32[]{:S(2)}, u32[]{:S(2)}) collective-permute-start(bf16[3,512,512]{2,1,0:T(8,128)(2,1)S(1)} %get-tuple-element.95.refs_2_), channel_id=1, source_target_pairs={{0,8},{8,0},{4,12},{12,4},{1,9},{9,1},{5,13},{13,5},{2,10},{10,2},... | collective-permute-start | bytes 4718600 | tf_op jit(solution)/shard_map/ppermute | solution.py:227
  316.0 62.6 %collective-permute-start.21 = (bf16[3,512,512]{2,1,0:T(8,128)(2,1)S(1)}, bf16[3,512,512]{2,1,0:T(8,128)(2,1)S(1)}, u32[]{:S(2)}, u32[]{:S(2)}) collective-permute-start(bf16[3,512,512]{2,1,0:T(8,128)(2,1)S(1)} %get-tuple-element.97), channel_id=1, source_target_pairs={{0,2},{1,3},{2,0},{3,1},{12,14},{13,15},{14,12},{15,13},{16,18},{1... | collective-permute-start | bytes 4718600 | tf_op jit(solution)/shard_map/ppermute | solution.py:218
  378.3 35.3 %collective-permute-start.22 = (bf16[3,512,512]{2,1,0:T(8,128)(2,1)}, bf16[3,512,512]{2,1,0:T(8,128)(2,1)S(1)}, u32[]{:S(2)}, u32[]{:S(2)}) collective-permute-start(bf16[3,512,512]{2,1,0:T(8,128)(2,1)} %get-tuple-element.99.refs_5_), channel_id=1, source_target_pairs={{0,2},{1,3},{2,0},{3,1},{4,6},{5,7},{6,4},{7,5},{8,10},{9,11},{10,... | collective-permute-start | bytes 4718600 | tf_op jit(solution)/shard_map/ppermute | solution.py:218
  386.6 48.2 %collective-permute-start.23 = (bf16[3,512,512]{2,1,0:T(8,128)(2,1)S(1)}, bf16[3,512,512]{2,1,0:T(8,128)(2,1)S(1)}, u32[]{:S(2)}, u32[]{:S(2)}) collective-permute-start(bf16[3,512,512]{2,1,0:T(8,128)(2,1)S(1)} %get-tuple-element.105.refs_2_), channel_id=1, source_target_pairs={{0,12},{12,0},{1,13},{13,1},{2,14},{14,2},{3,15},{15,3},{16,28},{2... | collective-permute-start | bytes 4718600 | tf_op jit(solution)/shard_map/ppermute | solution.py:227
  390.9 50.9 %collective-permute-start.24 = (bf16[3,512,512]{2,1,0:T(8,128)(2,1)}, bf16[3,512,512]{2,1,0:T(8,128)(2,1)}, u32[]{:S(2)}, u32[]{:S(2)}) collective-permute-start(bf16[3,512,512]{2,1,0:T(8,128)(2,1)} %get-tuple-element.93.refs_2_), channel_id=1, source_target_pairs={{4,5},{5,4},{6,7},{7,6},{8,9},{9,8},{10,11},{11,10},{20,21},{21,20... | collective-permute-start | bytes 4718600 | tf_op jit(solution)/shard_map/ppermute | solution.py:218
  392.8 51.2 %collective-permute-start.26 = (bf16[3,512,512]{2,1,0:T(8,128)(2,1)}, bf16[3,512,512]{2,1,0:T(8,128)(2,1)}, u32[]{:S(2)}, u32[]{:S(2)}) collective-permute-start(bf16[3,512,512]{2,1,0:T(8,128)(2,1)} %get-tuple-element.99.refs_5_), channel_id=1, source_target_pairs={{0,1},{1,0},{2,3},{3,2},{4,5},{5,4},{6,7},{7,6},{8,9},{9,8},{10,11... | collective-permute-start | bytes 4718600 | tf_op jit(solution)/shard_map/ppermute | solution.py:218
  413.6 32.5 %collective-permute-start.25 = (bf16[3,512,512]{2,1,0:T(8,128)(2,1)}, bf16[3,512,512]{2,1,0:T(8,128)(2,1)}, u32[]{:S(2)}, u32[]{:S(2)}) collective-permute-start(bf16[3,512,512]{2,1,0:T(8,128)(2,1)} %get-tuple-element.101.refs_3_), channel_id=1, source_target_pairs={{4,5},{5,4},{6,7},{7,6},{8,9},{9,8},{10,11},{11,10},{20,21},{21,20... | collective-permute-start | bytes 4718600 | tf_op jit(solution)/shard_map/ppermute | solution.py:218
  441.8 38.1 %collective-permute-start.29 = (bf16[3,512,512]{2,1,0:T(8,128)(2,1)}, bf16[3,512,512]{2,1,0:T(8,128)(2,1)S(1)}, u32[]{:S(2)}, u32[]{:S(2)}) collective-permute-start(bf16[3,512,512]{2,1,0:T(8,128)(2,1)} %get-tuple-element.109.refs_2_), channel_id=1, source_target_pairs={{0,2},{1,3},{2,0},{3,1},{12,14},{13,15},{14,12},{15,13},{16,18},{1... | collective-permute-start | bytes 4718600 | tf_op jit(solution)/shard_map/ppermute | solution.py:218
  444.0 51.1 %collective-permute-start.30 = (bf16[3,512,512]{2,1,0:T(8,128)(2,1)}, bf16[3,512,512]{2,1,0:T(8,128)(2,1)S(1)}, u32[]{:S(2)}, u32[]{:S(2)}) collective-permute-start(bf16[3,512,512]{2,1,0:T(8,128)(2,1)} %get-tuple-element.109.refs_2_), channel_id=1, source_target_pairs={{0,1},{1,0},{2,3},{3,2},{12,13},{13,12},{14,15},{15,14},{16,17},{1... | collective-permute-start | bytes 4718600 | tf_op jit(solution)/shard_map/ppermute | solution.py:218
  (35 other events, 348.4 us)

commit v4 on v3

v4 whole, which is shorter than its diff:
```python
import functools

import jax
import jax.numpy as jnp
from jax import lax
from jax.experimental import pallas as pl
from jax.experimental.pallas import tpu as pltpu
from jax.sharding import PartitionSpec as P

F32 = jnp.float32
BF16 = jnp.bfloat16
ANY = pl.BlockSpec(memory_space=pl.ANY)
TOKEN = jax.ShapeDtypeStruct((8, 128), F32)
TILE = 256


def tile_of(size):
    return TILE if size % TILE == 0 else size


def call(kernel, name, token, place, grid, in_specs, args, out_specs, out, aliases=None):
    def body(*refs):
        n = len(place)
        kernel(*refs[:n], *refs[n + 1 : -1])

    shift = len(place) + 1
    return pl.pallas_call(
        body,
        out_shape=(*out, TOKEN),
        grid_spec=pltpu.PrefetchScalarGridSpec(
            num_scalar_prefetch=len(place),
            grid=grid,
            in_specs=[ANY] + in_specs,
            out_specs=(*out_specs, ANY),
        ),
        input_output_aliases={k + shift: v for k, v in (aliases or {}).items()},
        compiler_params=pltpu.CompilerParams(vmem_limit_bytes=56 * 2**20),
        cost_estimate=pl.CostEstimate(flops=0, bytes_accessed=1024, transcendentals=0),
        name=name,
    )(*place, token, *args)


def tie_kernel(place, *refs):
    del place, refs


def tie(token, place, *held):
    n = len(held)
    shapes = [held_shape(h) for h in held]
    return call(tie_kernel, "tie", token, place, (1,), [ANY] * n, held, [ANY] * n, shapes, {k: k for k in range(n)})


def held_shape(a):
    return jax.ShapeDtypeStruct(a.shape, a.dtype)


def takes_part(place, part):
    return place[3 if part == "middle" else 4] == 1


def only(place, part, out):
    def run(body):
        if part is None:
            body()
            return
        pl.when(takes_part(place, part))(body)

        @pl.when(jnp.logical_not(takes_part(place, part)))
        def _():
            out[...] = jnp.zeros_like(out)

    return run


def whole_block(pieces, j):
    return jnp.concatenate([p[j] for p in pieces], axis=0) if len(pieces) > 1 else pieces[0][j]


def pairs_kernel(n_place, n_pieces, has_last, part, first, *refs):
    place, (b_i, b_i_core, block, *rest) = refs[:n_place], refs[n_place:]
    pieces, rest, out = rest[:n_pieces], rest[n_pieces:], rest[-1]
    across = (((1,), (1,)), ((), ()))

    @only(place[0], part, out)
    def _():
        value = lax.dot_general(b_i[0], block[0], across, preferred_element_type=F32)
        value += lax.dot_general(b_i_core[0], whole_block(pieces, 0), across, preferred_element_type=F32)
        if has_last:
            chip, vir_a, vir_b = rest[:3]
            value = value + chip[0].astype(F32)
            value = value / ((place[1][first + pl.program_id(0)] - vir_a[...]) - vir_b[...])
        out[0] = value.astype(BF16)


def pairs(token, place, b_i, block, own_j, part, which=None, last=None):
    (mine, core_part), (block, pieces) = b_i, block
    n_j, cols, depth = block.shape
    half, rows = core_part.shape[:2]
    first, count = (0, half) if which is None else (which, 1)

    def j_of(s):
        return s[0] if own_j else 1 - s[0]

    one = pl.BlockSpec((1, rows, cols), lambda i, s, *_: (i, 0, 0))
    block_specs = [pl.BlockSpec((1,) + p.shape[1:], lambda i, s, *_: (j_of(s), 0, 0)) for p in (block, *pieces)]
    in_specs = [
        pl.BlockSpec((1, rows, depth), lambda i, s, *_: (s[1] * half + first + i, 0, 0)),
        pl.BlockSpec((1, rows, depth), lambda i, s, *_: (first + i, 0, 0)),
    ] + block_specs
    args, name = [mine, core_part, block, *pieces], "pairs_for_chip"
    if last is not None:
        chip, occ, vir_a, vir_b = last
        place = place + (occ,)
        in_specs += [
            one,
            pl.BlockSpec((rows, 1), lambda i, s, *_: (0, 0)),
            pl.BlockSpec((1, cols), lambda i, s, *_: (0, 0)),
        ]
        args += [chip, vir_a, vir_b]
        name = "own_amplitudes"
    out = jax.ShapeDtypeStruct((count, rows, cols), BF16)
    kernel = functools.partial(pairs_kernel, len(place), len(pieces), last is not None, part, first)
    return call(kernel, name, token, place, (count,), in_specs, args, [one], [out])


def combine_kernel(part, place, held, mirror, *outs):
    for i, out in enumerate(outs):

        @pl.when((pl.program_id(0) == i) | (len(outs) == 1))
        def _():
            @only(place, part, out)
            def _():
                out[0] = (2.0 * held[0].astype(F32) - mirror[0].astype(F32).T).astype(BF16)


def combine_pairs(token, place, held, mirror, part, split):
    count, rows, cols = held.shape
    spec = pl.BlockSpec((1, rows, cols), lambda i, s: (i, 0, 0))
    out_specs, out = [spec], [held_shape(held)]
    if split:
        out_specs = [pl.BlockSpec((1, rows, cols), lambda i, s: (0, 0, 0))] * count
        out = [jax.ShapeDtypeStruct((1, rows, cols), BF16)] * count
    kernel = functools.partial(combine_kernel, part)
    *out, token = call(kernel, "combine_pairs", token, place, (count,), [spec, spec], [held, mirror], out_specs, out)
    return (out if split else out[0]), token


def gamma_kernel(terms, has_sum, place, *refs):
    x = place[0]
    refs, outs = list(refs[:-2]), refs[-2:]
    count, rows, tile = outs[0].shape
    held = []
    for own_pieces, core_pieces, part in terms:
        pairs, refs = refs[:2], refs[2:]
        blocks, refs = (refs[:own_pieces], refs[own_pieces : own_pieces + core_pieces]), refs[own_pieces + core_pieces :]
        held.append((pairs, blocks, part))

    def share(k, pairs, blocks):
        total = None
        for pair, j in zip(pairs, (x, 1 - x)):
            left = pair[...].reshape(count * rows, pair.shape[2])
            term = jnp.dot(left, whole_block(blocks[k], j), preferred_element_type=F32)
            total = term if total is None else total + term
        return total.reshape(count, rows, tile)

    for k, out in enumerate(outs):
        total = refs[k][...] if has_sum else None
        for pairs, blocks, part in held:
            if part is None:
                total = share(k, pairs, blocks) if total is None else total + share(k, pairs, blocks)
        if all(part is None for *_, part in held):
            out[...] = total.astype(out.dtype)
            continue
        out[...] = total
        for pairs, blocks, part in held:
            if part is not None:

                @pl.when(takes_part(place, part))
                def _():
                    out[...] += share(k, pairs, blocks)


def gamma_operands(terms, which, tile):
    in_specs, args, counts = [], [], []
    for same_j, other_j, (block, pieces), part in terms:
        for h in (same_j, other_j):
            if which is None or h.shape[0] == 1:
                in_specs.append(pl.BlockSpec(h.shape, lambda p, s: (0, 0, 0)))
            else:
                in_specs.append(pl.BlockSpec((1,) + h.shape[1:], lambda p, s: (which, 0, 0)))
        in_specs += [pl.BlockSpec(b.shape[:2] + (tile,), lambda p, s: (0, 0, p)) for b in (block, *pieces)]
        args += [same_j, other_j, block, *pieces]
        counts.append((1, len(pieces), part))
    return in_specs, args, counts


def chip_gamma(token, place, terms, before=None):
    half, rows = terms[0][0].shape[:2]
    depth = terms[0][2][0].shape[2]
    tile = tile_of(depth)
    in_specs, args, counts = gamma_operands(terms, None, tile)
    spec = pl.BlockSpec((half, rows, tile), lambda p, s: (0, 0, p))
    aliases = None
    if before is not None:
        aliases = {len(args): 0, len(args) + 1: 1}
        in_specs += [spec, spec]
        args += before
    out = [jax.ShapeDtypeStruct((half, rows, depth), F32)] * 2
    kernel = functools.partial(gamma_kernel, counts, before is not None)
    *out, token = call(kernel, "chip_gamma", token, place, (depth // tile,), in_specs, args, [spec, spec], out, aliases)
    return out, token


def last_gamma(token, place, which, terms, before, shape, result):
    half, rows, depth = before[0].shape
    tile = tile_of(depth)
    in_specs, args, counts = gamma_operands(terms, which, tile)
    spec = pl.BlockSpec((1, rows, tile), lambda p, s: (which, 0, p))
    in_specs += [spec, spec]
    args += before
    aliases, drop = None, 0
    if result is not None:
        aliases, drop = {len(args): 0}, 1
        in_specs.append(ANY)
        args.append(result)

    def kernel(place, *refs):
        n = len(refs) - 2
        gamma_kernel(counts, True, place, *refs[: n - drop], *refs[n:])

    out_specs = [
        pl.BlockSpec((1, rows, tile), lambda p, s: (s[1] * half + which, 0, p)),
        pl.BlockSpec((1, rows, tile), lambda p, s: (0, 0, p)),
    ]
    out = [jax.ShapeDtypeStruct(shape, F32), jax.ShapeDtypeStruct((1, rows, depth), BF16)]
    return call(kernel, "last_gamma", token, place, (depth // tile,), in_specs, args, out_specs, out, aliases)


def place_kernel(place, received, result, out):
    del place, result
    out[...] = received[...].astype(F32)


def place_gamma(token, place, which, received, result):
    half = result.shape[0] // 2
    _, rows, depth = received.shape
    tile = rows // 2
    return call(
        place_kernel,
        "place_gamma",
        token,
        place,
        (2,),
        [pl.BlockSpec((1, tile, depth), lambda p, s: (0, p, 0)), ANY],
        [received, result],
        [pl.BlockSpec((1, tile, depth), lambda p, s: ((1 - s[1]) * half + which, p, 0))],
        [held_shape(result)],
        {1: 0},
    )


def chain_device(b_occ_i, b_occ_j, eps_occ_i, eps_occ_j, eps_vir):
    n_i, rows, depth = b_occ_i.shape
    half = n_i // 2
    z, col = lax.axis_index("row"), lax.axis_index("col")
    x, core = col // 2, col % 2
    in_middle = (z == 1) | (z == 2)
    place = (jnp.stack([x, core, z, in_middle, ~in_middle]).astype(jnp.int32),)
    occ = lax.dynamic_slice_in_dim(eps_occ_i, core * half, half, 0) + eps_occ_j[x]
    token = jnp.zeros(TOKEN.shape, F32)

    def energies(block):
        return lax.dynamic_slice_in_dim(eps_vir, block * rows, rows, 0)

    vir_a = energies(z)[:, None]

    def to_col(values, flip, part):
        rows_in = {None: range(4), "middle": (1, 2), "ends": (0, 3)}[part]
        steps = [(4 * r + q, 4 * r + (q ^ flip)) for r in rows_in for q in range(4)]
        return lax.ppermute(values, ("row", "col"), steps)

    def to_core(values, part=None):
        return to_col(values, 1, part)

    def to_chip(values, part=None):
        return to_col(values, 2, part)

    def along(values, steps):
        return lax.ppermute(values, "row", steps)

    ends, middle = [(1, 0), (2, 3)], [(1, 2), (2, 1)]
    pairs_1 = [(0, 1), (1, 0), (2, 3), (3, 2)]
    pairs_2 = [(0, 2), (2, 0), (1, 3), (3, 1)]
    pairs_3 = [(0, 3), (3, 0)]
    b_i = b_occ_i, to_core(lax.dynamic_slice_in_dim(b_occ_i, (1 - core) * half, half, 0))

    def pass_on(block, part=None, which=None):
        nonlocal token
        out, token = pairs(token, place, b_i, block, False, part, which)
        return to_chip(out, part)

    def own(block, chip_sum, shift, part=None, which=None):
        nonlocal token
        vir_b = energies(z ^ shift)[None, :]
        out, token = pairs(token, place, b_i, block, True, part, which, (chip_sum, occ, vir_a, vir_b))
        return out

    def combine(held, mirror, part=None, split=False):
        nonlocal token
        out, token = combine_pairs(token, place, held, mirror, part, split)
        return out

    def forward(*values):
        nonlocal token
        *out, token = tie(token, place, *values)
        return out

    def both(values, part=None, n_pieces=1):
        return values, [to_core(p, part) for p in jnp.split(values, n_pieces, axis=1)]

    shape = b_occ_i.shape
    near = along(b_occ_j, pairs_1)
    across = along(b_occ_j, middle)
    here = both(b_occ_j)

    chip_0 = pass_on(here)
    held_0 = own(here, chip_0, 0)
    mine_0 = combine(held_0, held_0)

    near, across = forward(near, across)
    far_mid = along(near, middle)
    far_end = along(across, ends)
    near = both(near)
    across = both(across, "middle")
    chip_1 = pass_on(near)
    chip_12 = pass_on(across, "middle")

    held_1 = own(near, chip_1, 1)
    mirror_1 = along(held_1, pairs_1)
    (mine_0,) = forward(mine_0)
    other_0 = to_chip(mine_0)

    far_mid, far_end = forward(far_mid, far_end)
    last = along(far_mid, ends)
    far = both(jnp.where(in_middle, far_mid, far_end))
    chip_2 = pass_on(far)

    held_12 = own(across, chip_12, 3, "middle")
    mirror_12 = along(held_12, middle)
    gamma, token = chip_gamma(token, place, [(mine_0, other_0, here, None)])

    held_2 = own(far, chip_2, 2)
    mirror_2 = along(held_2, pairs_2)
    mine_1 = combine(held_1, mirror_1)
    other_1 = to_chip(mine_1)
    mine_12 = combine(held_12, mirror_12, "middle")
    other_12 = to_chip(mine_12, "middle")
    other_1, other_12 = forward(other_1, other_12)

    (last,) = forward(last)
    last = both(last, "ends", 4)
    chip_3 = [pass_on(last, "ends", i) for i in range(half)]

    terms = [(mine_1, other_1, near, None), (mine_12, other_12, across, "middle")]
    gamma, token = chip_gamma(token, place, terms, gamma)

    held_3 = [own(last, chip_3[i], 3, "ends", i) for i in range(half)]
    mirror_3 = [along(h, pairs_3) for h in held_3]

    mine_2 = combine(held_2, mirror_2, split=True)
    other_2 = [to_chip(m) for m in mine_2]
    mine_3 = [combine(h, m, "ends") for h, m in zip(held_3, mirror_3)]
    other_3 = [to_chip(m, "ends") for m in mine_3]

    result, received = None, []
    for i in range(half):
        terms = [(mine_2[i], other_2[i], far, None), (mine_3[i], other_3[i], last, None)]
        result, theirs, token = last_gamma(token, place, i, terms, gamma, shape, result)
        received.append(to_core(theirs))
    for i in range(half):
        result, token = place_gamma(token, place, i, received[i], result)
    return result


def general_device(b_occ_i, b_occ_j, eps_occ_i, eps_occ_j, eps_vir):
    rows = b_occ_i.shape[1]
    own_energy = lax.dynamic_slice_in_dim(eps_vir, lax.axis_index("row") * rows, rows, 0)
    gathered = lax.all_gather(b_occ_j, "row", axis=1, tiled=True)
    partial_value = jnp.einsum("iap,jbp->jiab", b_occ_i, gathered, preferred_element_type=F32)
    totals = lax.psum(partial_value.astype(BF16), "col").astype(F32)
    denominator = (
        eps_occ_j[:, None, None, None]
        + eps_occ_i[None, :, None, None]
        - own_energy[None, None, :, None]
        - eps_vir[None, None, None, :]
    )
    held = (totals / denominator).astype(BF16)
    mirror = jnp.swapaxes(lax.all_to_all(held, "row", split_axis=3, concat_axis=2, tiled=True), 2, 3)
    combined = (2.0 * held.astype(F32) - mirror.astype(F32)).astype(BF16)
    return jnp.einsum("jiab,jbp->iap", combined, gathered, preferred_element_type=F32)


def solution(mesh):
    placed = (
        P("groups", "row", "col"),
        P("groups", "row", "col"),
        P("groups"),
        P("groups"),
        P("groups"),
    )
    chain = mesh.shape["row"] == 4 and mesh.shape["col"] == 4
    return jax.shard_map(
        chain_device if chain else general_device,
        mesh=mesh,
        in_specs=placed,
        out_specs=P("groups", "row", "col"),
        check_vma=False,
    )
```

time: 508 us -> 521 us (1.026)
  the two profiles are of different devices: /device:TPU:1 before, /device:TPU:23 now
where the time goes in v4:
time: 521 us; the launch traced here: 519 us
  Pallas kernels  242 us (46%)
  waiting for transfers between devices  195 us (37%)
  starting transfers between devices  42.3 us (8%)
  local copies, waits for them, and re-layouts  35.6 us (7%)
    pallas_call x34, Pallas kernels, call(): pl.pallas_call(body, out_shape=(*out, TOKEN), grid_spec=pltpu.PrefetchSca...  242 us
    ppermute x28, waiting for transfers between devices, to_col(): return lax.ppermute(values, ('row', 'col'), steps)  189 us
    unnamed x72, local copies, waits for them, and re-layouts  25.3 us
    ppermute x28, starting transfers between devices, to_col(): return lax.ppermute(values, ('row', 'col'), steps)  24.9 us
    ppermute x11, starting transfers between devices, along(): return lax.ppermute(values, 'row', steps)  17.4 us
  transfers between devices with their start and end apart: 39, of which 11 were waited for; matrix products, arithmetic and copies ran while one was open for 1% of the time, Pallas kernels for 46%

profile of v4, /device:TPU:23, one launch (start us, length us, event | category | flops | bytes accessed | tf_op | source)
XLA Modules:
  0.0 519.0 jit_solution(11924242912546033138)
XLA Ops:
  0.0 4.8 constant_dynamic-slice_fusion
  9.4 8.5 %collective-permute-done.1.refs_5_.refs_6_ = bf16[2,512,1536]{2,1,0:T(8,128)(2,1)} collective-permute-done((bf16[2,512,1536]{2,1,0:T(8,128)(2,1)}, bf16[2,512,1536]{2,1,0:T(8,128)(2,1)}, u32[]{:S(2)}, u32[]{:S(2)}) %collective-permute-start.1) | collective-permute-done | bytes 3145760 | tf_op jit(solution)/shard_map/ppermute | solution.py:280
  18.5 10.2 %pairs_for_chip.7 = (bf16[3,512,512]{2,1,0:T(8,128)(2,1)}, f32[8,128]{1,0:T(8,128)}) custom-call(s32[5]{0:T(128)} %stack.31.refs_0_, f32[8,128]{1,0:T(8,128)} %broadcast_in_dim.21.refs_1_, bf16[6,512,1536]{2,1,0:T(8,128)(2,1)} %refs_3_.13, bf16[3,512,1536]{2,1,0:T(8,128)(2,1)} %collective-permute-done.refs_3_.refs_4_, bf16[2,512,1536]{2,1,0:T(8,128)(2,1)} %refs_4_.3, ...), custom_call_target="tpu_custom_call" | custom-call | bytes 1024 | tf_op jit(solution)/shard_map/pairs_for_chip/pallas_call | solution.py:27
  32.4 32.2 %collective-permute-done.2.refs_7_ = bf16[3,512,512]{2,1,0:T(8,128)(2,1)} collective-permute-done((bf16[3,512,512]{2,1,0:T(8,128)(2,1)}, bf16[3,512,512]{2,1,0:T(8,128)(2,1)}, u32[]{:S(2)}, u32[]{:S(2)}) %collective-permute-start.2) | collective-permute-done | bytes 1572896 | tf_op jit(solution)/shard_map/ppermute | solution.py:280
  64.6 10.9 %own_amplitudes.7 = (bf16[3,512,512]{2,1,0:T(8,128)(2,1)}, f32[8,128]{1,0:T(8,128)}) custom-call(s32[5]{0:T(128)} %stack.31.refs_0_, f32[3]{0:T(128)} %dynamic-slice_add_fusion.refs_1_, f32[8,128]{1,0:T(8,128)} %get-tuple-element.82.refs_2_, bf16[6,512,1536]{2,1,0:T(8,128)(2,1)} %refs_3_.13, bf16[3,512,1536]{2,1,0:T(8,128)(2,1)} %collective-permute-done.refs_3_.refs_4_, ...), custom_call_target="tpu_custom_call" | custom-call | bytes 1024 | tf_op jit(solution)/shard_map/own_amplitudes/pallas_call | solution.py:27
  75.5 5.0 combine_pairs.7
  93.9 10.0 %pairs_for_chip.8 = (bf16[3,512,512]{2,1,0:T(8,128)(2,1)}, f32[8,128]{1,0:T(8,128)}) custom-call(s32[5]{0:T(128)} %stack.31.refs_0_, f32[8,128]{1,0:T(8,128)} %get-tuple-element.87.refs_1_, bf16[6,512,1536]{2,1,0:T(8,128)(2,1)} %refs_3_.13, bf16[3,512,1536]{2,1,0:T(8,128)(2,1)} %collective-permute-done.refs_3_.refs_4_, ...), custom_call_target="tpu_custom_call" | custom-call | bytes 1024 | tf_op jit(solution)/shard_map/pairs_for_chip/pallas_call | solution.py:27
  105.9 10.1 %pairs_for_chip.9 = (bf16[3,512,512]{2,1,0:T(8,128)(2,1)}, f32[8,128]{1,0:T(8,128)}) custom-call(s32[5]{0:T(128)} %stack.31.refs_0_, f32[8,128]{1,0:T(8,128)} %get-tuple-element.89.refs_1_, bf16[6,512,1536]{2,1,0:T(8,128)(2,1)} %refs_3_.13, bf16[3,512,1536]{2,1,0:T(8,128)(2,1)} %collective-permute-done.refs_3_.refs_4_, ...), custom_call_target="tpu_custom_call" | custom-call | bytes 1024 | tf_op jit(solution)/shard_map/pairs_for_chip/pallas_call | solution.py:27
  116.0 23.9 %collective-permute-done.7.refs_7_ = bf16[3,512,512]{2,1,0:T(8,128)(2,1)S(1)} collective-permute-done((bf16[3,512,512]{2,1,0:T(8,128)(2,1)}, bf16[3,512,512]{2,1,0:T(8,128)(2,1)S(1)}, u32[]{:S(2)}, u32[]{:S(2)}) %collective-permute-start.7) | collective-permute-done | bytes 1572896 | tf_op jit(solution)/shard_map/ppermute | solution.py:280
  141.1 10.8 %own_amplitudes.8 = (bf16[3,512,512]{2,1,0:T(8,128)(2,1)}, f32[8,128]{1,0:T(8,128)}) custom-call(s32[5]{0:T(128)} %stack.31.refs_0_, f32[3]{0:T(128)} %dynamic-slice_add_fusion.refs_1_, f32[8,128]{1,0:T(8,128)} %get-tuple-element.91.refs_2_, bf16[6,512,1536]{2,1,0:T(8,128)(2,1)} %refs_3_.13, bf16[3,512,1536]{2,1,0:T(8,128)(2,1)} %collective-permute-done.refs_3_.refs_4_, ...), custom_call_target="tpu_custom_call" | custom-call | bytes 1024 | tf_op jit(solution)/shard_map/own_amplitudes/pallas_call | solution.py:27
  169.2 10.0 %pairs_for_chip.10 = (bf16[3,512,512]{2,1,0:T(8,128)(2,1)}, f32[8,128]{1,0:T(8,128)}) custom-call(s32[5]{0:T(128)} %stack.31.refs_0_, f32[8,128]{1,0:T(8,128)} %get-tuple-element.96.refs_1_, bf16[6,512,1536]{2,1,0:T(8,128)(2,1)} %refs_3_.13, bf16[3,512,1536]{2,1,0:T(8,128)(2,1)} %collective-permute-done.refs_3_.refs_4_, bf16[2,512,1536]{2,1,0:T(8,128)(2,1)} %copy-done.1, ...), custom_call_target="tpu_custom_call" | custom-call | bytes 1024 | tf_op jit(solution)/shard_map/pairs_for_chip/pallas_call | solution.py:27
  181.8 18.7 %collective-permute-done.11.refs_7_ = bf16[3,512,512]{2,1,0:T(8,128)(2,1)} collective-permute-done((bf16[3,512,512]{2,1,0:T(8,128)(2,1)}, bf16[3,512,512]{2,1,0:T(8,128)(2,1)}, u32[]{:S(2)}, u32[]{:S(2)}) %collective-permute-start.11) | collective-permute-done | bytes 1572896 | tf_op jit(solution)/shard_map/ppermute | solution.py:280
  200.4 10.8 %own_amplitudes.9 = (bf16[3,512,512]{2,1,0:T(8,128)(2,1)}, f32[8,128]{1,0:T(8,128)}) custom-call(s32[5]{0:T(128)} %stack.31.refs_0_, f32[3]{0:T(128)} %dynamic-slice_add_fusion.refs_1_, f32[8,128]{1,0:T(8,128)} %get-tuple-element.99.refs_2_, bf16[6,512,1536]{2,1,0:T(8,128)(2,1)} %refs_3_.13, bf16[3,512,1536]{2,1,0:T(8,128)(2,1)} %collective-permute-done.refs_3_.refs_4_, ...), custom_call_target="tpu_custom_call" | custom-call | bytes 1024 | tf_op jit(solution)/shard_map/own_amplitudes/pallas_call | solution.py:27
  215.0 19.2 %collective-permute-done.12.refs_3_ = bf16[3,512,512]{2,1,0:T(8,128)(2,1)} collective-permute-done((bf16[3,512,512]{2,1,0:T(8,128)(2,1)S(1)}, bf16[3,512,512]{2,1,0:T(8,128)(2,1)}, u32[]{:S(2)}, u32[]{:S(2)}) %collective-permute-start.12) | collective-permute-done | bytes 1572896 | tf_op jit(solution)/shard_map/ppermute | solution.py:280
  234.1 16.1 %chip_gamma.2 = (f32[3,512,1536]{2,1,0:T(8,128)}, f32[3,512,1536]{2,1,0:T(8,128)}, f32[8,128]{1,0:T(8,128)}) custom-call(s32[5]{0:T(128)} %stack.31.refs_0_, f32[8,128]{1,0:T(8,128)} %get-tuple-element.101.refs_1_, bf16[3,512,512]{2,1,0:T(8,128)(2,1)} %get-tuple-element.102.refs_2_, bf16[3,512,512]{2,1,0:T(8,128)(2,1)} %collective-permute-done.12.refs_3_, ...), custom_call_target="tpu_custom_call" | custom-call | bytes 1024 | tf_op jit(solution)/shard_map/chip_gamma/pallas_call | solution.py:27
  250.3 17.5 %collective-permute-done.13.refs_7_ = bf16[3,512,512]{2,1,0:T(8,128)(2,1)S(1)} collective-permute-done((bf16[3,512,512]{2,1,0:T(8,128)(2,1)}, bf16[3,512,512]{2,1,0:T(8,128)(2,1)S(1)}, u32[]{:S(2)}, u32[]{:S(2)}) %collective-permute-start.13) | collective-permute-done | bytes 1572896 | tf_op jit(solution)/shard_map/ppermute | solution.py:280
  268.9 10.8 %own_amplitudes.10 = (bf16[3,512,512]{2,1,0:T(8,128)(2,1)}, f32[8,128]{1,0:T(8,128)}) custom-call(s32[5]{0:T(128)} %stack.31.refs_0_, f32[3]{0:T(128)} %dynamic-slice_add_fusion.refs_1_, f32[8,128]{1,0:T(8,128)} %get-tuple-element.103.refs_2_, bf16[6,512,1536]{2,1,0:T(8,128)(2,1)} %refs_3_.13, bf16[3,512,1536]{2,1,0:T(8,128)(2,1)} %collective-permute-done.refs_3_.refs_4_, ...), custom_call_target="tpu_custom_call" | custom-call | bytes 1024 | tf_op jit(solution)/shard_map/own_amplitudes/pallas_call | solution.py:27
  280.8 4.9 combine_pairs.8
  293.9 33.9 %collective-permute-done.17.refs_3_ = bf16[3,512,512]{2,1,0:T(8,128)(2,1)S(1)} collective-permute-done((bf16[3,512,512]{2,1,0:T(8,128)(2,1)}, bf16[3,512,512]{2,1,0:T(8,128)(2,1)S(1)}, u32[]{:S(2)}, u32[]{:S(2)}) %collective-permute-start.17) | collective-permute-done | bytes 1572896 | tf_op jit(solution)/shard_map/ppermute | solution.py:280
  327.8 33.6 %collective-permute-done.16.refs_2_ = bf16[3,512,512]{2,1,0:T(8,128)(2,1)S(1)} collective-permute-done((bf16[3,512,512]{2,1,0:T(8,128)(2,1)}, bf16[3,512,512]{2,1,0:T(8,128)(2,1)S(1)}, u32[]{:S(2)}, u32[]{:S(2)}) %collective-permute-start.16) | collective-permute-done | bytes 1572896 | tf_op jit(solution)/shard_map/ppermute | solution.py:280
  387.1 31.2 %chip_gamma.3 = (f32[3,512,1536]{2,1,0:T(8,128)}, f32[3,512,1536]{2,1,0:T(8,128)}, f32[8,128]{1,0:T(8,128)}) custom-call(s32[5]{0:T(128)} %stack.31.refs_0_, f32[8,128]{1,0:T(8,128)} %get-tuple-element.117.refs_1_, bf16[3,512,512]{2,1,0:T(8,128)(2,1)} %get-tuple-element.110.refs_2_, ...), custom_call_target="tpu_custom_call", output_to_operand_aliasing={{0}: (10, {}), {1}: (11, {})} | custom-call | bytes 1024 | tf_op jit(solution)/shard_map/chip_gamma/pallas_call | solution.py:27
  456.1 14.3 %last_gamma.3 = (f32[6,512,1536]{2,1,0:T(8,128)}, bf16[1,512,1536]{2,1,0:T(8,128)(2,1)}, f32[8,128]{1,0:T(8,128)}) custom-call(s32[5]{0:T(128)} %stack.31.refs_0_, f32[8,128]{1,0:T(8,128)} %get-tuple-element.136.refs_1_, bf16[1,512,512]{2,1,0:T(8,128)(2,1)} %get-tuple-element.137.refs_2_, bf16[1,512,512]{2,1,0:T(8,128)(2,1)} %copy-done.22, ...), custom_call_target="tpu_custom_call" | custom-call | bytes 1024 | tf_op jit(solution)/shard_map/last_gamma/pallas_call | solution.py:27
  474.6 14.4 %last_gamma.4 = (f32[6,512,1536]{2,1,0:T(8,128)}, bf16[1,512,1536]{2,1,0:T(8,128)(2,1)}, f32[8,128]{1,0:T(8,128)}) custom-call(s32[5]{0:T(128)} %stack.31.refs_0_, f32[8,128]{1,0:T(8,128)} %get-tuple-element.141.refs_1_, bf16[1,512,512]{2,1,0:T(8,128)(2,1)} %get-tuple-element.142.refs_2_, ...), custom_call_target="tpu_custom_call", output_to_operand_aliasing={{0}: (15, {})} | custom-call | bytes 1024 | tf_op jit(solution)/shard_map/last_gamma/pallas_call | solution.py:27
  490.0 14.3 %last_gamma.5 = (f32[6,512,1536]{2,1,0:T(8,128)}, bf16[1,512,1536]{2,1,0:T(8,128)(2,1)}, f32[8,128]{1,0:T(8,128)}) custom-call(s32[5]{0:T(128)} %stack.31.refs_0_, f32[8,128]{1,0:T(8,128)} %get-tuple-element.145.refs_1_, bf16[1,512,512]{2,1,0:T(8,128)(2,1)} %get-tuple-element.146.refs_2_, ...), custom_call_target="tpu_custom_call", output_to_operand_aliasing={{0}: (15, {})} | custom-call | bytes 1024 | tf_op jit(solution)/shard_map/last_gamma/pallas_call | solution.py:27
  (169 shorter events, 142.4 us)
Async XLA Ops:
  5.5 75.0 %collective-permute-start.3 = (bf16[2,512,1536]{2,1,0:T(8,128)(2,1)}, bf16[2,512,1536]{2,1,0:T(8,128)(2,1)S(1)}, u32[]{:S(2)}, u32[]{:S(2)}) collective-permute-start(bf16[2,512,1536]{2,1,0:T(8,128)(2,1)} %refs_4_.3), channel_id=1, source_target_pairs={{0,4},{4,0},{8,12},{12,8},{1,5},{5,1},{9,13},{13,9},{2,6},{6,2},{1... | collective-permute-start | bytes 9437192 | tf_op jit(solution)/shard_map/ppermute | solution.py:289
  6.8 73.7 %collective-permute-start.4 = (bf16[2,512,1536]{2,1,0:T(8,128)(2,1)}, bf16[2,512,1536]{2,1,0:T(8,128)(2,1)}, u32[]{:S(2)}, u32[]{:S(2)}) collective-permute-start(bf16[2,512,1536]{2,1,0:T(8,128)(2,1)} %refs_4_.3), channel_id=1, source_target_pairs={{4,8},{8,4},{5,9},{9,5},{6,10},{10,6},{7,11},{11,7},{20,24},{24,20... | collective-permute-start | bytes 9437192 | tf_op jit(solution)/shard_map/ppermute | solution.py:289
  28.6 35.9 %collective-permute-start.2 = (bf16[3,512,512]{2,1,0:T(8,128)(2,1)}, bf16[3,512,512]{2,1,0:T(8,128)(2,1)}, u32[]{:S(2)}, u32[]{:S(2)}) collective-permute-start(bf16[3,512,512]{2,1,0:T(8,128)(2,1)} %get-tuple-element.83), channel_id=1, source_target_pairs={{0,2},{1,3},{2,0},{3,1},{4,6},{5,7},{6,4},{7,5},{8,10},{9,11},{10,... | collective-permute-start | bytes 4718600 | tf_op jit(solution)/shard_map/ppermute | solution.py:280
  86.0 71.4 %collective-permute-start.8 = (bf16[2,512,1536]{2,1,0:T(8,128)(2,1)}, bf16[2,512,1536]{2,1,0:T(8,128)(2,1)}, u32[]{:S(2)}, u32[]{:S(2)}) collective-permute-start(bf16[2,512,1536]{2,1,0:T(8,128)(2,1)} %get-tuple-element.88.refs_4_.refs_5_), channel_id=1, source_target_pairs={{4,8},{8,4},{5,9},{9,5},{6,10},{10,6},{7,11},{11,7},{20,24},{24,20... | collective-permute-start | bytes 9437192 | tf_op jit(solution)/shard_map/ppermute | solution.py:289
  88.0 70.3 %collective-permute-start.9 = (bf16[2,512,1536]{2,1,0:T(8,128)(2,1)}, bf16[2,512,1536]{2,1,0:T(8,128)(2,1)}, u32[]{:S(2)}, u32[]{:S(2)}) collective-permute-start(bf16[2,512,1536]{2,1,0:T(8,128)(2,1)} %get-tuple-element.90.refs_4_.refs_5_.refs_8_), channel_id=1, source_target_pairs={{4,0},{8,12},{5,1},{9,13},{6,2},{10,14},{7,3},{11,15},{20,16},{24,... | collective-permute-start | bytes 9437192 | tf_op jit(solution)/shard_map/ppermute | solution.py:289
  103.9 36.0 %collective-permute-start.7 = (bf16[3,512,512]{2,1,0:T(8,128)(2,1)}, bf16[3,512,512]{2,1,0:T(8,128)(2,1)S(1)}, u32[]{:S(2)}, u32[]{:S(2)}) collective-permute-start(bf16[3,512,512]{2,1,0:T(8,128)(2,1)} %get-tuple-element.92), channel_id=1, source_target_pairs={{0,2},{1,3},{2,0},{3,1},{4,6},{5,7},{6,4},{7,5},{8,10},{9,11},{10,... | collective-permute-start | bytes 4718600 | tf_op jit(solution)/shard_map/ppermute | solution.py:280
  162.2 38.2 %collective-permute-start.11 = (bf16[3,512,512]{2,1,0:T(8,128)(2,1)}, bf16[3,512,512]{2,1,0:T(8,128)(2,1)}, u32[]{:S(2)}, u32[]{:S(2)}) collective-permute-start(bf16[3,512,512]{2,1,0:T(8,128)(2,1)} %get-tuple-element.100), channel_id=1, source_target_pairs={{4,6},{5,7},{6,4},{7,5},{8,10},{9,11},{10,8},{11,9},{20,22},{21,23... | collective-permute-start | bytes 4718600 | tf_op jit(solution)/shard_map/ppermute | solution.py:280
  164.4 69.7 %collective-permute-start.12 = (bf16[3,512,512]{2,1,0:T(8,128)(2,1)S(1)}, bf16[3,512,512]{2,1,0:T(8,128)(2,1)}, u32[]{:S(2)}, u32[]{:S(2)}) collective-permute-start(bf16[3,512,512]{2,1,0:T(8,128)(2,1)S(1)} %copy-done.10), channel_id=1, source_target_pairs={{0,2},{1,3},{2,0},{3,1},{4,6},{5,7},{6,4},{7,5},{8,10},{9,11},{10,... | collective-permute-start | bytes 4718600 | tf_op jit(solution)/shard_map/ppermute | solution.py:280
  179.3 88.4 %collective-permute-start.13 = (bf16[3,512,512]{2,1,0:T(8,128)(2,1)}, bf16[3,512,512]{2,1,0:T(8,128)(2,1)S(1)}, u32[]{:S(2)}, u32[]{:S(2)}) collective-permute-start(bf16[3,512,512]{2,1,0:T(8,128)(2,1)} %get-tuple-element.104), channel_id=1, source_target_pairs={{0,2},{1,3},{2,0},{3,1},{4,6},{5,7},{6,4},{7,5},{8,10},{9,11},{10,... | collective-permute-start | bytes 4718600 | tf_op jit(solution)/shard_map/ppermute | solution.py:280
  179.6 100.2 %collective-permute-start.14 = (bf16[3,512,512]{2,1,0:T(8,128)(2,1)}, bf16[3,512,512]{2,1,0:T(8,128)(2,1)S(1)}, u32[]{:S(2)}, u32[]{:S(2)}) collective-permute-start(bf16[3,512,512]{2,1,0:T(8,128)(2,1)} %get-tuple-element.106.refs_2_), channel_id=1, source_target_pairs={{0,4},{4,0},{8,12},{12,8},{1,5},{5,1},{9,13},{13,9},{2,6},{6,2},{1... | collective-permute-start | bytes 4718600 | tf_op jit(solution)/shard_map/ppermute | solution.py:289
  211.3 74.4 %collective-permute-start.15 = (bf16[3,512,512]{2,1,0:T(8,128)(2,1)}, bf16[3,512,512]{2,1,0:T(8,128)(2,1)}, u32[]{:S(2)}, u32[]{:S(2)}) collective-permute-start(bf16[3,512,512]{2,1,0:T(8,128)(2,1)} %get-tuple-element.108.refs_2_), channel_id=1, source_target_pairs={{4,8},{8,4},{5,9},{9,5},{6,10},{10,6},{7,11},{11,7},{20,24},{24,20... | collective-permute-start | bytes 4718600 | tf_op jit(solution)/shard_map/ppermute | solution.py:289
  213.3 149.9 %collective-permute-start.18 = (bf16[2,512,1536]{2,1,0:T(8,128)(2,1)}, bf16[2,512,1536]{2,1,0:T(8,128)(2,1)S(1)}, u32[]{:S(2)}, u32[]{:S(2)}) collective-permute-start(bf16[2,512,1536]{2,1,0:T(8,128)(2,1)} %get-tuple-element.97), channel_id=1, source_target_pairs={{4,0},{8,12},{5,1},{9,13},{6,2},{10,14},{7,3},{11,15},{20,16},{24,... | collective-permute-start | bytes 9437192 | tf_op jit(solution)/shard_map/ppermute | solution.py:289
  290.5 37.3 %collective-permute-start.17 = (bf16[3,512,512]{2,1,0:T(8,128)(2,1)}, bf16[3,512,512]{2,1,0:T(8,128)(2,1)S(1)}, u32[]{:S(2)}, u32[]{:S(2)}) collective-permute-start(bf16[3,512,512]{2,1,0:T(8,128)(2,1)} %get-tuple-element.111.refs_6_), channel_id=1, source_target_pairs={{4,6},{5,7},{6,4},{7,5},{8,10},{9,11},{10,8},{11,9},{20,22},{21,23... | collective-permute-start | bytes 4718600 | tf_op jit(solution)/shard_map/ppermute | solution.py:280
  292.6 68.7 %collective-permute-start.16 = (bf16[3,512,512]{2,1,0:T(8,128)(2,1)}, bf16[3,512,512]{2,1,0:T(8,128)(2,1)S(1)}, u32[]{:S(2)}, u32[]{:S(2)}) collective-permute-start(bf16[3,512,512]{2,1,0:T(8,128)(2,1)} %get-tuple-element.110.refs_2_), channel_id=1, source_target_pairs={{0,2},{1,3},{2,0},{3,1},{4,6},{5,7},{6,4},{7,5},{8,10},{9,11},{10,... | collective-permute-start | bytes 4718600 | tf_op jit(solution)/shard_map/ppermute | solution.py:280
  293.9 142.5 %collective-permute-start.26 = (bf16[3,512,512]{2,1,0:T(8,128)(2,1)S(1)}, bf16[3,512,512]{2,1,0:T(8,128)(2,1)}, u32[]{:S(2)}, u32[]{:S(2)}) collective-permute-start(bf16[3,512,512]{2,1,0:T(8,128)(2,1)S(1)} %copy-done.18), channel_id=1, source_target_pairs={{0,8},{8,0},{4,12},{12,4},{1,9},{9,1},{5,13},{13,5},{2,10},{10,2},... | collective-permute-start | bytes 4718600 | tf_op jit(solution)/shard_map/ppermute | solution.py:289
  376.5 41.8 %collective-permute-start.23 = (bf16[1,512,512]{2,1,0:T(8,128)(2,1)}, bf16[1,512,512]{2,1,0:T(8,128)(2,1)S(1)}, u32[]{:S(2)}, u32[]{:S(2)}) collective-permute-start(bf16[1,512,512]{2,1,0:T(8,128)(2,1)} %get-tuple-element.123), channel_id=1, source_target_pairs={{0,2},{1,3},{2,0},{3,1},{12,14},{13,15},{14,12},{15,13},{16,18},{1... | collective-permute-start | bytes 1572872 | tf_op jit(solution)/shard_map/ppermute | solution.py:280
  381.4 42.8 %collective-permute-start.24 = (bf16[1,512,512]{2,1,0:T(8,128)(2,1)}, bf16[1,512,512]{2,1,0:T(8,128)(2,1)S(1)}, u32[]{:S(2)}, u32[]{:S(2)}) collective-permute-start(bf16[1,512,512]{2,1,0:T(8,128)(2,1)} %get-tuple-element.125), channel_id=1, source_target_pairs={{0,2},{1,3},{2,0},{3,1},{12,14},{13,15},{14,12},{15,13},{16,18},{1... | collective-permute-start | bytes 1572872 | tf_op jit(solution)/shard_map/ppermute | solution.py:280
  386.4 43.9 %collective-permute-start.25 = (bf16[1,512,512]{2,1,0:T(8,128)(2,1)}, bf16[1,512,512]{2,1,0:T(8,128)(2,1)S(1)}, u32[]{:S(2)}, u32[]{:S(2)}) collective-permute-start(bf16[1,512,512]{2,1,0:T(8,128)(2,1)} %get-tuple-element.127), channel_id=1, source_target_pairs={{0,2},{1,3},{2,0},{3,1},{12,14},{13,15},{14,12},{15,13},{16,18},{1... | collective-permute-start | bytes 1572872 | tf_op jit(solution)/shard_map/ppermute | solution.py:280
  445.6 28.1 %collective-permute-start.32 = (bf16[1,512,512]{2,1,0:T(8,128)(2,1)}, bf16[1,512,512]{2,1,0:T(8,128)(2,1)S(1)}, u32[]{:S(2)}, u32[]{:S(2)}) collective-permute-start(bf16[1,512,512]{2,1,0:T(8,128)(2,1)} %get-tuple-element.142.refs_2_), channel_id=1, source_target_pairs={{0,2},{1,3},{2,0},{3,1},{4,6},{5,7},{6,4},{7,5},{8,10},{9,11},{10,... | collective-permute-start | bytes 1572872 | tf_op jit(solution)/shard_map/ppermute | solution.py:280
  450.4 23.2 %collective-permute-start.33 = (bf16[1,512,512]{2,1,0:T(8,128)(2,1)}, bf16[1,512,512]{2,1,0:T(8,128)(2,1)S(1)}, u32[]{:S(2)}, u32[]{:S(2)}) collective-permute-start(bf16[1,512,512]{2,1,0:T(8,128)(2,1)} %get-tuple-element.143.refs_6_), channel_id=1, source_target_pairs={{0,2},{1,3},{2,0},{3,1},{12,14},{13,15},{14,12},{15,13},{16,18},{1... | collective-permute-start | bytes 1572872 | tf_op jit(solution)/shard_map/ppermute | solution.py:280
  451.1 37.9 %collective-permute-start.34 = (bf16[1,512,512]{2,1,0:T(8,128)(2,1)}, bf16[1,512,512]{2,1,0:T(8,128)(2,1)S(1)}, u32[]{:S(2)}, u32[]{:S(2)}) collective-permute-start(bf16[1,512,512]{2,1,0:T(8,128)(2,1)} %get-tuple-element.146.refs_2_), channel_id=1, source_target_pairs={{0,2},{1,3},{2,0},{3,1},{4,6},{5,7},{6,4},{7,5},{8,10},{9,11},{10,... | collective-permute-start | bytes 1572872 | tf_op jit(solution)/shard_map/ppermute | solution.py:280
  454.6 34.5 %collective-permute-start.35 = (bf16[1,512,512]{2,1,0:T(8,128)(2,1)}, bf16[1,512,512]{2,1,0:T(8,128)(2,1)S(1)}, u32[]{:S(2)}, u32[]{:S(2)}) collective-permute-start(bf16[1,512,512]{2,1,0:T(8,128)(2,1)} %get-tuple-element.147.refs_6_), channel_id=1, source_target_pairs={{0,2},{1,3},{2,0},{3,1},{12,14},{13,15},{14,12},{15,13},{16,18},{1... | collective-permute-start | bytes 1572872 | tf_op jit(solution)/shard_map/ppermute | solution.py:280
  470.4 34.5 %collective-permute-start.36 = (bf16[1,512,1536]{2,1,0:T(8,128)(2,1)}, bf16[1,512,1536]{2,1,0:T(8,128)(2,1)S(1)}, u32[]{:S(2)}, u32[]{:S(2)}) collective-permute-start(bf16[1,512,1536]{2,1,0:T(8,128)(2,1)} %get-tuple-element.150), channel_id=1, source_target_pairs={{0,1},{1,0},{2,3},{3,2},{4,5},{5,4},{6,7},{7,6},{8,9},{9,8},{10,11... | collective-permute-start | bytes 4718600 | tf_op jit(solution)/shard_map/ppermute | solution.py:280
  488.9 20.6 %collective-permute-start.37 = (bf16[1,512,1536]{2,1,0:T(8,128)(2,1)}, bf16[1,512,1536]{2,1,0:T(8,128)(2,1)S(1)}, u32[]{:S(2)}, u32[]{:S(2)}) collective-permute-start(bf16[1,512,1536]{2,1,0:T(8,128)(2,1)} %get-tuple-element.153), channel_id=1, source_target_pairs={{0,1},{1,0},{2,3},{3,2},{4,5},{5,4},{6,7},{7,6},{8,9},{9,8},{10,11... | collective-permute-start | bytes 4718600 | tf_op jit(solution)/shard_map/ppermute | solution.py:280
  (51 other events, 312.3 us)

commit v5 on v4

v5 whole, which is shorter than its diff:
```python
import functools

import jax
import jax.numpy as jnp
from jax import lax
from jax.experimental import pallas as pl
from jax.experimental.pallas import tpu as pltpu
from jax.sharding import PartitionSpec as P

F32 = jnp.float32
BF16 = jnp.bfloat16
ANY = pl.BlockSpec(memory_space=pl.ANY)
TOKEN = jax.ShapeDtypeStruct((8, 128), F32)
TILE = 256


def tile_of(size):
    return TILE if size % TILE == 0 else size


def call(kernel, name, token, place, grid, in_specs, args, out_specs, out, aliases=None, mib=8):
    def body(*refs):
        n = len(place)
        kernel(*refs[:n], *refs[n + 1 : -1])

    shift = len(place) + 1
    return pl.pallas_call(
        body,
        out_shape=(*out, TOKEN),
        grid_spec=pltpu.PrefetchScalarGridSpec(
            num_scalar_prefetch=len(place),
            grid=grid,
            in_specs=[ANY] + in_specs,
            out_specs=(*out_specs, ANY),
        ),
        input_output_aliases={k + shift: v for k, v in (aliases or {}).items()},
        compiler_params=pltpu.CompilerParams(vmem_limit_bytes=mib * 2**20),
        cost_estimate=pl.CostEstimate(flops=0, bytes_accessed=1024, transcendentals=0),
        name=name,
    )(*place, token, *args)


def tie_kernel(place, *refs):
    del place, refs


def tie(token, place, *held):
    n = len(held)
    shapes = [held_shape(h) for h in held]
    return call(tie_kernel, "tie", token, place, (1,), [ANY] * n, held, [ANY] * n, shapes, {k: k for k in range(n)})


def held_shape(a):
    return jax.ShapeDtypeStruct(a.shape, a.dtype)


def whole_block(pieces, j):
    return jnp.concatenate([p[j] for p in pieces], axis=0) if len(pieces) > 1 else pieces[0][j]


def pairs_kernel(n_place, n_pieces, has_last, first, *refs):
    place, (b_i, b_i_core, block, *rest) = refs[:n_place], refs[n_place:]
    pieces, rest, out = rest[:n_pieces], rest[n_pieces:], rest[-1]
    across = (((1,), (1,)), ((), ()))
    value = lax.dot_general(b_i[0], block[0], across, preferred_element_type=F32)
    value += lax.dot_general(b_i_core[0], whole_block(pieces, 0), across, preferred_element_type=F32)
    if has_last:
        chip, vir_a, vir_b = rest[:3]
        value = value + chip[0].astype(F32)
        value = value / ((place[1][first + pl.program_id(0)] - vir_a[...]) - vir_b[...])
    out[0] = value.astype(BF16)


def pairs(token, place, b_i, block, own_j, which=None, last=None):
    (mine, core_part), (block, passed, kept) = b_i, block
    pieces = kept if own_j else passed
    cols, depth = block.shape[1:]
    half, rows = core_part.shape[:2]
    first, count = (0, half) if which is None else (which, 1)

    def j_of(s):
        return s[0] if own_j else 1 - s[0]

    one = pl.BlockSpec((1, rows, cols), lambda i, s, *_: (i, 0, 0))
    in_specs = [
        pl.BlockSpec((1, rows, depth), lambda i, s, *_: (s[1] * half + first + i, 0, 0)),
        pl.BlockSpec((1, rows, depth), lambda i, s, *_: (first + i, 0, 0)),
        pl.BlockSpec((1, cols, depth), lambda i, s, *_: (j_of(s), 0, 0)),
    ]
    for p in pieces:
        one_j = p.shape[0] == 1
        in_specs.append(pl.BlockSpec((1,) + p.shape[1:], lambda i, s, *_, one_j=one_j: (0 if one_j else j_of(s), 0, 0)))
    args, name = [mine, core_part, block, *pieces], "pairs_for_chip"
    if last is not None:
        chip, occ, vir_a, vir_b = last
        place = place + (occ,)
        in_specs += [
            one,
            pl.BlockSpec((rows, 1), lambda i, s, *_: (0, 0)),
            pl.BlockSpec((1, cols), lambda i, s, *_: (0, 0)),
        ]
        args += [chip, vir_a, vir_b]
        name = "own_amplitudes"
    out = jax.ShapeDtypeStruct((count, rows, cols), BF16)
    kernel = functools.partial(pairs_kernel, len(place), len(pieces), last is not None, first)
    return call(kernel, name, token, place, (count,), in_specs, args, [one], [out], mib=24)


def combine_kernel(place, held, mirror, *outs):
    for i, out in enumerate(outs):

        @pl.when((pl.program_id(0) == i) | (len(outs) == 1))
        def _():
            out[0] = (2.0 * held[0].astype(F32) - mirror[0].astype(F32).T).astype(BF16)


def combine_pairs(token, place, held, mirror, split):
    count, rows, cols = held.shape
    spec = pl.BlockSpec((1, rows, cols), lambda i, s: (i, 0, 0))
    out_specs, out = [spec], [held_shape(held)]
    if split:
        out_specs = [pl.BlockSpec((1, rows, cols), lambda i, s: (0, 0, 0))] * count
        out = [jax.ShapeDtypeStruct((1, rows, cols), BF16)] * count
    *out, token = call(combine_kernel, "combine_pairs", token, place, (count,), [spec, spec], [held, mirror], out_specs, out, mib=12)
    return (out if split else out[0]), token


def gamma_kernel(terms, has_sum, place, *refs):
    x = place[0]
    refs, outs = list(refs[:-2]), refs[-2:]
    count, rows, tile = outs[0].shape
    held = []
    for n_passed, n_kept in terms:
        same_j, other_j, block = refs[:3]
        passed, kept = refs[3 : 3 + n_passed], refs[3 + n_passed : 3 + n_passed + n_kept]
        refs = refs[3 + n_passed + n_kept :]
        core_j = (0, 0) if n_kept else (x, 1 - x)
        held.append((same_j, (lambda block=block: block[x], lambda kept=kept or passed, j=core_j[0]: whole_block(kept, j))))
        held.append((other_j, (lambda block=block: block[1 - x], lambda passed=passed, j=core_j[1]: whole_block(passed, j))))
    for k, out in enumerate(outs):
        total = refs[k][...].reshape(count * rows, tile) if has_sum else None
        for pair, blocks in held:
            left = pair[...].reshape(count * rows, pair.shape[2])
            term = jnp.dot(left, blocks[k](), preferred_element_type=F32)
            total = term if total is None else total + term
        out[...] = total.reshape(count, rows, tile).astype(out.dtype)


def gamma_operands(terms, which, tile):
    in_specs, args, counts = [], [], []
    for same_j, other_j, (block, passed, kept) in terms:
        for h in (same_j, other_j):
            if which is None or h.shape[0] == 1:
                in_specs.append(pl.BlockSpec(h.shape, lambda p, s: (0, 0, 0), pipeline_mode=pl.Buffered(1)))
            else:
                in_specs.append(pl.BlockSpec((1,) + h.shape[1:], lambda p, s: (which, 0, 0)))
        kept = [] if kept is passed else kept
        blocks = [block, *passed, *kept]
        in_specs += [pl.BlockSpec(b.shape[:2] + (tile,), lambda p, s: (0, 0, p)) for b in blocks]
        args += [same_j, other_j, *blocks]
        counts.append((len(passed), len(kept)))
    return in_specs, args, counts


def chip_gamma(token, place, terms, before=None):
    half, rows = terms[0][0].shape[:2]
    depth = terms[0][2][0].shape[2]
    tile = tile_of(depth)
    in_specs, args, counts = gamma_operands(terms, None, tile)
    spec = pl.BlockSpec((half, rows, tile), lambda p, s: (0, 0, p))
    aliases = None
    if before is not None:
        aliases = {len(args): 0, len(args) + 1: 1}
        in_specs += [spec, spec]
        args += before
    out = [jax.ShapeDtypeStruct((half, rows, depth), F32)] * 2
    kernel = functools.partial(gamma_kernel, counts, before is not None)
    *out, token = call(kernel, "chip_gamma", token, place, (depth // tile,), in_specs, args, [spec, spec], out, aliases, mib=36)
    return out, token


def last_gamma(token, place, which, terms, before, shape, result):
    half, rows, depth = before[0].shape
    tile = tile_of(depth)
    in_specs, args, counts = gamma_operands(terms, which, tile)
    spec = pl.BlockSpec((1, rows, tile), lambda p, s: (which, 0, p))
    in_specs += [spec, spec]
    args += before
    aliases, drop = None, 0
    if result is not None:
        aliases, drop = {len(args): 0}, 1
        in_specs.append(ANY)
        args.append(result)

    def kernel(place, *refs):
        n = len(refs) - 2
        gamma_kernel(counts, True, place, *refs[: n - drop], *refs[n:])

    out_specs = [
        pl.BlockSpec((1, rows, tile), lambda p, s: (s[1] * half + which, 0, p)),
        pl.BlockSpec((1, rows, tile), lambda p, s: (0, 0, p)),
    ]
    out = [jax.ShapeDtypeStruct(shape, F32), jax.ShapeDtypeStruct((1, rows, depth), BF16)]
    return call(kernel, "last_gamma", token, place, (depth // tile,), in_specs, args, out_specs, out, aliases, mib=24)


def place_kernel(place, received, result, out):
    del place, result
    out[...] = received[...].astype(F32)


def place_gamma(token, place, which, received, result):
    half = result.shape[0] // 2
    _, rows, depth = received.shape
    tile = rows // 2
    return call(
        place_kernel,
        "place_gamma",
        token,
        place,
        (2,),
        [pl.BlockSpec((1, tile, depth), lambda p, s: (0, p, 0)), ANY],
        [received, result],
        [pl.BlockSpec((1, tile, depth), lambda p, s: ((1 - s[1]) * half + which, p, 0))],
        [held_shape(result)],
        {1: 0},
    )


def chain_device(b_occ_i, b_occ_j, eps_occ_i, eps_occ_j, eps_vir):
    n_i, rows, depth = b_occ_i.shape
    half = n_i // 2
    z, col = lax.axis_index("row"), lax.axis_index("col")
    x, core = col // 2, col % 2
    in_middle = (z == 1) | (z == 2)
    place = (jnp.stack([x, core]).astype(jnp.int32),)
    occ = lax.dynamic_slice_in_dim(eps_occ_i, core * half, half, 0) + eps_occ_j[x]
    token = jnp.zeros(TOKEN.shape, F32)
    shape = b_occ_i.shape

    def energies(block):
        return lax.dynamic_slice_in_dim(eps_vir, block * rows, rows, 0)

    vir_a = energies(z)[:, None]

    def to_core(values):
        return lax.ppermute(values, "col", [(q, q ^ 1) for q in range(4)])

    def to_chip(values):
        return lax.ppermute(values, "col", [(q, q ^ 2) for q in range(4)])

    def along(values, steps):
        return lax.ppermute(values, "row", steps)

    def swapped(values, distance):
        return along(values, [(k, k ^ distance) for k in range(4)])

    ends, middle = [(1, 0), (2, 3)], [(1, 2), (2, 1)]
    b_i = b_occ_i, to_core(lax.dynamic_slice_in_dim(b_occ_i, (1 - core) * half, half, 0))

    def pass_on(block, which=None):
        nonlocal token
        out, token = pairs(token, place, b_i, block, False, which)
        return to_chip(out)

    def own(block, chip_sum, distance, which=None):
        nonlocal token
        vir_b = energies(z ^ distance)[None, :]
        out, token = pairs(token, place, b_i, block, True, which, (chip_sum, occ, vir_a, vir_b))
        return out

    def combine(held, mirror, split=False):
        nonlocal token
        out, token = combine_pairs(token, place, held, mirror, split)
        return out

    def forward(*values):
        nonlocal token
        *out, token = tie(token, place, *values)
        return out

    def both(values):
        pieces = [to_core(values)]
        return values, pieces, pieces

    def both_in_pieces(values, n_pieces=2):
        def part(j):
            one = lax.dynamic_slice_in_dim(values, j, 1, 0)
            return [to_core(p) for p in jnp.split(one, n_pieces, axis=1)]

        return values, part(1 - x), part(x)

    near = swapped(b_occ_j, 1)
    across = along(b_occ_j, middle)
    here = both(b_occ_j)

    chip_0 = pass_on(here)
    held_0 = own(here, chip_0, 0)
    mine_0 = combine(held_0, held_0)
    other_0 = to_chip(mine_0)

    near, across = forward(near, across)
    far_mid = along(near, middle)
    far_end = along(across, ends)
    near = both(near)
    chip_1 = pass_on(near)
    gamma, token = chip_gamma(token, place, [(mine_0, other_0, here)])

    far_mid, far_end = forward(far_mid, far_end)
    last = along(far_mid, ends)
    far = both_in_pieces(jnp.where(in_middle, far_mid, far_end))
    held_1 = own(near, chip_1, 1)
    mirror_1 = swapped(held_1, 1)
    chip_2 = pass_on(far)

    held_2 = own(far, chip_2, 2)
    mirror_2 = swapped(held_2, 2)
    mine_1 = combine(held_1, mirror_1)
    other_1 = to_chip(mine_1)

    (last,) = forward(last)
    last = both_in_pieces(jnp.where(in_middle, across, last))
    chip_3 = [pass_on(last, 0)]
    last = last[:2] + (forward(*last[2]),)
    chip_3 += [pass_on(last, i) for i in range(1, half)]
    gamma, token = chip_gamma(token, place, [(mine_1, other_1, near)], gamma)
    mine_2 = combine(held_2, mirror_2, split=True)
    other_2 = [to_chip(m) for m in mine_2]
    held_3 = [own(last, chip_3[i], 3, i) for i in range(half)]
    mirror_3 = [swapped(h, 3) for h in held_3]
    mine_3 = [combine(h, m) for h, m in zip(held_3, mirror_3)]
    other_3 = [to_chip(m) for m in mine_3]

    result, received = None, []
    for i in range(half):
        terms = [(mine_2[i], other_2[i], far), (mine_3[i], other_3[i], last)]
        result, theirs, token = last_gamma(token, place, i, terms, gamma, shape, result)
        received.append(to_core(theirs))
    for i in range(half):
        result, token = place_gamma(token, place, i, received[i], result)
    return result


def general_device(b_occ_i, b_occ_j, eps_occ_i, eps_occ_j, eps_vir):
    rows = b_occ_i.shape[1]
    own_energy = lax.dynamic_slice_in_dim(eps_vir, lax.axis_index("row") * rows, rows, 0)
    gathered = lax.all_gather(b_occ_j, "row", axis=1, tiled=True)
    partial_value = jnp.einsum("iap,jbp->jiab", b_occ_i, gathered, preferred_element_type=F32)
    totals = lax.psum(partial_value.astype(BF16), "col").astype(F32)
    denominator = (
        eps_occ_j[:, None, None, None]
        + eps_occ_i[None, :, None, None]
        - own_energy[None, None, :, None]
        - eps_vir[None, None, None, :]
    )
    held = (totals / denominator).astype(BF16)
    mirror = jnp.swapaxes(lax.all_to_all(held, "row", split_axis=3, concat_axis=2, tiled=True), 2, 3)
    combined = (2.0 * held.astype(F32) - mirror.astype(F32)).astype(BF16)
    return jnp.einsum("jiab,jbp->iap", combined, gathered, preferred_element_type=F32)


def solution(mesh):
    placed = (
        P("groups", "row", "col"),
        P("groups", "row", "col"),
        P("groups"),
        P("groups"),
        P("groups"),
    )
    chain = mesh.shape["row"] == 4 and mesh.shape["col"] == 4
    return jax.shard_map(
        chain_device if chain else general_device,
        mesh=mesh,
        in_specs=placed,
        out_specs=P("groups", "row", "col"),
        check_vma=False,
    )
```

time: 521 us -> 471 us (0.904)
  the two profiles are of different devices: /device:TPU:23 before, /device:TPU:17 now
where the time goes in v5:
time: 471 us; the launch traced here: 470 us
  waiting for transfers between devices  231 us (49%)
  Pallas kernels  164 us (35%)
  starting transfers between devices  44.1 us (9%)
  local copies, waits for them, and re-layouts  24.3 us (5%)
  other arithmetic  5.33 us (1%)
    pallas_call x30, Pallas kernels, call(): pl.pallas_call(body, out_shape=(*out, TOKEN), grid_spec=pltpu.PrefetchSca...  164 us
    ppermute x10, waiting for transfers between devices, along(): return lax.ppermute(values, 'row', steps)  112 us
    ppermute x14, waiting for transfers between devices, to_chip(): return lax.ppermute(values, 'col', [(q, q ^ 2) for q in range(4)])  106 us
    unnamed x58, local copies, waits for them, and re-layouts  18.2 us
    ppermute x10, starting transfers between devices, along(): return lax.ppermute(values, 'row', steps)  17.7 us
    ppermute x14, starting transfers between devices, to_core(): return lax.ppermute(values, 'col', [(q, q ^ 1) for q in range(4)])  15.6 us
    ppermute x14, waiting for transfers between devices, to_core(): return lax.ppermute(values, 'col', [(q, q ^ 1) for q in range(4)])  13.5 us
    ppermute x14, starting transfers between devices, to_chip(): return lax.ppermute(values, 'col', [(q, q ^ 2) for q in range(4)])  10.8 us
  transfers between devices with their start and end apart: 38, of which 17 were waited for; matrix products, arithmetic and copies ran while one was open for 1% of the time, Pallas kernels for 34%

profile of v5, /device:TPU:17, one launch (start us, length us, event | category | flops | bytes accessed | tf_op | source)
XLA Modules:
  0.0 470.1 jit_solution(8305710744445354756)
XLA Ops:
  8.8 9.1 %collective-permute-done.1.refs_5_.refs_6_ = bf16[2,512,1536]{2,1,0:T(8,128)(2,1)} collective-permute-done((bf16[2,512,1536]{2,1,0:T(8,128)(2,1)}, bf16[2,512,1536]{2,1,0:T(8,128)(2,1)}, u32[]{:S(2)}, u32[]{:S(2)}) %collective-permute-start.1) | collective-permute-done | bytes 3145760 | tf_op jit(solution)/shard_map/ppermute | solution.py:247
  21.6 9.2 %pairs_for_chip.6 = (bf16[3,512,512]{2,1,0:T(8,128)(2,1)}, f32[8,128]{1,0:T(8,128)S(1)}) custom-call(s32[2]{0:T(128)S(1)} %pad_add_fusion.refs_0_, f32[8,128]{1,0:T(8,128)S(1)} %broadcast_in_dim.20.refs_1_, bf16[6,512,1536]{2,1,0:T(8,128)(2,1)S(1)} %copy-done, bf16[3,512,1536]{2,1,0:T(8,128)(2,1)} %collective-permute-done.refs_3_.refs_4_, ...), custom_call_target="tpu_custom_call" | custom-call | bytes 1024 | tf_op jit(solution)/shard_map/pairs_for_chip/pallas_call | solution.py:27
  33.5 33.2 %collective-permute-done.2.refs_7_ = bf16[3,512,512]{2,1,0:T(8,128)(2,1)} collective-permute-done((bf16[3,512,512]{2,1,0:T(8,128)(2,1)}, bf16[3,512,512]{2,1,0:T(8,128)(2,1)}, u32[]{:S(2)}, u32[]{:S(2)}) %collective-permute-start.2) | collective-permute-done | bytes 1572896 | tf_op jit(solution)/shard_map/ppermute | solution.py:250
  70.4 8.7 %own_amplitudes.6 = (bf16[3,512,512]{2,1,0:T(8,128)(2,1)S(1)}, f32[8,128]{1,0:T(8,128)S(1)}) custom-call(s32[2]{0:T(128)S(1)} %pad_add_fusion.refs_0_, f32[3]{0:T(128)S(1)} %dynamic-slice_add_fusion.refs_1_, f32[8,128]{1,0:T(8,128)S(1)} %get-tuple-element.74.refs_2_, bf16[6,512,1536]{2,1,0:T(8,128)(2,1)S(1)} %copy-done.1, ...), custom_call_target="tpu_custom_call" | custom-call | bytes 1024 | tf_op jit(solution)/shard_map/own_amplitudes/pallas_call | solution.py:27
  85.7 5.2 %collective-permute-start.8 = (bf16[2,512,1536]{2,1,0:T(8,128)(2,1)}, bf16[2,512,1536]{2,1,0:T(8,128)(2,1)}, u32[]{:S(2)}, u32[]{:S(2)}) collective-permute-start(bf16[2,512,1536]{2,1,0:T(8,128)(2,1)} %get-tuple-element.84), channel_id=1, source_target_pairs={{4,0},{8,12},{5,1},{9,13},{6,2},{10,14},{7,3},{11,15},{20,16},{24,... | collective-permute-start | bytes 9437192 | tf_op jit(solution)/shard_map/ppermute | solution.py:253
  95.8 7.9 %pairs_for_chip.7 = (bf16[3,512,512]{2,1,0:T(8,128)(2,1)S(1)}, f32[8,128]{1,0:T(8,128)S(1)}) custom-call(s32[2]{0:T(128)S(1)} %pad_add_fusion.refs_0_, f32[8,128]{1,0:T(8,128)S(1)} %get-tuple-element.79.refs_1_, bf16[6,512,1536]{2,1,0:T(8,128)(2,1)S(1)} %copy-done.2, bf16[3,512,1536]{2,1,0:T(8,128)(2,1)} %collective-permute-done.refs_3_.refs_4_, ...), custom_call_target="tpu_custom_call" | custom-call | bytes 1024 | tf_op jit(solution)/shard_map/pairs_for_chip/pallas_call | solution.py:27
  104.1 22.5 %collective-permute-done.6.refs_3_ = bf16[3,512,512]{2,1,0:T(8,128)(2,1)} collective-permute-done((bf16[3,512,512]{2,1,0:T(8,128)(2,1)}, bf16[3,512,512]{2,1,0:T(8,128)(2,1)}, u32[]{:S(2)}, u32[]{:S(2)}) %collective-permute-start.6) | collective-permute-done | bytes 1572896 | tf_op jit(solution)/shard_map/ppermute | solution.py:250
  126.5 16.0 %chip_gamma.2 = (f32[3,512,1536]{2,1,0:T(8,128)}, f32[3,512,1536]{2,1,0:T(8,128)}, f32[8,128]{1,0:T(8,128)S(1)}) custom-call(s32[2]{0:T(128)S(1)} %pad_add_fusion.refs_0_, f32[8,128]{1,0:T(8,128)S(1)} %get-tuple-element.81.refs_1_, bf16[3,512,512]{2,1,0:T(8,128)(2,1)} %get-tuple-element.82.refs_2_, bf16[3,512,512]{2,1,0:T(8,128)(2,1)} %collective-permute-done.6.refs_3_, ...), custom_call_target="tpu_custom_call" | custom-call | bytes 1024 | tf_op jit(solution)/shard_map/chip_gamma/pallas_call | solution.py:27
  142.6 12.7 %collective-permute-done.7.refs_2_ = bf16[2,512,1536]{2,1,0:T(8,128)(2,1)} collective-permute-done((bf16[2,512,1536]{2,1,0:T(8,128)(2,1)S(1)}, bf16[2,512,1536]{2,1,0:T(8,128)(2,1)}, u32[]{:S(2)}, u32[]{:S(2)}) %collective-permute-start.7) | collective-permute-done | bytes 3145760 | tf_op jit(solution)/shard_map/ppermute | solution.py:253
  168.6 8.0 %own_amplitudes.7 = (bf16[3,512,512]{2,1,0:T(8,128)(2,1)S(1)}, f32[8,128]{1,0:T(8,128)S(1)}) custom-call(s32[2]{0:T(128)S(1)} %pad_add_fusion.refs_0_, f32[3]{0:T(128)S(1)} %dynamic-slice_add_fusion.refs_1_, f32[8,128]{1,0:T(8,128)S(1)} %get-tuple-element.85.refs_2_, bf16[6,512,1536]{2,1,0:T(8,128)(2,1)S(1)} %bitcast.9, ...), custom_call_target="tpu_custom_call" | custom-call | bytes 1024 | tf_op jit(solution)/shard_map/own_amplitudes/pallas_call | solution.py:27
  176.7 7.4 %pairs_for_chip.8 = (bf16[3,512,512]{2,1,0:T(8,128)(2,1)S(1)}, f32[8,128]{1,0:T(8,128)S(1)}) custom-call(s32[2]{0:T(128)S(1)} %pad_add_fusion.refs_0_, f32[8,128]{1,0:T(8,128)S(1)} %get-tuple-element.87.refs_1_, bf16[6,512,1536]{2,1,0:T(8,128)(2,1)S(1)} %bitcast.9, bf16[3,512,1536]{2,1,0:T(8,128)(2,1)} %collective-permute-done.refs_3_.refs_4_, ...), custom_call_target="tpu_custom_call" | custom-call | bytes 1024 | tf_op jit(solution)/shard_map/pairs_for_chip/pallas_call | solution.py:27
  189.9 29.1 %collective-permute-done.14.refs_8_ = bf16[3,512,512]{2,1,0:T(8,128)(2,1)S(1)} collective-permute-done((bf16[3,512,512]{2,1,0:T(8,128)(2,1)S(1)}, bf16[3,512,512]{2,1,0:T(8,128)(2,1)S(1)}, u32[]{:S(2)}, u32[]{:S(2)}) %collective-permute-start.14) | collective-permute-done | bytes 1572896 | tf_op jit(solution)/shard_map/ppermute | solution.py:250
  219.0 8.4 %own_amplitudes.8 = (bf16[3,512,512]{2,1,0:T(8,128)(2,1)}, f32[8,128]{1,0:T(8,128)S(1)}) custom-call(s32[2]{0:T(128)S(1)} %pad_add_fusion.refs_0_, f32[3]{0:T(128)S(1)} %dynamic-slice_add_fusion.refs_1_, f32[8,128]{1,0:T(8,128)S(1)} %get-tuple-element.90.refs_2_, bf16[6,512,1536]{2,1,0:T(8,128)(2,1)S(1)} %bitcast.9, ...), custom_call_target="tpu_custom_call" | custom-call | bytes 1024 | tf_op jit(solution)/shard_map/own_amplitudes/pallas_call | solution.py:27
  227.4 34.1 %collective-permute-done.15.refs_3_ = bf16[3,512,512]{2,1,0:T(8,128)(2,1)S(1)} collective-permute-done((bf16[3,512,512]{2,1,0:T(8,128)(2,1)S(1)}, bf16[3,512,512]{2,1,0:T(8,128)(2,1)S(1)}, u32[]{:S(2)}, u32[]{:S(2)}) %collective-permute-start.15) | collective-permute-done | bytes 1572896 | tf_op jit(solution)/shard_map/ppermute | solution.py:253
  288.0 16.1 %collective-permute-done.21.refs_3_ = bf16[3,512,512]{2,1,0:T(8,128)(2,1)S(1)} collective-permute-done((bf16[3,512,512]{2,1,0:T(8,128)(2,1)S(1)}, bf16[3,512,512]{2,1,0:T(8,128)(2,1)S(1)}, u32[]{:S(2)}, u32[]{:S(2)}) %collective-permute-start.21) | collective-permute-done | bytes 1572896 | tf_op jit(solution)/shard_map/ppermute | solution.py:250
  308.6 20.1 %chip_gamma.3 = (f32[3,512,1536]{2,1,0:T(8,128)}, f32[3,512,1536]{2,1,0:T(8,128)}, f32[8,128]{1,0:T(8,128)S(1)}) custom-call(s32[2]{0:T(128)S(1)} %pad_add_fusion.refs_0_, f32[8,128]{1,0:T(8,128)S(1)} %get-tuple-element.100.refs_1_, bf16[3,512,512]{2,1,0:T(8,128)(2,1)S(1)} %copy-done.17, ...), custom_call_target="tpu_custom_call", output_to_operand_aliasing={{0}: (6, {}), {1}: (7, {})} | custom-call | bytes 1024 | tf_op jit(solution)/shard_map/chip_gamma/pallas_call | solution.py:27
  328.7 8.7 %collective-permute-done.22.refs_3_ = bf16[3,512,512]{2,1,0:T(8,128)(2,1)} collective-permute-done((bf16[3,512,512]{2,1,0:T(8,128)(2,1)}, bf16[3,512,512]{2,1,0:T(8,128)(2,1)}, u32[]{:S(2)}, u32[]{:S(2)}) %collective-permute-start.22) | collective-permute-done | bytes 1572896 | tf_op jit(solution)/shard_map/ppermute | solution.py:253
  355.8 35.8 %collective-permute-done.26.refs_3_ = bf16[1,512,512]{2,1,0:T(8,128)(2,1)S(1)} collective-permute-done((bf16[1,512,512]{2,1,0:T(8,128)(2,1)S(1)}, bf16[1,512,512]{2,1,0:T(8,128)(2,1)S(1)}, u32[]{:S(2)}, u32[]{:S(2)}) %collective-permute-start.26) | collective-permute-done | bytes 524320 | tf_op jit(solution)/shard_map/ppermute | solution.py:253
  394.0 8.9 %collective-permute-done.27.refs_3_ = bf16[1,512,512]{2,1,0:T(8,128)(2,1)S(1)} collective-permute-done((bf16[1,512,512]{2,1,0:T(8,128)(2,1)S(1)}, bf16[1,512,512]{2,1,0:T(8,128)(2,1)S(1)}, u32[]{:S(2)}, u32[]{:S(2)}) %collective-permute-start.27) | collective-permute-done | bytes 524320 | tf_op jit(solution)/shard_map/ppermute | solution.py:253
  403.7 10.4 %collective-permute-done.28.refs_3_ = bf16[1,512,512]{2,1,0:T(8,128)(2,1)S(1)} collective-permute-done((bf16[1,512,512]{2,1,0:T(8,128)(2,1)S(1)}, bf16[1,512,512]{2,1,0:T(8,128)(2,1)S(1)}, u32[]{:S(2)}, u32[]{:S(2)}) %collective-permute-start.28) | collective-permute-done | bytes 524320 | tf_op jit(solution)/shard_map/ppermute | solution.py:253
  416.5 11.3 %last_gamma.3 = (f32[6,512,1536]{2,1,0:T(8,128)}, bf16[1,512,1536]{2,1,0:T(8,128)(2,1)S(1)}, f32[8,128]{1,0:T(8,128)S(1)}) custom-call(s32[2]{0:T(128)S(1)} %pad_add_fusion.refs_0_, f32[8,128]{1,0:T(8,128)S(1)} %get-tuple-element.120.refs_1_, bf16[1,512,512]{2,1,0:T(8,128)(2,1)S(1)} %get-tuple-element.121.refs_2_, ...), custom_call_target="tpu_custom_call" | custom-call | bytes 1024 | tf_op jit(solution)/shard_map/last_gamma/pallas_call | solution.py:27
  429.7 11.3 %last_gamma.4 = (f32[6,512,1536]{2,1,0:T(8,128)}, bf16[1,512,1536]{2,1,0:T(8,128)(2,1)S(1)}, f32[8,128]{1,0:T(8,128)S(1)}) custom-call(s32[2]{0:T(128)S(1)} %pad_add_fusion.refs_0_, f32[8,128]{1,0:T(8,128)S(1)} %get-tuple-element.125.refs_1_, bf16[1,512,512]{2,1,0:T(8,128)(2,1)S(1)} %get-tuple-element.126.refs_2_, ...), custom_call_target="tpu_custom_call", output_to_operand_aliasing={{0}: (18, {})} | custom-call | bytes 1024 | tf_op jit(solution)/shard_map/last_gamma/pallas_call | solution.py:27
  443.5 5.0 %collective-permute-done.34.refs_10_ = bf16[1,512,512]{2,1,0:T(8,128)(2,1)S(1)} collective-permute-done((bf16[1,512,512]{2,1,0:T(8,128)(2,1)S(1)}, bf16[1,512,512]{2,1,0:T(8,128)(2,1)S(1)}, u32[]{:S(2)}, u32[]{:S(2)}) %collective-permute-start.34) | collective-permute-done | bytes 524320 | tf_op jit(solution)/shard_map/ppermute | solution.py:250
  448.5 11.3 %last_gamma.5 = (f32[6,512,1536]{2,1,0:T(8,128)}, bf16[1,512,1536]{2,1,0:T(8,128)(2,1)S(1)}, f32[8,128]{1,0:T(8,128)S(1)}) custom-call(s32[2]{0:T(128)S(1)} %pad_add_fusion.refs_0_, f32[8,128]{1,0:T(8,128)S(1)} %get-tuple-element.129.refs_1_, bf16[1,512,512]{2,1,0:T(8,128)(2,1)S(1)} %get-tuple-element.130.refs_2_, ...), custom_call_target="tpu_custom_call", output_to_operand_aliasing={{0}: (18, {})} | custom-call | bytes 1024 | tf_op jit(solution)/shard_map/last_gamma/pallas_call | solution.py:27
  (153 shorter events, 119.0 us)
Async XLA Ops:
  5.5 76.2 %collective-permute-start.3 = (bf16[2,512,1536]{2,1,0:T(8,128)(2,1)}, bf16[2,512,1536]{2,1,0:T(8,128)(2,1)S(1)}, u32[]{:S(2)}, u32[]{:S(2)}) collective-permute-start(bf16[2,512,1536]{2,1,0:T(8,128)(2,1)} %refs_4_.3), channel_id=1, source_target_pairs={{0,4},{4,0},{8,12},{12,8},{1,5},{5,1},{9,13},{13,9},{2,6},{6,2},{1... | collective-permute-start | bytes 9437192 | tf_op jit(solution)/shard_map/ppermute | solution.py:253
  6.8 74.9 %collective-permute-start.4 = (bf16[2,512,1536]{2,1,0:T(8,128)(2,1)}, bf16[2,512,1536]{2,1,0:T(8,128)(2,1)}, u32[]{:S(2)}, u32[]{:S(2)}) collective-permute-start(bf16[2,512,1536]{2,1,0:T(8,128)(2,1)} %refs_4_.3), channel_id=1, source_target_pairs={{4,8},{8,4},{5,9},{9,5},{6,10},{10,6},{7,11},{11,7},{20,24},{24,20... | collective-permute-start | bytes 9437192 | tf_op jit(solution)/shard_map/ppermute | solution.py:253
  30.8 35.9 %collective-permute-start.2 = (bf16[3,512,512]{2,1,0:T(8,128)(2,1)}, bf16[3,512,512]{2,1,0:T(8,128)(2,1)}, u32[]{:S(2)}, u32[]{:S(2)}) collective-permute-start(bf16[3,512,512]{2,1,0:T(8,128)(2,1)} %get-tuple-element.75), channel_id=1, source_target_pairs={{0,2},{1,3},{2,0},{3,1},{4,6},{5,7},{6,4},{7,5},{8,10},{9,11},{10,... | collective-permute-start | bytes 4718600 | tf_op jit(solution)/shard_map/ppermute | solution.py:250
  83.6 71.7 %collective-permute-start.7 = (bf16[2,512,1536]{2,1,0:T(8,128)(2,1)S(1)}, bf16[2,512,1536]{2,1,0:T(8,128)(2,1)}, u32[]{:S(2)}, u32[]{:S(2)}) collective-permute-start(bf16[2,512,1536]{2,1,0:T(8,128)(2,1)S(1)} %get-tuple-element.80.refs_4_.refs_5_), channel_id=1, source_target_pairs={{4,8},{8,4},{5,9},{9,5},{6,10},{10,6},{7,11},{11,7},{20,24},{24,20... | collective-permute-start | bytes 9437192 | tf_op jit(solution)/shard_map/ppermute | solution.py:253
  85.7 71.0 %collective-permute-start.8 = (bf16[2,512,1536]{2,1,0:T(8,128)(2,1)}, bf16[2,512,1536]{2,1,0:T(8,128)(2,1)}, u32[]{:S(2)}, u32[]{:S(2)}) collective-permute-start(bf16[2,512,1536]{2,1,0:T(8,128)(2,1)} %get-tuple-element.84), channel_id=1, source_target_pairs={{4,0},{8,12},{5,1},{9,13},{6,2},{10,14},{7,3},{11,15},{20,16},{24,... | collective-permute-start | bytes 9437192 | tf_op jit(solution)/shard_map/ppermute | solution.py:253
  90.9 35.7 %collective-permute-start.6 = (bf16[3,512,512]{2,1,0:T(8,128)(2,1)}, bf16[3,512,512]{2,1,0:T(8,128)(2,1)}, u32[]{:S(2)}, u32[]{:S(2)}) collective-permute-start(bf16[3,512,512]{2,1,0:T(8,128)(2,1)} %get-tuple-element.82.refs_2_), channel_id=1, source_target_pairs={{0,2},{1,3},{2,0},{3,1},{4,6},{5,7},{6,4},{7,5},{8,10},{9,11},{10,... | collective-permute-start | bytes 4718600 | tf_op jit(solution)/shard_map/ppermute | solution.py:250
  103.7 62.3 %collective-permute-start.9 = (bf16[3,512,512]{2,1,0:T(8,128)(2,1)S(1)}, bf16[3,512,512]{2,1,0:T(8,128)(2,1)S(1)}, u32[]{:S(2)}, u32[]{:S(2)}) collective-permute-start(bf16[3,512,512]{2,1,0:T(8,128)(2,1)S(1)} %get-tuple-element.86), channel_id=1, source_target_pairs={{0,2},{1,3},{2,0},{3,1},{4,6},{5,7},{6,4},{7,5},{8,10},{9,11},{10,... | collective-permute-start | bytes 4718600 | tf_op jit(solution)/shard_map/ppermute | solution.py:250
  157.2 105.7 %collective-permute-start.16 = (bf16[2,512,1536]{2,1,0:T(8,128)(2,1)}, bf16[2,512,1536]{2,1,0:T(8,128)(2,1)S(1)}, u32[]{:S(2)}, u32[]{:S(2)}) collective-permute-start(bf16[2,512,1536]{2,1,0:T(8,128)(2,1)} %get-tuple-element.88), channel_id=1, source_target_pairs={{4,0},{8,12},{5,1},{9,13},{6,2},{10,14},{7,3},{11,15},{20,16},{24,... | collective-permute-start | bytes 9437192 | tf_op jit(solution)/shard_map/ppermute | solution.py:253
  184.2 34.8 %collective-permute-start.14 = (bf16[3,512,512]{2,1,0:T(8,128)(2,1)S(1)}, bf16[3,512,512]{2,1,0:T(8,128)(2,1)S(1)}, u32[]{:S(2)}, u32[]{:S(2)}) collective-permute-start(bf16[3,512,512]{2,1,0:T(8,128)(2,1)S(1)} %get-tuple-element.91), channel_id=1, source_target_pairs={{0,2},{1,3},{2,0},{3,1},{4,6},{5,7},{6,4},{7,5},{8,10},{9,11},{10,... | collective-permute-start | bytes 4718600 | tf_op jit(solution)/shard_map/ppermute | solution.py:250
  185.5 76.1 %collective-permute-start.15 = (bf16[3,512,512]{2,1,0:T(8,128)(2,1)S(1)}, bf16[3,512,512]{2,1,0:T(8,128)(2,1)S(1)}, u32[]{:S(2)}, u32[]{:S(2)}) collective-permute-start(bf16[3,512,512]{2,1,0:T(8,128)(2,1)S(1)} %get-tuple-element.93.refs_2_), channel_id=1, source_target_pairs={{0,4},{4,0},{8,12},{12,8},{1,5},{5,1},{9,13},{13,9},{2,6},{6,2},{1... | collective-permute-start | bytes 4718600 | tf_op jit(solution)/shard_map/ppermute | solution.py:253
  268.0 36.1 %collective-permute-start.21 = (bf16[3,512,512]{2,1,0:T(8,128)(2,1)S(1)}, bf16[3,512,512]{2,1,0:T(8,128)(2,1)S(1)}, u32[]{:S(2)}, u32[]{:S(2)}) collective-permute-start(bf16[3,512,512]{2,1,0:T(8,128)(2,1)S(1)} %get-tuple-element.101.refs_2_), channel_id=1, source_target_pairs={{0,2},{1,3},{2,0},{3,1},{4,6},{5,7},{6,4},{7,5},{8,10},{9,11},{10,... | collective-permute-start | bytes 4718600 | tf_op jit(solution)/shard_map/ppermute | solution.py:250
  269.2 68.1 %collective-permute-start.22 = (bf16[3,512,512]{2,1,0:T(8,128)(2,1)}, bf16[3,512,512]{2,1,0:T(8,128)(2,1)}, u32[]{:S(2)}, u32[]{:S(2)}) collective-permute-start(bf16[3,512,512]{2,1,0:T(8,128)(2,1)} %get-tuple-element.105.refs_2_), channel_id=1, source_target_pairs={{0,8},{4,12},{8,0},{12,4},{1,9},{5,13},{9,1},{13,5},{2,10},{6,14},... | collective-permute-start | bytes 4718600 | tf_op jit(solution)/shard_map/ppermute | solution.py:253
  276.1 64.9 %collective-permute-start.23 = (bf16[1,512,512]{2,1,0:T(8,128)(2,1)}, bf16[1,512,512]{2,1,0:T(8,128)(2,1)}, u32[]{:S(2)}, u32[]{:S(2)}) collective-permute-start(bf16[1,512,512]{2,1,0:T(8,128)(2,1)} %get-tuple-element.109), channel_id=1, source_target_pairs={{0,2},{1,3},{2,0},{3,1},{4,6},{5,7},{6,4},{7,5},{8,10},{9,11},{10,... | collective-permute-start | bytes 1572872 | tf_op jit(solution)/shard_map/ppermute | solution.py:250
  281.9 63.9 %collective-permute-start.24 = (bf16[1,512,512]{2,1,0:T(8,128)(2,1)}, bf16[1,512,512]{2,1,0:T(8,128)(2,1)}, u32[]{:S(2)}, u32[]{:S(2)}) collective-permute-start(bf16[1,512,512]{2,1,0:T(8,128)(2,1)} %get-tuple-element.111), channel_id=1, source_target_pairs={{0,2},{1,3},{2,0},{3,1},{4,6},{5,7},{6,4},{7,5},{8,10},{9,11},{10,... | collective-permute-start | bytes 1572872 | tf_op jit(solution)/shard_map/ppermute | solution.py:250
  287.2 63.2 %collective-permute-start.25 = (bf16[1,512,512]{2,1,0:T(8,128)(2,1)}, bf16[1,512,512]{2,1,0:T(8,128)(2,1)}, u32[]{:S(2)}, u32[]{:S(2)}) collective-permute-start(bf16[1,512,512]{2,1,0:T(8,128)(2,1)} %get-tuple-element.113), channel_id=1, source_target_pairs={{0,2},{1,3},{2,0},{3,1},{4,6},{5,7},{6,4},{7,5},{8,10},{9,11},{10,... | collective-permute-start | bytes 1572872 | tf_op jit(solution)/shard_map/ppermute | solution.py:250
  344.9 46.7 %collective-permute-start.26 = (bf16[1,512,512]{2,1,0:T(8,128)(2,1)S(1)}, bf16[1,512,512]{2,1,0:T(8,128)(2,1)S(1)}, u32[]{:S(2)}, u32[]{:S(2)}) collective-permute-start(bf16[1,512,512]{2,1,0:T(8,128)(2,1)S(1)} %get-tuple-element.115.refs_2_), channel_id=1, source_target_pairs={{0,12},{4,8},{8,4},{12,0},{1,13},{5,9},{9,5},{13,1},{2,14},{6,10},... | collective-permute-start | bytes 1572872 | tf_op jit(solution)/shard_map/ppermute | solution.py:253
  349.8 53.1 %collective-permute-start.27 = (bf16[1,512,512]{2,1,0:T(8,128)(2,1)S(1)}, bf16[1,512,512]{2,1,0:T(8,128)(2,1)S(1)}, u32[]{:S(2)}, u32[]{:S(2)}) collective-permute-start(bf16[1,512,512]{2,1,0:T(8,128)(2,1)S(1)} %get-tuple-element.117.refs_2_), channel_id=1, source_target_pairs={{0,12},{4,8},{8,4},{12,0},{1,13},{5,9},{9,5},{13,1},{2,14},{6,10},... | collective-permute-start | bytes 1572872 | tf_op jit(solution)/shard_map/ppermute | solution.py:253
  354.7 59.5 %collective-permute-start.28 = (bf16[1,512,512]{2,1,0:T(8,128)(2,1)S(1)}, bf16[1,512,512]{2,1,0:T(8,128)(2,1)S(1)}, u32[]{:S(2)}, u32[]{:S(2)}) collective-permute-start(bf16[1,512,512]{2,1,0:T(8,128)(2,1)S(1)} %get-tuple-element.119.refs_2_), channel_id=1, source_target_pairs={{0,12},{4,8},{8,4},{12,0},{1,13},{5,9},{9,5},{13,1},{2,14},{6,10},... | collective-permute-start | bytes 1572872 | tf_op jit(solution)/shard_map/ppermute | solution.py:253
  355.6 59.3 %collective-permute-start.29 = (bf16[1,512,512]{2,1,0:T(8,128)(2,1)S(1)}, bf16[1,512,512]{2,1,0:T(8,128)(2,1)S(1)}, u32[]{:S(2)}, u32[]{:S(2)}) collective-permute-start(bf16[1,512,512]{2,1,0:T(8,128)(2,1)S(1)} %get-tuple-element.121.refs_2_), channel_id=1, source_target_pairs={{0,2},{1,3},{2,0},{3,1},{4,6},{5,7},{6,4},{7,5},{8,10},{9,11},{10,... | collective-permute-start | bytes 1572872 | tf_op jit(solution)/shard_map/ppermute | solution.py:250
  392.5 37.2 %collective-permute-start.31 = (bf16[1,512,512]{2,1,0:T(8,128)(2,1)S(1)}, bf16[1,512,512]{2,1,0:T(8,128)(2,1)S(1)}, u32[]{:S(2)}, u32[]{:S(2)}) collective-permute-start(bf16[1,512,512]{2,1,0:T(8,128)(2,1)S(1)} %get-tuple-element.126.refs_2_), channel_id=1, source_target_pairs={{0,2},{1,3},{2,0},{3,1},{4,6},{5,7},{6,4},{7,5},{8,10},{9,11},{10,... | collective-permute-start | bytes 1572872 | tf_op jit(solution)/shard_map/ppermute | solution.py:250
  403.7 26.1 %collective-permute-start.32 = (bf16[1,512,512]{2,1,0:T(8,128)(2,1)S(1)}, bf16[1,512,512]{2,1,0:T(8,128)(2,1)S(1)}, u32[]{:S(2)}, u32[]{:S(2)}) collective-permute-start(bf16[1,512,512]{2,1,0:T(8,128)(2,1)S(1)} %get-tuple-element.127.refs_9_), channel_id=1, source_target_pairs={{0,2},{1,3},{2,0},{3,1},{4,6},{5,7},{6,4},{7,5},{8,10},{9,11},{10,... | collective-permute-start | bytes 1572872 | tf_op jit(solution)/shard_map/ppermute | solution.py:250
  414.1 29.3 %collective-permute-start.33 = (bf16[1,512,512]{2,1,0:T(8,128)(2,1)S(1)}, bf16[1,512,512]{2,1,0:T(8,128)(2,1)S(1)}, u32[]{:S(2)}, u32[]{:S(2)}) collective-permute-start(bf16[1,512,512]{2,1,0:T(8,128)(2,1)S(1)} %get-tuple-element.130.refs_2_), channel_id=1, source_target_pairs={{0,2},{1,3},{2,0},{3,1},{4,6},{5,7},{6,4},{7,5},{8,10},{9,11},{10,... | collective-permute-start | bytes 1572872 | tf_op jit(solution)/shard_map/ppermute | solution.py:250
  414.9 33.6 %collective-permute-start.34 = (bf16[1,512,512]{2,1,0:T(8,128)(2,1)S(1)}, bf16[1,512,512]{2,1,0:T(8,128)(2,1)S(1)}, u32[]{:S(2)}, u32[]{:S(2)}) collective-permute-start(bf16[1,512,512]{2,1,0:T(8,128)(2,1)S(1)} %get-tuple-element.131.refs_9_), channel_id=1, source_target_pairs={{0,2},{1,3},{2,0},{3,1},{4,6},{5,7},{6,4},{7,5},{8,10},{9,11},{10,... | collective-permute-start | bytes 1572872 | tf_op jit(solution)/shard_map/ppermute | solution.py:250
  427.8 35.3 %collective-permute-start.35 = (bf16[1,512,1536]{2,1,0:T(8,128)(2,1)S(1)}, bf16[1,512,1536]{2,1,0:T(8,128)(2,1)S(1)}, u32[]{:S(2)}, u32[]{:S(2)}) collective-permute-start(bf16[1,512,1536]{2,1,0:T(8,128)(2,1)S(1)} %get-tuple-element.134), channel_id=1, source_target_pairs={{0,1},{1,0},{2,3},{3,2},{4,5},{5,4},{6,7},{7,6},{8,9},{9,8},{10,11... | collective-permute-start | bytes 4718600 | tf_op jit(solution)/shard_map/ppermute | solution.py:247
  (43 other events, 774.6 us)

commit v6 on v5

--- a/solution.py
+++ b/solution.py
@@ -12,6 +12,10 @@
 ANY = pl.BlockSpec(memory_space=pl.ANY)
 TOKEN = jax.ShapeDtypeStruct((8, 128), F32)
 TILE = 256
+
+
+def in_hbm(a):
+    return pltpu.with_memory_space_constraint(a, pltpu.HBM)
 
 
 def tile_of(size):
@@ -75,7 +79,7 @@
     (mine, core_part), (block, passed, kept) = b_i, block
     pieces = kept if own_j else passed
     cols, depth = block.shape[1:]
-    half, rows = core_part.shape[:2]
+    half, rows = core_part.shape[0] // 2, core_part.shape[1]
     first, count = (0, half) if which is None else (which, 1)
 
     def j_of(s):
@@ -84,7 +88,7 @@
     one = pl.BlockSpec((1, rows, cols), lambda i, s, *_: (i, 0, 0))
     in_specs = [
         pl.BlockSpec((1, rows, depth), lambda i, s, *_: (s[1] * half + first + i, 0, 0)),
-        pl.BlockSpec((1, rows, depth), lambda i, s, *_: (first + i, 0, 0)),
+        pl.BlockSpec((1, rows, depth), lambda i, s, *_: (s[1] * half + first + i, 0, 0)),
         pl.BlockSpec((1, cols, depth), lambda i, s, *_: (j_of(s), 0, 0)),
     ]
     for p in pieces:
@@ -256,7 +260,7 @@
         return along(values, [(k, k ^ distance) for k in range(4)])
 
     ends, middle = [(1, 0), (2, 3)], [(1, 2), (2, 1)]
-    b_i = b_occ_i, to_core(lax.dynamic_slice_in_dim(b_occ_i, (1 - core) * half, half, 0))
+    b_i = in_hbm(b_occ_i), in_hbm(to_core(b_occ_i))
 
     def pass_on(block, which=None):
         nonlocal token
@@ -283,12 +287,9 @@
         pieces = [to_core(values)]
         return values, pieces, pieces
 
-    def both_in_pieces(values, n_pieces=2):
-        def part(j):
-            one = lax.dynamic_slice_in_dim(values, j, 1, 0)
-            return [to_core(p) for p in jnp.split(one, n_pieces, axis=1)]
-
-        return values, part(1 - x), part(x)
+    def in_pieces(values, own_j, n_pieces=2):
+        one = lax.dynamic_slice_in_dim(values, x if own_j else 1 - x, 1, 0)
+        return [to_core(p) for p in jnp.split(one, n_pieces, axis=1)]
 
     near = swapped(b_occ_j, 1)
     across = along(b_occ_j, middle)
@@ -296,38 +297,43 @@
 
     chip_0 = pass_on(here)
     held_0 = own(here, chip_0, 0)
-    mine_0 = combine(held_0, held_0)
-    other_0 = to_chip(mine_0)
 
     near, across = forward(near, across)
     far_mid = along(near, middle)
     far_end = along(across, ends)
     near = both(near)
+    mine_0 = combine(held_0, held_0)
     chip_1 = pass_on(near)
-    gamma, token = chip_gamma(token, place, [(mine_0, other_0, here)])
-
+
+    held_1 = own(near, chip_1, 1)
+    mirror_1 = swapped(held_1, 1)
     far_mid, far_end = forward(far_mid, far_end)
     last = along(far_mid, ends)
-    far = both_in_pieces(jnp.where(in_middle, far_mid, far_end))
-    held_1 = own(near, chip_1, 1)
-    mirror_1 = swapped(held_1, 1)
+    far = jnp.where(in_middle, far_mid, far_end)
+    far = far, in_pieces(far, False), in_pieces(far, True)
     chip_2 = pass_on(far)
 
     held_2 = own(far, chip_2, 2)
     mirror_2 = swapped(held_2, 2)
+    (mine_0,) = forward(mine_0)
+    other_0 = to_chip(mine_0)
     mine_1 = combine(held_1, mirror_1)
     other_1 = to_chip(mine_1)
 
     (last,) = forward(last)
-    last = both_in_pieces(jnp.where(in_middle, across, last))
-    chip_3 = [pass_on(last, 0)]
-    last = last[:2] + (forward(*last[2]),)
-    chip_3 += [pass_on(last, i) for i in range(1, half)]
-    gamma, token = chip_gamma(token, place, [(mine_1, other_1, near)], gamma)
+    last = jnp.where(in_middle, across, last)
+    passed = in_pieces(last, False)
+    chip_3 = [pass_on((last, passed, None), 0)]
     mine_2 = combine(held_2, mirror_2, split=True)
     other_2 = [to_chip(m) for m in mine_2]
+    (last,) = forward(last)
+    last = last, passed, in_pieces(last, True)
+    chip_3.append(pass_on(last, 1))
+    other_0, other_1 = forward(other_0, other_1)
+    chip_3 += [pass_on(last, i) for i in range(2, half)]
     held_3 = [own(last, chip_3[i], 3, i) for i in range(half)]
     mirror_3 = [swapped(h, 3) for h in held_3]
+    gamma, token = chip_gamma(token, place, [(mine_0, other_0, here), (mine_1, other_1, near)])
     mine_3 = [combine(h, m) for h, m in zip(held_3, mirror_3)]
     other_3 = [to_chip(m) for m in mine_3]
 

time: 471 us -> 512 us (1.087)
  the two profiles are of different devices: /device:TPU:17 before, /device:TPU:1 now
where the time goes in v6:
time: 512 us; the launch traced here: 511 us
  waiting for transfers between devices  270 us (53%)
  Pallas kernels  158 us (31%)
  starting transfers between devices  67.1 us (13%)
  local copies, waits for them, and re-layouts  12.1 us (2%)
    ppermute x14, waiting for transfers between devices, to_chip(): return lax.ppermute(values, 'col', [(q, q ^ 2) for q in range(4)])  160 us
    pallas_call x31, Pallas kernels, call(): pl.pallas_call(body, out_shape=(*out, TOKEN), grid_spec=pltpu.PrefetchSca...  158 us
    ppermute x10, waiting for transfers between devices, along(): return lax.ppermute(values, 'row', steps)  86.1 us
    ppermute x10, starting transfers between devices, along(): return lax.ppermute(values, 'row', steps)  26.6 us
    ppermute x14, starting transfers between devices, to_core(): return lax.ppermute(values, 'col', [(q, q ^ 1) for q in range(4)])  25.6 us
    ppermute x14, waiting for transfers between devices, to_core(): return lax.ppermute(values, 'col', [(q, q ^ 1) for q in range(4)])  23.3 us
    ppermute x14, starting transfers between devices, to_chip(): return lax.ppermute(values, 'col', [(q, q ^ 2) for q in range(4)])  15 us
    unnamed x42, local copies, waits for them, and re-layouts  10.8 us
  transfers between devices with their start and end apart: 38, of which 19 were waited for; matrix products, arithmetic and copies ran while one was open for 1% of the time, Pallas kernels for 30%

profile of v6, /device:TPU:1, one launch (start us, length us, event | category | flops | bytes accessed | tf_op | source)
XLA Modules:
  0.0 511.3 jit_solution(16141625521384737489)
XLA Ops:
  5.2 14.3 %collective-permute-done.1.refs_5_.refs_6_ = bf16[2,512,1536]{2,1,0:T(8,128)(2,1)} collective-permute-done((bf16[2,512,1536]{2,1,0:T(8,128)(2,1)}, bf16[2,512,1536]{2,1,0:T(8,128)(2,1)}, u32[]{:S(2)}, u32[]{:S(2)}) %collective-permute-start.1) | collective-permute-done | bytes 3145760 | tf_op jit(solution)/shard_map/ppermute | solution.py:251
  21.4 9.4 %pairs_for_chip.6 = (bf16[3,512,512]{2,1,0:T(8,128)(2,1)}, f32[8,128]{1,0:T(8,128)S(1)}) custom-call(s32[2]{0:T(128)S(1)} %pad_add_fusion.refs_0_, f32[8,128]{1,0:T(8,128)S(1)} %broadcast_in_dim.20.refs_1_, bf16[6,512,1536]{2,1,0:T(8,128)(2,1)} %refs_3_.11, bf16[6,512,1536]{2,1,0:T(8,128)(2,1)} %collective-permute-done.refs_3_.refs_4_, ...), custom_call_target="tpu_custom_call" | custom-call | bytes 1024 | tf_op jit(solution)/shard_map/pairs_for_chip/pallas_call | solution.py:31
  34.8 33.1 %collective-permute-done.2.refs_7_ = bf16[3,512,512]{2,1,0:T(8,128)(2,1)} collective-permute-done((bf16[3,512,512]{2,1,0:T(8,128)(2,1)}, bf16[3,512,512]{2,1,0:T(8,128)(2,1)}, u32[]{:S(2)}, u32[]{:S(2)}) %collective-permute-start.2) | collective-permute-done | bytes 1572896 | tf_op jit(solution)/shard_map/ppermute | solution.py:254
  69.9 9.3 %own_amplitudes.6 = (bf16[3,512,512]{2,1,0:T(8,128)(2,1)S(1)}, f32[8,128]{1,0:T(8,128)S(1)}) custom-call(s32[2]{0:T(128)S(1)} %pad_add_fusion.refs_0_, f32[3]{0:T(128)S(1)} %dynamic-slice_add_fusion.refs_1_, f32[8,128]{1,0:T(8,128)S(1)} %get-tuple-element.75.refs_2_, bf16[6,512,1536]{2,1,0:T(8,128)(2,1)} %refs_3_.11, ...), custom_call_target="tpu_custom_call" | custom-call | bytes 1024 | tf_op jit(solution)/shard_map/own_amplitudes/pallas_call | solution.py:31
  86.7 9.5 %pairs_for_chip.7 = (bf16[3,512,512]{2,1,0:T(8,128)(2,1)}, f32[8,128]{1,0:T(8,128)S(1)}) custom-call(s32[2]{0:T(128)S(1)} %pad_add_fusion.refs_0_, f32[8,128]{1,0:T(8,128)S(1)} %get-tuple-element.80.refs_1_, bf16[6,512,1536]{2,1,0:T(8,128)(2,1)} %refs_3_.11, bf16[6,512,1536]{2,1,0:T(8,128)(2,1)} %collective-permute-done.refs_3_.refs_4_, ...), custom_call_target="tpu_custom_call" | custom-call | bytes 1024 | tf_op jit(solution)/shard_map/pairs_for_chip/pallas_call | solution.py:31
  97.7 34.9 %collective-permute-done.6.refs_7_ = bf16[3,512,512]{2,1,0:T(8,128)(2,1)} collective-permute-done((bf16[3,512,512]{2,1,0:T(8,128)(2,1)}, bf16[3,512,512]{2,1,0:T(8,128)(2,1)}, u32[]{:S(2)}, u32[]{:S(2)}) %collective-permute-start.6) | collective-permute-done | bytes 1572896 | tf_op jit(solution)/shard_map/ppermute | solution.py:254
  134.4 8.3 %own_amplitudes.7 = (bf16[3,512,512]{2,1,0:T(8,128)(2,1)S(1)}, f32[8,128]{1,0:T(8,128)S(1)}) custom-call(s32[2]{0:T(128)S(1)} %pad_add_fusion.refs_0_, f32[3]{0:T(128)S(1)} %dynamic-slice_add_fusion.refs_1_, f32[8,128]{1,0:T(8,128)S(1)} %get-tuple-element.82.refs_2_, bf16[6,512,1536]{2,1,0:T(8,128)(2,1)} %refs_3_.11, ...), custom_call_target="tpu_custom_call" | custom-call | bytes 1024 | tf_op jit(solution)/shard_map/own_amplitudes/pallas_call | solution.py:31
  142.7 12.5 %collective-permute-done.8.refs_3_ = bf16[2,512,1536]{2,1,0:T(8,128)(2,1)} collective-permute-done((bf16[2,512,1536]{2,1,0:T(8,128)(2,1)}, bf16[2,512,1536]{2,1,0:T(8,128)(2,1)}, u32[]{:S(2)}, u32[]{:S(2)}) %collective-permute-start.8) | collective-permute-done | bytes 3145760 | tf_op jit(solution)/shard_map/ppermute | solution.py:257
  163.5 8.2 %pairs_for_chip.8 = (bf16[3,512,512]{2,1,0:T(8,128)(2,1)S(1)}, f32[8,128]{1,0:T(8,128)S(1)}) custom-call(s32[2]{0:T(128)S(1)} %pad_add_fusion.refs_0_, f32[8,128]{1,0:T(8,128)S(1)} %get-tuple-element.86.refs_1_, bf16[6,512,1536]{2,1,0:T(8,128)(2,1)} %refs_3_.11, bf16[6,512,1536]{2,1,0:T(8,128)(2,1)} %collective-permute-done.refs_3_.refs_4_, ...), custom_call_target="tpu_custom_call" | custom-call | bytes 1024 | tf_op jit(solution)/shard_map/pairs_for_chip/pallas_call | solution.py:31
  179.5 27.9 %collective-permute-done.13.refs_8_ = bf16[3,512,512]{2,1,0:T(8,128)(2,1)S(1)} collective-permute-done((bf16[3,512,512]{2,1,0:T(8,128)(2,1)S(1)}, bf16[3,512,512]{2,1,0:T(8,128)(2,1)S(1)}, u32[]{:S(2)}, u32[]{:S(2)}) %collective-permute-start.13) | collective-permute-done | bytes 1572896 | tf_op jit(solution)/shard_map/ppermute | solution.py:254
  207.3 8.1 %own_amplitudes.8 = (bf16[3,512,512]{2,1,0:T(8,128)(2,1)S(1)}, f32[8,128]{1,0:T(8,128)S(1)}) custom-call(s32[2]{0:T(128)S(1)} %pad_add_fusion.refs_0_, f32[3]{0:T(128)S(1)} %dynamic-slice_add_fusion.refs_1_, f32[8,128]{1,0:T(8,128)S(1)} %get-tuple-element.89.refs_2_, bf16[6,512,1536]{2,1,0:T(8,128)(2,1)} %refs_3_.11, ...), custom_call_target="tpu_custom_call" | custom-call | bytes 1024 | tf_op jit(solution)/shard_map/own_amplitudes/pallas_call | solution.py:31
  215.4 4.7 collective-permute-start.18
  220.6 73.5 %collective-permute-done.14.refs_3_ = bf16[3,512,512]{2,1,0:T(8,128)(2,1)S(1)} collective-permute-done((bf16[3,512,512]{2,1,0:T(8,128)(2,1)S(1)}, bf16[3,512,512]{2,1,0:T(8,128)(2,1)S(1)}, u32[]{:S(2)}, u32[]{:S(2)}) %collective-permute-start.14) | collective-permute-done | bytes 1572896 | tf_op jit(solution)/shard_map/ppermute | solution.py:257
  316.6 13.0 %collective-permute-done.20.refs_3_ = bf16[3,512,512]{2,1,0:T(8,128)(2,1)S(1)} collective-permute-done((bf16[3,512,512]{2,1,0:T(8,128)(2,1)S(1)}, bf16[3,512,512]{2,1,0:T(8,128)(2,1)S(1)}, u32[]{:S(2)}, u32[]{:S(2)}) %collective-permute-start.20) | collective-permute-done | bytes 1572896 | tf_op jit(solution)/shard_map/ppermute | solution.py:254
  330.9 32.5 %collective-permute-done.19.refs_2_ = bf16[3,512,512]{2,1,0:T(8,128)(2,1)S(1)} collective-permute-done((bf16[3,512,512]{2,1,0:T(8,128)(2,1)S(1)}, bf16[3,512,512]{2,1,0:T(8,128)(2,1)S(1)}, u32[]{:S(2)}, u32[]{:S(2)}) %collective-permute-start.19) | collective-permute-done | bytes 1572896 | tf_op jit(solution)/shard_map/ppermute | solution.py:254
  369.4 5.2 %collective-permute-done.23.refs_8_ = bf16[1,512,512]{2,1,0:T(8,128)(2,1)S(1)} collective-permute-done((bf16[1,512,512]{2,1,0:T(8,128)(2,1)S(1)}, bf16[1,512,512]{2,1,0:T(8,128)(2,1)S(1)}, u32[]{:S(2)}, u32[]{:S(2)}) %collective-permute-start.23) | collective-permute-done | bytes 524320 | tf_op jit(solution)/shard_map/ppermute | solution.py:254
  374.6 4.3 own_amplitudes.9
  397.1 4.5 own_amplitudes.11
  406.1 25.4 %chip_gamma.1 = (f32[3,512,1536]{2,1,0:T(8,128)}, f32[3,512,1536]{2,1,0:T(8,128)}, f32[8,128]{1,0:T(8,128)S(1)}) custom-call(s32[2]{0:T(128)S(1)} %pad_add_fusion.refs_0_, f32[8,128]{1,0:T(8,128)S(1)} %get-tuple-element.113.refs_1_, bf16[3,512,512]{2,1,0:T(8,128)(2,1)S(1)} %get-tuple-element.104.refs_2_, ...), custom_call_target="tpu_custom_call" | custom-call | bytes 1024 | tf_op jit(solution)/shard_map/chip_gamma/pallas_call | solution.py:31
  447.7 11.4 %last_gamma.3 = (f32[6,512,1536]{2,1,0:T(8,128)}, bf16[1,512,1536]{2,1,0:T(8,128)(2,1)S(1)}, f32[8,128]{1,0:T(8,128)S(1)}) custom-call(s32[2]{0:T(128)S(1)} %pad_add_fusion.refs_0_, f32[8,128]{1,0:T(8,128)S(1)} %get-tuple-element.122.refs_1_, bf16[1,512,512]{2,1,0:T(8,128)(2,1)} %get-tuple-element.123.refs_2_, ...), custom_call_target="tpu_custom_call" | custom-call | bytes 1024 | tf_op jit(solution)/shard_map/last_gamma/pallas_call | solution.py:31
  459.1 7.8 %collective-permute-start.35 = (bf16[1,512,1536]{2,1,0:T(8,128)(2,1)S(1)}, bf16[1,512,1536]{2,1,0:T(8,128)(2,1)S(1)}, u32[]{:S(2)}, u32[]{:S(2)}) collective-permute-start(bf16[1,512,1536]{2,1,0:T(8,128)(2,1)S(1)} %get-tuple-element.136), channel_id=1, source_target_pairs={{0,1},{1,0},{2,3},{3,2},{4,5},{5,4},{6,7},{7,6},{8,9},{9,8},{10,11... | collective-permute-start | bytes 4718600 | tf_op jit(solution)/shard_map/ppermute | solution.py:251
  466.9 11.3 %last_gamma.4 = (f32[6,512,1536]{2,1,0:T(8,128)}, bf16[1,512,1536]{2,1,0:T(8,128)(2,1)S(1)}, f32[8,128]{1,0:T(8,128)S(1)}) custom-call(s32[2]{0:T(128)S(1)} %pad_add_fusion.refs_0_, f32[8,128]{1,0:T(8,128)S(1)} %get-tuple-element.127.refs_1_, bf16[1,512,512]{2,1,0:T(8,128)(2,1)S(1)} %copy-done.17, ...), custom_call_target="tpu_custom_call", output_to_operand_aliasing={{0}: (18, {})} | custom-call | bytes 1024 | tf_op jit(solution)/shard_map/last_gamma/pallas_call | solution.py:31
  478.2 7.4 %collective-permute-start.36 = (bf16[1,512,1536]{2,1,0:T(8,128)(2,1)S(1)}, bf16[1,512,1536]{2,1,0:T(8,128)(2,1)S(1)}, u32[]{:S(2)}, u32[]{:S(2)}) collective-permute-start(bf16[1,512,1536]{2,1,0:T(8,128)(2,1)S(1)} %get-tuple-element.139), channel_id=1, source_target_pairs={{0,1},{1,0},{2,3},{3,2},{4,5},{5,4},{6,7},{7,6},{8,9},{9,8},{10,11... | collective-permute-start | bytes 4718600 | tf_op jit(solution)/shard_map/ppermute | solution.py:251
  488.9 11.3 %last_gamma.5 = (f32[6,512,1536]{2,1,0:T(8,128)}, bf16[1,512,1536]{2,1,0:T(8,128)(2,1)S(1)}, f32[8,128]{1,0:T(8,128)S(1)}) custom-call(s32[2]{0:T(128)S(1)} %pad_add_fusion.refs_0_, f32[8,128]{1,0:T(8,128)S(1)} %get-tuple-element.131.refs_1_, bf16[1,512,512]{2,1,0:T(8,128)(2,1)S(1)} %get-tuple-element.132.refs_2_, ...), custom_call_target="tpu_custom_call", output_to_operand_aliasing={{0}: (18, {})} | custom-call | bytes 1024 | tf_op jit(solution)/shard_map/last_gamma/pallas_call | solution.py:31
  (136 shorter events, 123.2 us)
Async XLA Ops:
  0.5 78.6 %collective-permute-start.3 = (bf16[2,512,1536]{2,1,0:T(8,128)(2,1)}, bf16[2,512,1536]{2,1,0:T(8,128)(2,1)S(1)}, u32[]{:S(2)}, u32[]{:S(2)}) collective-permute-start(bf16[2,512,1536]{2,1,0:T(8,128)(2,1)} %refs_4_.3), channel_id=1, source_target_pairs={{0,4},{4,0},{8,12},{12,8},{1,5},{5,1},{9,13},{13,9},{2,6},{6,2},{1... | collective-permute-start | bytes 9437192 | tf_op jit(solution)/shard_map/ppermute | solution.py:257
  2.8 76.3 %collective-permute-start.4 = (bf16[2,512,1536]{2,1,0:T(8,128)(2,1)}, bf16[2,512,1536]{2,1,0:T(8,128)(2,1)}, u32[]{:S(2)}, u32[]{:S(2)}) collective-permute-start(bf16[2,512,1536]{2,1,0:T(8,128)(2,1)} %refs_4_.3), channel_id=1, source_target_pairs={{4,8},{8,4},{5,9},{9,5},{6,10},{10,6},{7,11},{11,7},{20,24},{24,20... | collective-permute-start | bytes 9437192 | tf_op jit(solution)/shard_map/ppermute | solution.py:257
  30.8 37.1 %collective-permute-start.2 = (bf16[3,512,512]{2,1,0:T(8,128)(2,1)}, bf16[3,512,512]{2,1,0:T(8,128)(2,1)}, u32[]{:S(2)}, u32[]{:S(2)}) collective-permute-start(bf16[3,512,512]{2,1,0:T(8,128)(2,1)} %get-tuple-element.76), channel_id=1, source_target_pairs={{0,2},{1,3},{2,0},{3,1},{4,6},{5,7},{6,4},{7,5},{8,10},{9,11},{10,... | collective-permute-start | bytes 4718600 | tf_op jit(solution)/shard_map/ppermute | solution.py:254
  80.7 62.0 %collective-permute-start.7 = (bf16[2,512,1536]{2,1,0:T(8,128)(2,1)S(1)}, bf16[2,512,1536]{2,1,0:T(8,128)(2,1)}, u32[]{:S(2)}, u32[]{:S(2)}) collective-permute-start(bf16[2,512,1536]{2,1,0:T(8,128)(2,1)S(1)} %get-tuple-element.81.refs_4_.refs_5_.refs_8_), channel_id=1, source_target_pairs={{4,8},{8,4},{5,9},{9,5},{6,10},{10,6},{7,11},{11,7},{20,24},{24,20... | collective-permute-start | bytes 9437192 | tf_op jit(solution)/shard_map/ppermute | solution.py:257
  83.0 72.3 %collective-permute-start.8 = (bf16[2,512,1536]{2,1,0:T(8,128)(2,1)}, bf16[2,512,1536]{2,1,0:T(8,128)(2,1)}, u32[]{:S(2)}, u32[]{:S(2)}) collective-permute-start(bf16[2,512,1536]{2,1,0:T(8,128)(2,1)} %get-tuple-element.85), channel_id=1, source_target_pairs={{4,0},{8,12},{5,1},{9,13},{6,2},{10,14},{7,3},{11,15},{20,16},{24,... | collective-permute-start | bytes 9437192 | tf_op jit(solution)/shard_map/ppermute | solution.py:257
  96.2 36.3 %collective-permute-start.6 = (bf16[3,512,512]{2,1,0:T(8,128)(2,1)}, bf16[3,512,512]{2,1,0:T(8,128)(2,1)}, u32[]{:S(2)}, u32[]{:S(2)}) collective-permute-start(bf16[3,512,512]{2,1,0:T(8,128)(2,1)} %get-tuple-element.83), channel_id=1, source_target_pairs={{0,2},{1,3},{2,0},{3,1},{4,6},{5,7},{6,4},{7,5},{8,10},{9,11},{10,... | collective-permute-start | bytes 4718600 | tf_op jit(solution)/shard_map/ppermute | solution.py:254
  155.8 141.1 %collective-permute-start.15 = (bf16[2,512,1536]{2,1,0:T(8,128)(2,1)}, bf16[2,512,1536]{2,1,0:T(8,128)(2,1)S(1)}, u32[]{:S(2)}, u32[]{:S(2)}) collective-permute-start(bf16[2,512,1536]{2,1,0:T(8,128)(2,1)} %get-tuple-element.87), channel_id=1, source_target_pairs={{4,0},{8,12},{5,1},{9,13},{6,2},{10,14},{7,3},{11,15},{20,16},{24,... | collective-permute-start | bytes 9437192 | tf_op jit(solution)/shard_map/ppermute | solution.py:257
  171.6 35.7 %collective-permute-start.13 = (bf16[3,512,512]{2,1,0:T(8,128)(2,1)S(1)}, bf16[3,512,512]{2,1,0:T(8,128)(2,1)S(1)}, u32[]{:S(2)}, u32[]{:S(2)}) collective-permute-start(bf16[3,512,512]{2,1,0:T(8,128)(2,1)S(1)} %get-tuple-element.90), channel_id=1, source_target_pairs={{0,2},{1,3},{2,0},{3,1},{4,6},{5,7},{6,4},{7,5},{8,10},{9,11},{10,... | collective-permute-start | bytes 4718600 | tf_op jit(solution)/shard_map/ppermute | solution.py:254
  172.9 121.2 %collective-permute-start.14 = (bf16[3,512,512]{2,1,0:T(8,128)(2,1)S(1)}, bf16[3,512,512]{2,1,0:T(8,128)(2,1)S(1)}, u32[]{:S(2)}, u32[]{:S(2)}) collective-permute-start(bf16[3,512,512]{2,1,0:T(8,128)(2,1)S(1)} %get-tuple-element.94.refs_2_), channel_id=1, source_target_pairs={{0,4},{4,0},{8,12},{12,8},{1,5},{5,1},{9,13},{13,9},{2,6},{6,2},{1... | collective-permute-start | bytes 4718600 | tf_op jit(solution)/shard_map/ppermute | solution.py:257
  215.4 92.1 %collective-permute-start.18 = (bf16[3,512,512]{2,1,0:T(8,128)(2,1)S(1)}, bf16[3,512,512]{2,1,0:T(8,128)(2,1)S(1)}, u32[]{:S(2)}, u32[]{:S(2)}) collective-permute-start(bf16[3,512,512]{2,1,0:T(8,128)(2,1)S(1)} %get-tuple-element.99.refs_2_), channel_id=1, source_target_pairs={{0,8},{4,12},{8,0},{12,4},{1,9},{5,13},{9,1},{13,5},{2,10},{6,14},... | collective-permute-start | bytes 4718600 | tf_op jit(solution)/shard_map/ppermute | solution.py:257
  295.4 34.3 %collective-permute-start.20 = (bf16[3,512,512]{2,1,0:T(8,128)(2,1)S(1)}, bf16[3,512,512]{2,1,0:T(8,128)(2,1)S(1)}, u32[]{:S(2)}, u32[]{:S(2)}) collective-permute-start(bf16[3,512,512]{2,1,0:T(8,128)(2,1)S(1)} %get-tuple-element.105.refs_6_), channel_id=1, source_target_pairs={{0,2},{1,3},{2,0},{3,1},{4,6},{5,7},{6,4},{7,5},{8,10},{9,11},{10,... | collective-permute-start | bytes 4718600 | tf_op jit(solution)/shard_map/ppermute | solution.py:254
  296.7 66.7 %collective-permute-start.19 = (bf16[3,512,512]{2,1,0:T(8,128)(2,1)S(1)}, bf16[3,512,512]{2,1,0:T(8,128)(2,1)S(1)}, u32[]{:S(2)}, u32[]{:S(2)}) collective-permute-start(bf16[3,512,512]{2,1,0:T(8,128)(2,1)S(1)} %get-tuple-element.104.refs_2_), channel_id=1, source_target_pairs={{0,2},{1,3},{2,0},{3,1},{4,6},{5,7},{6,4},{7,5},{8,10},{9,11},{10,... | collective-permute-start | bytes 4718600 | tf_op jit(solution)/shard_map/ppermute | solution.py:254
  310.6 64.0 %collective-permute-start.21 = (bf16[1,256,1536]{2,1,0:T(8,128)(2,1)S(1)}, bf16[1,256,1536]{2,1,0:T(8,128)(2,1)S(1)}, u32[]{:S(2)}, u32[]{:S(2)}) collective-permute-start(bf16[1,256,1536]{2,1,0:T(8,128)(2,1)S(1)} %get-tuple-element.146), channel_id=1, source_target_pairs={{0,1},{1,0},{2,3},{3,2},{4,5},{5,4},{6,7},{7,6},{8,9},{9,8},{10,11... | collective-permute-start | bytes 2359304 | tf_op jit(solution)/shard_map/ppermute | solution.py:251
  311.0 63.6 %collective-permute-start.22 = (bf16[1,256,1536]{2,1,0:T(8,128)(2,1)S(1)}, bf16[1,256,1536]{2,1,0:T(8,128)(2,1)S(1)}, u32[]{:S(2)}, u32[]{:S(2)}) collective-permute-start(bf16[1,256,1536]{2,1,0:T(8,128)(2,1)S(1)} %get-tuple-element.145), channel_id=1, source_target_pairs={{0,1},{1,0},{2,3},{3,2},{4,5},{5,4},{6,7},{7,6},{8,9},{9,8},{10,11... | collective-permute-start | bytes 2359304 | tf_op jit(solution)/shard_map/ppermute | solution.py:251
  311.1 63.4 %collective-permute-start.23 = (bf16[1,512,512]{2,1,0:T(8,128)(2,1)S(1)}, bf16[1,512,512]{2,1,0:T(8,128)(2,1)S(1)}, u32[]{:S(2)}, u32[]{:S(2)}) collective-permute-start(bf16[1,512,512]{2,1,0:T(8,128)(2,1)S(1)} %get-tuple-element.108), channel_id=1, source_target_pairs={{0,2},{1,3},{2,0},{3,1},{4,6},{5,7},{6,4},{7,5},{8,10},{9,11},{10,... | collective-permute-start | bytes 1572872 | tf_op jit(solution)/shard_map/ppermute | solution.py:254
  329.7 56.2 %collective-permute-start.24 = (bf16[1,512,512]{2,1,0:T(8,128)(2,1)S(1)}, bf16[1,512,512]{2,1,0:T(8,128)(2,1)S(1)}, u32[]{:S(2)}, u32[]{:S(2)}) collective-permute-start(bf16[1,512,512]{2,1,0:T(8,128)(2,1)S(1)} %get-tuple-element.110), channel_id=1, source_target_pairs={{0,2},{1,3},{2,0},{3,1},{4,6},{5,7},{6,4},{7,5},{8,10},{9,11},{10,... | collective-permute-start | bytes 1572872 | tf_op jit(solution)/shard_map/ppermute | solution.py:254
  378.9 52.7 %collective-permute-start.26 = (bf16[1,512,512]{2,1,0:T(8,128)(2,1)S(1)}, bf16[1,512,512]{2,1,0:T(8,128)(2,1)}, u32[]{:S(2)}, u32[]{:S(2)}) collective-permute-start(bf16[1,512,512]{2,1,0:T(8,128)(2,1)S(1)} %get-tuple-element.117.refs_2_), channel_id=1, source_target_pairs={{0,12},{4,8},{8,4},{12,0},{1,13},{5,9},{9,5},{13,1},{2,14},{6,10},... | collective-permute-start | bytes 1572872 | tf_op jit(solution)/shard_map/ppermute | solution.py:257
  390.1 45.1 %collective-permute-start.27 = (bf16[1,512,512]{2,1,0:T(8,128)(2,1)S(1)}, bf16[1,512,512]{2,1,0:T(8,128)(2,1)}, u32[]{:S(2)}, u32[]{:S(2)}) collective-permute-start(bf16[1,512,512]{2,1,0:T(8,128)(2,1)S(1)} %get-tuple-element.119.refs_2_), channel_id=1, source_target_pairs={{0,12},{4,8},{8,4},{12,0},{1,13},{5,9},{9,5},{13,1},{2,14},{6,10},... | collective-permute-start | bytes 1572872 | tf_op jit(solution)/shard_map/ppermute | solution.py:257
  401.6 35.7 %collective-permute-start.28 = (bf16[1,512,512]{2,1,0:T(8,128)(2,1)S(1)}, bf16[1,512,512]{2,1,0:T(8,128)(2,1)}, u32[]{:S(2)}, u32[]{:S(2)}) collective-permute-start(bf16[1,512,512]{2,1,0:T(8,128)(2,1)S(1)} %get-tuple-element.121.refs_2_), channel_id=1, source_target_pairs={{0,12},{4,8},{8,4},{12,0},{1,13},{5,9},{9,5},{13,1},{2,14},{6,10},... | collective-permute-start | bytes 1572872 | tf_op jit(solution)/shard_map/ppermute | solution.py:257
  404.9 35.5 %collective-permute-start.29 = (bf16[1,512,512]{2,1,0:T(8,128)(2,1)}, bf16[1,512,512]{2,1,0:T(8,128)(2,1)S(1)}, u32[]{:S(2)}, u32[]{:S(2)}) collective-permute-start(bf16[1,512,512]{2,1,0:T(8,128)(2,1)} %get-tuple-element.123.refs_2_), channel_id=1, source_target_pairs={{0,2},{1,3},{2,0},{3,1},{4,6},{5,7},{6,4},{7,5},{8,10},{9,11},{10,... | collective-permute-start | bytes 1572872 | tf_op jit(solution)/shard_map/ppermute | solution.py:254
  434.0 32.9 %collective-permute-start.31 = (bf16[1,512,512]{2,1,0:T(8,128)(2,1)S(1)}, bf16[1,512,512]{2,1,0:T(8,128)(2,1)S(1)}, u32[]{:S(2)}, u32[]{:S(2)}) collective-permute-start(bf16[1,512,512]{2,1,0:T(8,128)(2,1)S(1)} %copy-done.17), channel_id=1, source_target_pairs={{0,2},{1,3},{2,0},{3,1},{4,6},{5,7},{6,4},{7,5},{8,10},{9,11},{10,... | collective-permute-start | bytes 1572872 | tf_op jit(solution)/shard_map/ppermute | solution.py:254
  437.4 48.2 %collective-permute-start.33 = (bf16[1,512,512]{2,1,0:T(8,128)(2,1)S(1)}, bf16[1,512,512]{2,1,0:T(8,128)(2,1)S(1)}, u32[]{:S(2)}, u32[]{:S(2)}) collective-permute-start(bf16[1,512,512]{2,1,0:T(8,128)(2,1)S(1)} %get-tuple-element.132.refs_2_), channel_id=1, source_target_pairs={{0,2},{1,3},{2,0},{3,1},{4,6},{5,7},{6,4},{7,5},{8,10},{9,11},{10,... | collective-permute-start | bytes 1572872 | tf_op jit(solution)/shard_map/ppermute | solution.py:254
  440.4 48.5 %collective-permute-start.34 = (bf16[1,512,512]{2,1,0:T(8,128)(2,1)S(1)}, bf16[1,512,512]{2,1,0:T(8,128)(2,1)S(1)}, u32[]{:S(2)}, u32[]{:S(2)}) collective-permute-start(bf16[1,512,512]{2,1,0:T(8,128)(2,1)S(1)} %get-tuple-element.133.refs_9_), channel_id=1, source_target_pairs={{0,2},{1,3},{2,0},{3,1},{4,6},{5,7},{6,4},{7,5},{8,10},{9,11},{10,... | collective-permute-start | bytes 1572872 | tf_op jit(solution)/shard_map/ppermute | solution.py:254
  459.1 45.2 %collective-permute-start.35 = (bf16[1,512,1536]{2,1,0:T(8,128)(2,1)S(1)}, bf16[1,512,1536]{2,1,0:T(8,128)(2,1)S(1)}, u32[]{:S(2)}, u32[]{:S(2)}) collective-permute-start(bf16[1,512,1536]{2,1,0:T(8,128)(2,1)S(1)} %get-tuple-element.136), channel_id=1, source_target_pairs={{0,1},{1,0},{2,3},{3,2},{4,5},{5,4},{6,7},{7,6},{8,9},{9,8},{10,11... | collective-permute-start | bytes 4718600 | tf_op jit(solution)/shard_map/ppermute | solution.py:251
  (35 other events, 418.5 us)

commit v7 on v6

--- a/solution.py
+++ b/solution.py
@@ -231,120 +231,146 @@
     )
 
 
+ENDS, MIDDLE = [(1, 0), (2, 3)], [(1, 2), (2, 1)]
+ORDER = (
+    "chip_0", "hop_1", "own_0", "combine_0", "chip_1", "gamma_0", "hop_2", "own_1", "chip_2", "own_2", "hop_3",
+    "keep_3", "chip_3_0", "chip_3_1", "chip_3_2", "own_3_0", "combine_1", "own_3_1", "own_3_2", "combine_2",
+    "combine_3_0", "gamma_1", "combine_3_1", "last_0", "last_1", "combine_3_2", "last_2", "place_0", "place_1",
+    "place_2",
+)
+PIECES_2, PIECES_3, HALVES, SPLIT_1, SPLIT_2 = 1, 4, 1, False, False
+
+
+class Chain:
+    def __init__(self, b_occ_i, b_occ_j, eps_occ_i, eps_occ_j, eps_vir):
+        self.shape = b_occ_i.shape
+        self.half, self.rows = self.shape[0] // 2, self.shape[1]
+        self.z, col = lax.axis_index("row"), lax.axis_index("col")
+        self.x, core = col // 2, col % 2
+        self.in_middle = (self.z == 1) | (self.z == 2)
+        self.place = (jnp.stack([self.x, core]).astype(jnp.int32),)
+        self.occ = lax.dynamic_slice_in_dim(eps_occ_i, core * self.half, self.half, 0) + eps_occ_j[self.x]
+        self.eps_vir = eps_vir
+        self.token = jnp.zeros(TOKEN.shape, F32)
+        self.b_i = in_hbm(b_occ_i), in_hbm(self.to_core(b_occ_i))
+        here = [self.to_core(b_occ_j)]
+        self.block = {0: (b_occ_j, here, here)}
+        self.near, self.across = self.swapped(b_occ_j, 1), self.along(b_occ_j, MIDDLE)
+        self.chip, self.held, self.mirror, self.mine, self.other = {}, {}, {}, {}, {}
+        self.gamma, self.result, self.received = None, None, {}
+
+    def to_core(self, values):
+        return lax.ppermute(values, "col", [(q, q ^ 1) for q in range(4)])
+
+    def to_chip(self, values):
+        return lax.ppermute(values, "col", [(q, q ^ 2) for q in range(4)])
+
+    def along(self, values, steps):
+        return lax.ppermute(values, "row", steps)
+
+    def swapped(self, values, distance):
+        return self.along(values, [(k, k ^ distance) for k in range(4)])
+
+    def in_pieces(self, values, own_j, n_pieces):
+        one = lax.dynamic_slice_in_dim(values, self.x if own_j else 1 - self.x, 1, 0)
+        return [self.to_core(p) for p in jnp.split(one, n_pieces, axis=1)]
+
+    def energies(self, distance):
+        return lax.dynamic_slice_in_dim(self.eps_vir, (self.z ^ distance) * self.rows, self.rows, 0)
+
+    def forward(self, *values):
+        *out, self.token = tie(self.token, self.place, *values)
+        return out
+
+    def pass_on(self, k, which=None):
+        out, self.token = pairs(self.token, self.place, self.b_i, self.block[k], False, which)
+        self.chip[k, which] = self.to_chip(out)
+
+    def own(self, k, which=None):
+        last = self.chip[k, which], self.occ, self.energies(0)[:, None], self.energies(k)[None, :]
+        out, self.token = pairs(self.token, self.place, self.b_i, self.block[k], True, which, last)
+        self.held[k, which] = out
+        self.mirror[k, which] = out if k == 0 else self.swapped(out, k)
+
+    def combine(self, k, which=None, split=False, send=True):
+        out, self.token = combine_pairs(self.token, self.place, self.held[k, which], self.mirror[k, which], split)
+        outs = out if split else [out]
+        keys = [(k, i) for i in range(self.half)] if split else [(k, which)]
+        for key, o in zip(keys, outs):
+            self.mine[key] = o
+            if send:
+                self.other[key] = self.to_chip(o)
+
+    def send(self, k):
+        (self.mine[k, None],) = self.forward(self.mine[k, None])
+        self.other[k, None] = self.to_chip(self.mine[k, None])
+
+    def receive(self, k):
+        (self.other[k, None],) = self.forward(self.other[k, None])
+
+    def terms(self, *keys):
+        return [(self.mine[key], self.other[key], self.block[key[0]]) for key in keys]
+
+    def add(self, *keys):
+        self.gamma, self.token = chip_gamma(self.token, self.place, self.terms(*keys), self.gamma)
+
+    def hop_1(self):
+        self.near, self.across = self.forward(self.near, self.across)
+        self.far_mid, self.far_end = self.along(self.near, MIDDLE), self.along(self.across, ENDS)
+        near = [self.to_core(self.near)]
+        self.block[1] = self.near, near, near
+
+    def hop_2(self):
+        self.far_mid, self.far_end = self.forward(self.far_mid, self.far_end)
+        self.last = [self.along(p, ENDS) for p in jnp.split(self.far_mid, HALVES, axis=1)]
+        far = jnp.where(self.in_middle, self.far_mid, self.far_end)
+        self.block[2] = far, self.in_pieces(far, False, PIECES_2), self.in_pieces(far, True, PIECES_2)
+
+    def hop_3(self):
+        last = jnp.concatenate(self.forward(*self.last), axis=1)
+        self.last = jnp.where(self.in_middle, self.across, last)
+        self.block[3] = self.last, self.in_pieces(self.last, False, PIECES_3), None
+
+    def keep_3(self):
+        (last,) = self.forward(self.last)
+        self.block[3] = last, self.block[3][1], self.in_pieces(last, True, PIECES_3)
+
+    def last_sum(self, i, rounds):
+        keys = [(k, i if (k, i) in self.mine else None) for k in rounds]
+        self.result, theirs, self.token = last_gamma(
+            self.token, self.place, i, self.terms(*keys), self.gamma, self.shape, self.result
+        )
+        self.received[i] = self.to_core(theirs)
+
+    def put(self, i):
+        self.result, self.token = place_gamma(self.token, self.place, i, self.received[i], self.result)
+
+    def steps(self):
+        steps = {
+            "hop_1": self.hop_1, "hop_2": self.hop_2, "hop_3": self.hop_3, "keep_3": self.keep_3,
+            "combine_0": functools.partial(self.combine, 0, send="send_0" not in ORDER), "send_0": functools.partial(self.send, 0),
+            "combine_1": functools.partial(self.combine, 1, split=SPLIT_1), "combine_2": functools.partial(self.combine, 2, split=SPLIT_2),
+            "receive_0": functools.partial(self.receive, 0), "receive_1": functools.partial(self.receive, 1),
+            "receive_2": functools.partial(self.receive, 2),
+            "gamma_0": functools.partial(self.add, (0, None)), "gamma_1": functools.partial(self.add, (1, None)),
+            "gamma_01": functools.partial(self.add, (0, None), (1, None)),
+        }
+        for k in range(3):
+            steps[f"chip_{k}"], steps[f"own_{k}"] = functools.partial(self.pass_on, k), functools.partial(self.own, k)
+        rounds = (2, 3) if "gamma_1" in ORDER or "gamma_01" in ORDER else (1, 2, 3)
+        for i in range(self.half):
+            steps[f"chip_3_{i}"], steps[f"own_3_{i}"] = functools.partial(self.pass_on, 3, i), functools.partial(self.own, 3, i)
+            steps[f"combine_3_{i}"] = functools.partial(self.combine, 3, i)
+            steps[f"last_{i}"], steps[f"place_{i}"] = functools.partial(self.last_sum, i, rounds), functools.partial(self.put, i)
+        return steps
+
+
 def chain_device(b_occ_i, b_occ_j, eps_occ_i, eps_occ_j, eps_vir):
-    n_i, rows, depth = b_occ_i.shape
-    half = n_i // 2
-    z, col = lax.axis_index("row"), lax.axis_index("col")
-    x, core = col // 2, col % 2
-    in_middle = (z == 1) | (z == 2)
-    place = (jnp.stack([x, core]).astype(jnp.int32),)
-    occ = lax.dynamic_slice_in_dim(eps_occ_i, core * half, half, 0) + eps_occ_j[x]
-    token = jnp.zeros(TOKEN.shape, F32)
-    shape = b_occ_i.shape
-
-    def energies(block):
-        return lax.dynamic_slice_in_dim(eps_vir, block * rows, rows, 0)
-
-    vir_a = energies(z)[:, None]
-
-    def to_core(values):
-        return lax.ppermute(values, "col", [(q, q ^ 1) for q in range(4)])
-
-    def to_chip(values):
-        return lax.ppermute(values, "col", [(q, q ^ 2) for q in range(4)])
-
-    def along(values, steps):
-        return lax.ppermute(values, "row", steps)
-
-    def swapped(values, distance):
-        return along(values, [(k, k ^ distance) for k in range(4)])
-
-    ends, middle = [(1, 0), (2, 3)], [(1, 2), (2, 1)]
-    b_i = in_hbm(b_occ_i), in_hbm(to_core(b_occ_i))
-
-    def pass_on(block, which=None):
-        nonlocal token
-        out, token = pairs(token, place, b_i, block, False, which)
-        return to_chip(out)
-
-    def own(block, chip_sum, distance, which=None):
-        nonlocal token
-        vir_b = energies(z ^ distance)[None, :]
-        out, token = pairs(token, place, b_i, block, True, which, (chip_sum, occ, vir_a, vir_b))
-        return out
-
-    def combine(held, mirror, split=False):
-        nonlocal token
-        out, token = combine_pairs(token, place, held, mirror, split)
-        return out
-
-    def forward(*values):
-        nonlocal token
-        *out, token = tie(token, place, *values)
-        return out
-
-    def both(values):
-        pieces = [to_core(values)]
-        return values, pieces, pieces
-
-    def in_pieces(values, own_j, n_pieces=2):
-        one = lax.dynamic_slice_in_dim(values, x if own_j else 1 - x, 1, 0)
-        return [to_core(p) for p in jnp.split(one, n_pieces, axis=1)]
-
-    near = swapped(b_occ_j, 1)
-    across = along(b_occ_j, middle)
-    here = both(b_occ_j)
-
-    chip_0 = pass_on(here)
-    held_0 = own(here, chip_0, 0)
-
-    near, across = forward(near, across)
-    far_mid = along(near, middle)
-    far_end = along(across, ends)
-    near = both(near)
-    mine_0 = combine(held_0, held_0)
-    chip_1 = pass_on(near)
-
-    held_1 = own(near, chip_1, 1)
-    mirror_1 = swapped(held_1, 1)
-    far_mid, far_end = forward(far_mid, far_end)
-    last = along(far_mid, ends)
-    far = jnp.where(in_middle, far_mid, far_end)
-    far = far, in_pieces(far, False), in_pieces(far, True)
-    chip_2 = pass_on(far)
-
-    held_2 = own(far, chip_2, 2)
-    mirror_2 = swapped(held_2, 2)
-    (mine_0,) = forward(mine_0)
-    other_0 = to_chip(mine_0)
-    mine_1 = combine(held_1, mirror_1)
-    other_1 = to_chip(mine_1)
-
-    (last,) = forward(last)
-    last = jnp.where(in_middle, across, last)
-    passed = in_pieces(last, False)
-    chip_3 = [pass_on((last, passed, None), 0)]
-    mine_2 = combine(held_2, mirror_2, split=True)
-    other_2 = [to_chip(m) for m in mine_2]
-    (last,) = forward(last)
-    last = last, passed, in_pieces(last, True)
-    chip_3.append(pass_on(last, 1))
-    other_0, other_1 = forward(other_0, other_1)
-    chip_3 += [pass_on(last, i) for i in range(2, half)]
-    held_3 = [own(last, chip_3[i], 3, i) for i in range(half)]
-    mirror_3 = [swapped(h, 3) for h in held_3]
-    gamma, token = chip_gamma(token, place, [(mine_0, other_0, here), (mine_1, other_1, near)])
-    mine_3 = [combine(h, m) for h, m in zip(held_3, mirror_3)]
-    other_3 = [to_chip(m) for m in mine_3]
-
-    result, received = None, []
-    for i in range(half):
-        terms = [(mine_2[i], other_2[i], far), (mine_3[i], other_3[i], last)]
-        result, theirs, token = last_gamma(token, place, i, terms, gamma, shape, result)
-        received.append(to_core(theirs))
-    for i in range(half):
-        result, token = place_gamma(token, place, i, received[i], result)
-    return result
+    chain = Chain(b_occ_i, b_occ_j, eps_occ_i, eps_occ_j, eps_vir)
+    steps = chain.steps()
+    for name in ORDER:
+        steps[name]()
+    return chain.result
 
 
 def general_device(b_occ_i, b_occ_j, eps_occ_i, eps_occ_j, eps_vir):

time: 512 us -> 424 us (0.83); the launches traced: 511 us -> 418 us
  waiting for transfers between devices: 270 us -> 186 us
  starting transfers between devices: 67.1 us -> 49.4 us
  Pallas kernels: 158 us -> 166 us
    ppermute x14 -> x12, waiting for transfers between devices: 160 us -> 99.4 us  [to_chip(): return lax.ppermute(values, 'col', [(q, q ^ 2) for q in range(4)])]
    ppermute x14 -> x16, starting transfers between devices: 25.6 us -> 11.7 us  [to_core(): return lax.ppermute(values, 'col', [(q, q ^ 1) for q in range(4)])]
    ppermute x10, waiting for transfers between devices: 86.1 us -> 73 us  [along(): return lax.ppermute(values, 'row', steps)]
    ppermute x14 -> x16, waiting for transfers between devices: 23.3 us -> 14 us  [to_core(): return lax.ppermute(values, 'col', [(q, q ^ 1) for q in range(4)])]
    pallas_call x31 -> x30, Pallas kernels: 158 us -> 166 us  [call(): pl.pallas_call(body, out_shape=(*out, TOKEN), grid_spec=pltpu.PrefetchSca...]
    unnamed x42 -> x28, local copies, waits for them, and re-layouts: 10.8 us -> 7.5 us
    ppermute x14 -> x12, starting transfers between devices: 15 us -> 13.2 us  [to_chip(): return lax.ppermute(values, 'col', [(q, q ^ 2) for q in range(4)])]
  transfers between devices with their start and end apart: 38 -> 38, of which waited for: 19 -> 14; matrix products, arithmetic and copies ran while one was open for 1% -> 2% of each run, Pallas kernels for 30% -> 39%
where the time goes in v7:
time: 424 us; the launch traced here: 418 us
  waiting for transfers between devices  186 us (44%)
  Pallas kernels  166 us (39%)
  starting transfers between devices  49.4 us (12%)
  local copies, waits for them, and re-layouts  9.96 us (2%)
  other arithmetic  5.17 us (1%)
    pallas_call x30, Pallas kernels, call(): pl.pallas_call(body, out_shape=(*out, TOKEN), grid_spec=pltpu.PrefetchSca...  166 us
    ppermute x12, waiting for transfers between devices, to_chip(): return lax.ppermute(values, 'col', [(q, q ^ 2) for q in range(4)])  99.4 us
    ppermute x10, waiting for transfers between devices, along(): return lax.ppermute(values, 'row', steps)  73 us
    ppermute x10, starting transfers between devices, along(): return lax.ppermute(values, 'row', steps)  24.5 us
    ppermute x16, waiting for transfers between devices, to_core(): return lax.ppermute(values, 'col', [(q, q ^ 1) for q in range(4)])  14 us
    ppermute x12, starting transfers between devices, to_chip(): return lax.ppermute(values, 'col', [(q, q ^ 2) for q in range(4)])  13.2 us
    ppermute x16, starting transfers between devices, to_core(): return lax.ppermute(values, 'col', [(q, q ^ 1) for q in range(4)])  11.7 us
  transfers between devices with their start and end apart: 38, of which 14 were waited for; matrix products, arithmetic and copies ran while one was open for 2% of the time, Pallas kernels for 39%

profile of v7, /device:TPU:1, one launch (start us, length us, event | category | flops | bytes accessed | tf_op | source)
XLA Modules:
  0.0 417.6 jit_solution(7084086495658583880)
XLA Ops:
  6.2 13.3 %collective-permute-done.1.refs_5_.refs_6_ = bf16[2,512,1536]{2,1,0:T(8,128)(2,1)} collective-permute-done((bf16[2,512,1536]{2,1,0:T(8,128)(2,1)}, bf16[2,512,1536]{2,1,0:T(8,128)(2,1)}, u32[]{:S(2)}, u32[]{:S(2)}) %collective-permute-start.1) | collective-permute-done | bytes 3145760 | tf_op jit(solution)/shard_map/ppermute | solution.py:263
  21.4 9.4 %pairs_for_chip.6 = (bf16[3,512,512]{2,1,0:T(8,128)(2,1)}, f32[8,128]{1,0:T(8,128)S(1)}) custom-call(s32[2]{0:T(128)S(1)} %pad_add_fusion.refs_0_, f32[8,128]{1,0:T(8,128)S(1)} %broadcast_in_dim.12.refs_1_, bf16[6,512,1536]{2,1,0:T(8,128)(2,1)} %refs_3_.11, bf16[6,512,1536]{2,1,0:T(8,128)(2,1)} %collective-permute-done.refs_3_.refs_4_, ...), custom_call_target="tpu_custom_call" | custom-call | bytes 1024 | tf_op jit(solution)/shard_map/pairs_for_chip/pallas_call | solution.py:31
  33.2 40.8 %collective-permute-done.2.refs_2_ = bf16[2,512,1536]{2,1,0:T(8,128)(2,1)S(1)} collective-permute-done((bf16[2,512,1536]{2,1,0:T(8,128)(2,1)}, bf16[2,512,1536]{2,1,0:T(8,128)(2,1)S(1)}, u32[]{:S(2)}, u32[]{:S(2)}) %collective-permute-start.2) | collective-permute-done | bytes 3145760 | tf_op jit(solution)/shard_map/ppermute | solution.py:269
  82.9 9.3 %own_amplitudes.6 = (bf16[3,512,512]{2,1,0:T(8,128)(2,1)S(1)}, f32[8,128]{1,0:T(8,128)S(1)}) custom-call(s32[2]{0:T(128)S(1)} %pad_add_fusion.refs_0_, f32[3]{0:T(128)S(1)} %dynamic-slice_add_fusion.refs_1_, f32[8,128]{1,0:T(8,128)S(1)} %get-tuple-element.72.refs_2_, bf16[6,512,1536]{2,1,0:T(8,128)(2,1)} %refs_3_.11, ...), custom_call_target="tpu_custom_call" | custom-call | bytes 1024 | tf_op jit(solution)/shard_map/own_amplitudes/pallas_call | solution.py:31
  96.0 8.7 %pairs_for_chip.7 = (bf16[3,512,512]{2,1,0:T(8,128)(2,1)S(1)}, f32[8,128]{1,0:T(8,128)S(1)}) custom-call(s32[2]{0:T(128)S(1)} %pad_add_fusion.refs_0_, f32[8,128]{1,0:T(8,128)S(1)} %get-tuple-element.76.refs_1_, bf16[6,512,1536]{2,1,0:T(8,128)(2,1)} %refs_3_.11, bf16[6,512,1536]{2,1,0:T(8,128)(2,1)} %collective-permute-done.refs_3_.refs_4_, ...), custom_call_target="tpu_custom_call" | custom-call | bytes 1024 | tf_op jit(solution)/shard_map/pairs_for_chip/pallas_call | solution.py:31
  105.1 26.0 %collective-permute-done.6.refs_3_ = bf16[3,512,512]{2,1,0:T(8,128)(2,1)} collective-permute-done((bf16[3,512,512]{2,1,0:T(8,128)(2,1)}, bf16[3,512,512]{2,1,0:T(8,128)(2,1)}, u32[]{:S(2)}, u32[]{:S(2)}) %collective-permute-start.6) | collective-permute-done | bytes 1572896 | tf_op jit(solution)/shard_map/ppermute | solution.py:266
  131.1 15.5 %chip_gamma.2 = (f32[3,512,1536]{2,1,0:T(8,128)}, f32[3,512,1536]{2,1,0:T(8,128)}, f32[8,128]{1,0:T(8,128)S(1)}) custom-call(s32[2]{0:T(128)S(1)} %pad_add_fusion.refs_0_, f32[8,128]{1,0:T(8,128)S(1)} %get-tuple-element.78.refs_1_, bf16[3,512,512]{2,1,0:T(8,128)(2,1)} %get-tuple-element.79.refs_2_, bf16[3,512,512]{2,1,0:T(8,128)(2,1)} %collective-permute-done.6.refs_3_, ...), custom_call_target="tpu_custom_call" | custom-call | bytes 1024 | tf_op jit(solution)/shard_map/chip_gamma/pallas_call | solution.py:31
  154.6 10.3 %collective-permute-done.9.refs_7_ = bf16[3,512,512]{2,1,0:T(8,128)(2,1)S(1)} collective-permute-done((bf16[3,512,512]{2,1,0:T(8,128)(2,1)S(1)}, bf16[3,512,512]{2,1,0:T(8,128)(2,1)S(1)}, u32[]{:S(2)}, u32[]{:S(2)}) %collective-permute-start.9) | collective-permute-done | bytes 1572896 | tf_op jit(solution)/shard_map/ppermute | solution.py:266
  164.8 8.5 %own_amplitudes.7 = (bf16[3,512,512]{2,1,0:T(8,128)(2,1)S(1)}, f32[8,128]{1,0:T(8,128)S(1)}) custom-call(s32[2]{0:T(128)S(1)} %pad_add_fusion.refs_0_, f32[3]{0:T(128)S(1)} %dynamic-slice_add_fusion.refs_1_, f32[8,128]{1,0:T(8,128)S(1)} %get-tuple-element.82.refs_2_, bf16[6,512,1536]{2,1,0:T(8,128)(2,1)} %refs_3_.11, ...), custom_call_target="tpu_custom_call" | custom-call | bytes 1024 | tf_op jit(solution)/shard_map/own_amplitudes/pallas_call | solution.py:31
  173.4 9.5 %pairs_for_chip.8 = (bf16[3,512,512]{2,1,0:T(8,128)(2,1)}, f32[8,128]{1,0:T(8,128)S(1)}) custom-call(s32[2]{0:T(128)S(1)} %pad_add_fusion.refs_0_, f32[8,128]{1,0:T(8,128)S(1)} %get-tuple-element.84.refs_1_, bf16[6,512,1536]{2,1,0:T(8,128)(2,1)} %refs_3_.11, bf16[6,512,1536]{2,1,0:T(8,128)(2,1)} %collective-permute-done.refs_3_.refs_4_, ...), custom_call_target="tpu_custom_call" | custom-call | bytes 1024 | tf_op jit(solution)/shard_map/pairs_for_chip/pallas_call | solution.py:31
  188.4 30.1 %collective-permute-done.12.refs_7_ = bf16[3,512,512]{2,1,0:T(8,128)(2,1)} collective-permute-done((bf16[3,512,512]{2,1,0:T(8,128)(2,1)}, bf16[3,512,512]{2,1,0:T(8,128)(2,1)}, u32[]{:S(2)}, u32[]{:S(2)}) %collective-permute-start.12) | collective-permute-done | bytes 1572896 | tf_op jit(solution)/shard_map/ppermute | solution.py:266
  218.5 9.3 %own_amplitudes.8 = (bf16[3,512,512]{2,1,0:T(8,128)(2,1)S(1)}, f32[8,128]{1,0:T(8,128)S(1)}) custom-call(s32[2]{0:T(128)S(1)} %pad_add_fusion.refs_0_, f32[3]{0:T(128)S(1)} %dynamic-slice_add_fusion.refs_1_, f32[8,128]{1,0:T(8,128)S(1)} %get-tuple-element.87.refs_2_, bf16[6,512,1536]{2,1,0:T(8,128)(2,1)} %refs_3_.11, ...), custom_call_target="tpu_custom_call" | custom-call | bytes 1024 | tf_op jit(solution)/shard_map/own_amplitudes/pallas_call | solution.py:31
  256.9 4.3 %own_amplitudes.9 = (bf16[1,512,512]{2,1,0:T(8,128)(2,1)S(1)}, f32[8,128]{1,0:T(8,128)S(1)}) custom-call(s32[2]{0:T(128)S(1)} %pad_add_fusion.refs_0_, f32[3]{0:T(128)S(1)} %dynamic-slice_add_fusion.refs_1_, f32[8,128]{1,0:T(8,128)S(1)} %get-tuple-element.96.refs_2_, bf16[6,512,1536]{2,1,0:T(8,128)(2,1)} %refs_3_.11, ...), custom_call_target="tpu_custom_call" | custom-call | bytes 1024 | tf_op jit(solution)/shard_map/own_amplitudes/pallas_call | solution.py:31
  266.3 13.2 %collective-permute-done.24.refs_10_ = bf16[1,512,512]{2,1,0:T(8,128)(2,1)S(1)} collective-permute-done((bf16[1,512,512]{2,1,0:T(8,128)(2,1)S(1)}, bf16[1,512,512]{2,1,0:T(8,128)(2,1)S(1)}, u32[]{:S(2)}, u32[]{:S(2)}) %collective-permute-start.24) | collective-permute-done | bytes 524320 | tf_op jit(solution)/shard_map/ppermute | solution.py:266
  279.5 4.3 %own_amplitudes.10 = (bf16[1,512,512]{2,1,0:T(8,128)(2,1)S(1)}, f32[8,128]{1,0:T(8,128)S(1)}) custom-call(s32[2]{0:T(128)S(1)} %pad_add_fusion.refs_0_, f32[3]{0:T(128)S(1)} %dynamic-slice_add_fusion.refs_1_, f32[8,128]{1,0:T(8,128)S(1)} %get-tuple-element.100.refs_2_, bf16[6,512,1536]{2,1,0:T(8,128)(2,1)} %refs_3_.11, ...), custom_call_target="tpu_custom_call" | custom-call | bytes 1024 | tf_op jit(solution)/shard_map/own_amplitudes/pallas_call | solution.py:31
  283.8 4.3 %own_amplitudes.11 = (bf16[1,512,512]{2,1,0:T(8,128)(2,1)S(1)}, f32[8,128]{1,0:T(8,128)S(1)}) custom-call(s32[2]{0:T(128)S(1)} %pad_add_fusion.refs_0_, f32[3]{0:T(128)S(1)} %dynamic-slice_add_fusion.refs_1_, f32[8,128]{1,0:T(8,128)S(1)} %get-tuple-element.102.refs_2_, bf16[6,512,1536]{2,1,0:T(8,128)(2,1)} %refs_3_.11, ...), custom_call_target="tpu_custom_call" | custom-call | bytes 1024 | tf_op jit(solution)/shard_map/own_amplitudes/pallas_call | solution.py:31
  288.1 17.5 %collective-permute-done.26.refs_3_ = bf16[3,512,512]{2,1,0:T(8,128)(2,1)S(1)} collective-permute-done((bf16[3,512,512]{2,1,0:T(8,128)(2,1)S(1)}, bf16[3,512,512]{2,1,0:T(8,128)(2,1)S(1)}, u32[]{:S(2)}, u32[]{:S(2)}) %collective-permute-start.26) | collective-permute-done | bytes 1572896 | tf_op jit(solution)/shard_map/ppermute | solution.py:269
  311.4 11.1 %collective-permute-done.27.refs_3_ = bf16[1,512,512]{2,1,0:T(8,128)(2,1)S(1)} collective-permute-done((bf16[1,512,512]{2,1,0:T(8,128)(2,1)S(1)}, bf16[1,512,512]{2,1,0:T(8,128)(2,1)S(1)}, u32[]{:S(2)}, u32[]{:S(2)}) %collective-permute-start.27) | collective-permute-done | bytes 524320 | tf_op jit(solution)/shard_map/ppermute | solution.py:269
  323.6 20.1 %chip_gamma.3 = (f32[3,512,1536]{2,1,0:T(8,128)}, f32[3,512,1536]{2,1,0:T(8,128)}, f32[8,128]{1,0:T(8,128)S(1)}) custom-call(s32[2]{0:T(128)S(1)} %pad_add_fusion.refs_0_, f32[8,128]{1,0:T(8,128)S(1)} %get-tuple-element.108.refs_1_, bf16[3,512,512]{2,1,0:T(8,128)(2,1)S(1)} %get-tuple-element.109.refs_2_, ...), custom_call_target="tpu_custom_call", output_to_operand_aliasing={{0}: (6, {}), {1}: (7, {})} | custom-call | bytes 1024 | tf_op jit(solution)/shard_map/chip_gamma/pallas_call | solution.py:31
  347.8 10.4 %collective-permute-done.31.refs_8_ = bf16[1,512,512]{2,1,0:T(8,128)(2,1)S(1)} collective-permute-done((bf16[1,512,512]{2,1,0:T(8,128)(2,1)S(1)}, bf16[1,512,512]{2,1,0:T(8,128)(2,1)S(1)}, u32[]{:S(2)}, u32[]{:S(2)}) %collective-permute-start.31) | collective-permute-done | bytes 524320 | tf_op jit(solution)/shard_map/ppermute | solution.py:266
  361.8 11.2 %last_gamma.3 = (f32[6,512,1536]{2,1,0:T(8,128)}, bf16[1,512,1536]{2,1,0:T(8,128)(2,1)S(1)}, f32[8,128]{1,0:T(8,128)S(1)}) custom-call(s32[2]{0:T(128)S(1)} %pad_add_fusion.refs_0_, f32[8,128]{1,0:T(8,128)S(1)} %get-tuple-element.114.refs_1_, bf16[3,512,512]{2,1,0:T(8,128)(2,1)S(1)} %get-tuple-element.115.refs_2_, ...), custom_call_target="tpu_custom_call" | custom-call | bytes 1024 | tf_op jit(solution)/shard_map/last_gamma/pallas_call | solution.py:31
  373.0 11.2 %last_gamma.4 = (f32[6,512,1536]{2,1,0:T(8,128)}, bf16[1,512,1536]{2,1,0:T(8,128)(2,1)S(1)}, f32[8,128]{1,0:T(8,128)S(1)}) custom-call(s32[2]{0:T(128)S(1)} %pad_add_fusion.refs_0_, f32[8,128]{1,0:T(8,128)S(1)} %get-tuple-element.119.refs_1_, bf16[3,512,512]{2,1,0:T(8,128)(2,1)S(1)} %get-tuple-element.115.refs_2_, ...), custom_call_target="tpu_custom_call", output_to_operand_aliasing={{0}: (20, {})} | custom-call | bytes 1024 | tf_op jit(solution)/shard_map/last_gamma/pallas_call | solution.py:31
  388.4 8.3 %collective-permute-done.34.refs_8_ = bf16[1,512,512]{2,1,0:T(8,128)(2,1)S(1)} collective-permute-done((bf16[1,512,512]{2,1,0:T(8,128)(2,1)S(1)}, bf16[1,512,512]{2,1,0:T(8,128)(2,1)S(1)}, u32[]{:S(2)}, u32[]{:S(2)}) %collective-permute-start.34) | collective-permute-done | bytes 524320 | tf_op jit(solution)/shard_map/ppermute | solution.py:266
  396.7 11.2 %last_gamma.5 = (f32[6,512,1536]{2,1,0:T(8,128)}, bf16[1,512,1536]{2,1,0:T(8,128)(2,1)S(1)}, f32[8,128]{1,0:T(8,128)S(1)}) custom-call(s32[2]{0:T(128)S(1)} %pad_add_fusion.refs_0_, f32[8,128]{1,0:T(8,128)S(1)} %get-tuple-element.124.refs_1_, bf16[3,512,512]{2,1,0:T(8,128)(2,1)S(1)} %get-tuple-element.115.refs_2_, ...), custom_call_target="tpu_custom_call", output_to_operand_aliasing={{0}: (20, {})} | custom-call | bytes 1024 | tf_op jit(solution)/shard_map/last_gamma/pallas_call | solution.py:31
  (121 shorter events, 99.6 us)
Async XLA Ops:
  0.5 32.7 %collective-permute-start.3 = (bf16[2,512,1536]{2,1,0:T(8,128)(2,1)}, bf16[2,512,1536]{2,1,0:T(8,128)(2,1)}, u32[]{:S(2)}, u32[]{:S(2)}) collective-permute-start(bf16[2,512,1536]{2,1,0:T(8,128)(2,1)} %refs_4_.3), channel_id=1, source_target_pairs={{4,8},{8,4},{5,9},{9,5},{6,10},{10,6},{7,11},{11,7},{20,24},{24,20... | collective-permute-start | bytes 9437192 | tf_op jit(solution)/shard_map/ppermute | solution.py:269
  2.9 71.1 %collective-permute-start.2 = (bf16[2,512,1536]{2,1,0:T(8,128)(2,1)}, bf16[2,512,1536]{2,1,0:T(8,128)(2,1)S(1)}, u32[]{:S(2)}, u32[]{:S(2)}) collective-permute-start(bf16[2,512,1536]{2,1,0:T(8,128)(2,1)} %refs_4_.3), channel_id=1, source_target_pairs={{0,4},{4,0},{8,12},{12,8},{1,5},{5,1},{9,13},{13,9},{2,6},{6,2},{1... | collective-permute-start | bytes 9437192 | tf_op jit(solution)/shard_map/ppermute | solution.py:269
  30.8 50.2 %collective-permute-start.4 = (bf16[3,512,512]{2,1,0:T(8,128)(2,1)}, bf16[3,512,512]{2,1,0:T(8,128)(2,1)}, u32[]{:S(2)}, u32[]{:S(2)}) collective-permute-start(bf16[3,512,512]{2,1,0:T(8,128)(2,1)} %get-tuple-element.73), channel_id=1, source_target_pairs={{0,2},{1,3},{2,0},{3,1},{4,6},{5,7},{6,4},{7,5},{8,10},{9,11},{10,... | collective-permute-start | bytes 4718600 | tf_op jit(solution)/shard_map/ppermute | solution.py:266
  74.5 21.5 %collective-permute-start.5 = (bf16[2,512,1536]{2,1,0:T(8,128)(2,1)S(1)}, bf16[2,512,1536]{2,1,0:T(8,128)(2,1)}, u32[]{:S(2)}, u32[]{:S(2)}) collective-permute-start(bf16[2,512,1536]{2,1,0:T(8,128)(2,1)S(1)} %get-tuple-element.77.refs_4_.refs_5_), channel_id=1, source_target_pairs={{0,1},{1,0},{2,3},{3,2},{4,5},{5,4},{6,7},{7,6},{8,9},{9,8},{10,11... | collective-permute-start | bytes 9437192 | tf_op jit(solution)/shard_map/ppermute | solution.py:263
  76.0 71.9 %collective-permute-start.8 = (bf16[2,512,1536]{2,1,0:T(8,128)(2,1)}, bf16[2,512,1536]{2,1,0:T(8,128)(2,1)}, u32[]{:S(2)}, u32[]{:S(2)}) collective-permute-start(bf16[2,512,1536]{2,1,0:T(8,128)(2,1)} %get-tuple-element.81), channel_id=1, source_target_pairs={{4,0},{8,12},{5,1},{9,13},{6,2},{10,14},{7,3},{11,15},{20,16},{24,... | collective-permute-start | bytes 9437192 | tf_op jit(solution)/shard_map/ppermute | solution.py:269
  77.3 70.6 %collective-permute-start.7 = (bf16[2,512,1536]{2,1,0:T(8,128)(2,1)S(1)}, bf16[2,512,1536]{2,1,0:T(8,128)(2,1)}, u32[]{:S(2)}, u32[]{:S(2)}) collective-permute-start(bf16[2,512,1536]{2,1,0:T(8,128)(2,1)S(1)} %get-tuple-element.77.refs_4_.refs_5_), channel_id=1, source_target_pairs={{4,8},{8,4},{5,9},{9,5},{6,10},{10,6},{7,11},{11,7},{20,24},{24,20... | collective-permute-start | bytes 9437192 | tf_op jit(solution)/shard_map/ppermute | solution.py:269
  94.8 36.3 %collective-permute-start.6 = (bf16[3,512,512]{2,1,0:T(8,128)(2,1)}, bf16[3,512,512]{2,1,0:T(8,128)(2,1)}, u32[]{:S(2)}, u32[]{:S(2)}) collective-permute-start(bf16[3,512,512]{2,1,0:T(8,128)(2,1)} %get-tuple-element.79.refs_2_), channel_id=1, source_target_pairs={{0,2},{1,3},{2,0},{3,1},{4,6},{5,7},{6,4},{7,5},{8,10},{9,11},{10,... | collective-permute-start | bytes 4718600 | tf_op jit(solution)/shard_map/ppermute | solution.py:266
  104.8 60.1 %collective-permute-start.9 = (bf16[3,512,512]{2,1,0:T(8,128)(2,1)S(1)}, bf16[3,512,512]{2,1,0:T(8,128)(2,1)S(1)}, u32[]{:S(2)}, u32[]{:S(2)}) collective-permute-start(bf16[3,512,512]{2,1,0:T(8,128)(2,1)S(1)} %get-tuple-element.83), channel_id=1, source_target_pairs={{0,2},{1,3},{2,0},{3,1},{4,6},{5,7},{6,4},{7,5},{8,10},{9,11},{10,... | collective-permute-start | bytes 4718600 | tf_op jit(solution)/shard_map/ppermute | solution.py:266
  152.1 21.3 %collective-permute-start.10 = (bf16[1,512,1536]{2,1,0:T(8,128)(2,1)S(1)}, bf16[1,512,1536]{2,1,0:T(8,128)(2,1)S(1)}, u32[]{:S(2)}, u32[]{:S(2)}) collective-permute-start(bf16[1,512,1536]{2,1,0:T(8,128)(2,1)S(1)} %get-tuple-element.146), channel_id=1, source_target_pairs={{0,1},{1,0},{2,3},{3,2},{4,5},{5,4},{6,7},{7,6},{8,9},{9,8},{10,11... | collective-permute-start | bytes 4718600 | tf_op jit(solution)/shard_map/ppermute | solution.py:263
  152.9 74.9 %collective-permute-start.13 = (bf16[2,512,1536]{2,1,0:T(8,128)(2,1)}, bf16[2,512,1536]{2,1,0:T(8,128)(2,1)}, u32[]{:S(2)}, u32[]{:S(2)}) collective-permute-start(bf16[2,512,1536]{2,1,0:T(8,128)(2,1)} %get-tuple-element.85), channel_id=1, source_target_pairs={{4,0},{8,12},{5,1},{9,13},{6,2},{10,14},{7,3},{11,15},{20,16},{24,... | collective-permute-start | bytes 9437192 | tf_op jit(solution)/shard_map/ppermute | solution.py:269
  154.4 34.1 %collective-permute-start.11 = (bf16[1,512,1536]{2,1,0:T(8,128)(2,1)}, bf16[1,512,1536]{2,1,0:T(8,128)(2,1)}, u32[]{:S(2)}, u32[]{:S(2)}) collective-permute-start(bf16[1,512,1536]{2,1,0:T(8,128)(2,1)} %get-tuple-element.145), channel_id=1, source_target_pairs={{0,1},{1,0},{2,3},{3,2},{4,5},{5,4},{6,7},{7,6},{8,9},{9,8},{10,11... | collective-permute-start | bytes 4718600 | tf_op jit(solution)/shard_map/ppermute | solution.py:263
  182.9 35.6 %collective-permute-start.12 = (bf16[3,512,512]{2,1,0:T(8,128)(2,1)}, bf16[3,512,512]{2,1,0:T(8,128)(2,1)}, u32[]{:S(2)}, u32[]{:S(2)}) collective-permute-start(bf16[3,512,512]{2,1,0:T(8,128)(2,1)} %get-tuple-element.88), channel_id=1, source_target_pairs={{0,2},{1,3},{2,0},{3,1},{4,6},{5,7},{6,4},{7,5},{8,10},{9,11},{10,... | collective-permute-start | bytes 4718600 | tf_op jit(solution)/shard_map/ppermute | solution.py:266
  184.2 79.4 %collective-permute-start.23 = (bf16[3,512,512]{2,1,0:T(8,128)(2,1)}, bf16[3,512,512]{2,1,0:T(8,128)(2,1)S(1)}, u32[]{:S(2)}, u32[]{:S(2)}) collective-permute-start(bf16[3,512,512]{2,1,0:T(8,128)(2,1)} %copy-done.9), channel_id=1, source_target_pairs={{0,4},{4,0},{8,12},{12,8},{1,5},{5,1},{9,13},{13,9},{2,6},{6,2},{1... | collective-permute-start | bytes 4718600 | tf_op jit(solution)/shard_map/ppermute | solution.py:269
  232.9 72.7 %collective-permute-start.26 = (bf16[3,512,512]{2,1,0:T(8,128)(2,1)S(1)}, bf16[3,512,512]{2,1,0:T(8,128)(2,1)S(1)}, u32[]{:S(2)}, u32[]{:S(2)}) collective-permute-start(bf16[3,512,512]{2,1,0:T(8,128)(2,1)S(1)} %get-tuple-element.105.refs_2_), channel_id=1, source_target_pairs={{0,8},{4,12},{8,0},{12,4},{1,9},{5,13},{9,1},{13,5},{2,10},{6,14},... | collective-permute-start | bytes 4718600 | tf_op jit(solution)/shard_map/ppermute | solution.py:269
  254.2 29.6 %collective-permute-start.25 = (bf16[1,512,512]{2,1,0:T(8,128)(2,1)S(1)}, bf16[1,512,512]{2,1,0:T(8,128)(2,1)S(1)}, u32[]{:S(2)}, u32[]{:S(2)}) collective-permute-start(bf16[1,512,512]{2,1,0:T(8,128)(2,1)S(1)} %get-tuple-element.103), channel_id=1, source_target_pairs={{0,2},{1,3},{2,0},{3,1},{4,6},{5,7},{6,4},{7,5},{8,10},{9,11},{10,... | collective-permute-start | bytes 1572872 | tf_op jit(solution)/shard_map/ppermute | solution.py:266
  254.5 25.0 %collective-permute-start.24 = (bf16[1,512,512]{2,1,0:T(8,128)(2,1)S(1)}, bf16[1,512,512]{2,1,0:T(8,128)(2,1)S(1)}, u32[]{:S(2)}, u32[]{:S(2)}) collective-permute-start(bf16[1,512,512]{2,1,0:T(8,128)(2,1)S(1)} %get-tuple-element.101), channel_id=1, source_target_pairs={{0,2},{1,3},{2,0},{3,1},{4,6},{5,7},{6,4},{7,5},{8,10},{9,11},{10,... | collective-permute-start | bytes 1572872 | tf_op jit(solution)/shard_map/ppermute | solution.py:266
  265.1 58.5 %collective-permute-start.28 = (bf16[3,512,512]{2,1,0:T(8,128)(2,1)S(1)}, bf16[3,512,512]{2,1,0:T(8,128)(2,1)S(1)}, u32[]{:S(2)}, u32[]{:S(2)}) collective-permute-start(bf16[3,512,512]{2,1,0:T(8,128)(2,1)S(1)} %get-tuple-element.109.refs_2_), channel_id=1, source_target_pairs={{0,2},{1,3},{2,0},{3,1},{4,6},{5,7},{6,4},{7,5},{8,10},{9,11},{10,... | collective-permute-start | bytes 4718600 | tf_op jit(solution)/shard_map/ppermute | solution.py:266
  306.8 51.3 %collective-permute-start.30 = (bf16[3,512,512]{2,1,0:T(8,128)(2,1)S(1)}, bf16[3,512,512]{2,1,0:T(8,128)(2,1)S(1)}, u32[]{:S(2)}, u32[]{:S(2)}) collective-permute-start(bf16[3,512,512]{2,1,0:T(8,128)(2,1)S(1)} %get-tuple-element.115.refs_2_), channel_id=1, source_target_pairs={{0,2},{1,3},{2,0},{3,1},{4,6},{5,7},{6,4},{7,5},{8,10},{9,11},{10,... | collective-permute-start | bytes 4718600 | tf_op jit(solution)/shard_map/ppermute | solution.py:266
  310.2 33.4 %collective-permute-start.29 = (bf16[1,512,512]{2,1,0:T(8,128)(2,1)S(1)}, bf16[1,512,512]{2,1,0:T(8,128)(2,1)S(1)}, u32[]{:S(2)}, u32[]{:S(2)}) collective-permute-start(bf16[1,512,512]{2,1,0:T(8,128)(2,1)S(1)} %get-tuple-element.113.refs_2_), channel_id=1, source_target_pairs={{0,12},{4,8},{8,4},{12,0},{1,13},{5,9},{9,5},{13,1},{2,14},{6,10},... | collective-permute-start | bytes 1572872 | tf_op jit(solution)/shard_map/ppermute | solution.py:269
  323.2 34.9 %collective-permute-start.31 = (bf16[1,512,512]{2,1,0:T(8,128)(2,1)S(1)}, bf16[1,512,512]{2,1,0:T(8,128)(2,1)S(1)}, u32[]{:S(2)}, u32[]{:S(2)}) collective-permute-start(bf16[1,512,512]{2,1,0:T(8,128)(2,1)S(1)} %get-tuple-element.116.refs_7_), channel_id=1, source_target_pairs={{0,2},{1,3},{2,0},{3,1},{4,6},{5,7},{6,4},{7,5},{8,10},{9,11},{10,... | collective-permute-start | bytes 1572872 | tf_op jit(solution)/shard_map/ppermute | solution.py:266
  344.4 28.6 %collective-permute-start.32 = (bf16[1,512,512]{2,1,0:T(8,128)(2,1)S(1)}, bf16[1,512,512]{2,1,0:T(8,128)(2,1)S(1)}, u32[]{:S(2)}, u32[]{:S(2)}) collective-permute-start(bf16[1,512,512]{2,1,0:T(8,128)(2,1)S(1)} %get-tuple-element.120.refs_7_), channel_id=1, source_target_pairs={{0,2},{1,3},{2,0},{3,1},{4,6},{5,7},{6,4},{7,5},{8,10},{9,11},{10,... | collective-permute-start | bytes 1572872 | tf_op jit(solution)/shard_map/ppermute | solution.py:266
  345.7 38.6 %collective-permute-start.33 = (bf16[1,512,512]{2,1,0:T(8,128)(2,1)S(1)}, bf16[1,512,512]{2,1,0:T(8,128)(2,1)S(1)}, u32[]{:S(2)}, u32[]{:S(2)}) collective-permute-start(bf16[1,512,512]{2,1,0:T(8,128)(2,1)S(1)} %get-tuple-element.123.refs_2_), channel_id=1, source_target_pairs={{0,12},{4,8},{8,4},{12,0},{1,13},{5,9},{9,5},{13,1},{2,14},{6,10},... | collective-permute-start | bytes 1572872 | tf_op jit(solution)/shard_map/ppermute | solution.py:269
  386.2 24.5 %collective-permute-start.35 = (bf16[1,512,1536]{2,1,0:T(8,128)(2,1)S(1)}, bf16[1,512,1536]{2,1,0:T(8,128)(2,1)S(1)}, u32[]{:S(2)}, u32[]{:S(2)}) collective-permute-start(bf16[1,512,1536]{2,1,0:T(8,128)(2,1)S(1)} %get-tuple-element.128), channel_id=1, source_target_pairs={{0,1},{1,0},{2,3},{3,2},{4,5},{5,4},{6,7},{7,6},{8,9},{9,8},{10,11... | collective-permute-start | bytes 4718600 | tf_op jit(solution)/shard_map/ppermute | solution.py:263
  388.4 24.5 %collective-permute-start.36 = (bf16[1,512,1536]{2,1,0:T(8,128)(2,1)S(1)}, bf16[1,512,1536]{2,1,0:T(8,128)(2,1)S(1)}, u32[]{:S(2)}, u32[]{:S(2)}) collective-permute-start(bf16[1,512,1536]{2,1,0:T(8,128)(2,1)S(1)} %get-tuple-element.131), channel_id=1, source_target_pairs={{0,1},{1,0},{2,3},{3,2},{4,5},{5,4},{6,7},{7,6},{8,9},{9,8},{10,11... | collective-permute-start | bytes 4718600 | tf_op jit(solution)/shard_map/ppermute | solution.py:263
  (28 other events, 330.0 us)

commit v8 on v7

--- a/solution.py
+++ b/solution.py
@@ -80,7 +80,7 @@
     pieces = kept if own_j else passed
     cols, depth = block.shape[1:]
     half, rows = core_part.shape[0] // 2, core_part.shape[1]
-    first, count = (0, half) if which is None else (which, 1)
+    first, count = (0, half) if which is None else which
 
     def j_of(s):
         return s[0] if own_j else 1 - s[0]
@@ -150,14 +150,15 @@
         out[...] = total.reshape(count, rows, tile).astype(out.dtype)
 
 
-def gamma_operands(terms, which, tile):
+def gamma_operands(terms, which, tile, half):
     in_specs, args, counts = [], [], []
     for same_j, other_j, (block, passed, kept) in terms:
         for h in (same_j, other_j):
             if which is None or h.shape[0] == 1:
                 in_specs.append(pl.BlockSpec(h.shape, lambda p, s: (0, 0, 0), pipeline_mode=pl.Buffered(1)))
             else:
-                in_specs.append(pl.BlockSpec((1,) + h.shape[1:], lambda p, s: (which, 0, 0)))
+                at = which - (0 if h.shape[0] == half else [f for f, n in GROUPS if f <= which < f + n][0])
+                in_specs.append(pl.BlockSpec((1,) + h.shape[1:], lambda p, s, at=at: (at, 0, 0)))
         kept = [] if kept is passed else kept
         blocks = [block, *passed, *kept]
         in_specs += [pl.BlockSpec(b.shape[:2] + (tile,), lambda p, s: (0, 0, p)) for b in blocks]
@@ -170,7 +171,7 @@
     half, rows = terms[0][0].shape[:2]
     depth = terms[0][2][0].shape[2]
     tile = tile_of(depth)
-    in_specs, args, counts = gamma_operands(terms, None, tile)
+    in_specs, args, counts = gamma_operands(terms, None, tile, half)
     spec = pl.BlockSpec((half, rows, tile), lambda p, s: (0, 0, p))
     aliases = None
     if before is not None:
@@ -179,14 +180,15 @@
         args += before
     out = [jax.ShapeDtypeStruct((half, rows, depth), F32)] * 2
     kernel = functools.partial(gamma_kernel, counts, before is not None)
-    *out, token = call(kernel, "chip_gamma", token, place, (depth // tile,), in_specs, args, [spec, spec], out, aliases, mib=36)
+    name = f"chip_gamma_{len(terms)}_{len(before or [])}"
+    *out, token = call(kernel, name, token, place, (depth // tile,), in_specs, args, [spec, spec], out, aliases, mib=28 + 6 * len(terms))
     return out, token
 
 
 def last_gamma(token, place, which, terms, before, shape, result):
     half, rows, depth = before[0].shape
     tile = tile_of(depth)
-    in_specs, args, counts = gamma_operands(terms, which, tile)
+    in_specs, args, counts = gamma_operands(terms, which, tile, half)
     spec = pl.BlockSpec((1, rows, tile), lambda p, s: (which, 0, p))
     in_specs += [spec, spec]
     args += before
@@ -205,7 +207,7 @@
         pl.BlockSpec((1, rows, tile), lambda p, s: (0, 0, p)),
     ]
     out = [jax.ShapeDtypeStruct(shape, F32), jax.ShapeDtypeStruct((1, rows, depth), BF16)]
-    return call(kernel, "last_gamma", token, place, (depth // tile,), in_specs, args, out_specs, out, aliases, mib=24)
+    return call(kernel, f"last_gamma_{len(terms)}", token, place, (depth // tile,), in_specs, args, out_specs, out, aliases, mib=24)
 
 
 def place_kernel(place, received, result, out):
@@ -238,7 +240,8 @@
     "combine_3_0", "gamma_1", "combine_3_1", "last_0", "last_1", "combine_3_2", "last_2", "place_0", "place_1",
     "place_2",
 )
-PIECES_2, PIECES_3, HALVES, SPLIT_1, SPLIT_2 = 1, 4, 1, False, False
+PIECES_2, PIECES_3, HALVES, SPLIT_1, SPLIT_2 = 2, 4, 1, False, False
+GROUPS = ((0, 1), (1, 1), (2, 1))
 
 
 class Chain:
@@ -311,8 +314,9 @@
     def terms(self, *keys):
         return [(self.mine[key], self.other[key], self.block[key[0]]) for key in keys]
 
-    def add(self, *keys):
-        self.gamma, self.token = chip_gamma(self.token, self.place, self.terms(*keys), self.gamma)
+    def add(self, *rounds):
+        out, self.token = chip_gamma(self.token, self.place, self.terms(*((k, None) for k in rounds)), self.gamma)
+        self.gamma = [in_hbm(o) for o in out]
 
     def hop_1(self):
         self.near, self.across = self.forward(self.near, self.across)
@@ -336,7 +340,8 @@
         self.block[3] = last, self.block[3][1], self.in_pieces(last, True, PIECES_3)
 
     def last_sum(self, i, rounds):
-        keys = [(k, i if (k, i) in self.mine else None) for k in rounds]
+        group = [g for g in GROUPS if g[0] <= i < sum(g)][0]
+        keys = [(k, group if k == 3 else i if (k, i) in self.mine else None) for k in rounds]
         self.result, theirs, self.token = last_gamma(
             self.token, self.place, i, self.terms(*keys), self.gamma, self.shape, self.result
         )
@@ -352,15 +357,18 @@
             "combine_1": functools.partial(self.combine, 1, split=SPLIT_1), "combine_2": functools.partial(self.combine, 2, split=SPLIT_2),
             "receive_0": functools.partial(self.receive, 0), "receive_1": functools.partial(self.receive, 1),
             "receive_2": functools.partial(self.receive, 2),
-            "gamma_0": functools.partial(self.add, (0, None)), "gamma_1": functools.partial(self.add, (1, None)),
-            "gamma_01": functools.partial(self.add, (0, None), (1, None)),
+            "gamma_0": functools.partial(self.add, 0), "gamma_1": functools.partial(self.add, 1),
+            "gamma_2": functools.partial(self.add, 2), "gamma_01": functools.partial(self.add, 0, 1),
+            "gamma_12": functools.partial(self.add, 1, 2), "gamma_012": functools.partial(self.add, 0, 1, 2),
         }
         for k in range(3):
             steps[f"chip_{k}"], steps[f"own_{k}"] = functools.partial(self.pass_on, k), functools.partial(self.own, k)
-        rounds = (2, 3) if "gamma_1" in ORDER or "gamma_01" in ORDER else (1, 2, 3)
+        added = "".join(name for name in ORDER if name.startswith("gamma"))
+        rounds = [k for k in range(4) if str(k) not in added]
+        for n, group in enumerate(GROUPS):
+            steps[f"chip_3_{n}"], steps[f"own_3_{n}"] = functools.partial(self.pass_on, 3, group), functools.partial(self.own, 3, group)
+            steps[f"combine_3_{n}"] = functools.partial(self.combine, 3, group)
         for i in range(self.half):
-            steps[f"chip_3_{i}"], steps[f"own_3_{i}"] = functools.partial(self.pass_on, 3, i), functools.partial(self.own, 3, i)
-            steps[f"combine_3_{i}"] = functools.partial(self.combine, 3, i)
             steps[f"last_{i}"], steps[f"place_{i}"] = functools.partial(self.last_sum, i, rounds), functools.partial(self.put, i)
         return steps
 

time: 424 us -> 421 us (level)
  waiting for transfers between devices: 186 us -> 181 us
    ppermute x16 -> x18, starting transfers between devices: 11.7 us -> 12.9 us  [to_core(): return lax.ppermute(values, 'col', [(q, q ^ 1) for q in range(4)])]
    ppermute x16 -> x18, waiting for transfers between devices: 14 us -> 14.1 us  [to_core(): return lax.ppermute(values, 'col', [(q, q ^ 1) for q in range(4)])]
  transfers between devices with their start and end apart: 38 -> 40, of which waited for: 14 -> 12; matrix products, arithmetic and copies ran while one was open for 2% -> 2% of each run, Pallas kernels for 39% -> 39%
where the time goes in v8:
time: 421 us; the launch traced here: 414 us
  waiting for transfers between devices  181 us (43%)
  Pallas kernels  167 us (40%)
  starting transfers between devices  51.6 us (12%)
  local copies, waits for them, and re-layouts  9.86 us (2%)
  other arithmetic  5.24 us (1%)
    pallas_call x30, Pallas kernels, call(): pl.pallas_call(body, out_shape=(*out, TOKEN), grid_spec=pltpu.PrefetchSca...  167 us
    ppermute x12, waiting for transfers between devices, to_chip(): return lax.ppermute(values, 'col', [(q, q ^ 2) for q in range(4)])  97.2 us
    ppermute x10, waiting for transfers between devices, along(): return lax.ppermute(values, 'row', steps)  69.4 us
    ppermute x10, starting transfers between devices, along(): return lax.ppermute(values, 'row', steps)  25.3 us
    ppermute x18, waiting for transfers between devices, to_core(): return lax.ppermute(values, 'col', [(q, q ^ 1) for q in range(4)])  14.1 us
    ppermute x12, starting transfers between devices, to_chip(): return lax.ppermute(values, 'col', [(q, q ^ 2) for q in range(4)])  13.3 us
    ppermute x18, starting transfers between devices, to_core(): return lax.ppermute(values, 'col', [(q, q ^ 1) for q in range(4)])  12.9 us
  transfers between devices with their start and end apart: 40, of which 12 were waited for; matrix products, arithmetic and copies ran while one was open for 2% of the time, Pallas kernels for 39%

profile of v8, /device:TPU:1, one launch (start us, length us, event | category | flops | bytes accessed | tf_op | source)
XLA Modules:
  0.0 414.3 jit_solution(12832243141458830496)
XLA Ops:
  6.2 13.3 %collective-permute-done.1.refs_5_.refs_6_ = bf16[2,512,1536]{2,1,0:T(8,128)(2,1)} collective-permute-done((bf16[2,512,1536]{2,1,0:T(8,128)(2,1)}, bf16[2,512,1536]{2,1,0:T(8,128)(2,1)}, u32[]{:S(2)}, u32[]{:S(2)}) %collective-permute-start.1) | collective-permute-done | bytes 3145760 | tf_op jit(solution)/shard_map/ppermute | solution.py:266
  21.4 9.4 %pairs_for_chip.6 = (bf16[3,512,512]{2,1,0:T(8,128)(2,1)}, f32[8,128]{1,0:T(8,128)S(1)}) custom-call(s32[2]{0:T(128)S(1)} %pad_add_fusion.refs_0_, f32[8,128]{1,0:T(8,128)S(1)} %broadcast_in_dim.12.refs_1_, bf16[6,512,1536]{2,1,0:T(8,128)(2,1)} %refs_3_.11, bf16[6,512,1536]{2,1,0:T(8,128)(2,1)} %collective-permute-done.refs_3_.refs_4_, ...), custom_call_target="tpu_custom_call" | custom-call | bytes 1024 | tf_op jit(solution)/shard_map/pairs_for_chip/pallas_call | solution.py:31
  33.2 40.8 %collective-permute-done.2.refs_2_ = bf16[2,512,1536]{2,1,0:T(8,128)(2,1)S(1)} collective-permute-done((bf16[2,512,1536]{2,1,0:T(8,128)(2,1)}, bf16[2,512,1536]{2,1,0:T(8,128)(2,1)S(1)}, u32[]{:S(2)}, u32[]{:S(2)}) %collective-permute-start.2) | collective-permute-done | bytes 3145760 | tf_op jit(solution)/shard_map/ppermute | solution.py:272
  83.1 9.3 %own_amplitudes.6 = (bf16[3,512,512]{2,1,0:T(8,128)(2,1)S(1)}, f32[8,128]{1,0:T(8,128)S(1)}) custom-call(s32[2]{0:T(128)S(1)} %pad_add_fusion.refs_0_, f32[3]{0:T(128)S(1)} %dynamic-slice_add_fusion.refs_1_, f32[8,128]{1,0:T(8,128)S(1)} %get-tuple-element.72.refs_2_, bf16[6,512,1536]{2,1,0:T(8,128)(2,1)} %refs_3_.11, ...), custom_call_target="tpu_custom_call" | custom-call | bytes 1024 | tf_op jit(solution)/shard_map/own_amplitudes/pallas_call | solution.py:31
  96.2 8.7 %pairs_for_chip.7 = (bf16[3,512,512]{2,1,0:T(8,128)(2,1)S(1)}, f32[8,128]{1,0:T(8,128)S(1)}) custom-call(s32[2]{0:T(128)S(1)} %pad_add_fusion.refs_0_, f32[8,128]{1,0:T(8,128)S(1)} %get-tuple-element.76.refs_1_, bf16[6,512,1536]{2,1,0:T(8,128)(2,1)} %refs_3_.11, bf16[6,512,1536]{2,1,0:T(8,128)(2,1)} %collective-permute-done.refs_3_.refs_4_, ...), custom_call_target="tpu_custom_call" | custom-call | bytes 1024 | tf_op jit(solution)/shard_map/pairs_for_chip/pallas_call | solution.py:31
  105.2 26.0 %collective-permute-done.6.refs_3_ = bf16[3,512,512]{2,1,0:T(8,128)(2,1)} collective-permute-done((bf16[3,512,512]{2,1,0:T(8,128)(2,1)}, bf16[3,512,512]{2,1,0:T(8,128)(2,1)}, u32[]{:S(2)}, u32[]{:S(2)}) %collective-permute-start.6) | collective-permute-done | bytes 1572896 | tf_op jit(solution)/shard_map/ppermute | solution.py:269
  131.2 15.7 %chip_gamma_1_0.1 = (f32[3,512,1536]{2,1,0:T(8,128)S(1)}, f32[3,512,1536]{2,1,0:T(8,128)}, f32[8,128]{1,0:T(8,128)S(1)}) custom-call(s32[2]{0:T(128)S(1)} %pad_add_fusion.refs_0_, f32[8,128]{1,0:T(8,128)S(1)} %get-tuple-element.78.refs_1_, bf16[3,512,512]{2,1,0:T(8,128)(2,1)} %get-tuple-element.79.refs_2_, ...), custom_call_target="tpu_custom_call" | custom-call | bytes 1024 | tf_op jit(solution)/shard_map/chip_gamma_1_0/pallas_call | solution.py:31
  157.4 7.6 %collective-permute-done.9.refs_7_ = bf16[3,512,512]{2,1,0:T(8,128)(2,1)S(1)} collective-permute-done((bf16[3,512,512]{2,1,0:T(8,128)(2,1)S(1)}, bf16[3,512,512]{2,1,0:T(8,128)(2,1)S(1)}, u32[]{:S(2)}, u32[]{:S(2)}) %collective-permute-start.9) | collective-permute-done | bytes 1572896 | tf_op jit(solution)/shard_map/ppermute | solution.py:269
  165.0 8.5 %own_amplitudes.7 = (bf16[3,512,512]{2,1,0:T(8,128)(2,1)S(1)}, f32[8,128]{1,0:T(8,128)S(1)}) custom-call(s32[2]{0:T(128)S(1)} %pad_add_fusion.refs_0_, f32[3]{0:T(128)S(1)} %dynamic-slice_add_fusion.refs_1_, f32[8,128]{1,0:T(8,128)S(1)} %get-tuple-element.82.refs_2_, bf16[6,512,1536]{2,1,0:T(8,128)(2,1)} %refs_3_.11, ...), custom_call_target="tpu_custom_call" | custom-call | bytes 1024 | tf_op jit(solution)/shard_map/own_amplitudes/pallas_call | solution.py:31
  173.6 9.4 %pairs_for_chip.8 = (bf16[3,512,512]{2,1,0:T(8,128)(2,1)}, f32[8,128]{1,0:T(8,128)S(1)}) custom-call(s32[2]{0:T(128)S(1)} %pad_add_fusion.refs_0_, f32[8,128]{1,0:T(8,128)S(1)} %get-tuple-element.84.refs_1_, bf16[6,512,1536]{2,1,0:T(8,128)(2,1)} %refs_3_.11, bf16[6,512,1536]{2,1,0:T(8,128)(2,1)} %collective-permute-done.refs_3_.refs_4_, ...), custom_call_target="tpu_custom_call" | custom-call | bytes 1024 | tf_op jit(solution)/shard_map/pairs_for_chip/pallas_call | solution.py:31
  185.3 5.1 %collective-permute-start.25 = (bf16[3,512,512]{2,1,0:T(8,128)(2,1)}, bf16[3,512,512]{2,1,0:T(8,128)(2,1)S(1)}, u32[]{:S(2)}, u32[]{:S(2)}) collective-permute-start(bf16[3,512,512]{2,1,0:T(8,128)(2,1)} %copy-done.11), channel_id=1, source_target_pairs={{0,4},{4,0},{8,12},{12,8},{1,5},{5,1},{9,13},{13,9},{2,6},{6,2},{1... | collective-permute-start | bytes 4718600 | tf_op jit(solution)/shard_map/ppermute | solution.py:272
  190.4 28.3 %collective-permute-done.14.refs_8_ = bf16[3,512,512]{2,1,0:T(8,128)(2,1)} collective-permute-done((bf16[3,512,512]{2,1,0:T(8,128)(2,1)}, bf16[3,512,512]{2,1,0:T(8,128)(2,1)}, u32[]{:S(2)}, u32[]{:S(2)}) %collective-permute-start.14) | collective-permute-done | bytes 1572896 | tf_op jit(solution)/shard_map/ppermute | solution.py:269
  218.6 9.2 %own_amplitudes.8 = (bf16[3,512,512]{2,1,0:T(8,128)(2,1)S(1)}, f32[8,128]{1,0:T(8,128)S(1)}) custom-call(s32[2]{0:T(128)S(1)} %pad_add_fusion.refs_0_, f32[3]{0:T(128)S(1)} %dynamic-slice_add_fusion.refs_1_, f32[8,128]{1,0:T(8,128)S(1)} %get-tuple-element.87.refs_2_, bf16[6,512,1536]{2,1,0:T(8,128)(2,1)} %refs_3_.11, ...), custom_call_target="tpu_custom_call" | custom-call | bytes 1024 | tf_op jit(solution)/shard_map/own_amplitudes/pallas_call | solution.py:31
  257.0 4.3 %own_amplitudes.9 = (bf16[1,512,512]{2,1,0:T(8,128)(2,1)S(1)}, f32[8,128]{1,0:T(8,128)S(1)}) custom-call(s32[2]{0:T(128)S(1)} %pad_add_fusion.refs_0_, f32[3]{0:T(128)S(1)} %dynamic-slice_add_fusion.refs_1_, f32[8,128]{1,0:T(8,128)S(1)} %get-tuple-element.96.refs_2_, bf16[6,512,1536]{2,1,0:T(8,128)(2,1)} %refs_3_.11, ...), custom_call_target="tpu_custom_call" | custom-call | bytes 1024 | tf_op jit(solution)/shard_map/own_amplitudes/pallas_call | solution.py:31
  264.1 15.5 %collective-permute-done.26.refs_10_ = bf16[1,512,512]{2,1,0:T(8,128)(2,1)S(1)} collective-permute-done((bf16[1,512,512]{2,1,0:T(8,128)(2,1)S(1)}, bf16[1,512,512]{2,1,0:T(8,128)(2,1)S(1)}, u32[]{:S(2)}, u32[]{:S(2)}) %collective-permute-start.26) | collective-permute-done | bytes 524320 | tf_op jit(solution)/shard_map/ppermute | solution.py:269
  283.9 4.3 %own_amplitudes.11 = (bf16[1,512,512]{2,1,0:T(8,128)(2,1)S(1)}, f32[8,128]{1,0:T(8,128)S(1)}) custom-call(s32[2]{0:T(128)S(1)} %pad_add_fusion.refs_0_, f32[3]{0:T(128)S(1)} %dynamic-slice_add_fusion.refs_1_, f32[8,128]{1,0:T(8,128)S(1)} %get-tuple-element.102.refs_2_, bf16[6,512,1536]{2,1,0:T(8,128)(2,1)} %refs_3_.11, ...), custom_call_target="tpu_custom_call" | custom-call | bytes 1024 | tf_op jit(solution)/shard_map/own_amplitudes/pallas_call | solution.py:31
  288.2 17.4 %collective-permute-done.28.refs_3_ = bf16[3,512,512]{2,1,0:T(8,128)(2,1)S(1)} collective-permute-done((bf16[3,512,512]{2,1,0:T(8,128)(2,1)S(1)}, bf16[3,512,512]{2,1,0:T(8,128)(2,1)S(1)}, u32[]{:S(2)}, u32[]{:S(2)}) %collective-permute-start.28) | collective-permute-done | bytes 1572896 | tf_op jit(solution)/shard_map/ppermute | solution.py:272
  311.4 11.1 %collective-permute-done.29.refs_3_ = bf16[1,512,512]{2,1,0:T(8,128)(2,1)S(1)} collective-permute-done((bf16[1,512,512]{2,1,0:T(8,128)(2,1)S(1)}, bf16[1,512,512]{2,1,0:T(8,128)(2,1)S(1)}, u32[]{:S(2)}, u32[]{:S(2)}) %collective-permute-start.29) | collective-permute-done | bytes 524320 | tf_op jit(solution)/shard_map/ppermute | solution.py:272
  323.7 20.0 %chip_gamma_1_2.1 = (f32[3,512,1536]{2,1,0:T(8,128)}, f32[3,512,1536]{2,1,0:T(8,128)}, f32[8,128]{1,0:T(8,128)S(1)}) custom-call(s32[2]{0:T(128)S(1)} %pad_add_fusion.refs_0_, f32[8,128]{1,0:T(8,128)S(1)} %get-tuple-element.108.refs_1_, bf16[3,512,512]{2,1,0:T(8,128)(2,1)S(1)} %get-tuple-element.109.refs_2_, ...), custom_call_target="tpu_custom_call", output_to_operand_aliasing={{0}: (6, {}), {1}: (7, {})} | custom-call | bytes 1024 | tf_op jit(solution)/shard_map/chip_gamma_1_2/pallas_call | solution.py:31
  347.9 10.3 %collective-permute-done.33.refs_10_ = bf16[1,512,512]{2,1,0:T(8,128)(2,1)S(1)} collective-permute-done((bf16[1,512,512]{2,1,0:T(8,128)(2,1)S(1)}, bf16[1,512,512]{2,1,0:T(8,128)(2,1)S(1)}, u32[]{:S(2)}, u32[]{:S(2)}) %collective-permute-start.33) | collective-permute-done | bytes 524320 | tf_op jit(solution)/shard_map/ppermute | solution.py:269
  358.2 11.3 %last_gamma_2.3 = (f32[6,512,1536]{2,1,0:T(8,128)}, bf16[1,512,1536]{2,1,0:T(8,128)(2,1)S(1)}, f32[8,128]{1,0:T(8,128)S(1)}) custom-call(s32[2]{0:T(128)S(1)} %pad_add_fusion.refs_0_, f32[8,128]{1,0:T(8,128)S(1)} %get-tuple-element.114.refs_1_, bf16[3,512,512]{2,1,0:T(8,128)(2,1)S(1)} %get-tuple-element.115.refs_2_, ...), custom_call_target="tpu_custom_call" | custom-call | bytes 1024 | tf_op jit(solution)/shard_map/last_gamma_2/pallas_call | solution.py:31
  369.6 11.3 %last_gamma_2.4 = (f32[6,512,1536]{2,1,0:T(8,128)}, bf16[1,512,1536]{2,1,0:T(8,128)(2,1)S(1)}, f32[8,128]{1,0:T(8,128)S(1)}) custom-call(s32[2]{0:T(128)S(1)} %pad_add_fusion.refs_0_, f32[8,128]{1,0:T(8,128)S(1)} %get-tuple-element.119.refs_1_, bf16[3,512,512]{2,1,0:T(8,128)(2,1)S(1)} %get-tuple-element.115.refs_2_, ...), custom_call_target="tpu_custom_call", output_to_operand_aliasing={{0}: (22, {})} | custom-call | bytes 1024 | tf_op jit(solution)/shard_map/last_gamma_2/pallas_call | solution.py:31
  385.0 8.3 %collective-permute-done.36.refs_10_ = bf16[1,512,512]{2,1,0:T(8,128)(2,1)S(1)} collective-permute-done((bf16[1,512,512]{2,1,0:T(8,128)(2,1)S(1)}, bf16[1,512,512]{2,1,0:T(8,128)(2,1)S(1)}, u32[]{:S(2)}, u32[]{:S(2)}) %collective-permute-start.36) | collective-permute-done | bytes 524320 | tf_op jit(solution)/shard_map/ppermute | solution.py:269
  393.3 11.3 %last_gamma_2.5 = (f32[6,512,1536]{2,1,0:T(8,128)}, bf16[1,512,1536]{2,1,0:T(8,128)(2,1)S(1)}, f32[8,128]{1,0:T(8,128)S(1)}) custom-call(s32[2]{0:T(128)S(1)} %pad_add_fusion.refs_0_, f32[8,128]{1,0:T(8,128)S(1)} %get-tuple-element.124.refs_1_, bf16[3,512,512]{2,1,0:T(8,128)(2,1)S(1)} %get-tuple-element.115.refs_2_, ...), custom_call_target="tpu_custom_call", output_to_operand_aliasing={{0}: (22, {})} | custom-call | bytes 1024 | tf_op jit(solution)/shard_map/last_gamma_2/pallas_call | solution.py:31
  (129 shorter events, 97.4 us)
Async XLA Ops:
  0.0 19.5 %collective-permute-start = (bf16[6,512,1536]{2,1,0:T(8,128)(2,1)}, bf16[6,512,1536]{2,1,0:T(8,128)(2,1)}, u32[]{:S(2)}, u32[]{:S(2)}) collective-permute-start(bf16[6,512,1536]{2,1,0:T(8,128)(2,1)} %refs_3_.11), channel_id=1, source_target_pairs={{0,1},{1,0},{2,3},{3,2},{4,5},{5,4},{6,7},{7,6},{8,9},{9,8},{10,11... | collective-permute-start | bytes 28311560 | tf_op jit(solution)/shard_map/ppermute | solution.py:266
  0.1 19.4 %collective-permute-start.1 = (bf16[2,512,1536]{2,1,0:T(8,128)(2,1)}, bf16[2,512,1536]{2,1,0:T(8,128)(2,1)}, u32[]{:S(2)}, u32[]{:S(2)}) collective-permute-start(bf16[2,512,1536]{2,1,0:T(8,128)(2,1)} %refs_4_.3), channel_id=1, source_target_pairs={{0,1},{1,0},{2,3},{3,2},{4,5},{5,4},{6,7},{7,6},{8,9},{9,8},{10,11... | collective-permute-start | bytes 9437192 | tf_op jit(solution)/shard_map/ppermute | solution.py:266
  0.5 32.7 %collective-permute-start.3 = (bf16[2,512,1536]{2,1,0:T(8,128)(2,1)}, bf16[2,512,1536]{2,1,0:T(8,128)(2,1)}, u32[]{:S(2)}, u32[]{:S(2)}) collective-permute-start(bf16[2,512,1536]{2,1,0:T(8,128)(2,1)} %refs_4_.3), channel_id=1, source_target_pairs={{4,8},{8,4},{5,9},{9,5},{6,10},{10,6},{7,11},{11,7},{20,24},{24,20... | collective-permute-start | bytes 9437192 | tf_op jit(solution)/shard_map/ppermute | solution.py:272
  2.8 71.2 %collective-permute-start.2 = (bf16[2,512,1536]{2,1,0:T(8,128)(2,1)}, bf16[2,512,1536]{2,1,0:T(8,128)(2,1)S(1)}, u32[]{:S(2)}, u32[]{:S(2)}) collective-permute-start(bf16[2,512,1536]{2,1,0:T(8,128)(2,1)} %refs_4_.3), channel_id=1, source_target_pairs={{0,4},{4,0},{8,12},{12,8},{1,5},{5,1},{9,13},{13,9},{2,6},{6,2},{1... | collective-permute-start | bytes 9437192 | tf_op jit(solution)/shard_map/ppermute | solution.py:272
  30.8 50.3 %collective-permute-start.4 = (bf16[3,512,512]{2,1,0:T(8,128)(2,1)}, bf16[3,512,512]{2,1,0:T(8,128)(2,1)}, u32[]{:S(2)}, u32[]{:S(2)}) collective-permute-start(bf16[3,512,512]{2,1,0:T(8,128)(2,1)} %get-tuple-element.73), channel_id=1, source_target_pairs={{0,2},{1,3},{2,0},{3,1},{4,6},{5,7},{6,4},{7,5},{8,10},{9,11},{10,... | collective-permute-start | bytes 4718600 | tf_op jit(solution)/shard_map/ppermute | solution.py:269
  74.5 21.6 %collective-permute-start.5 = (bf16[2,512,1536]{2,1,0:T(8,128)(2,1)S(1)}, bf16[2,512,1536]{2,1,0:T(8,128)(2,1)}, u32[]{:S(2)}, u32[]{:S(2)}) collective-permute-start(bf16[2,512,1536]{2,1,0:T(8,128)(2,1)S(1)} %get-tuple-element.77.refs_4_.refs_5_), channel_id=1, source_target_pairs={{0,1},{1,0},{2,3},{3,2},{4,5},{5,4},{6,7},{7,6},{8,9},{9,8},{10,11... | collective-permute-start | bytes 9437192 | tf_op jit(solution)/shard_map/ppermute | solution.py:266
  76.0 74.5 %collective-permute-start.8 = (bf16[2,512,1536]{2,1,0:T(8,128)(2,1)}, bf16[2,512,1536]{2,1,0:T(8,128)(2,1)}, u32[]{:S(2)}, u32[]{:S(2)}) collective-permute-start(bf16[2,512,1536]{2,1,0:T(8,128)(2,1)} %get-tuple-element.81), channel_id=1, source_target_pairs={{4,0},{8,12},{5,1},{9,13},{6,2},{10,14},{7,3},{11,15},{20,16},{24,... | collective-permute-start | bytes 9437192 | tf_op jit(solution)/shard_map/ppermute | solution.py:272
  77.3 73.2 %collective-permute-start.7 = (bf16[2,512,1536]{2,1,0:T(8,128)(2,1)S(1)}, bf16[2,512,1536]{2,1,0:T(8,128)(2,1)}, u32[]{:S(2)}, u32[]{:S(2)}) collective-permute-start(bf16[2,512,1536]{2,1,0:T(8,128)(2,1)S(1)} %get-tuple-element.77.refs_4_.refs_5_), channel_id=1, source_target_pairs={{4,8},{8,4},{5,9},{9,5},{6,10},{10,6},{7,11},{11,7},{20,24},{24,20... | collective-permute-start | bytes 9437192 | tf_op jit(solution)/shard_map/ppermute | solution.py:272
  94.9 36.3 %collective-permute-start.6 = (bf16[3,512,512]{2,1,0:T(8,128)(2,1)}, bf16[3,512,512]{2,1,0:T(8,128)(2,1)}, u32[]{:S(2)}, u32[]{:S(2)}) collective-permute-start(bf16[3,512,512]{2,1,0:T(8,128)(2,1)} %get-tuple-element.79.refs_2_), channel_id=1, source_target_pairs={{0,2},{1,3},{2,0},{3,1},{4,6},{5,7},{6,4},{7,5},{8,10},{9,11},{10,... | collective-permute-start | bytes 4718600 | tf_op jit(solution)/shard_map/ppermute | solution.py:269
  104.9 60.0 %collective-permute-start.9 = (bf16[3,512,512]{2,1,0:T(8,128)(2,1)S(1)}, bf16[3,512,512]{2,1,0:T(8,128)(2,1)S(1)}, u32[]{:S(2)}, u32[]{:S(2)}) collective-permute-start(bf16[3,512,512]{2,1,0:T(8,128)(2,1)S(1)} %get-tuple-element.83), channel_id=1, source_target_pairs={{0,2},{1,3},{2,0},{3,1},{4,6},{5,7},{6,4},{7,5},{8,10},{9,11},{10,... | collective-permute-start | bytes 4718600 | tf_op jit(solution)/shard_map/ppermute | solution.py:269
  151.0 76.8 %collective-permute-start.15 = (bf16[2,512,1536]{2,1,0:T(8,128)(2,1)}, bf16[2,512,1536]{2,1,0:T(8,128)(2,1)}, u32[]{:S(2)}, u32[]{:S(2)}) collective-permute-start(bf16[2,512,1536]{2,1,0:T(8,128)(2,1)} %get-tuple-element.85), channel_id=1, source_target_pairs={{4,0},{8,12},{5,1},{9,13},{6,2},{10,14},{7,3},{11,15},{20,16},{24,... | collective-permute-start | bytes 9437192 | tf_op jit(solution)/shard_map/ppermute | solution.py:272
  183.0 35.6 %collective-permute-start.14 = (bf16[3,512,512]{2,1,0:T(8,128)(2,1)}, bf16[3,512,512]{2,1,0:T(8,128)(2,1)}, u32[]{:S(2)}, u32[]{:S(2)}) collective-permute-start(bf16[3,512,512]{2,1,0:T(8,128)(2,1)} %get-tuple-element.88), channel_id=1, source_target_pairs={{0,2},{1,3},{2,0},{3,1},{4,6},{5,7},{6,4},{7,5},{8,10},{9,11},{10,... | collective-permute-start | bytes 4718600 | tf_op jit(solution)/shard_map/ppermute | solution.py:269
  185.3 76.0 %collective-permute-start.25 = (bf16[3,512,512]{2,1,0:T(8,128)(2,1)}, bf16[3,512,512]{2,1,0:T(8,128)(2,1)S(1)}, u32[]{:S(2)}, u32[]{:S(2)}) collective-permute-start(bf16[3,512,512]{2,1,0:T(8,128)(2,1)} %copy-done.11), channel_id=1, source_target_pairs={{0,4},{4,0},{8,12},{12,8},{1,5},{5,1},{9,13},{13,9},{2,6},{6,2},{1... | collective-permute-start | bytes 4718600 | tf_op jit(solution)/shard_map/ppermute | solution.py:272
  232.9 72.7 %collective-permute-start.28 = (bf16[3,512,512]{2,1,0:T(8,128)(2,1)S(1)}, bf16[3,512,512]{2,1,0:T(8,128)(2,1)S(1)}, u32[]{:S(2)}, u32[]{:S(2)}) collective-permute-start(bf16[3,512,512]{2,1,0:T(8,128)(2,1)S(1)} %get-tuple-element.105.refs_2_), channel_id=1, source_target_pairs={{0,8},{4,12},{8,0},{12,4},{1,9},{5,13},{9,1},{13,5},{2,10},{6,14},... | collective-permute-start | bytes 4718600 | tf_op jit(solution)/shard_map/ppermute | solution.py:272
  254.3 29.6 %collective-permute-start.27 = (bf16[1,512,512]{2,1,0:T(8,128)(2,1)S(1)}, bf16[1,512,512]{2,1,0:T(8,128)(2,1)S(1)}, u32[]{:S(2)}, u32[]{:S(2)}) collective-permute-start(bf16[1,512,512]{2,1,0:T(8,128)(2,1)S(1)} %get-tuple-element.103), channel_id=1, source_target_pairs={{0,2},{1,3},{2,0},{3,1},{4,6},{5,7},{6,4},{7,5},{8,10},{9,11},{10,... | collective-permute-start | bytes 1572872 | tf_op jit(solution)/shard_map/ppermute | solution.py:269
  254.6 25.0 %collective-permute-start.26 = (bf16[1,512,512]{2,1,0:T(8,128)(2,1)S(1)}, bf16[1,512,512]{2,1,0:T(8,128)(2,1)S(1)}, u32[]{:S(2)}, u32[]{:S(2)}) collective-permute-start(bf16[1,512,512]{2,1,0:T(8,128)(2,1)S(1)} %get-tuple-element.101), channel_id=1, source_target_pairs={{0,2},{1,3},{2,0},{3,1},{4,6},{5,7},{6,4},{7,5},{8,10},{9,11},{10,... | collective-permute-start | bytes 1572872 | tf_op jit(solution)/shard_map/ppermute | solution.py:269
  262.8 60.8 %collective-permute-start.30 = (bf16[3,512,512]{2,1,0:T(8,128)(2,1)S(1)}, bf16[3,512,512]{2,1,0:T(8,128)(2,1)S(1)}, u32[]{:S(2)}, u32[]{:S(2)}) collective-permute-start(bf16[3,512,512]{2,1,0:T(8,128)(2,1)S(1)} %get-tuple-element.109.refs_2_), channel_id=1, source_target_pairs={{0,2},{1,3},{2,0},{3,1},{4,6},{5,7},{6,4},{7,5},{8,10},{9,11},{10,... | collective-permute-start | bytes 4718600 | tf_op jit(solution)/shard_map/ppermute | solution.py:269
  306.9 51.3 %collective-permute-start.32 = (bf16[3,512,512]{2,1,0:T(8,128)(2,1)S(1)}, bf16[3,512,512]{2,1,0:T(8,128)(2,1)S(1)}, u32[]{:S(2)}, u32[]{:S(2)}) collective-permute-start(bf16[3,512,512]{2,1,0:T(8,128)(2,1)S(1)} %get-tuple-element.115.refs_2_), channel_id=1, source_target_pairs={{0,2},{1,3},{2,0},{3,1},{4,6},{5,7},{6,4},{7,5},{8,10},{9,11},{10,... | collective-permute-start | bytes 4718600 | tf_op jit(solution)/shard_map/ppermute | solution.py:269
  310.3 33.4 %collective-permute-start.31 = (bf16[1,512,512]{2,1,0:T(8,128)(2,1)S(1)}, bf16[1,512,512]{2,1,0:T(8,128)(2,1)S(1)}, u32[]{:S(2)}, u32[]{:S(2)}) collective-permute-start(bf16[1,512,512]{2,1,0:T(8,128)(2,1)S(1)} %get-tuple-element.113.refs_2_), channel_id=1, source_target_pairs={{0,12},{4,8},{8,4},{12,0},{1,13},{5,9},{9,5},{13,1},{2,14},{6,10},... | collective-permute-start | bytes 1572872 | tf_op jit(solution)/shard_map/ppermute | solution.py:272
  323.3 34.9 %collective-permute-start.33 = (bf16[1,512,512]{2,1,0:T(8,128)(2,1)S(1)}, bf16[1,512,512]{2,1,0:T(8,128)(2,1)S(1)}, u32[]{:S(2)}, u32[]{:S(2)}) collective-permute-start(bf16[1,512,512]{2,1,0:T(8,128)(2,1)S(1)} %get-tuple-element.116.refs_9_), channel_id=1, source_target_pairs={{0,2},{1,3},{2,0},{3,1},{4,6},{5,7},{6,4},{7,5},{8,10},{9,11},{10,... | collective-permute-start | bytes 1572872 | tf_op jit(solution)/shard_map/ppermute | solution.py:269
  344.5 25.1 %collective-permute-start.34 = (bf16[1,512,512]{2,1,0:T(8,128)(2,1)S(1)}, bf16[1,512,512]{2,1,0:T(8,128)(2,1)S(1)}, u32[]{:S(2)}, u32[]{:S(2)}) collective-permute-start(bf16[1,512,512]{2,1,0:T(8,128)(2,1)S(1)} %get-tuple-element.120.refs_9_), channel_id=1, source_target_pairs={{0,2},{1,3},{2,0},{3,1},{4,6},{5,7},{6,4},{7,5},{8,10},{9,11},{10,... | collective-permute-start | bytes 1572872 | tf_op jit(solution)/shard_map/ppermute | solution.py:269
  345.8 35.1 %collective-permute-start.35 = (bf16[1,512,512]{2,1,0:T(8,128)(2,1)S(1)}, bf16[1,512,512]{2,1,0:T(8,128)(2,1)S(1)}, u32[]{:S(2)}, u32[]{:S(2)}) collective-permute-start(bf16[1,512,512]{2,1,0:T(8,128)(2,1)S(1)} %get-tuple-element.123.refs_2_), channel_id=1, source_target_pairs={{0,12},{4,8},{8,4},{12,0},{1,13},{5,9},{9,5},{13,1},{2,14},{6,10},... | collective-permute-start | bytes 1572872 | tf_op jit(solution)/shard_map/ppermute | solution.py:272
  382.8 24.5 %collective-permute-start.37 = (bf16[1,512,1536]{2,1,0:T(8,128)(2,1)S(1)}, bf16[1,512,1536]{2,1,0:T(8,128)(2,1)S(1)}, u32[]{:S(2)}, u32[]{:S(2)}) collective-permute-start(bf16[1,512,1536]{2,1,0:T(8,128)(2,1)S(1)} %get-tuple-element.128), channel_id=1, source_target_pairs={{0,1},{1,0},{2,3},{3,2},{4,5},{5,4},{6,7},{7,6},{8,9},{9,8},{10,11... | collective-permute-start | bytes 4718600 | tf_op jit(solution)/shard_map/ppermute | solution.py:266
  385.0 24.6 %collective-permute-start.38 = (bf16[1,512,1536]{2,1,0:T(8,128)(2,1)S(1)}, bf16[1,512,1536]{2,1,0:T(8,128)(2,1)S(1)}, u32[]{:S(2)}, u32[]{:S(2)}) collective-permute-start(bf16[1,512,1536]{2,1,0:T(8,128)(2,1)S(1)} %get-tuple-element.131), channel_id=1, source_target_pairs={{0,1},{1,0},{2,3},{3,2},{4,5},{5,4},{6,7},{7,6},{8,9},{9,8},{10,11... | collective-permute-start | bytes 4718600 | tf_op jit(solution)/shard_map/ppermute | solution.py:266
  (32 other events, 373.6 us)

commit v9 on v8

--- a/solution.py
+++ b/solution.py
@@ -237,8 +237,8 @@
 ORDER = (
     "chip_0", "hop_1", "own_0", "combine_0", "chip_1", "gamma_0", "hop_2", "own_1", "chip_2", "own_2", "hop_3",
     "keep_3", "chip_3_0", "chip_3_1", "chip_3_2", "own_3_0", "combine_1", "own_3_1", "own_3_2", "combine_2",
-    "combine_3_0", "gamma_1", "combine_3_1", "last_0", "last_1", "combine_3_2", "last_2", "place_0", "place_1",
-    "place_2",
+    "receive_1", "gamma_1", "combine_3_0", "receive_2", "combine_3_1", "last_0", "combine_3_2", "last_1", "last_2",
+    "place_0", "place_1", "place_2",
 )
 PIECES_2, PIECES_3, HALVES, SPLIT_1, SPLIT_2 = 2, 4, 1, False, False
 GROUPS = ((0, 1), (1, 1), (2, 1))

time: 421 us -> 412 us (0.979)
  waiting for transfers between devices: 181 us -> 170 us
    ppermute x10, waiting for transfers between devices: 69.4 us -> 58.3 us  [along(): return lax.ppermute(values, 'row', steps)]
    pallas_call x30 -> x32, Pallas kernels: 167 us -> 168 us  [call(): pl.pallas_call(body, out_shape=(*out, TOKEN), grid_spec=pltpu.PrefetchSca...]
  transfers between devices with their start and end apart: 40 -> 40, of which waited for: 12 -> 12; matrix products, arithmetic and copies ran while one was open for 2% -> 2% of each run, Pallas kernels for 39% -> 41%
where the time goes in v9:
time: 412 us; the launch traced here: 404 us
  waiting for transfers between devices  170 us (41%)
  Pallas kernels  168 us (41%)
  starting transfers between devices  50.1 us (12%)
  local copies, waits for them, and re-layouts  9.81 us (2%)
  other arithmetic  5.18 us (1%)
    pallas_call x32, Pallas kernels, call(): pl.pallas_call(body, out_shape=(*out, TOKEN), grid_spec=pltpu.PrefetchSca...  168 us
    ppermute x12, waiting for transfers between devices, to_chip(): return lax.ppermute(values, 'col', [(q, q ^ 2) for q in range(4)])  98 us
    ppermute x10, waiting for transfers between devices, along(): return lax.ppermute(values, 'row', steps)  58.3 us
    ppermute x10, starting transfers between devices, along(): return lax.ppermute(values, 'row', steps)  25.3 us
    ppermute x18, waiting for transfers between devices, to_core(): return lax.ppermute(values, 'col', [(q, q ^ 1) for q in range(4)])  14.1 us
    ppermute x12, starting transfers between devices, to_chip(): return lax.ppermute(values, 'col', [(q, q ^ 2) for q in range(4)])  14.1 us
    ppermute x18, starting transfers between devices, to_core(): return lax.ppermute(values, 'col', [(q, q ^ 1) for q in range(4)])  10.7 us
  transfers between devices with their start and end apart: 40, of which 12 were waited for; matrix products, arithmetic and copies ran while one was open for 2% of the time, Pallas kernels for 41%

profile of v9, /device:TPU:1, one launch (start us, length us, event | category | flops | bytes accessed | tf_op | source)
XLA Modules:
  0.0 403.7 jit_solution(4818655392324039978)
XLA Ops:
  6.2 13.3 %collective-permute-done.1.refs_5_.refs_6_ = bf16[2,512,1536]{2,1,0:T(8,128)(2,1)} collective-permute-done((bf16[2,512,1536]{2,1,0:T(8,128)(2,1)}, bf16[2,512,1536]{2,1,0:T(8,128)(2,1)}, u32[]{:S(2)}, u32[]{:S(2)}) %collective-permute-start.1) | collective-permute-done | bytes 3145760 | tf_op jit(solution)/shard_map/ppermute | solution.py:266
  21.4 9.4 %pairs_for_chip.6 = (bf16[3,512,512]{2,1,0:T(8,128)(2,1)}, f32[8,128]{1,0:T(8,128)S(1)}) custom-call(s32[2]{0:T(128)S(1)} %pad_add_fusion.refs_0_, f32[8,128]{1,0:T(8,128)S(1)} %broadcast_in_dim.12.refs_1_, bf16[6,512,1536]{2,1,0:T(8,128)(2,1)} %refs_3_.11, bf16[6,512,1536]{2,1,0:T(8,128)(2,1)} %collective-permute-done.refs_3_.refs_4_, ...), custom_call_target="tpu_custom_call" | custom-call | bytes 1024 | tf_op jit(solution)/shard_map/pairs_for_chip/pallas_call | solution.py:31
  33.2 40.8 %collective-permute-done.2.refs_2_ = bf16[2,512,1536]{2,1,0:T(8,128)(2,1)S(1)} collective-permute-done((bf16[2,512,1536]{2,1,0:T(8,128)(2,1)}, bf16[2,512,1536]{2,1,0:T(8,128)(2,1)S(1)}, u32[]{:S(2)}, u32[]{:S(2)}) %collective-permute-start.2) | collective-permute-done | bytes 3145760 | tf_op jit(solution)/shard_map/ppermute | solution.py:272
  82.9 9.3 %own_amplitudes.6 = (bf16[3,512,512]{2,1,0:T(8,128)(2,1)S(1)}, f32[8,128]{1,0:T(8,128)S(1)}) custom-call(s32[2]{0:T(128)S(1)} %pad_add_fusion.refs_0_, f32[3]{0:T(128)S(1)} %dynamic-slice_add_fusion.refs_1_, f32[8,128]{1,0:T(8,128)S(1)} %get-tuple-element.76.refs_2_, bf16[6,512,1536]{2,1,0:T(8,128)(2,1)} %refs_3_.11, ...), custom_call_target="tpu_custom_call" | custom-call | bytes 1024 | tf_op jit(solution)/shard_map/own_amplitudes/pallas_call | solution.py:31
  96.0 8.7 %pairs_for_chip.7 = (bf16[3,512,512]{2,1,0:T(8,128)(2,1)S(1)}, f32[8,128]{1,0:T(8,128)S(1)}) custom-call(s32[2]{0:T(128)S(1)} %pad_add_fusion.refs_0_, f32[8,128]{1,0:T(8,128)S(1)} %get-tuple-element.80.refs_1_, bf16[6,512,1536]{2,1,0:T(8,128)(2,1)} %refs_3_.11, bf16[6,512,1536]{2,1,0:T(8,128)(2,1)} %collective-permute-done.refs_3_.refs_4_, ...), custom_call_target="tpu_custom_call" | custom-call | bytes 1024 | tf_op jit(solution)/shard_map/pairs_for_chip/pallas_call | solution.py:31
  105.1 26.0 %collective-permute-done.6.refs_3_ = bf16[3,512,512]{2,1,0:T(8,128)(2,1)} collective-permute-done((bf16[3,512,512]{2,1,0:T(8,128)(2,1)}, bf16[3,512,512]{2,1,0:T(8,128)(2,1)}, u32[]{:S(2)}, u32[]{:S(2)}) %collective-permute-start.6) | collective-permute-done | bytes 1572896 | tf_op jit(solution)/shard_map/ppermute | solution.py:269
  131.1 15.7 %chip_gamma_1_0.1 = (f32[3,512,1536]{2,1,0:T(8,128)S(1)}, f32[3,512,1536]{2,1,0:T(8,128)}, f32[8,128]{1,0:T(8,128)S(1)}) custom-call(s32[2]{0:T(128)S(1)} %pad_add_fusion.refs_0_, f32[8,128]{1,0:T(8,128)S(1)} %get-tuple-element.82.refs_1_, bf16[3,512,512]{2,1,0:T(8,128)(2,1)} %get-tuple-element.83.refs_2_, ...), custom_call_target="tpu_custom_call" | custom-call | bytes 1024 | tf_op jit(solution)/shard_map/chip_gamma_1_0/pallas_call | solution.py:31
  157.2 7.6 %collective-permute-done.9.refs_7_ = bf16[3,512,512]{2,1,0:T(8,128)(2,1)S(1)} collective-permute-done((bf16[3,512,512]{2,1,0:T(8,128)(2,1)S(1)}, bf16[3,512,512]{2,1,0:T(8,128)(2,1)S(1)}, u32[]{:S(2)}, u32[]{:S(2)}) %collective-permute-start.9) | collective-permute-done | bytes 1572896 | tf_op jit(solution)/shard_map/ppermute | solution.py:269
  164.8 8.5 %own_amplitudes.7 = (bf16[3,512,512]{2,1,0:T(8,128)(2,1)S(1)}, f32[8,128]{1,0:T(8,128)S(1)}) custom-call(s32[2]{0:T(128)S(1)} %pad_add_fusion.refs_0_, f32[3]{0:T(128)S(1)} %dynamic-slice_add_fusion.refs_1_, f32[8,128]{1,0:T(8,128)S(1)} %get-tuple-element.86.refs_2_, bf16[6,512,1536]{2,1,0:T(8,128)(2,1)} %refs_3_.11, ...), custom_call_target="tpu_custom_call" | custom-call | bytes 1024 | tf_op jit(solution)/shard_map/own_amplitudes/pallas_call | solution.py:31
  173.4 9.4 %pairs_for_chip.8 = (bf16[3,512,512]{2,1,0:T(8,128)(2,1)}, f32[8,128]{1,0:T(8,128)S(1)}) custom-call(s32[2]{0:T(128)S(1)} %pad_add_fusion.refs_0_, f32[8,128]{1,0:T(8,128)S(1)} %get-tuple-element.88.refs_1_, bf16[6,512,1536]{2,1,0:T(8,128)(2,1)} %refs_3_.11, bf16[6,512,1536]{2,1,0:T(8,128)(2,1)} %collective-permute-done.refs_3_.refs_4_, ...), custom_call_target="tpu_custom_call" | custom-call | bytes 1024 | tf_op jit(solution)/shard_map/pairs_for_chip/pallas_call | solution.py:31
  185.2 5.0 %collective-permute-start.25 = (bf16[3,512,512]{2,1,0:T(8,128)(2,1)}, bf16[3,512,512]{2,1,0:T(8,128)(2,1)S(1)}, u32[]{:S(2)}, u32[]{:S(2)}) collective-permute-start(bf16[3,512,512]{2,1,0:T(8,128)(2,1)} %copy-done.11), channel_id=1, source_target_pairs={{0,4},{4,0},{8,12},{12,8},{1,5},{5,1},{9,13},{13,9},{2,6},{6,2},{1... | collective-permute-start | bytes 4718600 | tf_op jit(solution)/shard_map/ppermute | solution.py:272
  190.2 28.3 %collective-permute-done.14.refs_8_ = bf16[3,512,512]{2,1,0:T(8,128)(2,1)} collective-permute-done((bf16[3,512,512]{2,1,0:T(8,128)(2,1)}, bf16[3,512,512]{2,1,0:T(8,128)(2,1)}, u32[]{:S(2)}, u32[]{:S(2)}) %collective-permute-start.14) | collective-permute-done | bytes 1572896 | tf_op jit(solution)/shard_map/ppermute | solution.py:269
  218.5 9.2 %own_amplitudes.8 = (bf16[3,512,512]{2,1,0:T(8,128)(2,1)S(1)}, f32[8,128]{1,0:T(8,128)S(1)}) custom-call(s32[2]{0:T(128)S(1)} %pad_add_fusion.refs_0_, f32[3]{0:T(128)S(1)} %dynamic-slice_add_fusion.refs_1_, f32[8,128]{1,0:T(8,128)S(1)} %get-tuple-element.91.refs_2_, bf16[6,512,1536]{2,1,0:T(8,128)(2,1)} %refs_3_.11, ...), custom_call_target="tpu_custom_call" | custom-call | bytes 1024 | tf_op jit(solution)/shard_map/own_amplitudes/pallas_call | solution.py:31
  256.9 4.3 %own_amplitudes.9 = (bf16[1,512,512]{2,1,0:T(8,128)(2,1)S(1)}, f32[8,128]{1,0:T(8,128)S(1)}) custom-call(s32[2]{0:T(128)S(1)} %pad_add_fusion.refs_0_, f32[3]{0:T(128)S(1)} %dynamic-slice_add_fusion.refs_1_, f32[8,128]{1,0:T(8,128)S(1)} %get-tuple-element.100.refs_2_, bf16[6,512,1536]{2,1,0:T(8,128)(2,1)} %refs_3_.11, ...), custom_call_target="tpu_custom_call" | custom-call | bytes 1024 | tf_op jit(solution)/shard_map/own_amplitudes/pallas_call | solution.py:31
  263.9 15.5 %collective-permute-done.26.refs_10_ = bf16[1,512,512]{2,1,0:T(8,128)(2,1)S(1)} collective-permute-done((bf16[1,512,512]{2,1,0:T(8,128)(2,1)S(1)}, bf16[1,512,512]{2,1,0:T(8,128)(2,1)S(1)}, u32[]{:S(2)}, u32[]{:S(2)}) %collective-permute-start.26) | collective-permute-done | bytes 524320 | tf_op jit(solution)/shard_map/ppermute | solution.py:269
  279.4 4.3 %own_amplitudes.10 = (bf16[1,512,512]{2,1,0:T(8,128)(2,1)S(1)}, f32[8,128]{1,0:T(8,128)S(1)}) custom-call(s32[2]{0:T(128)S(1)} %pad_add_fusion.refs_0_, f32[3]{0:T(128)S(1)} %dynamic-slice_add_fusion.refs_1_, f32[8,128]{1,0:T(8,128)S(1)} %get-tuple-element.104.refs_2_, bf16[6,512,1536]{2,1,0:T(8,128)(2,1)} %refs_3_.11, ...), custom_call_target="tpu_custom_call" | custom-call | bytes 1024 | tf_op jit(solution)/shard_map/own_amplitudes/pallas_call | solution.py:31
  283.7 4.3 %own_amplitudes.11 = (bf16[1,512,512]{2,1,0:T(8,128)(2,1)S(1)}, f32[8,128]{1,0:T(8,128)S(1)}) custom-call(s32[2]{0:T(128)S(1)} %pad_add_fusion.refs_0_, f32[3]{0:T(128)S(1)} %dynamic-slice_add_fusion.refs_1_, f32[8,128]{1,0:T(8,128)S(1)} %get-tuple-element.106.refs_2_, bf16[6,512,1536]{2,1,0:T(8,128)(2,1)} %refs_3_.11, ...), custom_call_target="tpu_custom_call" | custom-call | bytes 1024 | tf_op jit(solution)/shard_map/own_amplitudes/pallas_call | solution.py:31
  288.0 17.5 %collective-permute-done.28.refs_3_ = bf16[3,512,512]{2,1,0:T(8,128)(2,1)S(1)} collective-permute-done((bf16[3,512,512]{2,1,0:T(8,128)(2,1)S(1)}, bf16[3,512,512]{2,1,0:T(8,128)(2,1)S(1)}, u32[]{:S(2)}, u32[]{:S(2)}) %collective-permute-start.28) | collective-permute-done | bytes 1572896 | tf_op jit(solution)/shard_map/ppermute | solution.py:272
  313.7 20.1 %chip_gamma_1_2.1 = (f32[3,512,1536]{2,1,0:T(8,128)}, f32[3,512,1536]{2,1,0:T(8,128)}, f32[8,128]{1,0:T(8,128)S(1)}) custom-call(s32[2]{0:T(128)S(1)} %pad_add_fusion.refs_0_, f32[8,128]{1,0:T(8,128)S(1)} %get-tuple-element.112.refs_1_, bf16[3,512,512]{2,1,0:T(8,128)(2,1)S(1)} %get-tuple-element.111.refs_2_, ...), custom_call_target="tpu_custom_call", output_to_operand_aliasing={{0}: (6, {}), {1}: (7, {})} | custom-call | bytes 1024 | tf_op jit(solution)/shard_map/chip_gamma_1_2/pallas_call | solution.py:31
  338.0 8.9 %collective-permute-done.31.refs_2_ = bf16[3,512,512]{2,1,0:T(8,128)(2,1)S(1)} collective-permute-done((bf16[3,512,512]{2,1,0:T(8,128)(2,1)S(1)}, bf16[3,512,512]{2,1,0:T(8,128)(2,1)S(1)}, u32[]{:S(2)}, u32[]{:S(2)}) %collective-permute-start.31) | collective-permute-done | bytes 1572896 | tf_op jit(solution)/shard_map/ppermute | solution.py:269
  349.4 8.7 %collective-permute-done.33.refs_10_ = bf16[1,512,512]{2,1,0:T(8,128)(2,1)S(1)} collective-permute-done((bf16[1,512,512]{2,1,0:T(8,128)(2,1)S(1)}, bf16[1,512,512]{2,1,0:T(8,128)(2,1)S(1)}, u32[]{:S(2)}, u32[]{:S(2)}) %collective-permute-start.33) | collective-permute-done | bytes 524320 | tf_op jit(solution)/shard_map/ppermute | solution.py:269
  358.1 11.3 %last_gamma_2.3 = (f32[6,512,1536]{2,1,0:T(8,128)}, bf16[1,512,1536]{2,1,0:T(8,128)(2,1)S(1)}, f32[8,128]{1,0:T(8,128)S(1)}) custom-call(s32[2]{0:T(128)S(1)} %pad_add_fusion.refs_0_, f32[8,128]{1,0:T(8,128)S(1)} %get-tuple-element.122.refs_1_, bf16[3,512,512]{2,1,0:T(8,128)(2,1)S(1)} %get-tuple-element.119.refs_2_, ...), custom_call_target="tpu_custom_call" | custom-call | bytes 1024 | tf_op jit(solution)/shard_map/last_gamma_2/pallas_call | solution.py:31
  373.6 11.3 %last_gamma_2.4 = (f32[6,512,1536]{2,1,0:T(8,128)}, bf16[1,512,1536]{2,1,0:T(8,128)(2,1)S(1)}, f32[8,128]{1,0:T(8,128)S(1)}) custom-call(s32[2]{0:T(128)S(1)} %pad_add_fusion.refs_0_, f32[8,128]{1,0:T(8,128)S(1)} %get-tuple-element.129.refs_1_, bf16[3,512,512]{2,1,0:T(8,128)(2,1)S(1)} %get-tuple-element.119.refs_2_, ...), custom_call_target="tpu_custom_call", output_to_operand_aliasing={{0}: (22, {})} | custom-call | bytes 1024 | tf_op jit(solution)/shard_map/last_gamma_2/pallas_call | solution.py:31
  384.9 11.3 %last_gamma_2.5 = (f32[6,512,1536]{2,1,0:T(8,128)}, bf16[1,512,1536]{2,1,0:T(8,128)(2,1)S(1)}, f32[8,128]{1,0:T(8,128)S(1)}) custom-call(s32[2]{0:T(128)S(1)} %pad_add_fusion.refs_0_, f32[8,128]{1,0:T(8,128)S(1)} %get-tuple-element.132.refs_1_, bf16[3,512,512]{2,1,0:T(8,128)(2,1)S(1)} %get-tuple-element.119.refs_2_, ...), custom_call_target="tpu_custom_call", output_to_operand_aliasing={{0}: (22, {})} | custom-call | bytes 1024 | tf_op jit(solution)/shard_map/last_gamma_2/pallas_call | solution.py:31
  (131 shorter events, 94.4 us)
Async XLA Ops:
  0.0 19.5 %collective-permute-start = (bf16[6,512,1536]{2,1,0:T(8,128)(2,1)}, bf16[6,512,1536]{2,1,0:T(8,128)(2,1)}, u32[]{:S(2)}, u32[]{:S(2)}) collective-permute-start(bf16[6,512,1536]{2,1,0:T(8,128)(2,1)} %refs_3_.11), channel_id=1, source_target_pairs={{0,1},{1,0},{2,3},{3,2},{4,5},{5,4},{6,7},{7,6},{8,9},{9,8},{10,11... | collective-permute-start | bytes 28311560 | tf_op jit(solution)/shard_map/ppermute | solution.py:266
  0.1 19.4 %collective-permute-start.1 = (bf16[2,512,1536]{2,1,0:T(8,128)(2,1)}, bf16[2,512,1536]{2,1,0:T(8,128)(2,1)}, u32[]{:S(2)}, u32[]{:S(2)}) collective-permute-start(bf16[2,512,1536]{2,1,0:T(8,128)(2,1)} %refs_4_.3), channel_id=1, source_target_pairs={{0,1},{1,0},{2,3},{3,2},{4,5},{5,4},{6,7},{7,6},{8,9},{9,8},{10,11... | collective-permute-start | bytes 9437192 | tf_op jit(solution)/shard_map/ppermute | solution.py:266
  0.5 32.7 %collective-permute-start.3 = (bf16[2,512,1536]{2,1,0:T(8,128)(2,1)}, bf16[2,512,1536]{2,1,0:T(8,128)(2,1)}, u32[]{:S(2)}, u32[]{:S(2)}) collective-permute-start(bf16[2,512,1536]{2,1,0:T(8,128)(2,1)} %refs_4_.3), channel_id=1, source_target_pairs={{4,8},{8,4},{5,9},{9,5},{6,10},{10,6},{7,11},{11,7},{20,24},{24,20... | collective-permute-start | bytes 9437192 | tf_op jit(solution)/shard_map/ppermute | solution.py:272
  2.8 71.2 %collective-permute-start.2 = (bf16[2,512,1536]{2,1,0:T(8,128)(2,1)}, bf16[2,512,1536]{2,1,0:T(8,128)(2,1)S(1)}, u32[]{:S(2)}, u32[]{:S(2)}) collective-permute-start(bf16[2,512,1536]{2,1,0:T(8,128)(2,1)} %refs_4_.3), channel_id=1, source_target_pairs={{0,4},{4,0},{8,12},{12,8},{1,5},{5,1},{9,13},{13,9},{2,6},{6,2},{1... | collective-permute-start | bytes 9437192 | tf_op jit(solution)/shard_map/ppermute | solution.py:272
  30.8 50.2 %collective-permute-start.4 = (bf16[3,512,512]{2,1,0:T(8,128)(2,1)}, bf16[3,512,512]{2,1,0:T(8,128)(2,1)}, u32[]{:S(2)}, u32[]{:S(2)}) collective-permute-start(bf16[3,512,512]{2,1,0:T(8,128)(2,1)} %get-tuple-element.77), channel_id=1, source_target_pairs={{0,2},{1,3},{2,0},{3,1},{4,6},{5,7},{6,4},{7,5},{8,10},{9,11},{10,... | collective-permute-start | bytes 4718600 | tf_op jit(solution)/shard_map/ppermute | solution.py:269
  74.5 21.5 %collective-permute-start.5 = (bf16[2,512,1536]{2,1,0:T(8,128)(2,1)S(1)}, bf16[2,512,1536]{2,1,0:T(8,128)(2,1)}, u32[]{:S(2)}, u32[]{:S(2)}) collective-permute-start(bf16[2,512,1536]{2,1,0:T(8,128)(2,1)S(1)} %get-tuple-element.81.refs_4_.refs_5_), channel_id=1, source_target_pairs={{0,1},{1,0},{2,3},{3,2},{4,5},{5,4},{6,7},{7,6},{8,9},{9,8},{10,11... | collective-permute-start | bytes 9437192 | tf_op jit(solution)/shard_map/ppermute | solution.py:266
  76.0 74.4 %collective-permute-start.8 = (bf16[2,512,1536]{2,1,0:T(8,128)(2,1)}, bf16[2,512,1536]{2,1,0:T(8,128)(2,1)}, u32[]{:S(2)}, u32[]{:S(2)}) collective-permute-start(bf16[2,512,1536]{2,1,0:T(8,128)(2,1)} %get-tuple-element.85), channel_id=1, source_target_pairs={{4,0},{8,12},{5,1},{9,13},{6,2},{10,14},{7,3},{11,15},{20,16},{24,... | collective-permute-start | bytes 9437192 | tf_op jit(solution)/shard_map/ppermute | solution.py:272
  77.3 73.1 %collective-permute-start.7 = (bf16[2,512,1536]{2,1,0:T(8,128)(2,1)S(1)}, bf16[2,512,1536]{2,1,0:T(8,128)(2,1)}, u32[]{:S(2)}, u32[]{:S(2)}) collective-permute-start(bf16[2,512,1536]{2,1,0:T(8,128)(2,1)S(1)} %get-tuple-element.81.refs_4_.refs_5_), channel_id=1, source_target_pairs={{4,8},{8,4},{5,9},{9,5},{6,10},{10,6},{7,11},{11,7},{20,24},{24,20... | collective-permute-start | bytes 9437192 | tf_op jit(solution)/shard_map/ppermute | solution.py:272
  94.8 36.3 %collective-permute-start.6 = (bf16[3,512,512]{2,1,0:T(8,128)(2,1)}, bf16[3,512,512]{2,1,0:T(8,128)(2,1)}, u32[]{:S(2)}, u32[]{:S(2)}) collective-permute-start(bf16[3,512,512]{2,1,0:T(8,128)(2,1)} %get-tuple-element.83.refs_2_), channel_id=1, source_target_pairs={{0,2},{1,3},{2,0},{3,1},{4,6},{5,7},{6,4},{7,5},{8,10},{9,11},{10,... | collective-permute-start | bytes 4718600 | tf_op jit(solution)/shard_map/ppermute | solution.py:269
  104.8 60.1 %collective-permute-start.9 = (bf16[3,512,512]{2,1,0:T(8,128)(2,1)S(1)}, bf16[3,512,512]{2,1,0:T(8,128)(2,1)S(1)}, u32[]{:S(2)}, u32[]{:S(2)}) collective-permute-start(bf16[3,512,512]{2,1,0:T(8,128)(2,1)S(1)} %get-tuple-element.87), channel_id=1, source_target_pairs={{0,2},{1,3},{2,0},{3,1},{4,6},{5,7},{6,4},{7,5},{8,10},{9,11},{10,... | collective-permute-start | bytes 4718600 | tf_op jit(solution)/shard_map/ppermute | solution.py:269
  150.9 76.8 %collective-permute-start.15 = (bf16[2,512,1536]{2,1,0:T(8,128)(2,1)}, bf16[2,512,1536]{2,1,0:T(8,128)(2,1)}, u32[]{:S(2)}, u32[]{:S(2)}) collective-permute-start(bf16[2,512,1536]{2,1,0:T(8,128)(2,1)} %get-tuple-element.89), channel_id=1, source_target_pairs={{4,0},{8,12},{5,1},{9,13},{6,2},{10,14},{7,3},{11,15},{20,16},{24,... | collective-permute-start | bytes 9437192 | tf_op jit(solution)/shard_map/ppermute | solution.py:272
  182.9 35.6 %collective-permute-start.14 = (bf16[3,512,512]{2,1,0:T(8,128)(2,1)}, bf16[3,512,512]{2,1,0:T(8,128)(2,1)}, u32[]{:S(2)}, u32[]{:S(2)}) collective-permute-start(bf16[3,512,512]{2,1,0:T(8,128)(2,1)} %get-tuple-element.92), channel_id=1, source_target_pairs={{0,2},{1,3},{2,0},{3,1},{4,6},{5,7},{6,4},{7,5},{8,10},{9,11},{10,... | collective-permute-start | bytes 4718600 | tf_op jit(solution)/shard_map/ppermute | solution.py:269
  185.2 76.0 %collective-permute-start.25 = (bf16[3,512,512]{2,1,0:T(8,128)(2,1)}, bf16[3,512,512]{2,1,0:T(8,128)(2,1)S(1)}, u32[]{:S(2)}, u32[]{:S(2)}) collective-permute-start(bf16[3,512,512]{2,1,0:T(8,128)(2,1)} %copy-done.11), channel_id=1, source_target_pairs={{0,4},{4,0},{8,12},{12,8},{1,5},{5,1},{9,13},{13,9},{2,6},{6,2},{1... | collective-permute-start | bytes 4718600 | tf_op jit(solution)/shard_map/ppermute | solution.py:272
  232.8 72.7 %collective-permute-start.28 = (bf16[3,512,512]{2,1,0:T(8,128)(2,1)S(1)}, bf16[3,512,512]{2,1,0:T(8,128)(2,1)S(1)}, u32[]{:S(2)}, u32[]{:S(2)}) collective-permute-start(bf16[3,512,512]{2,1,0:T(8,128)(2,1)S(1)} %get-tuple-element.109.refs_2_), channel_id=1, source_target_pairs={{0,8},{4,12},{8,0},{12,4},{1,9},{5,13},{9,1},{13,5},{2,10},{6,14},... | collective-permute-start | bytes 4718600 | tf_op jit(solution)/shard_map/ppermute | solution.py:272
  254.1 29.6 %collective-permute-start.27 = (bf16[1,512,512]{2,1,0:T(8,128)(2,1)S(1)}, bf16[1,512,512]{2,1,0:T(8,128)(2,1)S(1)}, u32[]{:S(2)}, u32[]{:S(2)}) collective-permute-start(bf16[1,512,512]{2,1,0:T(8,128)(2,1)S(1)} %get-tuple-element.107), channel_id=1, source_target_pairs={{0,2},{1,3},{2,0},{3,1},{4,6},{5,7},{6,4},{7,5},{8,10},{9,11},{10,... | collective-permute-start | bytes 1572872 | tf_op jit(solution)/shard_map/ppermute | solution.py:269
  254.4 25.0 %collective-permute-start.26 = (bf16[1,512,512]{2,1,0:T(8,128)(2,1)S(1)}, bf16[1,512,512]{2,1,0:T(8,128)(2,1)S(1)}, u32[]{:S(2)}, u32[]{:S(2)}) collective-permute-start(bf16[1,512,512]{2,1,0:T(8,128)(2,1)S(1)} %get-tuple-element.105), channel_id=1, source_target_pairs={{0,2},{1,3},{2,0},{3,1},{4,6},{5,7},{6,4},{7,5},{8,10},{9,11},{10,... | collective-permute-start | bytes 1572872 | tf_op jit(solution)/shard_map/ppermute | solution.py:269
  262.7 50.5 %collective-permute-start.29 = (bf16[3,512,512]{2,1,0:T(8,128)(2,1)S(1)}, bf16[3,512,512]{2,1,0:T(8,128)(2,1)S(1)}, u32[]{:S(2)}, u32[]{:S(2)}) collective-permute-start(bf16[3,512,512]{2,1,0:T(8,128)(2,1)S(1)} %get-tuple-element.111.refs_2_), channel_id=1, source_target_pairs={{0,2},{1,3},{2,0},{3,1},{4,6},{5,7},{6,4},{7,5},{8,10},{9,11},{10,... | collective-permute-start | bytes 4718600 | tf_op jit(solution)/shard_map/ppermute | solution.py:269
  306.8 40.1 %collective-permute-start.31 = (bf16[3,512,512]{2,1,0:T(8,128)(2,1)S(1)}, bf16[3,512,512]{2,1,0:T(8,128)(2,1)S(1)}, u32[]{:S(2)}, u32[]{:S(2)}) collective-permute-start(bf16[3,512,512]{2,1,0:T(8,128)(2,1)S(1)} %get-tuple-element.119.refs_2_), channel_id=1, source_target_pairs={{0,2},{1,3},{2,0},{3,1},{4,6},{5,7},{6,4},{7,5},{8,10},{9,11},{10,... | collective-permute-start | bytes 4718600 | tf_op jit(solution)/shard_map/ppermute | solution.py:269
  308.0 25.8 %collective-permute-start.30 = (bf16[1,512,512]{2,1,0:T(8,128)(2,1)S(1)}, bf16[1,512,512]{2,1,0:T(8,128)(2,1)S(1)}, u32[]{:S(2)}, u32[]{:S(2)}) collective-permute-start(bf16[1,512,512]{2,1,0:T(8,128)(2,1)S(1)} %get-tuple-element.117.refs_2_), channel_id=1, source_target_pairs={{0,12},{4,8},{8,4},{12,0},{1,13},{5,9},{9,5},{13,1},{2,14},{6,10},... | collective-permute-start | bytes 1572872 | tf_op jit(solution)/shard_map/ppermute | solution.py:272
  310.2 37.2 %collective-permute-start.32 = (bf16[1,512,512]{2,1,0:T(8,128)(2,1)S(1)}, bf16[1,512,512]{2,1,0:T(8,128)(2,1)S(1)}, u32[]{:S(2)}, u32[]{:S(2)}) collective-permute-start(bf16[1,512,512]{2,1,0:T(8,128)(2,1)S(1)} %get-tuple-element.121.refs_2_), channel_id=1, source_target_pairs={{0,12},{4,8},{8,4},{12,0},{1,13},{5,9},{9,5},{13,1},{2,14},{6,10},... | collective-permute-start | bytes 1572872 | tf_op jit(solution)/shard_map/ppermute | solution.py:272
  334.6 23.5 %collective-permute-start.33 = (bf16[1,512,512]{2,1,0:T(8,128)(2,1)S(1)}, bf16[1,512,512]{2,1,0:T(8,128)(2,1)S(1)}, u32[]{:S(2)}, u32[]{:S(2)}) collective-permute-start(bf16[1,512,512]{2,1,0:T(8,128)(2,1)S(1)} %get-tuple-element.124.refs_9_), channel_id=1, source_target_pairs={{0,2},{1,3},{2,0},{3,1},{4,6},{5,7},{6,4},{7,5},{8,10},{9,11},{10,... | collective-permute-start | bytes 1572872 | tf_op jit(solution)/shard_map/ppermute | solution.py:269
  335.8 33.6 %collective-permute-start.34 = (bf16[1,512,512]{2,1,0:T(8,128)(2,1)S(1)}, bf16[1,512,512]{2,1,0:T(8,128)(2,1)S(1)}, u32[]{:S(2)}, u32[]{:S(2)}) collective-permute-start(bf16[1,512,512]{2,1,0:T(8,128)(2,1)S(1)} %get-tuple-element.128.refs_2_), channel_id=1, source_target_pairs={{0,12},{4,8},{8,4},{12,0},{1,13},{5,9},{9,5},{13,1},{2,14},{6,10},... | collective-permute-start | bytes 1572872 | tf_op jit(solution)/shard_map/ppermute | solution.py:272
  348.2 25.4 %collective-permute-start.35 = (bf16[1,512,512]{2,1,0:T(8,128)(2,1)S(1)}, bf16[1,512,512]{2,1,0:T(8,128)(2,1)S(1)}, u32[]{:S(2)}, u32[]{:S(2)}) collective-permute-start(bf16[1,512,512]{2,1,0:T(8,128)(2,1)S(1)} %get-tuple-element.130.refs_9_), channel_id=1, source_target_pairs={{0,2},{1,3},{2,0},{3,1},{4,6},{5,7},{6,4},{7,5},{8,10},{9,11},{10,... | collective-permute-start | bytes 1572872 | tf_op jit(solution)/shard_map/ppermute | solution.py:269
  371.3 25.3 %collective-permute-start.37 = (bf16[1,512,1536]{2,1,0:T(8,128)(2,1)S(1)}, bf16[1,512,1536]{2,1,0:T(8,128)(2,1)S(1)}, u32[]{:S(2)}, u32[]{:S(2)}) collective-permute-start(bf16[1,512,1536]{2,1,0:T(8,128)(2,1)S(1)} %get-tuple-element.136), channel_id=1, source_target_pairs={{0,1},{1,0},{2,3},{3,2},{4,5},{5,4},{6,7},{7,6},{8,9},{9,8},{10,11... | collective-permute-start | bytes 4718600 | tf_op jit(solution)/shard_map/ppermute | solution.py:266
  (32 other events, 343.4 us)

commit v10 on v9

--- a/solution.py
+++ b/solution.py
@@ -187,7 +187,7 @@
 
 def last_gamma(token, place, which, terms, before, shape, result):
     half, rows, depth = before[0].shape
-    tile = tile_of(depth)
+    tile = 2 * TILE if depth % (2 * TILE) == 0 else depth
     in_specs, args, counts = gamma_operands(terms, which, tile, half)
     spec = pl.BlockSpec((1, rows, tile), lambda p, s: (which, 0, p))
     in_specs += [spec, spec]
@@ -207,7 +207,7 @@
         pl.BlockSpec((1, rows, tile), lambda p, s: (0, 0, p)),
     ]
     out = [jax.ShapeDtypeStruct(shape, F32), jax.ShapeDtypeStruct((1, rows, depth), BF16)]
-    return call(kernel, f"last_gamma_{len(terms)}", token, place, (depth // tile,), in_specs, args, out_specs, out, aliases, mib=24)
+    return call(kernel, f"last_gamma_{len(terms)}", token, place, (depth // tile,), in_specs, args, out_specs, out, aliases, mib=36)
 
 
 def place_kernel(place, received, result, out):

time: 412 us -> 409 us (level)
  no operation moved by 1% of the time
where the time goes in v10:
time: 409 us; the launch traced here: 401 us
  waiting for transfers between devices  170 us (42%)
  Pallas kernels  165 us (40%)
  starting transfers between devices  50.1 us (12%)
  local copies, waits for them, and re-layouts  9.83 us (2%)
  other arithmetic  5.18 us (1%)
    pallas_call x32, Pallas kernels, call(): pl.pallas_call(body, out_shape=(*out, TOKEN), grid_spec=pltpu.PrefetchSca...  165 us
    ppermute x12, waiting for transfers between devices, to_chip(): return lax.ppermute(values, 'col', [(q, q ^ 2) for q in range(4)])  98 us
    ppermute x10, waiting for transfers between devices, along(): return lax.ppermute(values, 'row', steps)  58.3 us
    ppermute x10, starting transfers between devices, along(): return lax.ppermute(values, 'row', steps)  25.3 us
    ppermute x12, starting transfers between devices, to_chip(): return lax.ppermute(values, 'col', [(q, q ^ 2) for q in range(4)])  14.1 us
    ppermute x18, waiting for transfers between devices, to_core(): return lax.ppermute(values, 'col', [(q, q ^ 1) for q in range(4)])  14.1 us
    ppermute x18, starting transfers between devices, to_core(): return lax.ppermute(values, 'col', [(q, q ^ 1) for q in range(4)])  10.7 us
  transfers between devices with their start and end apart: 40, of which 12 were waited for; matrix products, arithmetic and copies ran while one was open for 2% of the time, Pallas kernels for 41%

profile of v10, /device:TPU:1, one launch (start us, length us, event | category | flops | bytes accessed | tf_op | source)
XLA Modules:
  0.0 401.2 jit_solution(6389321734343711312)
XLA Ops:
  6.2 13.3 %collective-permute-done.1.refs_5_.refs_6_ = bf16[2,512,1536]{2,1,0:T(8,128)(2,1)} collective-permute-done((bf16[2,512,1536]{2,1,0:T(8,128)(2,1)}, bf16[2,512,1536]{2,1,0:T(8,128)(2,1)}, u32[]{:S(2)}, u32[]{:S(2)}) %collective-permute-start.1) | collective-permute-done | bytes 3145760 | tf_op jit(solution)/shard_map/ppermute | solution.py:266
  21.4 9.4 %pairs_for_chip.6 = (bf16[3,512,512]{2,1,0:T(8,128)(2,1)}, f32[8,128]{1,0:T(8,128)S(1)}) custom-call(s32[2]{0:T(128)S(1)} %pad_add_fusion.refs_0_, f32[8,128]{1,0:T(8,128)S(1)} %broadcast_in_dim.12.refs_1_, bf16[6,512,1536]{2,1,0:T(8,128)(2,1)} %refs_3_.11, bf16[6,512,1536]{2,1,0:T(8,128)(2,1)} %collective-permute-done.refs_3_.refs_4_, ...), custom_call_target="tpu_custom_call" | custom-call | bytes 1024 | tf_op jit(solution)/shard_map/pairs_for_chip/pallas_call | solution.py:31
  33.2 40.8 %collective-permute-done.2.refs_2_ = bf16[2,512,1536]{2,1,0:T(8,128)(2,1)S(1)} collective-permute-done((bf16[2,512,1536]{2,1,0:T(8,128)(2,1)}, bf16[2,512,1536]{2,1,0:T(8,128)(2,1)S(1)}, u32[]{:S(2)}, u32[]{:S(2)}) %collective-permute-start.2) | collective-permute-done | bytes 3145760 | tf_op jit(solution)/shard_map/ppermute | solution.py:272
  82.9 9.3 %own_amplitudes.6 = (bf16[3,512,512]{2,1,0:T(8,128)(2,1)S(1)}, f32[8,128]{1,0:T(8,128)S(1)}) custom-call(s32[2]{0:T(128)S(1)} %pad_add_fusion.refs_0_, f32[3]{0:T(128)S(1)} %dynamic-slice_add_fusion.refs_1_, f32[8,128]{1,0:T(8,128)S(1)} %get-tuple-element.76.refs_2_, bf16[6,512,1536]{2,1,0:T(8,128)(2,1)} %refs_3_.11, ...), custom_call_target="tpu_custom_call" | custom-call | bytes 1024 | tf_op jit(solution)/shard_map/own_amplitudes/pallas_call | solution.py:31
  96.0 8.7 %pairs_for_chip.7 = (bf16[3,512,512]{2,1,0:T(8,128)(2,1)S(1)}, f32[8,128]{1,0:T(8,128)S(1)}) custom-call(s32[2]{0:T(128)S(1)} %pad_add_fusion.refs_0_, f32[8,128]{1,0:T(8,128)S(1)} %get-tuple-element.80.refs_1_, bf16[6,512,1536]{2,1,0:T(8,128)(2,1)} %refs_3_.11, bf16[6,512,1536]{2,1,0:T(8,128)(2,1)} %collective-permute-done.refs_3_.refs_4_, ...), custom_call_target="tpu_custom_call" | custom-call | bytes 1024 | tf_op jit(solution)/shard_map/pairs_for_chip/pallas_call | solution.py:31
  105.1 26.0 %collective-permute-done.6.refs_3_ = bf16[3,512,512]{2,1,0:T(8,128)(2,1)} collective-permute-done((bf16[3,512,512]{2,1,0:T(8,128)(2,1)}, bf16[3,512,512]{2,1,0:T(8,128)(2,1)}, u32[]{:S(2)}, u32[]{:S(2)}) %collective-permute-start.6) | collective-permute-done | bytes 1572896 | tf_op jit(solution)/shard_map/ppermute | solution.py:269
  131.1 15.7 %chip_gamma_1_0.1 = (f32[3,512,1536]{2,1,0:T(8,128)S(1)}, f32[3,512,1536]{2,1,0:T(8,128)}, f32[8,128]{1,0:T(8,128)S(1)}) custom-call(s32[2]{0:T(128)S(1)} %pad_add_fusion.refs_0_, f32[8,128]{1,0:T(8,128)S(1)} %get-tuple-element.82.refs_1_, bf16[3,512,512]{2,1,0:T(8,128)(2,1)} %get-tuple-element.83.refs_2_, ...), custom_call_target="tpu_custom_call" | custom-call | bytes 1024 | tf_op jit(solution)/shard_map/chip_gamma_1_0/pallas_call | solution.py:31
  157.2 7.6 %collective-permute-done.9.refs_7_ = bf16[3,512,512]{2,1,0:T(8,128)(2,1)S(1)} collective-permute-done((bf16[3,512,512]{2,1,0:T(8,128)(2,1)S(1)}, bf16[3,512,512]{2,1,0:T(8,128)(2,1)S(1)}, u32[]{:S(2)}, u32[]{:S(2)}) %collective-permute-start.9) | collective-permute-done | bytes 1572896 | tf_op jit(solution)/shard_map/ppermute | solution.py:269
  164.8 8.5 %own_amplitudes.7 = (bf16[3,512,512]{2,1,0:T(8,128)(2,1)S(1)}, f32[8,128]{1,0:T(8,128)S(1)}) custom-call(s32[2]{0:T(128)S(1)} %pad_add_fusion.refs_0_, f32[3]{0:T(128)S(1)} %dynamic-slice_add_fusion.refs_1_, f32[8,128]{1,0:T(8,128)S(1)} %get-tuple-element.86.refs_2_, bf16[6,512,1536]{2,1,0:T(8,128)(2,1)} %refs_3_.11, ...), custom_call_target="tpu_custom_call" | custom-call | bytes 1024 | tf_op jit(solution)/shard_map/own_amplitudes/pallas_call | solution.py:31
  173.4 9.4 %pairs_for_chip.8 = (bf16[3,512,512]{2,1,0:T(8,128)(2,1)}, f32[8,128]{1,0:T(8,128)S(1)}) custom-call(s32[2]{0:T(128)S(1)} %pad_add_fusion.refs_0_, f32[8,128]{1,0:T(8,128)S(1)} %get-tuple-element.88.refs_1_, bf16[6,512,1536]{2,1,0:T(8,128)(2,1)} %refs_3_.11, bf16[6,512,1536]{2,1,0:T(8,128)(2,1)} %collective-permute-done.refs_3_.refs_4_, ...), custom_call_target="tpu_custom_call" | custom-call | bytes 1024 | tf_op jit(solution)/shard_map/pairs_for_chip/pallas_call | solution.py:31
  185.2 5.0 %collective-permute-start.25 = (bf16[3,512,512]{2,1,0:T(8,128)(2,1)}, bf16[3,512,512]{2,1,0:T(8,128)(2,1)S(1)}, u32[]{:S(2)}, u32[]{:S(2)}) collective-permute-start(bf16[3,512,512]{2,1,0:T(8,128)(2,1)} %copy-done.11), channel_id=1, source_target_pairs={{0,4},{4,0},{8,12},{12,8},{1,5},{5,1},{9,13},{13,9},{2,6},{6,2},{1... | collective-permute-start | bytes 4718600 | tf_op jit(solution)/shard_map/ppermute | solution.py:272
  190.2 28.3 %collective-permute-done.14.refs_8_ = bf16[3,512,512]{2,1,0:T(8,128)(2,1)} collective-permute-done((bf16[3,512,512]{2,1,0:T(8,128)(2,1)}, bf16[3,512,512]{2,1,0:T(8,128)(2,1)}, u32[]{:S(2)}, u32[]{:S(2)}) %collective-permute-start.14) | collective-permute-done | bytes 1572896 | tf_op jit(solution)/shard_map/ppermute | solution.py:269
  218.5 9.2 %own_amplitudes.8 = (bf16[3,512,512]{2,1,0:T(8,128)(2,1)S(1)}, f32[8,128]{1,0:T(8,128)S(1)}) custom-call(s32[2]{0:T(128)S(1)} %pad_add_fusion.refs_0_, f32[3]{0:T(128)S(1)} %dynamic-slice_add_fusion.refs_1_, f32[8,128]{1,0:T(8,128)S(1)} %get-tuple-element.91.refs_2_, bf16[6,512,1536]{2,1,0:T(8,128)(2,1)} %refs_3_.11, ...), custom_call_target="tpu_custom_call" | custom-call | bytes 1024 | tf_op jit(solution)/shard_map/own_amplitudes/pallas_call | solution.py:31
  256.9 4.3 %own_amplitudes.9 = (bf16[1,512,512]{2,1,0:T(8,128)(2,1)S(1)}, f32[8,128]{1,0:T(8,128)S(1)}) custom-call(s32[2]{0:T(128)S(1)} %pad_add_fusion.refs_0_, f32[3]{0:T(128)S(1)} %dynamic-slice_add_fusion.refs_1_, f32[8,128]{1,0:T(8,128)S(1)} %get-tuple-element.100.refs_2_, bf16[6,512,1536]{2,1,0:T(8,128)(2,1)} %refs_3_.11, ...), custom_call_target="tpu_custom_call" | custom-call | bytes 1024 | tf_op jit(solution)/shard_map/own_amplitudes/pallas_call | solution.py:31
  263.9 15.5 %collective-permute-done.26.refs_10_ = bf16[1,512,512]{2,1,0:T(8,128)(2,1)S(1)} collective-permute-done((bf16[1,512,512]{2,1,0:T(8,128)(2,1)S(1)}, bf16[1,512,512]{2,1,0:T(8,128)(2,1)S(1)}, u32[]{:S(2)}, u32[]{:S(2)}) %collective-permute-start.26) | collective-permute-done | bytes 524320 | tf_op jit(solution)/shard_map/ppermute | solution.py:269
  279.4 4.3 %own_amplitudes.10 = (bf16[1,512,512]{2,1,0:T(8,128)(2,1)S(1)}, f32[8,128]{1,0:T(8,128)S(1)}) custom-call(s32[2]{0:T(128)S(1)} %pad_add_fusion.refs_0_, f32[3]{0:T(128)S(1)} %dynamic-slice_add_fusion.refs_1_, f32[8,128]{1,0:T(8,128)S(1)} %get-tuple-element.104.refs_2_, bf16[6,512,1536]{2,1,0:T(8,128)(2,1)} %refs_3_.11, ...), custom_call_target="tpu_custom_call" | custom-call | bytes 1024 | tf_op jit(solution)/shard_map/own_amplitudes/pallas_call | solution.py:31
  283.7 4.3 %own_amplitudes.11 = (bf16[1,512,512]{2,1,0:T(8,128)(2,1)S(1)}, f32[8,128]{1,0:T(8,128)S(1)}) custom-call(s32[2]{0:T(128)S(1)} %pad_add_fusion.refs_0_, f32[3]{0:T(128)S(1)} %dynamic-slice_add_fusion.refs_1_, f32[8,128]{1,0:T(8,128)S(1)} %get-tuple-element.106.refs_2_, bf16[6,512,1536]{2,1,0:T(8,128)(2,1)} %refs_3_.11, ...), custom_call_target="tpu_custom_call" | custom-call | bytes 1024 | tf_op jit(solution)/shard_map/own_amplitudes/pallas_call | solution.py:31
  288.0 17.5 %collective-permute-done.28.refs_3_ = bf16[3,512,512]{2,1,0:T(8,128)(2,1)S(1)} collective-permute-done((bf16[3,512,512]{2,1,0:T(8,128)(2,1)S(1)}, bf16[3,512,512]{2,1,0:T(8,128)(2,1)S(1)}, u32[]{:S(2)}, u32[]{:S(2)}) %collective-permute-start.28) | collective-permute-done | bytes 1572896 | tf_op jit(solution)/shard_map/ppermute | solution.py:272
  313.7 20.1 %chip_gamma_1_2.1 = (f32[3,512,1536]{2,1,0:T(8,128)}, f32[3,512,1536]{2,1,0:T(8,128)}, f32[8,128]{1,0:T(8,128)S(1)}) custom-call(s32[2]{0:T(128)S(1)} %pad_add_fusion.refs_0_, f32[8,128]{1,0:T(8,128)S(1)} %get-tuple-element.112.refs_1_, bf16[3,512,512]{2,1,0:T(8,128)(2,1)S(1)} %get-tuple-element.111.refs_2_, ...), custom_call_target="tpu_custom_call", output_to_operand_aliasing={{0}: (6, {}), {1}: (7, {})} | custom-call | bytes 1024 | tf_op jit(solution)/shard_map/chip_gamma_1_2/pallas_call | solution.py:31
  338.0 8.9 %collective-permute-done.31.refs_2_ = bf16[3,512,512]{2,1,0:T(8,128)(2,1)S(1)} collective-permute-done((bf16[3,512,512]{2,1,0:T(8,128)(2,1)S(1)}, bf16[3,512,512]{2,1,0:T(8,128)(2,1)S(1)}, u32[]{:S(2)}, u32[]{:S(2)}) %collective-permute-start.31) | collective-permute-done | bytes 1572896 | tf_op jit(solution)/shard_map/ppermute | solution.py:269
  349.4 8.7 %collective-permute-done.33.refs_10_ = bf16[1,512,512]{2,1,0:T(8,128)(2,1)S(1)} collective-permute-done((bf16[1,512,512]{2,1,0:T(8,128)(2,1)S(1)}, bf16[1,512,512]{2,1,0:T(8,128)(2,1)S(1)}, u32[]{:S(2)}, u32[]{:S(2)}) %collective-permute-start.33) | collective-permute-done | bytes 524320 | tf_op jit(solution)/shard_map/ppermute | solution.py:269
  358.1 10.5 %last_gamma_2.3 = (f32[6,512,1536]{2,1,0:T(8,128)}, bf16[1,512,1536]{2,1,0:T(8,128)(2,1)S(1)}, f32[8,128]{1,0:T(8,128)S(1)}) custom-call(s32[2]{0:T(128)S(1)} %pad_add_fusion.refs_0_, f32[8,128]{1,0:T(8,128)S(1)} %get-tuple-element.122.refs_1_, bf16[3,512,512]{2,1,0:T(8,128)(2,1)S(1)} %get-tuple-element.119.refs_2_, ...), custom_call_target="tpu_custom_call" | custom-call | bytes 1024 | tf_op jit(solution)/shard_map/last_gamma_2/pallas_call | solution.py:31
  372.7 10.5 %last_gamma_2.4 = (f32[6,512,1536]{2,1,0:T(8,128)}, bf16[1,512,1536]{2,1,0:T(8,128)(2,1)S(1)}, f32[8,128]{1,0:T(8,128)S(1)}) custom-call(s32[2]{0:T(128)S(1)} %pad_add_fusion.refs_0_, f32[8,128]{1,0:T(8,128)S(1)} %get-tuple-element.129.refs_1_, bf16[3,512,512]{2,1,0:T(8,128)(2,1)S(1)} %get-tuple-element.119.refs_2_, ...), custom_call_target="tpu_custom_call", output_to_operand_aliasing={{0}: (22, {})} | custom-call | bytes 1024 | tf_op jit(solution)/shard_map/last_gamma_2/pallas_call | solution.py:31
  383.2 10.5 %last_gamma_2.5 = (f32[6,512,1536]{2,1,0:T(8,128)}, bf16[1,512,1536]{2,1,0:T(8,128)(2,1)S(1)}, f32[8,128]{1,0:T(8,128)S(1)}) custom-call(s32[2]{0:T(128)S(1)} %pad_add_fusion.refs_0_, f32[8,128]{1,0:T(8,128)S(1)} %get-tuple-element.132.refs_1_, bf16[3,512,512]{2,1,0:T(8,128)(2,1)S(1)} %get-tuple-element.119.refs_2_, ...), custom_call_target="tpu_custom_call", output_to_operand_aliasing={{0}: (22, {})} | custom-call | bytes 1024 | tf_op jit(solution)/shard_map/last_gamma_2/pallas_call | solution.py:31
  (131 shorter events, 94.4 us)
Async XLA Ops:
  0.0 19.5 %collective-permute-start = (bf16[6,512,1536]{2,1,0:T(8,128)(2,1)}, bf16[6,512,1536]{2,1,0:T(8,128)(2,1)}, u32[]{:S(2)}, u32[]{:S(2)}) collective-permute-start(bf16[6,512,1536]{2,1,0:T(8,128)(2,1)} %refs_3_.11), channel_id=1, source_target_pairs={{0,1},{1,0},{2,3},{3,2},{4,5},{5,4},{6,7},{7,6},{8,9},{9,8},{10,11... | collective-permute-start | bytes 28311560 | tf_op jit(solution)/shard_map/ppermute | solution.py:266
  0.1 19.4 %collective-permute-start.1 = (bf16[2,512,1536]{2,1,0:T(8,128)(2,1)}, bf16[2,512,1536]{2,1,0:T(8,128)(2,1)}, u32[]{:S(2)}, u32[]{:S(2)}) collective-permute-start(bf16[2,512,1536]{2,1,0:T(8,128)(2,1)} %refs_4_.3), channel_id=1, source_target_pairs={{0,1},{1,0},{2,3},{3,2},{4,5},{5,4},{6,7},{7,6},{8,9},{9,8},{10,11... | collective-permute-start | bytes 9437192 | tf_op jit(solution)/shard_map/ppermute | solution.py:266
  0.5 32.7 %collective-permute-start.3 = (bf16[2,512,1536]{2,1,0:T(8,128)(2,1)}, bf16[2,512,1536]{2,1,0:T(8,128)(2,1)}, u32[]{:S(2)}, u32[]{:S(2)}) collective-permute-start(bf16[2,512,1536]{2,1,0:T(8,128)(2,1)} %refs_4_.3), channel_id=1, source_target_pairs={{4,8},{8,4},{5,9},{9,5},{6,10},{10,6},{7,11},{11,7},{20,24},{24,20... | collective-permute-start | bytes 9437192 | tf_op jit(solution)/shard_map/ppermute | solution.py:272
  2.8 71.2 %collective-permute-start.2 = (bf16[2,512,1536]{2,1,0:T(8,128)(2,1)}, bf16[2,512,1536]{2,1,0:T(8,128)(2,1)S(1)}, u32[]{:S(2)}, u32[]{:S(2)}) collective-permute-start(bf16[2,512,1536]{2,1,0:T(8,128)(2,1)} %refs_4_.3), channel_id=1, source_target_pairs={{0,4},{4,0},{8,12},{12,8},{1,5},{5,1},{9,13},{13,9},{2,6},{6,2},{1... | collective-permute-start | bytes 9437192 | tf_op jit(solution)/shard_map/ppermute | solution.py:272
  30.8 50.2 %collective-permute-start.4 = (bf16[3,512,512]{2,1,0:T(8,128)(2,1)}, bf16[3,512,512]{2,1,0:T(8,128)(2,1)}, u32[]{:S(2)}, u32[]{:S(2)}) collective-permute-start(bf16[3,512,512]{2,1,0:T(8,128)(2,1)} %get-tuple-element.77), channel_id=1, source_target_pairs={{0,2},{1,3},{2,0},{3,1},{4,6},{5,7},{6,4},{7,5},{8,10},{9,11},{10,... | collective-permute-start | bytes 4718600 | tf_op jit(solution)/shard_map/ppermute | solution.py:269
  74.5 21.5 %collective-permute-start.5 = (bf16[2,512,1536]{2,1,0:T(8,128)(2,1)S(1)}, bf16[2,512,1536]{2,1,0:T(8,128)(2,1)}, u32[]{:S(2)}, u32[]{:S(2)}) collective-permute-start(bf16[2,512,1536]{2,1,0:T(8,128)(2,1)S(1)} %get-tuple-element.81.refs_4_.refs_5_), channel_id=1, source_target_pairs={{0,1},{1,0},{2,3},{3,2},{4,5},{5,4},{6,7},{7,6},{8,9},{9,8},{10,11... | collective-permute-start | bytes 9437192 | tf_op jit(solution)/shard_map/ppermute | solution.py:266
  76.0 74.4 %collective-permute-start.8 = (bf16[2,512,1536]{2,1,0:T(8,128)(2,1)}, bf16[2,512,1536]{2,1,0:T(8,128)(2,1)}, u32[]{:S(2)}, u32[]{:S(2)}) collective-permute-start(bf16[2,512,1536]{2,1,0:T(8,128)(2,1)} %get-tuple-element.85), channel_id=1, source_target_pairs={{4,0},{8,12},{5,1},{9,13},{6,2},{10,14},{7,3},{11,15},{20,16},{24,... | collective-permute-start | bytes 9437192 | tf_op jit(solution)/shard_map/ppermute | solution.py:272
  77.3 73.1 %collective-permute-start.7 = (bf16[2,512,1536]{2,1,0:T(8,128)(2,1)S(1)}, bf16[2,512,1536]{2,1,0:T(8,128)(2,1)}, u32[]{:S(2)}, u32[]{:S(2)}) collective-permute-start(bf16[2,512,1536]{2,1,0:T(8,128)(2,1)S(1)} %get-tuple-element.81.refs_4_.refs_5_), channel_id=1, source_target_pairs={{4,8},{8,4},{5,9},{9,5},{6,10},{10,6},{7,11},{11,7},{20,24},{24,20... | collective-permute-start | bytes 9437192 | tf_op jit(solution)/shard_map/ppermute | solution.py:272
  94.8 36.3 %collective-permute-start.6 = (bf16[3,512,512]{2,1,0:T(8,128)(2,1)}, bf16[3,512,512]{2,1,0:T(8,128)(2,1)}, u32[]{:S(2)}, u32[]{:S(2)}) collective-permute-start(bf16[3,512,512]{2,1,0:T(8,128)(2,1)} %get-tuple-element.83.refs_2_), channel_id=1, source_target_pairs={{0,2},{1,3},{2,0},{3,1},{4,6},{5,7},{6,4},{7,5},{8,10},{9,11},{10,... | collective-permute-start | bytes 4718600 | tf_op jit(solution)/shard_map/ppermute | solution.py:269
  104.8 60.1 %collective-permute-start.9 = (bf16[3,512,512]{2,1,0:T(8,128)(2,1)S(1)}, bf16[3,512,512]{2,1,0:T(8,128)(2,1)S(1)}, u32[]{:S(2)}, u32[]{:S(2)}) collective-permute-start(bf16[3,512,512]{2,1,0:T(8,128)(2,1)S(1)} %get-tuple-element.87), channel_id=1, source_target_pairs={{0,2},{1,3},{2,0},{3,1},{4,6},{5,7},{6,4},{7,5},{8,10},{9,11},{10,... | collective-permute-start | bytes 4718600 | tf_op jit(solution)/shard_map/ppermute | solution.py:269
  150.9 76.8 %collective-permute-start.15 = (bf16[2,512,1536]{2,1,0:T(8,128)(2,1)}, bf16[2,512,1536]{2,1,0:T(8,128)(2,1)}, u32[]{:S(2)}, u32[]{:S(2)}) collective-permute-start(bf16[2,512,1536]{2,1,0:T(8,128)(2,1)} %get-tuple-element.89), channel_id=1, source_target_pairs={{4,0},{8,12},{5,1},{9,13},{6,2},{10,14},{7,3},{11,15},{20,16},{24,... | collective-permute-start | bytes 9437192 | tf_op jit(solution)/shard_map/ppermute | solution.py:272
  182.9 35.6 %collective-permute-start.14 = (bf16[3,512,512]{2,1,0:T(8,128)(2,1)}, bf16[3,512,512]{2,1,0:T(8,128)(2,1)}, u32[]{:S(2)}, u32[]{:S(2)}) collective-permute-start(bf16[3,512,512]{2,1,0:T(8,128)(2,1)} %get-tuple-element.92), channel_id=1, source_target_pairs={{0,2},{1,3},{2,0},{3,1},{4,6},{5,7},{6,4},{7,5},{8,10},{9,11},{10,... | collective-permute-start | bytes 4718600 | tf_op jit(solution)/shard_map/ppermute | solution.py:269
  185.2 76.0 %collective-permute-start.25 = (bf16[3,512,512]{2,1,0:T(8,128)(2,1)}, bf16[3,512,512]{2,1,0:T(8,128)(2,1)S(1)}, u32[]{:S(2)}, u32[]{:S(2)}) collective-permute-start(bf16[3,512,512]{2,1,0:T(8,128)(2,1)} %copy-done.11), channel_id=1, source_target_pairs={{0,4},{4,0},{8,12},{12,8},{1,5},{5,1},{9,13},{13,9},{2,6},{6,2},{1... | collective-permute-start | bytes 4718600 | tf_op jit(solution)/shard_map/ppermute | solution.py:272
  232.8 72.7 %collective-permute-start.28 = (bf16[3,512,512]{2,1,0:T(8,128)(2,1)S(1)}, bf16[3,512,512]{2,1,0:T(8,128)(2,1)S(1)}, u32[]{:S(2)}, u32[]{:S(2)}) collective-permute-start(bf16[3,512,512]{2,1,0:T(8,128)(2,1)S(1)} %get-tuple-element.109.refs_2_), channel_id=1, source_target_pairs={{0,8},{4,12},{8,0},{12,4},{1,9},{5,13},{9,1},{13,5},{2,10},{6,14},... | collective-permute-start | bytes 4718600 | tf_op jit(solution)/shard_map/ppermute | solution.py:272
  254.1 29.6 %collective-permute-start.27 = (bf16[1,512,512]{2,1,0:T(8,128)(2,1)S(1)}, bf16[1,512,512]{2,1,0:T(8,128)(2,1)S(1)}, u32[]{:S(2)}, u32[]{:S(2)}) collective-permute-start(bf16[1,512,512]{2,1,0:T(8,128)(2,1)S(1)} %get-tuple-element.107), channel_id=1, source_target_pairs={{0,2},{1,3},{2,0},{3,1},{4,6},{5,7},{6,4},{7,5},{8,10},{9,11},{10,... | collective-permute-start | bytes 1572872 | tf_op jit(solution)/shard_map/ppermute | solution.py:269
  254.4 25.0 %collective-permute-start.26 = (bf16[1,512,512]{2,1,0:T(8,128)(2,1)S(1)}, bf16[1,512,512]{2,1,0:T(8,128)(2,1)S(1)}, u32[]{:S(2)}, u32[]{:S(2)}) collective-permute-start(bf16[1,512,512]{2,1,0:T(8,128)(2,1)S(1)} %get-tuple-element.105), channel_id=1, source_target_pairs={{0,2},{1,3},{2,0},{3,1},{4,6},{5,7},{6,4},{7,5},{8,10},{9,11},{10,... | collective-permute-start | bytes 1572872 | tf_op jit(solution)/shard_map/ppermute | solution.py:269
  262.7 50.5 %collective-permute-start.29 = (bf16[3,512,512]{2,1,0:T(8,128)(2,1)S(1)}, bf16[3,512,512]{2,1,0:T(8,128)(2,1)S(1)}, u32[]{:S(2)}, u32[]{:S(2)}) collective-permute-start(bf16[3,512,512]{2,1,0:T(8,128)(2,1)S(1)} %get-tuple-element.111.refs_2_), channel_id=1, source_target_pairs={{0,2},{1,3},{2,0},{3,1},{4,6},{5,7},{6,4},{7,5},{8,10},{9,11},{10,... | collective-permute-start | bytes 4718600 | tf_op jit(solution)/shard_map/ppermute | solution.py:269
  306.8 40.1 %collective-permute-start.31 = (bf16[3,512,512]{2,1,0:T(8,128)(2,1)S(1)}, bf16[3,512,512]{2,1,0:T(8,128)(2,1)S(1)}, u32[]{:S(2)}, u32[]{:S(2)}) collective-permute-start(bf16[3,512,512]{2,1,0:T(8,128)(2,1)S(1)} %get-tuple-element.119.refs_2_), channel_id=1, source_target_pairs={{0,2},{1,3},{2,0},{3,1},{4,6},{5,7},{6,4},{7,5},{8,10},{9,11},{10,... | collective-permute-start | bytes 4718600 | tf_op jit(solution)/shard_map/ppermute | solution.py:269
  308.0 25.8 %collective-permute-start.30 = (bf16[1,512,512]{2,1,0:T(8,128)(2,1)S(1)}, bf16[1,512,512]{2,1,0:T(8,128)(2,1)S(1)}, u32[]{:S(2)}, u32[]{:S(2)}) collective-permute-start(bf16[1,512,512]{2,1,0:T(8,128)(2,1)S(1)} %get-tuple-element.117.refs_2_), channel_id=1, source_target_pairs={{0,12},{4,8},{8,4},{12,0},{1,13},{5,9},{9,5},{13,1},{2,14},{6,10},... | collective-permute-start | bytes 1572872 | tf_op jit(solution)/shard_map/ppermute | solution.py:272
  310.2 37.2 %collective-permute-start.32 = (bf16[1,512,512]{2,1,0:T(8,128)(2,1)S(1)}, bf16[1,512,512]{2,1,0:T(8,128)(2,1)S(1)}, u32[]{:S(2)}, u32[]{:S(2)}) collective-permute-start(bf16[1,512,512]{2,1,0:T(8,128)(2,1)S(1)} %get-tuple-element.121.refs_2_), channel_id=1, source_target_pairs={{0,12},{4,8},{8,4},{12,0},{1,13},{5,9},{9,5},{13,1},{2,14},{6,10},... | collective-permute-start | bytes 1572872 | tf_op jit(solution)/shard_map/ppermute | solution.py:272
  334.6 23.5 %collective-permute-start.33 = (bf16[1,512,512]{2,1,0:T(8,128)(2,1)S(1)}, bf16[1,512,512]{2,1,0:T(8,128)(2,1)S(1)}, u32[]{:S(2)}, u32[]{:S(2)}) collective-permute-start(bf16[1,512,512]{2,1,0:T(8,128)(2,1)S(1)} %get-tuple-element.124.refs_9_), channel_id=1, source_target_pairs={{0,2},{1,3},{2,0},{3,1},{4,6},{5,7},{6,4},{7,5},{8,10},{9,11},{10,... | collective-permute-start | bytes 1572872 | tf_op jit(solution)/shard_map/ppermute | solution.py:269
  335.8 32.8 %collective-permute-start.34 = (bf16[1,512,512]{2,1,0:T(8,128)(2,1)S(1)}, bf16[1,512,512]{2,1,0:T(8,128)(2,1)S(1)}, u32[]{:S(2)}, u32[]{:S(2)}) collective-permute-start(bf16[1,512,512]{2,1,0:T(8,128)(2,1)S(1)} %get-tuple-element.128.refs_2_), channel_id=1, source_target_pairs={{0,12},{4,8},{8,4},{12,0},{1,13},{5,9},{9,5},{13,1},{2,14},{6,10},... | collective-permute-start | bytes 1572872 | tf_op jit(solution)/shard_map/ppermute | solution.py:272
  348.2 24.6 %collective-permute-start.35 = (bf16[1,512,512]{2,1,0:T(8,128)(2,1)S(1)}, bf16[1,512,512]{2,1,0:T(8,128)(2,1)S(1)}, u32[]{:S(2)}, u32[]{:S(2)}) collective-permute-start(bf16[1,512,512]{2,1,0:T(8,128)(2,1)S(1)} %get-tuple-element.130.refs_9_), channel_id=1, source_target_pairs={{0,2},{1,3},{2,0},{3,1},{4,6},{5,7},{6,4},{7,5},{8,10},{9,11},{10,... | collective-permute-start | bytes 1572872 | tf_op jit(solution)/shard_map/ppermute | solution.py:269
  370.5 23.7 %collective-permute-start.37 = (bf16[1,512,1536]{2,1,0:T(8,128)(2,1)S(1)}, bf16[1,512,1536]{2,1,0:T(8,128)(2,1)S(1)}, u32[]{:S(2)}, u32[]{:S(2)}) collective-permute-start(bf16[1,512,1536]{2,1,0:T(8,128)(2,1)S(1)} %get-tuple-element.136), channel_id=1, source_target_pairs={{0,1},{1,0},{2,3},{3,2},{4,5},{5,4},{6,7},{7,6},{8,9},{9,8},{10,11... | collective-permute-start | bytes 4718600 | tf_op jit(solution)/shard_map/ppermute | solution.py:266
  (32 other events, 341.7 us)
